TPU v7x, 32 devices: a whole 2x2x4 slice. The times are simulated.
32 devices in a mesh: img: 4 (over x, core), pix: 8 (over z, y).
Axes of the slice: x: 2, y: 2, z: 4, core: 2. Of those that a mesh axis runs over, the one named last changes fastest.
Arguments:
- rgb_pixels: bfloat16 [16, 3, 50176], P('img', None, 'pix'), may hold values from -6 to 6
- keep_mask: int32 [16, 50176], P('img', 'pix'), may hold values 0 or 1
- latent_array: bfloat16 [512, 1024], P('pix'), may hold values from -6 to 6
- gain_input: float32 [261], replicated, may hold values from 0.5 to 1.5
- gain_latent: float32 [1024], replicated, may hold values from 0.5 to 1.5
- w_query: bfloat16 [1024, 1024], P('pix'), may hold values from -0.1875 to 0.1875
- w_key: bfloat16 [261, 1024], P(None, 'pix'), may hold values from -0.375 to 0.375
- w_value: bfloat16 [261, 1024], P(None, 'pix'), may hold values from -0.375 to 0.375
- w_cross_out: bfloat16 [1024, 1024], P('pix'), may hold values from -0.75 to 0.75
- gain_mlp_one: float32 [1024], replicated, may hold values from 0.5 to 1.5
- w_up_one: bfloat16 [1024, 1024], P(None, 'pix'), may hold values from -0.1875 to 0.1875
- w_down_one: bfloat16 [1024, 1024], P('pix'), may hold values from -0.1875 to 0.1875
- gain_self: float32 [1024], replicated, may hold values from 0.5 to 1.5
- w_self_query: bfloat16 [1024, 1024], P('pix'), may hold values from -0.1875 to 0.1875
- w_self_key: bfloat16 [1024, 1024], P('pix'), may hold values from -0.1875 to 0.1875
- w_self_value: bfloat16 [1024, 1024], P('pix'), may hold values from -0.1875 to 0.1875
- w_self_out: bfloat16 [1024, 1024], P('pix'), may hold values from -1 to 1
- gain_mlp_two: float32 [1024], replicated, may hold values from 0.5 to 1.5
- w_up_two: bfloat16 [1024, 1024], P(None, 'pix'), may hold values from -0.1875 to 0.1875
- w_down_two: bfloat16 [1024, 1024], P('pix'), may hold values from -0.1875 to 0.1875
- cotangent: bfloat16 [16, 512, 1024], P('img', 'pix'), may hold values from -6 to 6
Outputs:
- latent_out: bfloat16 [16, 512, 1024], P('img', 'pix')
- grad_pixels: float32 [16, 3, 50176], P('img', None, 'pix')
- grad_latent_array: float32 [512, 1024], P('pix')
- grad_gain_input: float32 [261], replicated
- grad_gain_latent: float32 [1024], replicated
- grad_w_query: float32 [1024, 1024], P('pix')
- grad_w_key: float32 [261, 1024], P(None, 'pix')
- grad_w_value: float32 [261, 1024], P(None, 'pix')
- grad_w_cross_out: float32 [1024, 1024], P('pix')
- grad_gain_mlp_one: float32 [1024], replicated
- grad_w_up_one: float32 [1024, 1024], P(None, 'pix')
- grad_w_down_one: float32 [1024, 1024], P('pix')
- grad_gain_self: float32 [1024], replicated
- grad_w_self_query: float32 [1024, 1024], P('pix')
- grad_w_self_key: float32 [1024, 1024], P('pix')
- grad_w_self_value: float32 [1024, 1024], P('pix')
- grad_w_self_out: float32 [1024, 1024], P('pix')
- grad_gain_mlp_two: float32 [1024], replicated
- grad_w_up_two: float32 [1024, 1024], P(None, 'pix')
- grad_w_down_two: float32 [1024, 1024], P('pix')
All inputs are finite; a program needn't handle non-finite values. No bound on the sum of `keep_mask` on one device may be relied on, other than what follows from the above.
Results may differ from a plain program's by a relative error of at most 0.033.
Values may be sent and summed in bfloat16 or wider, within the bound.
A program may use at most 448 MiB of HBM per device.

v0:
```python
import jax
import jax.numpy as jnp
from jax import lax
from jax.sharding import PartitionSpec as P

HEADS = 8
HEAD_DIM = 128
BANDS = 64
SIDE = 224


eps = 1e-05


def merged(value, axis, join):
    pieces = jax.tree.map(lambda part: lax.all_gather(part, axis), value)
    head = jax.tree.map(lambda part: part[0], pieces)
    tail = jax.tree.map(lambda part: part[1:], pieces)
    total, _ = lax.scan(lambda total, share: (join(total, share), None), head, tail)
    return total


def layer_norm(rows, gain):
    average = jnp.mean(rows, axis=-1, keepdims=True)
    centred = rows - average
    spread = jnp.mean(centred * centred, axis=-1, keepdims=True)
    return centred * lax.rsqrt(spread + eps) * gain


def fourier_rows(position, image_side, band_count):
    row_pos = (position // image_side).astype(jnp.float32) * (2.0 / (image_side - 1)) - 1.0
    col_pos = (position % image_side).astype(jnp.float32) * (2.0 / (image_side - 1)) - 1.0
    band_steps = lax.iota(jnp.int32, band_count).astype(jnp.float32)
    frequency = 1.0 + band_steps * ((image_side / 2.0 - 1.0) / (band_count - 1))
    row_angle = jnp.pi * row_pos[:, None] * frequency[None, :]
    col_angle = jnp.pi * col_pos[:, None] * frequency[None, :]
    return jnp.concatenate(
        [
            row_pos[:, None],
            col_pos[:, None],
            jnp.sin(row_angle),
            jnp.sin(col_angle),
            jnp.cos(row_angle),
            jnp.cos(col_angle),
        ],
        axis=1,
    )


def merge_softmax(first, second):
    highest = jnp.maximum(first[0], second[0])
    return (
        highest,
        first[1] * jnp.exp(first[0] - highest) + second[1] * jnp.exp(second[0] - highest),
    )


def share_rows(rows):
    return lax.all_gather(rows, "pix", axis=0, tiled=True)


def sum_rows(term, count):
    return lax.psum_scatter(
        term(jnp.int32(0), count * lax.axis_size("pix")).astype(jnp.bfloat16),
        "pix",
        scatter_dimension=0,
        tiled=True,
    ).astype(jnp.float32)


def feed_forward(resid, gain, up_mat, down_mat):
    normed = layer_norm(resid, gain).astype(jnp.bfloat16)
    group_rows = share_rows(normed)
    pre_act = jnp.dot(group_rows, up_mat, preferred_element_type=jnp.float32)
    hidden = jax.nn.gelu(pre_act).astype(jnp.bfloat16)

    def project(first, count):
        return jnp.dot(hidden, down_mat, preferred_element_type=jnp.float32)

    branch = sum_rows(project, resid.shape[0])
    return (resid + branch, (group_rows, pre_act, hidden))


def feed_back(resid, gain, up_mat, down_mat, saved, grad_resid):
    group_rows, pre_act, hidden = saved
    grad_branch = grad_resid.astype(jnp.bfloat16)
    grad_group = share_rows(grad_branch)
    grad_down = jnp.einsum("rh,rd->hd", hidden, grad_group, preferred_element_type=jnp.float32)
    grad_hidden = jnp.einsum("rd,hd->rh", grad_group, down_mat, preferred_element_type=jnp.float32)
    _, gelu_back = jax.vjp(jax.nn.gelu, pre_act)
    grad_pre = gelu_back(grad_hidden)[0].astype(jnp.bfloat16)
    grad_up = jnp.einsum("rd,rh->dh", group_rows, grad_pre, preferred_element_type=jnp.float32)

    def spread_back(first, count):
        return jnp.einsum("rh,dh->rd", grad_pre, up_mat, preferred_element_type=jnp.float32)

    grad_normed = sum_rows(spread_back, resid.shape[0])
    _, norm_back = jax.vjp(layer_norm, resid, gain)
    grad_input, grad_gain = norm_back(grad_normed)
    return (grad_resid + grad_input, grad_gain, grad_up, grad_down)


def local(
    rgb_pixels,
    keep_mask,
    latent_array,
    gain_input,
    gain_latent,
    w_query,
    w_key,
    w_value,
    w_cross_out,
    gain_mlp_one,
    w_up_one,
    w_down_one,
    gain_self,
    w_self_query,
    w_self_key,
    w_self_value,
    w_self_out,
    gain_mlp_two,
    w_up_two,
    w_down_two,
    cotangent,
):
    images = rgb_pixels.shape[0]
    pixels_here = rgb_pixels.shape[2]
    rows_here = latent_array.shape[0]
    width = latent_array.shape[1]
    rows_flat = images * rows_here
    pix_index = lax.axis_index("pix")
    width_scale = width ** (-0.5)
    head_scale = HEAD_DIM ** (-0.5)
    (
        latent_full,
        query_mat,
        key_mat,
        value_mat,
        cross_out,
        self_query,
        self_key,
        self_value,
        self_out,
    ) = (
        lax.all_gather(latent_array, "pix", axis=0, tiled=True),
        lax.all_gather(w_query, "pix", axis=0, tiled=True),
        lax.all_gather(w_key, "pix", axis=1, tiled=True),
        lax.all_gather(w_value, "pix", axis=1, tiled=True),
        lax.all_gather(w_cross_out, "pix", axis=0, tiled=True),
        lax.all_gather(w_self_query, "pix", axis=0, tiled=True),
        lax.all_gather(w_self_key, "pix", axis=0, tiled=True),
        lax.all_gather(w_self_value, "pix", axis=0, tiled=True),
        lax.all_gather(w_self_out, "pix", axis=0, tiled=True),
    )
    up_one, down_one, up_two, down_two = (w_up_one, w_down_one, w_up_two, w_down_two)
    position = pix_index * pixels_here + lax.iota(jnp.int32, pixels_here)
    features = fourier_rows(position, SIDE, BANDS)
    colours = jnp.swapaxes(rgb_pixels, 1, 2).astype(jnp.float32)
    inputs = jnp.concatenate(
        [colours, jnp.broadcast_to(features[None], (images,) + features.shape)], axis=2
    )
    normed_in = layer_norm(inputs, gain_input).astype(jnp.bfloat16)
    keys = jnp.einsum("ipc,cd->ipd", normed_in, key_mat, preferred_element_type=jnp.float32).astype(
        jnp.bfloat16
    )
    values = jnp.einsum(
        "ipc,cd->ipd", normed_in, value_mat, preferred_element_type=jnp.float32
    ).astype(jnp.bfloat16)
    latent_float = latent_full.astype(jnp.float32)
    latent_normed = layer_norm(latent_float, gain_latent).astype(jnp.bfloat16)
    queries = jnp.dot(latent_normed, query_mat, preferred_element_type=jnp.float32).astype(
        jnp.bfloat16
    )
    allowed = keep_mask.astype(jnp.float32)[:, None, :]
    scores = (
        jnp.einsum("qd,ipd->iqp", queries, keys, preferred_element_type=jnp.float32) * width_scale
    )
    local_top = jnp.max(scores, axis=2)
    local_total = jnp.sum(jnp.exp(scores - local_top[:, :, None]) * allowed, axis=2)
    row_top, row_total = merged((local_top, local_total), "pix", merge_softmax)
    probs_low = (jnp.exp(scores - row_top[:, :, None]) * allowed / row_total[:, :, None]).astype(
        jnp.bfloat16
    )
    summed_rows = lax.psum_scatter(
        jnp.einsum("iqp,ipd->qid", probs_low, values, preferred_element_type=jnp.float32).astype(
            jnp.bfloat16
        ),
        "pix",
        scatter_dimension=0,
        tiled=True,
    ).astype(jnp.float32)
    attended = jnp.swapaxes(summed_rows, 0, 1).astype(jnp.bfloat16)
    resid_one = latent_array.astype(jnp.float32)[None] + jnp.einsum(
        "ird,de->ire", attended, cross_out, preferred_element_type=jnp.float32
    )
    resid_one_flat = resid_one.reshape(rows_flat, width)
    resid_two, saved_one = feed_forward(resid_one_flat, gain_mlp_one, up_one, down_one)
    normed_two = layer_norm(resid_two, gain_self).astype(jnp.bfloat16)
    head_queries = (
        jnp.dot(normed_two, self_query, preferred_element_type=jnp.float32)
        .astype(jnp.bfloat16)
        .reshape(images, rows_here, HEADS, HEAD_DIM)
    )
    local_keys = (
        jnp.dot(normed_two, self_key, preferred_element_type=jnp.float32)
        .astype(jnp.bfloat16)
        .reshape(images, rows_here, width)
    )
    local_values = (
        jnp.dot(normed_two, self_value, preferred_element_type=jnp.float32)
        .astype(jnp.bfloat16)
        .reshape(images, rows_here, width)
    )
    keys_all, values_all = (
        lax.all_gather(local_keys, "pix", axis=1, tiled=True),
        lax.all_gather(local_values, "pix", axis=1, tiled=True),
    )
    head_keys = keys_all.reshape(images, keys_all.shape[1], HEADS, HEAD_DIM)
    head_values = values_all.reshape(images, values_all.shape[1], HEADS, HEAD_DIM)
    scores_two = (
        jnp.einsum("irhd,ikhd->ihrk", head_queries, head_keys, preferred_element_type=jnp.float32)
        * head_scale
    )
    shifted = jnp.exp(scores_two - jnp.max(scores_two, axis=3, keepdims=True))
    probs_two = shifted / jnp.sum(shifted, axis=3, keepdims=True)
    probs_two_low = probs_two.astype(jnp.bfloat16)
    mixed = (
        jnp.einsum(
            "ihrk,ikhd->irhd", probs_two_low, head_values, preferred_element_type=jnp.float32
        )
        .reshape(rows_flat, width)
        .astype(jnp.bfloat16)
    )
    resid_three = resid_two + jnp.dot(mixed, self_out, preferred_element_type=jnp.float32)
    final, saved_two = feed_forward(resid_three, gain_mlp_two, up_two, down_two)
    latent_out = final.astype(jnp.bfloat16).reshape(images, rows_here, width)
    grad_final = cotangent.astype(jnp.float32).reshape(rows_flat, width)
    grad_three, grad_gain_two, grad_up_two, grad_down_two = feed_back(
        resid_three, gain_mlp_two, up_two, down_two, saved_two, grad_final
    )
    grad_branch = grad_three.astype(jnp.bfloat16)
    grad_self_out = jnp.einsum("rd,re->de", mixed, grad_branch, preferred_element_type=jnp.float32)
    grad_mixed = (
        jnp.einsum("re,de->rd", grad_branch, self_out, preferred_element_type=jnp.float32)
        .astype(jnp.bfloat16)
        .reshape(images, rows_here, HEADS, HEAD_DIM)
    )
    grad_probs_two = jnp.einsum(
        "irhd,ikhd->ihrk", grad_mixed, head_values, preferred_element_type=jnp.float32
    )
    grad_vals_all = jnp.einsum(
        "ihrk,irhd->ikhd", probs_two_low, grad_mixed, preferred_element_type=jnp.float32
    ).reshape(images, -1, width)
    delta_two = jnp.sum(probs_two * grad_probs_two, axis=3, keepdims=True)
    grad_scores_two = (probs_two * (grad_probs_two - delta_two)).astype(jnp.bfloat16)
    grad_queries_two = (
        (
            jnp.einsum(
                "ihrk,ikhd->irhd", grad_scores_two, head_keys, preferred_element_type=jnp.float32
            )
            * head_scale
        )
        .astype(jnp.bfloat16)
        .reshape(rows_flat, width)
    )
    grad_keys_all = (
        jnp.einsum(
            "ihrk,irhd->ikhd", grad_scores_two, head_queries, preferred_element_type=jnp.float32
        )
        * head_scale
    ).reshape(images, -1, width)
    grad_keys_own, grad_vals_own = (
        lax.psum_scatter(
            grad_keys_all.astype(jnp.bfloat16), "pix", scatter_dimension=1, tiled=True
        ).astype(jnp.float32),
        lax.psum_scatter(
            grad_vals_all.astype(jnp.bfloat16), "pix", scatter_dimension=1, tiled=True
        ).astype(jnp.float32),
    )
    grad_keys_low = grad_keys_own.astype(jnp.bfloat16).reshape(rows_flat, width)
    grad_vals_low = grad_vals_own.astype(jnp.bfloat16).reshape(rows_flat, width)
    grad_self_query = jnp.einsum(
        "rd,re->de", normed_two, grad_queries_two, preferred_element_type=jnp.float32
    )
    grad_self_key = jnp.einsum(
        "rd,re->de", normed_two, grad_keys_low, preferred_element_type=jnp.float32
    )
    grad_self_value = jnp.einsum(
        "rd,re->de", normed_two, grad_vals_low, preferred_element_type=jnp.float32
    )
    grad_normed_two = jnp.einsum(
        "re,de->rd", grad_queries_two, self_query, preferred_element_type=jnp.float32
    )
    grad_normed_two = grad_normed_two + jnp.einsum(
        "re,de->rd", grad_keys_low, self_key, preferred_element_type=jnp.float32
    )
    grad_normed_two = grad_normed_two + jnp.einsum(
        "re,de->rd", grad_vals_low, self_value, preferred_element_type=jnp.float32
    )
    _, norm_two_back = jax.vjp(layer_norm, resid_two, gain_self)
    grad_in_two, grad_gain_attn = norm_two_back(grad_normed_two)
    grad_two = grad_three + grad_in_two
    grad_one, grad_gain_one, grad_up_one, grad_down_one = feed_back(
        resid_one_flat, gain_mlp_one, up_one, down_one, saved_one, grad_two
    )
    grad_cross = grad_one.astype(jnp.bfloat16).reshape(images, rows_here, width)
    grad_cross_out = jnp.einsum(
        "ird,ire->de", attended, grad_cross, preferred_element_type=jnp.float32
    )
    grad_attended = jnp.einsum(
        "ire,de->ird", grad_cross, cross_out, preferred_element_type=jnp.float32
    ).astype(jnp.bfloat16)
    latent_residual = jnp.sum(grad_one.reshape(images, rows_here, width), axis=0)
    grad_att_all = lax.all_gather(grad_attended, "pix", axis=1, tiled=True)
    scores_again = (
        jnp.einsum("qd,ipd->iqp", queries, keys, preferred_element_type=jnp.float32) * width_scale
    )
    probs_true = jnp.exp(scores_again - row_top[:, :, None]) * allowed / row_total[:, :, None]
    probs_again = probs_true.astype(jnp.bfloat16)
    grad_probs_one = jnp.einsum(
        "iqd,ipd->iqp", grad_att_all, values, preferred_element_type=jnp.float32
    )
    delta_one = lax.psum(jnp.sum(probs_true * grad_probs_one, axis=2), "pix")
    grad_scores_one = (probs_true * (grad_probs_one - delta_one[:, :, None])).astype(jnp.bfloat16)
    grad_values = jnp.einsum(
        "iqp,iqd->ipd", probs_again, grad_att_all, preferred_element_type=jnp.float32
    ).astype(jnp.bfloat16)
    grad_keys = (
        jnp.einsum("iqp,qd->ipd", grad_scores_one, queries, preferred_element_type=jnp.float32)
        * width_scale
    ).astype(jnp.bfloat16)
    grad_queries_part = (
        jnp.einsum("iqp,ipd->qd", grad_scores_one, keys, preferred_element_type=jnp.float32)
        * width_scale
    )
    grad_key_mat = jnp.einsum(
        "ipc,ipd->cd", normed_in, grad_keys, preferred_element_type=jnp.float32
    )
    grad_value_mat = jnp.einsum(
        "ipc,ipd->cd", normed_in, grad_values, preferred_element_type=jnp.float32
    )
    grad_normed_in = jnp.einsum(
        "ipd,cd->ipc", grad_keys, key_mat, preferred_element_type=jnp.float32
    )
    grad_normed_in = grad_normed_in + jnp.einsum(
        "ipd,cd->ipc", grad_values, value_mat, preferred_element_type=jnp.float32
    )
    _, input_back = jax.vjp(layer_norm, inputs, gain_input)
    grad_inputs, grad_gain_in_part = input_back(grad_normed_in)
    grad_pixels = jnp.swapaxes(grad_inputs[:, :, :3], 1, 2)
    grad_queries_sum, grad_gain_input, grad_gain_mlp_one, grad_gain_self, grad_gain_mlp_two = (
        lax.psum(
            (grad_queries_part, grad_gain_in_part, grad_gain_one, grad_gain_attn, grad_gain_two),
            ("img", "pix"),
        )
    )
    queries_grad_low = grad_queries_sum.astype(jnp.bfloat16)
    rows_query = w_query.shape[0]
    latent_cols = lax.dynamic_slice_in_dim(latent_normed, pix_index * rows_query, rows_query, 1)
    grad_w_query = jnp.einsum(
        "lr,ld->rd", latent_cols, queries_grad_low, preferred_element_type=jnp.float32
    )
    grad_latent_normed = jnp.einsum(
        "ld,rd->lr", queries_grad_low, query_mat, preferred_element_type=jnp.float32
    )
    _, latent_back = jax.vjp(layer_norm, latent_float, gain_latent)
    grad_latent_full, grad_gain_latent = latent_back(grad_latent_normed)
    grad_latent_own = lax.dynamic_slice_in_dim(
        grad_latent_full, pix_index * rows_here, rows_here, 0
    )
    (
        cross_key_part,
        cross_value_part,
        cross_output_part,
        latent_query_part,
        latent_key_part,
        latent_value_part,
        latent_output_part,
    ) = (
        lax.psum_scatter(
            grad_key_mat.astype(jnp.bfloat16), "pix", scatter_dimension=1, tiled=True
        ).astype(jnp.float32),
        lax.psum_scatter(
            grad_value_mat.astype(jnp.bfloat16), "pix", scatter_dimension=1, tiled=True
        ).astype(jnp.float32),
        lax.psum_scatter(
            grad_cross_out.astype(jnp.bfloat16), "pix", scatter_dimension=0, tiled=True
        ).astype(jnp.float32),
        lax.psum_scatter(
            grad_self_query.astype(jnp.bfloat16), "pix", scatter_dimension=0, tiled=True
        ).astype(jnp.float32),
        lax.psum_scatter(
            grad_self_key.astype(jnp.bfloat16), "pix", scatter_dimension=0, tiled=True
        ).astype(jnp.float32),
        lax.psum_scatter(
            grad_self_value.astype(jnp.bfloat16), "pix", scatter_dimension=0, tiled=True
        ).astype(jnp.float32),
        lax.psum_scatter(
            grad_self_out.astype(jnp.bfloat16), "pix", scatter_dimension=0, tiled=True
        ).astype(jnp.float32),
    )
    shard_up_one, shard_down_one, shard_up_two, shard_down_two = (
        grad_up_one,
        grad_down_one,
        grad_up_two,
        grad_down_two,
    )
    (
        grad_w_key,
        grad_w_value,
        grad_w_cross_out,
        grad_w_self_query,
        grad_w_self_key,
        grad_w_self_value,
        grad_w_self_out,
        grad_w_up_one,
        grad_w_down_one,
        grad_w_up_two,
        grad_w_down_two,
        latent_summed,
    ) = (
        lax.psum(cross_key_part.astype(jnp.bfloat16), "img").astype(jnp.float32),
        lax.psum(cross_value_part.astype(jnp.bfloat16), "img").astype(jnp.float32),
        lax.psum(cross_output_part.astype(jnp.bfloat16), "img").astype(jnp.float32),
        lax.psum(latent_query_part.astype(jnp.bfloat16), "img").astype(jnp.float32),
        lax.psum(latent_key_part.astype(jnp.bfloat16), "img").astype(jnp.float32),
        lax.psum(latent_value_part.astype(jnp.bfloat16), "img").astype(jnp.float32),
        lax.psum(latent_output_part.astype(jnp.bfloat16), "img").astype(jnp.float32),
        lax.psum(shard_up_one.astype(jnp.bfloat16), "img").astype(jnp.float32),
        lax.psum(shard_down_one.astype(jnp.bfloat16), "img").astype(jnp.float32),
        lax.psum(shard_up_two.astype(jnp.bfloat16), "img").astype(jnp.float32),
        lax.psum(shard_down_two.astype(jnp.bfloat16), "img").astype(jnp.float32),
        lax.psum(latent_residual.astype(jnp.bfloat16), "img").astype(jnp.float32),
    )
    grad_latent_array = latent_summed + grad_latent_own
    return (
        latent_out,
        grad_pixels,
        grad_latent_array,
        grad_gain_input,
        grad_gain_latent,
        grad_w_query,
        grad_w_key,
        grad_w_value,
        grad_w_cross_out,
        grad_gain_mlp_one,
        grad_w_up_one,
        grad_w_down_one,
        grad_gain_self,
        grad_w_self_query,
        grad_w_self_key,
        grad_w_self_value,
        grad_w_self_out,
        grad_gain_mlp_two,
        grad_w_up_two,
        grad_w_down_two,
    )


def solution(mesh):
    return jax.shard_map(
        local,
        mesh=mesh,
        in_specs=(
            P("img", None, "pix"),
            P("img", "pix"),
            P("pix", None),
            P(),
            P(),
            P("pix", None),
            P(None, "pix"),
            P(None, "pix"),
            P("pix", None),
            P(),
            P(None, "pix"),
            P("pix", None),
            P(),
            P("pix", None),
            P("pix", None),
            P("pix", None),
            P("pix", None),
            P(),
            P(None, "pix"),
            P("pix", None),
            P("img", "pix", None),
        ),
        out_specs=(
            P("img", "pix", None),
            P("img", None, "pix"),
            P("pix", None),
            P(),
            P(),
            P("pix", None),
            P(None, "pix"),
            P(None, "pix"),
            P("pix", None),
            P(),
            P(None, "pix"),
            P("pix", None),
            P(),
            P("pix", None),
            P("pix", None),
            P("pix", None),
            P("pix", None),
            P(),
            P(None, "pix"),
            P("pix", None),
        ),
        check_vma=False,
    )
```

profile of v0, /device:TPU:0, one launch (start us, length us, event | category | flops | bytes accessed | tf_op | source)
XLA Modules:
  0.0 2676.4 jit_solution(4938616403629773454)
XLA Ops:
  132.4 37.7 %convolution_convert_fusion.1 = bf16[4,6272,1024]{2,1,0:T(8,128)(2,1)} fusion(bf16[261,1024]{1,0:T(8,128)(2,1)S(1)} %copy-done.52, f32[4,6272,258]{1,2,0:T(8,128)} %copy-done.2, f32[4,6272,3]{1,2,0:T(4,128)S(1)} %copy-done.28, f32[261]{0:T(512)S(1)} %copy-done.102, f32[4,6272]{1,0:T(4,128)S(1)} %fusion.114, f32[4,6272]{1,0:T(4,128)S(1)} %copy-done.45), kind=kOutput, calls=%fused_computation.19 | convolution fusion | flops 13468667904 | bytes 78308368 | tf_op jit(solution)/shard_map/ipc,cd->ipd/dot_general | solution.py:163
  170.1 38.0 %convolution_convert_fusion.2 = bf16[4,6272,1024]{2,1,0:T(8,128)(2,1)} fusion(bf16[261,1024]{1,0:T(8,128)(2,1)S(1)} %copy-done.50, f32[4,6272,258]{1,2,0:T(8,128)} %copy-done.2, f32[4,6272,3]{1,2,0:T(4,128)S(1)} %copy-done.28, f32[261]{0:T(512)S(1)} %copy-done.102, f32[4,6272]{1,0:T(4,128)S(1)} %fusion.114, f32[4,6272]{1,0:T(4,128)S(1)} %copy-done.45), kind=kOutput, calls=%fused_computation.20 | convolution fusion | flops 13468667904 | bytes 78308368 | tf_op jit(solution)/shard_map/ipc,cd->ipd/dot_general | solution.py:166
  217.3 43.1 %bitcast_reduce_fusion = (f32[4,512]{1,0:T(4,128)S(1)}, f32[4,6272,512]{2,1,0:T(8,128)}) fusion(bf16[4,6272,1024]{2,1,0:T(8,128)(2,1)} %convolution_convert_fusion.1, bf16[512,1024,1]{1,0,2:T(8,128)(2,1)S(1)} %fusion.42), kind=kOutput, calls=%fused_computation.9 | convolution fusion | flops 26332362752 | bytes 103817216 | tf_op jit(solution)/shard_map/qd,ipd->iqp/dot_general | solution.py:176
  343.6 43.6 %convert_bitcast_fusion = bf16[512,4,1024]{0,2,1:T(8,128)(2,1)} fusion(bf16[4,6272,1024]{2,1,0:T(8,128)(2,1)} %convolution_convert_fusion.2, f32[4,6272,512]{2,1,0:T(8,128)} %get-tuple-element.193, f32[4,512]{1,0:T(4,128)S(1)} %get-tuple-element.49, f32[4,512]{1,0:T(4,128)S(1)} %get-tuple-element.48, f32[4,6272]{1,0:T(4,128)S(1)} %copy-done.47), kind=kOutput, calls=%fused_computation.42 | convolution fusion | flops 26372997120 | bytes 107071488 | tf_op jit(solution)/shard_map/iqp,ipd->qid/dot_general | solution.py:185
  397.5 152.6 %all-reduce.7.cloned.1.call-done = bf16[512,4,1024]{2,1,0:T(4,128)(2,1)} async-done(((bf16[512,4,1024]{2,1,0:T(4,128)(2,1)}), bf16[512,4,1024]{2,1,0:T(4,128)(2,1)}) %all-reduce.7.cloned.1.call-update) | async-done | bytes 4194320
  551.3 49.1 %all-gather.23.cloned.1.call-done = bf16[1024,1024]{1,0:T(8,128)(2,1)} async-done(((bf16[128,1024]{1,0:T(8,128)(2,1)}), bf16[1024,1024]{1,0:T(8,128)(2,1)}) %all-gather.23.cloned.1.call-update) | async-done | bytes 2097168 | tf_op jit(solution)/shard_map/all_gather | solution.py:149
  604.4 72.0 %all-gather.25.cloned.1.call-done = bf16[2048,1024]{1,0:T(8,128)(2,1)} async-done(((bf16[256,1024]{1,0:T(8,128)(2,1)}), bf16[2048,1024]{1,0:T(8,128)(2,1)}) %all-gather.25.cloned.1.call-update) | async-done | bytes 4194320 | tf_op jit(solution)/shard_map/all_gather | solution.py:59
  686.4 84.2 %reduce-scatter.18.cloned.1.call-done = bf16[256,1024]{1,0:T(8,128)(2,1)} async-done(((bf16[2048,1024]{1,0:T(8,128)(2,1)}), bf16[256,1024]{1,0:T(8,128)(2,1)}) %reduce-scatter.18.cloned.1.call-update) | async-done | bytes 524304 | tf_op jit(solution)/shard_map/reduce_scatter | solution.py:63
  772.4 49.7 %all-gather.33.cloned.1.call-done = bf16[1024,1024]{1,0:T(8,128)(2,1)} async-done(((bf16[128,1024]{1,0:T(8,128)(2,1)}), bf16[1024,1024]{1,0:T(8,128)(2,1)}) %all-gather.33.cloned.1.call-update) | async-done | bytes 2097168 | tf_op jit(solution)/shard_map/all_gather | solution.py:151
  825.6 46.6 %all-gather.27.cloned.1.call-done = bf16[1024,1024]{1,0:T(8,128)(2,1)} async-done(((bf16[128,1024]{1,0:T(8,128)(2,1)}), bf16[1024,1024]{1,0:T(8,128)(2,1)}) %all-gather.27.cloned.1.call-update) | async-done | bytes 2097168 | tf_op jit(solution)/shard_map/all_gather | solution.py:152
  877.1 45.2 %all-gather.31.cloned.1.call-done = bf16[1024,1024]{1,0:T(8,128)(2,1)} async-done(((bf16[128,1024]{1,0:T(8,128)(2,1)}), bf16[1024,1024]{1,0:T(8,128)(2,1)}) %all-gather.31.cloned.1.call-update) | async-done | bytes 2097168 | tf_op jit(solution)/shard_map/all_gather | solution.py:150
  924.8 72.3 %all-gather.35.cloned.1.call-done = bf16[4,512,1024]{2,0,1:T(4,128)(2,1)} async-done(((bf16[4,64,1024]{2,0,1:T(4,128)(2,1)}), bf16[4,512,1024]{2,0,1:T(4,128)(2,1)}) %all-gather.35.cloned.1.call-update) | async-done | bytes 4194320 | tf_op jit(solution)/shard_map/all_gather | solution.py:215
  1004.9 66.7 %all-gather.29.cloned.1.call-done = bf16[4,512,1024]{2,0,1:T(4,128)(2,1)} async-done(((bf16[4,64,1024]{2,0,1:T(4,128)(2,1)}), bf16[4,512,1024]{2,0,1:T(4,128)(2,1)}) %all-gather.29.cloned.1.call-update) | async-done | bytes 4194320 | tf_op jit(solution)/shard_map/all_gather | solution.py:216
  1126.7 69.2 %all-gather.41.cloned.1.call-done = bf16[2048,1024]{1,0:T(8,128)(2,1)} async-done(((bf16[256,1024]{1,0:T(8,128)(2,1)}), bf16[2048,1024]{1,0:T(8,128)(2,1)}) %all-gather.41.cloned.1.call-update) | async-done | bytes 4194320 | tf_op jit(solution)/shard_map/all_gather | solution.py:59
  1200.4 70.0 %all-gather.39.cloned.1.call-done = bf16[2048,1024]{1,0:T(8,128)(2,1)} async-done(((bf16[256,1024]{1,0:T(8,128)(2,1)}), bf16[2048,1024]{1,0:T(8,128)(2,1)}) %all-gather.39.cloned.1.call-update) | async-done | bytes 4194320 | tf_op jit(solution)/shard_map/all_gather | solution.py:59
  1285.0 81.0 %reduce-scatter.22.cloned.1.call-done = bf16[256,1024]{1,0:T(8,128)(2,1)} async-done(((bf16[2048,1024]{1,0:T(8,128)(2,1)}), bf16[256,1024]{1,0:T(8,128)(2,1)}) %reduce-scatter.22.cloned.1.call-update) | async-done | bytes 524304 | tf_op jit(solution)/shard_map/reduce_scatter | solution.py:63
  1368.2 89.1 %reduce-scatter.20.cloned.1.call-done = bf16[256,1024]{1,0:T(8,128)(2,1)} async-done(((bf16[2048,1024]{1,0:T(8,128)(2,1)}), bf16[256,1024]{1,0:T(8,128)(2,1)}) %reduce-scatter.20.cloned.1.call-update) | async-done | bytes 524304 | tf_op jit(solution)/shard_map/reduce_scatter | solution.py:63
  1496.1 69.7 %reduce-scatter.24.cloned.1.call-done = bf16[4,64,1024]{2,1,0:T(8,128)(2,1)} async-done(((bf16[4,512,1024]{2,1,0:T(8,128)(2,1)}), bf16[4,64,1024]{2,1,0:T(8,128)(2,1)}) %reduce-scatter.24.cloned.1.call-update) | async-done | bytes 524304 | tf_op jit(solution)/shard_map/reduce_scatter | solution.py:273
  1569.2 88.2 %reduce-scatter.26.cloned.1.call-done = bf16[4,64,1024]{2,1,0:T(8,128)(2,1)} async-done(((bf16[4,512,1024]{2,1,0:T(8,128)(2,1)}), bf16[4,64,1024]{2,1,0:T(8,128)(2,1)}) %reduce-scatter.26.cloned.1.call-update) | async-done | bytes 524304 | tf_op jit(solution)/shard_map/reduce_scatter | solution.py:276
  1663.8 73.3 %all-gather.43.cloned.1.call-done = bf16[2048,1024]{1,0:T(8,128)(2,1)} async-done(((bf16[256,1024]{1,0:T(8,128)(2,1)}), bf16[2048,1024]{1,0:T(8,128)(2,1)}) %all-gather.43.cloned.1.call-update) | async-done | bytes 4194320 | tf_op jit(solution)/shard_map/all_gather | solution.py:59
  1745.7 86.0 %reduce-scatter.28.cloned.1.call-done = bf16[256,1024]{1,0:T(8,128)(2,1)} async-done(((bf16[2048,1024]{1,0:T(8,128)(2,1)}), bf16[256,1024]{1,0:T(8,128)(2,1)}) %reduce-scatter.28.cloned.1.call-update) | async-done | bytes 524304 | tf_op jit(solution)/shard_map/reduce_scatter | solution.py:63
  1840.7 73.2 %all-gather.45.cloned.1.call-done = bf16[4,512,1024]{2,1,0:T(8,128)(2,1)} async-done(((bf16[4,64,1024]{2,1,0:T(8,128)(2,1)}), bf16[4,512,1024]{2,1,0:T(8,128)(2,1)}) %all-gather.45.cloned.1.call-update) | async-done | bytes 4194320 | tf_op jit(solution)/shard_map/all_gather | solution.py:314
  1914.0 58.0 %multiply_reduce_fusion = (f32[4,512]{1,0:T(4,128)S(1)}, f32[4,512,6272]{1,2,0:T(8,128)}) fusion(f32[4,512]{1,0:T(4,128)S(1)} %get-tuple-element.49, f32[4,6272]{1,0:T(4,128)S(1)} %copy-done.47, f32[4,512]{1,0:T(4,128)S(1)} %get-tuple-element.48, f32[4,6272,512]{2,1,0:T(8,128)} %get-tuple-element.193, ...), kind=kOutput, calls=%fused_computation.17 | convolution fusion | flops 26383742976 | bytes 158459904 | tf_op jit(solution)/shard_map/iqd,ipd->iqp/dot_general | solution.py:320
  1991.0 43.4 %convolution_convert_fusion = bf16[4,6272,1024]{2,1,0:T(8,128)(2,1)} fusion(bf16[4,512,1024]{2,1,0:T(8,128)(2,1)} %all-gather.45.cloned.1.call-done, f32[4,6272,512]{2,1,0:T(8,128)} %get-tuple-element.193, f32[4,512]{1,0:T(4,128)S(1)} %get-tuple-element.49, f32[4,512]{1,0:T(4,128)S(1)} %get-tuple-element.48, f32[4,6272]{1,0:T(4,128)S(1)} %copy-done.47), kind=kOutput, calls=%fused_computation.18 | convolution fusion | flops 26396590080 | bytes 107071488 | tf_op jit(solution)/shard_map/iqp,iqd->ipd/dot_general | solution.py:325
  2063.4 41.5 %multiply_convert_fusion.1 = bf16[4,512,6272]{1,2,0:T(8,128)(2,1)} fusion(f32[4,512,6272]{1,2,0:T(8,128)} %get-tuple-element.206, f32[4,512]{1,0:T(4,128)S(1)} %psum.126, f32[4,512]{1,0:T(4,128)S(1)} %get-tuple-element.49, f32[4,6272]{1,0:T(4,128)S(1)} %copy-done.47, f32[4,512]{1,0:T(4,128)S(1)} %get-tuple-element.48, f32[4,6272,512]{2,1,0:T(8,128)} %get-tuple-element.193), kind=kLoop, calls=%fused_computation.16 | loop fusion | flops 89915392 | bytes 128575488 | tf_op jit(solution)/shard_map/convert_element_type | solution.py:324
  2105.0 35.2 %multiply_convert_fusion = bf16[4,6272,1024]{2,1,0:T(8,128)(2,1)} fusion(bf16[4,512,6272]{1,2,0:T(8,128)(2,1)} %multiply_convert_fusion.1, bf16[512,1024,1]{1,0,2:T(8,128)(2,1)S(1)} %copy-done.107), kind=kOutput, calls=%fused_computation.6 | convolution fusion | flops 26358054912 | bytes 78118912 | tf_op jit(solution)/shard_map/iqp,qd->ipd/dot_general | solution.py:329
  2192.2 37.5 %bitcast_multiply_fusion.1 = f32[512,1024]{1,0:T(8,128)} fusion(bf16[4,512,6272]{1,2,0:T(8,128)(2,1)} %multiply_convert_fusion.1, bf16[4,6272,1024]{2,1,0:T(8,128)(2,1)} %convolution_convert_fusion.1), kind=kOutput, calls=%fused_computation.67 | convolution fusion | flops 26307198976 | bytes 79167488 | tf_op jit(solution)/shard_map/iqp,ipd->qd/dot_general | solution.py:333
  2259.9 44.5 %fusion.16 = (f32[261]{0:T(512)S(1)}, f32[4,6272]{1,0:T(4,128)S(1)}, f32[4,6272,261]{1,2,0:T(8,128)}) fusion(f32[4,6272,258]{1,2,0:T(8,128)} %copy-done.2, f32[4,6272,3]{1,2,0:T(4,128)S(1)} %copy-done.29, f32[4,6272]{1,0:T(4,128)S(1)} %copy-done.60, f32[4,6272]{1,0:T(4,128)S(1)} %copy-done.46, f32[261]{0:T(512)S(1)} %copy-done.103, ...), kind=kOutput, calls=%fused_computation.30 | convolution fusion | flops 13469143040 | bytes 130793512 | tf_op jit(solution)/shard_map/ipd,cd->ipc/dot_general | solution.py:345
  2335.2 82.1 %all-reduce.10 = (bf16[512,1024]{1,0:T(8,128)(2,1)S(1)}, f32[261]{0:T(512)}, f32[1024]{0:T(1024)}, f32[1024]{0:T(1024)}, f32[1024]{0:T(1024)}) all-reduce(f32[512,1024]{1,0:T(8,128)} %bitcast_multiply_fusion.1, f32[261]{0:T(512)S(1)} %get-tuple-element.130, f32[1024]{0:T(1024)S(1)} %copy-done.84, ...), channel_id=1, replica_groups=mesh['img'=4,'pix'=8] {'img','pix'}, use_global_device_ids=true, to_apply=%region_40.41 | all-reduce | flops 527621 | bytes 3172392 | tf_op jit(solution)/shard_map/psum | solution.py:352
  2446.5 70.1 %reduce-scatter.34.cloned.1.call-done = bf16[128,1024]{1,0:T(8,128)(2,1)} async-done(((bf16[1024,1024]{1,0:T(8,128)(2,1)}), bf16[128,1024]{1,0:T(8,128)(2,1)}) %reduce-scatter.34.cloned.1.call-update) | async-done | bytes 262160 | tf_op jit(solution)/shard_map/reduce_scatter | solution.py:392
  2516.5 70.4 %reduce-scatter.30.cloned.1.call-done = bf16[128,1024]{1,0:T(8,128)(2,1)} async-done(((bf16[1024,1024]{1,0:T(8,128)(2,1)}), bf16[128,1024]{1,0:T(8,128)(2,1)}) %reduce-scatter.30.cloned.1.call-update) | async-done | bytes 262160 | tf_op jit(solution)/shard_map/reduce_scatter | solution.py:386
  2594.1 59.2 %all-reduce.9.cloned.1.call-done = (bf16[64,1024]{1,0:T(8,128)(2,1)}, bf16[261,128]{1,0:T(8,128)(2,1)}, bf16[261,128]{1,0:T(8,128)(2,1)}, bf16[128,1024]{1,0:T(8...) async-done(((bf16[64,1024]{1,0:T(8,128)(2,1)}, ...) | async-done | bytes 2624016 | tf_op jit(solution)/shard_map/psum | solution.py:433
  (430 shorter events, 617.8 us)
Async XLA Ops:
  7.2 1263.2 %copy-start = (bf16[1024,128]{1,0:T(8,128)(2,1)S(1)}, bf16[1024,128]{1,0:T(8,128)(2,1)}, u32[]{:S(2)}) copy-start(bf16[1024,128]{1,0:T(8,128)(2,1)} %param.41) | copy-start | bytes 786436
  7.2 200.9 %all-gather.19.cloned.1.call-start = ((), (), s32[]{:S(2)}) async-start(), calls=%async_computation.13 | async-start | bytes 1179648 | tf_op jit(solution)/shard_map/all_gather | solution.py:145
  7.9 206.1 %all-gather.21.cloned.1.call-start = ((), (), s32[]{:S(2)}) async-start(), calls=%async_computation.14 | async-start | bytes 2359296 | tf_op jit(solution)/shard_map/all_gather | solution.py:146
  8.7 541.4 %all-reduce.7.cloned.1.call-start = ((), (), s32[]{:S(2)}) async-start(), calls=%async_computation.40 | async-start | bytes 8388608
  395.3 205.1 %all-gather.23.cloned.1.call-start = ((), (), s32[]{:S(2)}) async-start(), calls=%async_computation.15 | async-start | bytes 2359296 | tf_op jit(solution)/shard_map/all_gather | solution.py:149
  395.9 280.5 %all-gather.25.cloned.1.call-start = ((), (), s32[]{:S(2)}) async-start(), calls=%async_computation.16 | async-start | bytes 4718592 | tf_op jit(solution)/shard_map/all_gather | solution.py:59
  396.2 280.2 %copy-start.42 = (bf16[1024,128]{1,0:T(8,128)(2,1)S(1)}, bf16[1024,128]{1,0:T(8,128)(2,1)}, u32[]{:S(2)}) copy-start(bf16[1024,128]{1,0:T(8,128)(2,1)} %param.33) | copy-start | bytes 786436
  604.3 166.3 %reduce-scatter.18.cloned.1.call-start = ((), (), s32[]{:S(2)}) async-start(), calls=%async_computation.17 | async-start | bytes 4718592 | tf_op jit(solution)/shard_map/reduce_scatter | solution.py:63
  684.1 137.9 %all-gather.33.cloned.1.call-start = ((), (), s32[]{:S(2)}) async-start(), calls=%async_computation.21 | async-start | bytes 2359296 | tf_op jit(solution)/shard_map/all_gather | solution.py:151
  684.9 187.3 %all-gather.27.cloned.1.call-start = ((), (), s32[]{:S(2)}) async-start(), calls=%async_computation.18 | async-start | bytes 2359296 | tf_op jit(solution)/shard_map/all_gather | solution.py:152
  685.6 236.8 %all-gather.31.cloned.1.call-start = ((), (), s32[]{:S(2)}) async-start(), calls=%async_computation.20 | async-start | bytes 2359296 | tf_op jit(solution)/shard_map/all_gather | solution.py:150
  686.3 310.7 %all-gather.35.cloned.1.call-start = ((), (), s32[]{:S(2)}) async-start(), calls=%async_computation.22 | async-start | bytes 4718592 | tf_op jit(solution)/shard_map/all_gather | solution.py:215
  825.6 246.1 %all-gather.29.cloned.1.call-start = ((), (), s32[]{:S(2)}) async-start(), calls=%async_computation.19 | async-start | bytes 4718592 | tf_op jit(solution)/shard_map/all_gather | solution.py:216
  875.8 245.9 %all-gather.37.cloned.1.call-start = ((), (), s32[]{:S(2)}) async-start(), calls=%async_computation.23 | async-start | bytes 2359296 | tf_op jit(solution)/shard_map/all_gather | solution.py:153
  876.3 319.6 %all-gather.41.cloned.1.call-start = ((), (), s32[]{:S(2)}) async-start(), calls=%async_computation.26 | async-start | bytes 4718592 | tf_op jit(solution)/shard_map/all_gather | solution.py:59
  877.1 393.3 %all-gather.39.cloned.1.call-start = ((), (), s32[]{:S(2)}) async-start(), calls=%async_computation.24 | async-start | bytes 4718592 | tf_op jit(solution)/shard_map/all_gather | solution.py:59
  1126.7 239.4 %reduce-scatter.22.cloned.1.call-start = ((), (), s32[]{:S(2)}) async-start(), calls=%async_computation.27 | async-start | bytes 4718592 | tf_op jit(solution)/shard_map/reduce_scatter | solution.py:63
  1279.6 177.7 %reduce-scatter.20.cloned.1.call-start = ((), (), s32[]{:S(2)}) async-start(), calls=%async_computation.25 | async-start | bytes 4718592 | tf_op jit(solution)/shard_map/reduce_scatter | solution.py:63
  1285.0 280.8 %reduce-scatter.24.cloned.1.call-start = ((), (), s32[]{:S(2)}) async-start(), calls=%async_computation.28 | async-start | bytes 4718592 | tf_op jit(solution)/shard_map/reduce_scatter | solution.py:273
  1477.6 179.9 %reduce-scatter.26.cloned.1.call-start = ((), (), s32[]{:S(2)}) async-start(), calls=%async_computation.29 | async-start | bytes 4718592 | tf_op jit(solution)/shard_map/reduce_scatter | solution.py:276
  1489.5 247.5 %all-gather.43.cloned.1.call-start = ((), (), s32[]{:S(2)}) async-start(), calls=%async_computation.30 | async-start | bytes 4718592 | tf_op jit(solution)/shard_map/all_gather | solution.py:59
  1663.7 168.0 %reduce-scatter.28.cloned.1.call-start = ((), (), s32[]{:S(2)}) async-start(), calls=%async_computation.31 | async-start | bytes 4718592 | tf_op jit(solution)/shard_map/reduce_scatter | solution.py:63
  1745.2 168.7 %all-gather.45.cloned.1.call-start = ((), (), s32[]{:S(2)}) async-start(), calls=%async_computation.32 | async-start | bytes 4718592 | tf_op jit(solution)/shard_map/all_gather | solution.py:314
  1840.7 576.7 %reduce-scatter.42.cloned.1.call-start = ((), (), s32[]{:S(2)}) async-start(), calls=%async_computation.39 | async-start | bytes 884736
  2063.2 355.9 %reduce-scatter.40.cloned.1.call-start = ((), (), s32[]{:S(2)}) async-start(), calls=%async_computation.38 | async-start | bytes 884736
  2169.1 251.6 %reduce-scatter.38.cloned.1.call-start = ((), (), s32[]{:S(2)}) async-start(), calls=%async_computation.37 | async-start | bytes 2359296 | tf_op jit(solution)/shard_map/reduce_scatter | solution.py:398
  2171.3 249.4 %reduce-scatter.32.cloned.1.call-start = ((), (), s32[]{:S(2)}) async-start(), calls=%async_computation.34 | async-start | bytes 2359296 | tf_op jit(solution)/shard_map/reduce_scatter | solution.py:389
  2173.5 273.0 %reduce-scatter.36.cloned.1.call-start = ((), (), s32[]{:S(2)}) async-start(), calls=%async_computation.36 | async-start | bytes 2359296 | tf_op jit(solution)/shard_map/reduce_scatter | solution.py:395
  2175.9 340.6 %reduce-scatter.34.cloned.1.call-start = ((), (), s32[]{:S(2)}) async-start(), calls=%async_computation.35 | async-start | bytes 2359296 | tf_op jit(solution)/shard_map/reduce_scatter | solution.py:392
  2178.1 408.9 %reduce-scatter.30.cloned.1.call-start = ((), (), s32[]{:S(2)}) async-start(), calls=%async_computation.33 | async-start | bytes 2359296 | tf_op jit(solution)/shard_map/reduce_scatter | solution.py:386
  2191.7 461.6 %all-reduce.9.cloned.1.call-start = ((), (), s32[]{:S(2)}) async-start(), calls=%async_computation.41 | async-start | bytes 5251072 | tf_op jit(solution)/shard_map/psum | solution.py:433
  2333.0 254.0 %copy-start.7 = (bf16[512,1024]{1,0:T(8,128)(2,1)S(1)}, bf16[512,1024]{1,0:T(8,128)(2,1)}, u32[]{:S(2)}) copy-start(bf16[512,1024]{1,0:T(8,128)(2,1)} %all-gather.19.cloned.1.call-done) | copy-start | bytes 3145732
  (105 other events, 4811.2 us)
Sparse Core Ops, SparseCore 0:
  10.2 45.4 all-gather.18
  57.8 50.1 all-gather.20
  395.4 154.6 all-reduce.6
  552.1 48.2 all-gather.22
  604.4 71.8 all-gather.24
  684.2 86.3 reduce-scatter.17
  773.0 49.0 all-gather.32
  824.4 47.7 all-gather.26
  874.5 47.7 all-gather.30
  925.1 71.8 all-gather.34
  1000.0 71.6 all-gather.28
  1073.9 47.7 all-gather.36
  1124.0 71.8 all-gather.40
  1198.7 71.6 all-gather.38
  1279.7 86.3 reduce-scatter.21
  1369.6 87.6 reduce-scatter.19
  1477.7 88.0 reduce-scatter.23
  1569.3 88.1 reduce-scatter.25
  1663.8 73.1 all-gather.42
  1745.4 86.3 reduce-scatter.27
  1840.8 73.1 all-gather.44
  2063.3 59.7 reduce-scatter.41
  2169.3 59.7 reduce-scatter.39
  2232.4 66.8 reduce-scatter.37
  2302.8 71.5 reduce-scatter.31
  2377.8 68.6 reduce-scatter.35
  2449.8 66.6 reduce-scatter.33
  2520.1 66.8 reduce-scatter.29
  2592.0 61.3 all-reduce.8
where the time goes:
time: 2690 us; the launch traced here: 2680 us
  waiting for transfers between devices  1600 us (59%)
  matrix products  571 us (21%)
  blocking collectives  225 us (8%)
  other arithmetic  167 us (6%)
  local copies, waits for them, and re-layouts  95.6 us (4%)
    reduce_scatter x4, waiting for transfers between devices, sum_rows(): lax.psum_scatter(term(jnp.int32(0), count * lax.axis_size('pix')).astype(...  340 us
    all_gather x4, waiting for transfers between devices, share_rows(): return lax.all_gather(rows, 'pix', axis=0, tiled=True)  284 us
    unnamed x32, waiting for transfers between devices  158 us
    reduce_scatter x1, waiting for transfers between devices, local(): lax.psum_scatter(grad_vals_all.astype(jnp.bfloat16), 'pix', scatter_dimen...  88.2 us
    psum x1, blocking collectives, local(): lax.psum((grad_queries_part, grad_gain_in_part, grad_gain_one, grad_gain_...  82.1 us
    all_gather x1, waiting for transfers between devices, local(): grad_att_all = lax.all_gather(grad_attended, 'pix', axis=1, tiled=True)  73.2 us
    all_gather x1, waiting for transfers between devices, local(): lax.all_gather(local_keys, 'pix', axis=1, tiled=True)  72.3 us
    reduce_scatter x1, waiting for transfers between devices, local(): lax.psum_scatter(grad_cross_out.astype(jnp.bfloat16), 'pix', scatter_dime...  70.4 us
  transfers between devices with their start and end apart: 29, of which 23 were waited for; matrix products, arithmetic and copies ran while one was open for 18% of the time, Pallas kernels for 0%

commit v1 on v0

v1 whole, which is shorter than its diff:
```python
import functools

import jax
import jax.numpy as jnp
from jax import lax
from jax.experimental import pallas as pl
from jax.experimental.pallas import tpu as pltpu
from jax.sharding import PartitionSpec as P

HEADS = 8
HEAD_DIM = 128
BANDS = 64
SIDE = 224
CHANNELS = 256
LOG2E = 1.4426950408889634

eps = 1e-05
f32 = jnp.float32
bf16 = jnp.bfloat16


def exact(left, right):
    return jnp.dot(left, right, precision=lax.Precision.HIGHEST, preferred_element_type=f32)


def mm(left, right):
    return jnp.dot(left, right, preferred_element_type=f32)


def mm_nt(left, right):
    return lax.dot_general(left, right, (((1,), (1,)), ((), ())), preferred_element_type=f32)


def mm_tn(left, right):
    return lax.dot_general(left, right, (((0,), (0,)), ((), ())), preferred_element_type=f32)


def layer_norm(rows, gain):
    average = jnp.mean(rows, axis=-1, keepdims=True)
    centred = rows - average
    spread = jnp.mean(centred * centred, axis=-1, keepdims=True)
    return centred * lax.rsqrt(spread + eps) * gain


def angles(index):
    place = index.astype(f32) * (2.0 / (SIDE - 1)) - 1.0
    steps = lax.iota(jnp.int32, BANDS).astype(f32)
    frequency = 1.0 + steps * ((SIDE / 2.0 - 1.0) / (BANDS - 1))
    angle = jnp.pi * place[:, None] * frequency[None, :]
    return place[:, None], jnp.sin(angle), jnp.cos(angle)


def pixel_tile(pixels):
    return 896 if pixels % 896 == 0 else pixels


def score_kernel(x_ref, xt_ref, at_ref, u_ref, m_ref, acc, top):
    step = pl.program_id(1)

    @pl.when(step == 0)
    def _():
        acc[...] = jnp.zeros_like(acc)
        top[...] = jnp.full_like(top, -jnp.inf)

    scores = mm(x_ref[...], at_ref[...])
    old = top[0:1, :]
    new = jnp.maximum(old, jnp.max(scores, axis=0, keepdims=True))
    weights = jnp.exp2(scores - new).astype(bf16)
    acc[...] = acc[...] * jnp.exp2(old - new) + mm(xt_ref[0], weights)
    top[...] = jnp.broadcast_to(new, top.shape)

    @pl.when(step == pl.num_programs(1) - 1)
    def _():
        u_ref[0] = acc[...]
        m_ref[0] = top[...]


def score_pass(x, xt, at):
    images, rows, pixels = xt.shape
    tile = pixel_tile(pixels)
    steps = pixels // tile
    latents = at.shape[1]
    return pl.pallas_call(
        score_kernel,
        grid=(images, steps),
        in_specs=[
            pl.BlockSpec((tile, CHANNELS), lambda i, t: (i * steps + t, 0)),
            pl.BlockSpec((1, rows, tile), lambda i, t: (i, 0, t)),
            pl.BlockSpec((CHANNELS, latents), lambda i, t: (0, 0)),
        ],
        out_specs=[
            pl.BlockSpec((1, rows, latents), lambda i, t: (i, 0, 0)),
            pl.BlockSpec((1, 8, latents), lambda i, t: (i, 0, 0)),
        ],
        out_shape=[
            jax.ShapeDtypeStruct((images, rows, latents), f32),
            jax.ShapeDtypeStruct((images, 8, latents), f32),
        ],
        scratch_shapes=[pltpu.VMEM((rows, latents), f32), pltpu.VMEM((8, latents), f32)],
        compiler_params=pltpu.CompilerParams(vmem_limit_bytes=40 * 2**20),
        cost_estimate=pl.CostEstimate(
            flops=4 * images * pixels * CHANNELS * latents,
            bytes_accessed=4 * images * pixels * CHANNELS,
            transcendentals=images * pixels * latents,
        ),
    )(x, xt, at)


def grad_kernel(x_ref, xt_ref, at_ref, bt_ref, a_ref, b_ref, stat_ref, t_ref, out_ref):
    first = (pl.program_id(0) == 0) & (pl.program_id(1) == 0)

    @pl.when(first)
    def _():
        t_ref[...] = jnp.zeros_like(t_ref)

    x = x_ref[...]
    scores = mm(x, at_ref[...])
    grad_p = mm(x, bt_ref[0])
    probs = jnp.exp2(scores - stat_ref[0, 0:1, :])
    grad_s = (probs * (grad_p - stat_ref[0, 1:2, :])).astype(bf16)
    probs = probs.astype(bf16)
    t_ref[...] += mm(xt_ref[0], grad_s)
    back = mm(grad_s, a_ref[...]) + mm(probs, b_ref[0])
    along = jnp.sum(back * x.astype(f32), axis=1, keepdims=True)
    half = back[:, CHANNELS - 128 :]
    lane = lax.broadcasted_iota(jnp.int32, half.shape, 1)
    half = jnp.where(lane == 120, along, half)
    out_ref[0] = half.T[120:128, :]


def grad_pass(x, xt, at, bt, a, b, stat):
    images, rows, pixels = xt.shape
    tile = pixel_tile(pixels)
    steps = pixels // tile
    latents = at.shape[1]
    return pl.pallas_call(
        grad_kernel,
        grid=(images, steps),
        in_specs=[
            pl.BlockSpec((tile, CHANNELS), lambda i, t: (i * steps + t, 0)),
            pl.BlockSpec((1, rows, tile), lambda i, t: (i, 0, t)),
            pl.BlockSpec((CHANNELS, latents), lambda i, t: (0, 0)),
            pl.BlockSpec((1, CHANNELS, latents), lambda i, t: (i, 0, 0)),
            pl.BlockSpec((latents, CHANNELS), lambda i, t: (0, 0)),
            pl.BlockSpec((1, latents, CHANNELS), lambda i, t: (i, 0, 0)),
            pl.BlockSpec((1, 8, latents), lambda i, t: (i, 0, 0)),
        ],
        out_specs=[
            pl.BlockSpec((rows, latents), lambda i, t: (0, 0)),
            pl.BlockSpec((1, 8, tile), lambda i, t: (i, 0, t)),
        ],
        out_shape=[
            jax.ShapeDtypeStruct((rows, latents), f32),
            jax.ShapeDtypeStruct((images, 8, pixels), f32),
        ],
        compiler_params=pltpu.CompilerParams(vmem_limit_bytes=40 * 2**20),
        cost_estimate=pl.CostEstimate(
            flops=10 * images * pixels * CHANNELS * latents,
            bytes_accessed=4 * images * pixels * CHANNELS,
            transcendentals=images * pixels * latents,
        ),
    )(x, xt, at, bt, a, b, stat)


MESH = pl.DeviceIdType.MESH
DMA = pltpu.SemaphoreType.DMA


def ring_place(count):
    me = lax.axis_index("pix")
    return jnp.where(me % 2 == 0, me // 2, count - 1 - me // 2)


def ring_device(place, count):
    place = lax.rem(place + 2 * count, count)
    return jnp.where(place < count // 2, 2 * place, 2 * (count - 1 - place) + 1)


def greet(devices):
    barrier = pltpu.get_barrier_semaphore()
    for device in devices:
        pl.semaphore_signal(barrier, inc=1, device_id=device, device_id_type=MESH)
    pl.semaphore_wait(barrier, len(devices))


def gather_kernel(count, shapes, *refs):
    number = len(shapes)
    sources, fulls = refs[:number], refs[number : 2 * number]
    local_sem, send_sem, recv_sem, hand_send, hand_recv = refs[2 * number :]
    group, me = lax.axis_index("img"), lax.axis_index("pix")
    core = lax.rem(group, 2)
    place = ring_place(count)
    sides = ((group, ring_device(place + 1, count)), (group, ring_device(place - 1, count)))
    other = (group + 1 - 2 * core, me)
    greet(sides + (other,))
    own = [
        pltpu.make_async_copy(sources[a], fulls[a].at[:, me], local_sem.at[a])
        for a in range(number)
    ]
    for copy in own:
        copy.start()
    first = [sum(shape[0] for shape in shapes[:a]) for a in range(number)]

    def spot(a, k, stage, way, source):
        wide = shapes[a][2] // 4
        columns = pl.ds(pl.multiple_of((core * 2 + way) * wide, 128), wide)
        if source:
            return sources[a].at[k, :, columns]
        origin = ring_device(place - stage if way == 0 else place + stage, count)
        return fulls[a].at[k, origin, :, columns]

    def hop(a, k, stage, way):
        return pltpu.make_async_remote_copy(
            spot(a, k, stage, way, stage == 0),
            spot(a, k, stage, way, False),
            send_sem.at[stage, way, first[a] + k],
            recv_sem.at[stage, way, first[a] + k],
            device_id=sides[way],
            device_id_type=MESH,
        )

    def hand(a, k, stage, way):
        part = spot(a, k, stage, way, False)
        return pltpu.make_async_remote_copy(
            part,
            part,
            hand_send.at[stage - 1, way, first[a] + k],
            hand_recv.at[stage - 1, way, first[a] + k],
            device_id=other,
            device_id_type=MESH,
        )

    for stage in range(count):
        for a in range(number):

            @pl.loop(0, shapes[a][0])
            def _(k):
                for way in range(2):
                    if stage > 0:
                        hop(a, k, stage - 1, way).wait_recv()
                    if stage < count - 1:
                        hop(a, k, stage, way).start()
                    if stage > 0:
                        hand(a, k, stage, way).start()

    for copy in own:
        copy.wait()
    for stage in range(count):
        for a in range(number):

            @pl.loop(0, shapes[a][0])
            def _(k):
                for way in range(2):
                    if stage < count - 1:
                        hop(a, k, stage, way).wait_send()
                    if stage > 0:
                        hand(a, k, stage, way).wait()


def ring_gather(arrays, collective_id):
    count = lax.axis_size("pix")
    shapes = [array.shape for array in arrays]
    total = sum(shape[0] for shape in shapes)
    anywhere = pl.BlockSpec(memory_space=pl.ANY)
    return pl.pallas_call(
        functools.partial(gather_kernel, count, shapes),
        out_shape=[
            jax.ShapeDtypeStruct((shape[0], count) + shape[1:], array.dtype)
            for shape, array in zip(shapes, arrays)
        ],
        in_specs=[anywhere] * len(arrays),
        out_specs=[anywhere] * len(arrays),
        scratch_shapes=[DMA((len(arrays),))] + [DMA((count - 1, 2, total))] * 4,
        compiler_params=pltpu.CompilerParams(collective_id=collective_id, has_side_effects=True),
    )(*arrays)


def reduce_kernel(
    count,
    teams,
    xs_ref,
    gs_ref,
    out_ref,
    xv,
    gv,
    first,
    held,
    across,
    done,
    load_sem,
    pair_send,
    pair_recv,
    send_sem,
    recv_sem,
    cross_send,
    cross_recv,
    out_sem,
    hand_send,
    hand_recv,
):
    number, rows, width = gs_ref.shape
    kinds = xs_ref.shape[0]
    depth = xs_ref.shape[3]
    half, wide = width // 2, width // 4
    group, me = lax.axis_index("img"), lax.axis_index("pix")
    core, team = lax.rem(group, 2), group // 2
    place = ring_place(count)
    sides = ((group, ring_device(place + 1, count)), (group, ring_device(place - 1, count)))
    other = (group + 1 - 2 * core, me)
    partners = [(lax.rem(team + d, teams) * 2 + core, me) for d in range(1, teams)]
    greet(sides + (other,) + tuple(partners))

    mine = pl.ds(pl.multiple_of(core * rows, 16), rows)

    def load_x(j):
        return pltpu.make_async_copy(xs_ref.at[j], xv.at[j, :, mine], load_sem.at[0, j])

    def load_g(k):
        part = gs_ref.at[k, :, pl.ds(pl.multiple_of(core * half, 128), half)]
        return pltpu.make_async_copy(part, gv.at[k, mine], load_sem.at[1, k])

    def pair_x(j):
        return pltpu.make_async_remote_copy(
            xs_ref.at[j],
            xv.at[j, :, mine],
            pair_send.at[0, j],
            pair_recv.at[0, j],
            device_id=other,
            device_id_type=MESH,
        )

    def pair_g(k):
        part = gs_ref.at[k, :, pl.ds(pl.multiple_of((1 - core) * half, 128), half)]
        return pltpu.make_async_remote_copy(
            part,
            gv.at[k, mine],
            pair_send.at[1, k],
            pair_recv.at[1, k],
            device_id=other,
            device_id_type=MESH,
        )

    for j in range(number):
        if j < kinds:
            load_x(j).start()
            pair_x(j).start()
        load_g(j).start()
        pair_g(j).start()

    def part(k, owner, way):
        j = jnp.maximum(k - (number - kinds), 0)
        return mm_tn(xv[j, owner], gv[k, :, way * wide : (way + 1) * wide])

    def hop(k, stage, way):
        source = first.at[k, way] if stage == 0 else held.at[k, way, stage - 1]
        return pltpu.make_async_remote_copy(
            source,
            held.at[k, way, stage],
            send_sem.at[stage, way, k],
            recv_sem.at[stage, way, k],
            device_id=sides[way],
            device_id_type=MESH,
        )

    def cross(k, way, d):
        return pltpu.make_async_remote_copy(
            across.at[team, k, way],
            across.at[team, k, way],
            cross_send.at[d, way, k],
            cross_recv.at[d, way, k],
            device_id=partners[d],
            device_id_type=MESH,
        )

    for stage in range(count):

        @pl.loop(0, number)
        def _(k):
            if stage == 0:
                j = jnp.maximum(k - (number - kinds), 0)

                @pl.when((k == 0) | (k > number - kinds))
                def _():
                    load_x(j).wait()
                    pair_x(j).wait_recv()

                load_g(k).wait()
                pair_g(k).wait_recv()
            for way in range(2):
                step = stage + 1
                owner = ring_device(place - step if way == 0 else place + step, count)
                total = part(k, owner, way)
                if stage == 0:
                    first[k, way] = total.astype(bf16)
                    hop(k, 0, way).start()
                else:
                    hop(k, stage - 1, way).wait_recv()
                    total = total + held[k, way, stage - 1].astype(f32)
                    if stage < count - 1:
                        held[k, way, stage - 1] = total.astype(bf16)
                        hop(k, stage, way).start()
                    else:
                        across[team, k, way] = total.astype(bf16)
                        for d in range(teams - 1):
                            cross(k, way, d).start()

    def finish(k):
        columns = pl.ds(pl.multiple_of(core * half, 128), half)
        return pltpu.make_async_copy(done.at[k], out_ref.at[k, :, columns], out_sem.at[k])

    def hand(k):
        columns = pl.ds(pl.multiple_of(core * half, 128), half)
        return pltpu.make_async_remote_copy(
            done.at[k],
            out_ref.at[k, :, columns],
            hand_send.at[k],
            hand_recv.at[k],
            device_id=other,
            device_id_type=MESH,
        )

    @pl.loop(0, number)
    def _(k):
        for way in range(2):
            for d in range(teams - 1):
                cross(k, way, d).wait_recv()
            total = across[0, k, way].astype(f32)
            for t in range(1, teams):
                total = total + across[t, k, way].astype(f32)
            done[k, :, way * wide : (way + 1) * wide] = total
        finish(k).start()
        hand(k).start()

    @pl.loop(0, number)
    def _(k):
        finish(k).wait()
        hand(k).wait()
        pair_g(k).wait_send()
        for way in range(2):
            for stage in range(count - 1):
                hop(k, stage, way).wait_send()
            for d in range(teams - 1):
                cross(k, way, d).wait_send()

    @pl.loop(0, kinds)
    def _(j):
        pair_x(j).wait_send()


def ring_reduce(xs, gs, collective_id):
    count = lax.axis_size("pix")
    teams = lax.axis_size("img") // 2
    kinds, rows, columns = xs.shape
    number, _, width = gs.shape
    depth = columns // count
    xs = jnp.swapaxes(xs.reshape(kinds, rows, count, depth), 1, 2)
    anywhere = pl.BlockSpec(memory_space=pl.ANY)
    chunk = (depth, width // 4)
    return pl.pallas_call(
        functools.partial(reduce_kernel, count, teams),
        out_shape=jax.ShapeDtypeStruct((number, depth, width), f32),
        in_specs=[anywhere] * 2,
        out_specs=anywhere,
        scratch_shapes=[
            pltpu.VMEM((kinds, count, 2 * rows, depth), bf16),
            pltpu.VMEM((number, 2 * rows, width // 2), bf16),
            pltpu.VMEM((number, 2) + chunk, bf16),
            pltpu.VMEM((number, 2, count - 1) + chunk, bf16),
            pltpu.VMEM((teams, number, 2) + chunk, bf16),
            pltpu.VMEM((number, depth, width // 2), f32),
            DMA((2, number)),
            DMA((2, number)),
            DMA((2, number)),
            DMA((count - 1, 2, number)),
            DMA((count - 1, 2, number)),
            DMA((teams - 1, 2, number)),
            DMA((teams - 1, 2, number)),
            DMA((number,)),
            DMA((number,)),
            DMA((number,)),
        ],
        compiler_params=pltpu.CompilerParams(
            collective_id=collective_id, has_side_effects=True, vmem_limit_bytes=48 * 2**20
        ),
    )(xs, gs)


def norm_back(resid, gain, grad):
    _, back = jax.vjp(layer_norm, resid, gain)
    return back(grad)


def ffn(resid, gain, up_t, down):
    normed = layer_norm(resid, gain).astype(bf16)
    pre = mm_nt(normed, up_t)
    hidden = jax.nn.gelu(pre).astype(bf16)
    return resid + mm(hidden, down), (normed, pre, hidden)


def ffn_back(resid, gain, up_t, down, saved, grad):
    normed, pre, hidden = saved
    branch = grad.astype(bf16)
    _, gelu_back = jax.vjp(jax.nn.gelu, pre)
    grad_pre = gelu_back(mm_nt(branch, down))[0].astype(bf16)
    grad_input, grad_gain = norm_back(resid, gain, mm(grad_pre, up_t))
    return grad + grad_input, grad_gain, grad_pre, branch


def local(
    rgb_pixels,
    keep_mask,
    latent_array,
    gain_input,
    gain_latent,
    w_query,
    w_key,
    w_value,
    w_cross_out,
    gain_mlp_one,
    w_up_one,
    w_down_one,
    gain_self,
    w_self_query,
    w_self_key,
    w_self_value,
    w_self_out,
    gain_mlp_two,
    w_up_two,
    w_down_two,
    cotangent,
):
    images, _, pixels = rgb_pixels.shape
    rows_here, width = latent_array.shape
    count = lax.axis_size("pix")
    me = lax.axis_index("pix")
    latents = rows_here * count
    sharers = count // images
    rows_own = latents // sharers
    slot = me % sharers
    depth = w_query.shape[0]
    channels = gain_input.shape[0]
    width_scale = width ** (-0.5)
    head_scale = HEAD_DIM ** (-0.5)
    groups = [[i * sharers + j for j in range(sharers)] for i in range(images)]

    side = -(-channels // 512) * 512
    key_t = jnp.pad(w_key.T, ((0, 0), (0, side - channels)))
    latent_full, query_mat, key_full = ring_gather([latent_array[None], w_query[None], key_t[None]], 0)
    latent_full = latent_full.reshape(latents, width)
    query_mat = query_mat.reshape(width, width)
    key_full = key_full.reshape(width, side)
    key_mat = key_full[:, :channels].T
    value_out = lax.psum(mm(w_value, w_cross_out).astype(bf16), "pix")
    shards = jnp.stack(
        [
            w_up_one.T,
            w_down_one,
            w_self_query,
            w_self_key,
            w_self_value,
            w_self_out,
            w_up_two.T,
            w_down_two,
        ]
    )
    (whole,) = ring_gather([shards], 1)
    up_one, down_one, self_query, self_key, self_value, self_out, up_two, down_two = [
        whole[k].reshape(width, width) for k in range(8)
    ]

    lines = pixels // SIDE
    u, sin_u, cos_u = angles(me * lines + lax.iota(jnp.int32, lines))
    w, sin_w, cos_w = angles(lax.iota(jnp.int32, SIDE))

    def zeros(rows, columns):
        return jnp.zeros((rows, columns), f32)

    pad = CHANNELS - 4 - SIDE - lines
    table = jnp.concatenate(
        [
            jnp.concatenate(
                [zeros(SIDE, 4), w, zeros(SIDE, BANDS), sin_w, zeros(SIDE, BANDS), cos_w], axis=1
            ),
            jnp.concatenate(
                [zeros(lines, 3), u, zeros(lines, 1), sin_u, zeros(lines, BANDS), cos_u, zeros(lines, BANDS)],
                axis=1,
            ),
            zeros(pad, channels),
            jnp.eye(3, channels, dtype=f32),
            jnp.ones((1, channels), f32),
        ],
        axis=0,
    )
    row_sum = u[:, 0] + jnp.sum(sin_u + cos_u, axis=1)
    col_sum = w[:, 0] + jnp.sum(sin_w + cos_w, axis=1)
    row_square = u[:, 0] ** 2 + jnp.sum(sin_u**2 + cos_u**2, axis=1)
    col_square = w[:, 0] ** 2 + jnp.sum(sin_w**2 + cos_w**2, axis=1)
    feature_sum = (row_sum[:, None] + col_sum[None, :]).reshape(1, pixels)
    feature_square = (row_square[:, None] + col_square[None, :]).reshape(1, pixels)
    colours = rgb_pixels.astype(f32)
    average = (jnp.sum(colours, axis=1) + feature_sum) / channels
    spread = (jnp.sum(colours**2, axis=1) + feature_square) / channels - average**2
    scale = lax.rsqrt(spread + eps)
    keep = keep_mask.astype(f32)

    position = lax.iota(jnp.int32, pixels)
    column, line = position % SIDE, position // SIDE + SIDE
    channel = lax.iota(jnp.int32, CHANNELS - 4)
    hot = (channel[:, None] == column[None, :]) | (channel[:, None] == line[None, :])
    small = jnp.concatenate(
        [colours * scale[:, None, :], (-average * scale)[:, None, :]], axis=1
    )
    xt = jnp.concatenate(
        [
            jnp.where(hot[None], (scale * keep)[:, None, :], 0.0).astype(bf16),
            (small * keep[:, None, :]).astype(bf16),
            keep[:, None, :].astype(bf16),
            jnp.zeros((images, 15, pixels), bf16),
        ],
        axis=1,
    )
    x = jnp.concatenate(
        [
            jnp.where(hot.T[None], scale[:, :, None], 0.0).astype(bf16),
            jnp.swapaxes(small, 1, 2).astype(bf16),
        ],
        axis=2,
    ).reshape(images * pixels, CHANNELS)

    latent_float = latent_full.astype(f32)
    latent_normed = layer_norm(latent_float, gain_latent).astype(bf16)
    queries = mm(latent_normed, query_mat).astype(bf16)
    gained = table * gain_input[None, :]
    score_mat = mm_nt(queries, key_mat) * width_scale
    score_x = exact(score_mat, gained.T)
    at = (score_x.T * LOG2E).astype(bf16)
    a_low = score_x.astype(bf16)

    weighted, tops = score_pass(x, xt, at)
    tops = tops[:, 0, :]
    totals = weighted[:, CHANNELS, :]
    raw = jnp.einsum(
        "kc,ikq->icq",
        table,
        weighted[:, :CHANNELS, :],
        precision=lax.Precision.HIGHEST,
        preferred_element_type=f32,
    )

    def by_owner(value):
        lead = value.shape[1]
        split = value.reshape(images, lead, sharers, rows_own)
        return jnp.swapaxes(split, 1, 2).reshape(count, lead, rows_own)

    raw_parts = lax.all_to_all(
        by_owner(raw).astype(bf16), "pix", split_axis=0, concat_axis=0, tiled=True
    )
    stat_parts = lax.all_to_all(
        by_owner(jnp.stack([tops, totals], axis=1)), "pix", split_axis=0, concat_axis=0, tiled=True
    )
    top = jnp.max(stat_parts[:, 0, :], axis=0)
    share = jnp.exp2(stat_parts[:, 0, :] - top[None, :])
    total = jnp.sum(share * stat_parts[:, 1, :], axis=0)
    share = share / total[None, :]
    raw_t = jnp.sum(raw_parts.astype(f32) * share[:, None, :], axis=0)
    norm_log = top + jnp.log2(total)

    mean_t = raw_t * gain_input[:, None]
    mean_low = mean_t.astype(bf16)
    own = lax.dynamic_slice_in_dim(latent_float, slot * rows_own, rows_own, 0)
    resid_one = own + mm_tn(mean_low, value_out)
    resid_two, saved_one = ffn(resid_one, gain_mlp_one, up_one, down_one)
    normed_two = layer_norm(resid_two, gain_self).astype(bf16)
    heads_q = mm(normed_two, self_query).astype(bf16).reshape(rows_own, HEADS, HEAD_DIM)
    own_kv = jnp.stack([mm(normed_two, self_key), mm(normed_two, self_value)]).astype(bf16)
    all_kv = lax.all_gather(own_kv, "pix", axis=1, tiled=True, axis_index_groups=groups)
    heads_k, heads_v = [all_kv[k].reshape(latents, HEADS, HEAD_DIM) for k in range(2)]
    scores = jnp.einsum("rhd,khd->hrk", heads_q, heads_k, preferred_element_type=f32) * head_scale
    shifted = jnp.exp(scores - jnp.max(scores, axis=2, keepdims=True))
    probs = shifted / jnp.sum(shifted, axis=2, keepdims=True)
    probs_low = probs.astype(bf16)
    mixed = (
        jnp.einsum("hrk,khd->rhd", probs_low, heads_v, preferred_element_type=f32)
        .reshape(rows_own, width)
        .astype(bf16)
    )
    resid_three = resid_two + mm(mixed, self_out)
    final, saved_two = ffn(resid_three, gain_mlp_two, up_two, down_two)

    per = rows_own // rows_here
    pieces = final.astype(bf16).reshape(per, rows_here, width)
    target = lax.iota(jnp.int32, count)
    mine = (target // per == slot)[:, None, None]
    outgoing = jnp.where(mine, jnp.tile(pieces, (count // per, 1, 1)), jnp.zeros((), bf16))
    incoming = lax.all_to_all(outgoing, "pix", split_axis=0, concat_axis=0, tiled=True)
    incoming = incoming.reshape(images, sharers, rows_here, width)
    latent_out = lax.dynamic_index_in_dim(incoming, me // per, axis=1, keepdims=False)

    outgoing = jnp.where(
        (lax.iota(jnp.int32, sharers) == me // per)[None, :, None, None],
        cotangent[:, None],
        jnp.zeros((), bf16),
    ).reshape(count, rows_here, width)
    incoming = lax.all_to_all(outgoing, "pix", split_axis=0, concat_axis=0, tiled=True)
    grad_final = lax.dynamic_slice_in_dim(incoming, slot * per, per, 0).reshape(rows_own, width)
    grad_final = grad_final.astype(f32)

    grad_three, grad_gain_two, grad_pre_two, branch_two = ffn_back(
        resid_three, gain_mlp_two, up_two, down_two, saved_two, grad_final
    )
    branch = grad_three.astype(bf16)
    grad_mixed = mm_nt(branch, self_out).astype(bf16).reshape(rows_own, HEADS, HEAD_DIM)
    grad_probs = jnp.einsum("rhd,khd->hrk", grad_mixed, heads_v, preferred_element_type=f32)
    grad_v_all = jnp.einsum("hrk,rhd->khd", probs_low, grad_mixed, preferred_element_type=f32)
    delta = jnp.sum(probs * grad_probs, axis=2, keepdims=True)
    grad_scores = (probs * (grad_probs - delta)).astype(bf16)
    grad_q = (
        (jnp.einsum("hrk,khd->rhd", grad_scores, heads_k, preferred_element_type=f32) * head_scale)
        .astype(bf16)
        .reshape(rows_own, width)
    )
    grad_k_all = (
        jnp.einsum("hrk,rhd->khd", grad_scores, heads_q, preferred_element_type=f32) * head_scale
    )
    grad_kv = lax.psum_scatter(
        jnp.stack([grad_k_all, grad_v_all]).reshape(2, latents, width).astype(bf16),
        "pix",
        scatter_dimension=1,
        tiled=True,
        axis_index_groups=groups,
    )
    grad_k, grad_v = grad_kv[0], grad_kv[1]
    grad_normed_two = (
        mm_nt(grad_q, self_query) + mm_nt(grad_k, self_key) + mm_nt(grad_v, self_value)
    )
    grad_in_two, grad_gain_attn = norm_back(resid_two, gain_self, grad_normed_two)
    grad_two = grad_three + grad_in_two
    grad_one, grad_gain_one, grad_pre_one, branch_one = ffn_back(
        resid_one, gain_mlp_one, up_one, down_one, saved_one, grad_two
    )
    grad_cross = grad_one.astype(bf16)
    back_mat = mm_nt(grad_cross, value_out)
    delta_one = jnp.sum(back_mat * mean_t.T, axis=1)
    gain_part = jnp.sum(back_mat * raw_t.T, axis=0)

    back_all = lax.all_gather(back_mat.astype(bf16), "pix", axis=0, tiled=True)
    stats = lax.all_gather(jnp.stack([norm_log, delta_one]), "pix", axis=0)
    stats = jnp.swapaxes(stats, 0, 1).reshape(2, images, latents)
    stats = jnp.pad(jnp.swapaxes(stats, 0, 1), ((0, 0), (0, 6), (0, 0)))
    back_x = exact(back_all.astype(f32), gained.T).astype(bf16).reshape(images, latents, CHANNELS)
    grad_t, pixel_out = grad_pass(x, xt, at, jnp.swapaxes(back_x, 1, 2), a_low, back_x, stats)
    moved = (pixel_out[:, 4:7] - pixel_out[:, 7:8] / channels) - (
        (colours - average[:, None, :]) * scale[:, None, :]
    ) * (pixel_out[:, 0:1] / channels)
    grad_pixels = moved * (scale * keep)[:, None, :]

    grad_raw = exact(grad_t[:CHANNELS].T, table)
    gain_part = gain_part + jnp.sum(score_mat * grad_raw, axis=0)
    grad_raw, gain_in, gain_one, gain_attn, gain_two = lax.psum(
        (grad_raw, gain_part, grad_gain_one, grad_gain_attn, grad_gain_two), ("img", "pix")
    )
    grad_x = (grad_raw * (gain_input * width_scale)[None, :]).astype(bf16)
    query_grad = mm(grad_x, key_mat).astype(bf16)
    latent_cols = lax.dynamic_slice_in_dim(latent_normed, me * depth, depth, 1)
    grad_w_query = mm_tn(latent_cols, query_grad)
    grad_latent_full, grad_gain_latent = norm_back(
        latent_float, gain_latent, mm_nt(query_grad, query_mat)
    )
    grad_latent_own = lax.dynamic_slice_in_dim(grad_latent_full, me * rows_here, rows_here, 0)
    key_cols = w_key.shape[1]
    grad_w_key = mm_tn(grad_x, lax.dynamic_slice_in_dim(queries, me * key_cols, key_cols, 1))

    share_rows = -(-channels // count)
    picks = jnp.eye(rows_own, latents, dtype=bf16)
    picks = jnp.roll(picks, slot * rows_own, axis=1).reshape(rows_own, count, rows_here)
    mean_rows = jnp.pad(mean_low.T, ((0, 0), (0, share_rows * count - channels)))
    mean_rows = mean_rows.reshape(rows_own, count, share_rows)
    last = jnp.concatenate(
        [picks, mean_rows, jnp.zeros((rows_own, count, depth - rows_here - share_rows), bf16)],
        axis=2,
    ).reshape(rows_own, width)
    normed_one, _, hidden_one = saved_one
    normed_last, _, hidden_last = saved_two
    xs = jnp.stack(
        [normed_two, mixed, grad_pre_one, hidden_one, grad_pre_two, hidden_last, last]
    )
    gs = jnp.stack(
        [
            grad_q,
            grad_k,
            grad_v,
            branch,
            normed_one,
            branch_one,
            normed_last,
            branch_two,
            grad_cross,
        ]
    )
    summed = ring_reduce(xs, gs, 2)
    g_sq, g_sk, g_sv, g_so, g_up_one, g_down_one, g_up_two, g_down_two, rest = [
        summed[k] for k in range(9)
    ]
    cross_sum = lax.all_gather(
        rest[rows_here : rows_here + share_rows].astype(bf16), "pix", axis=0, tiled=True
    )[:channels]
    grad_w_value = mm_nt(cross_sum, w_cross_out)
    grad_w_cross_out = mm_tn(w_value, cross_sum)
    grad_latent_array = rest[:rows_here] + grad_latent_own
    return (
        latent_out,
        grad_pixels,
        grad_latent_array,
        gain_in,
        grad_gain_latent,
        grad_w_query,
        grad_w_key,
        grad_w_value,
        grad_w_cross_out,
        gain_one,
        g_up_one.T,
        g_down_one,
        gain_attn,
        g_sq,
        g_sk,
        g_sv,
        g_so,
        gain_two,
        g_up_two.T,
        g_down_two,
    )


def solution(mesh):
    rows, columns, copied = P("pix", None), P(None, "pix"), P()
    return jax.shard_map(
        local,
        mesh=mesh,
        in_specs=(
            P("img", None, "pix"),
            P("img", "pix"),
            rows,
            copied,
            copied,
            rows,
            columns,
            columns,
            rows,
            copied,
            columns,
            rows,
            copied,
            rows,
            rows,
            rows,
            rows,
            copied,
            columns,
            rows,
            P("img", "pix", None),
        ),
        out_specs=(
            P("img", "pix", None),
            P("img", None, "pix"),
            rows,
            copied,
            copied,
            rows,
            columns,
            columns,
            rows,
            copied,
            columns,
            rows,
            copied,
            rows,
            rows,
            rows,
            rows,
            copied,
            columns,
            rows,
        ),
        check_vma=False,
    )
```

time: 2690 us -> 885 us (0.33)
  waiting for transfers between devices: 1600 us -> 112 us
  matrix products: 571 us -> 73.5 us
  Pallas kernels: 0 us -> 349 us
  blocking collectives: 225 us -> 96.7 us
  other arithmetic: 167 us -> 82.9 us
  starting transfers between devices: 2.37 us -> 37.3 us
    all_gather x14 -> x2, waiting for transfers between devices: 718 us -> 17.7 us  [the longest x1 17.7 us: local(): lax.all_gather(own_kv, 'pix', axis=1, tiled=True, axis_index_groups=groups)]
    reduce_scatter x11 -> x1, waiting for transfers between devices: 665 us -> 5.34 us  [local(): lax.psum_scatter(jnp.stack([grad_k_all, grad_v_all]).reshape(2, latents,...]
    dot_general x48 -> x36, matrix products: 571 us -> 68.8 us  [the longest x12 20.6 us: mm_nt(): lax.dot_general(left, right, (((1,), (1,)), ((), ())), preferred_element_...]
    pallas_call x0 -> x5, Pallas kernels: none -> 349 us  [the longest x2 134 us: ring_gather(): pl.pallas_call(functools.partial(gather_kernel, count, shapes), out_shape...]
    unnamed x32 -> x5, waiting for transfers between devices: 158 us -> 0.08 us
    all_gather x4 -> x2, blocking collectives: 124 us -> 59.3 us  [the longest x1 33 us: local(): lax.all_gather(rest[rows_here:rows_here + share_rows].astype(bf16), 'pix'...]
    psum x2 -> x1, blocking collectives: 101 us -> 37.5 us  [local(): lax.psum((grad_raw, gain_part, grad_gain_one, grad_gain_attn, grad_gain_t...]
    convert_element_type x23 -> x12, other arithmetic: 70 us -> 23 us  [the longest x1 8.06 us: local(): jnp.where(hot.T[None], scale[:, :, None], 0.0).astype(bf16)]
  transfers between devices with their start and end apart: 29 -> 9, of which waited for: 23 -> 4; matrix products, arithmetic and copies ran while one was open for 18% -> 20% of each run, Pallas kernels for 0% -> 32%
where the time goes in v1:
time: 885 us; the launch traced here: 878 us
  Pallas kernels  349 us (39%)
  waiting for transfers between devices  112 us (13%)
  local copies, waits for them, and re-layouts  111 us (13%)
  blocking collectives  96.7 us (11%)
  other arithmetic  82.9 us (9%)
  matrix products  73.5 us (8%)
  starting transfers between devices  37.3 us (4%)
  between operations  15.3 us (2%)
    pallas_call x2, Pallas kernels, ring_gather(): pl.pallas_call(functools.partial(gather_kernel, count, shapes), out_shape...  134 us
    pallas_call x1, Pallas kernels, ring_reduce(): pl.pallas_call(functools.partial(reduce_kernel, count, teams), out_shape=...  115 us
    psum x1, waiting for transfers between devices, local(): lax.psum((grad_raw, gain_part, grad_gain_one, grad_gain_attn, grad_gain_t...  84.4 us
    pallas_call x1, Pallas kernels, grad_pass(): pl.pallas_call(grad_kernel, grid=(images, steps), in_specs=[pl.BlockSpec(...  66.5 us
    unnamed x189, local copies, waits for them, and re-layouts  40.4 us
    psum x1, blocking collectives, local(): lax.psum((grad_raw, gain_part, grad_gain_one, grad_gain_attn, grad_gain_t...  37.5 us
    pallas_call x1, Pallas kernels, score_pass(): pl.pallas_call(score_kernel, grid=(images, steps), in_specs=[pl.BlockSpec...  33.4 us
    all_gather x1, blocking collectives, local(): lax.all_gather(rest[rows_here:rows_here + share_rows].astype(bf16), 'pix'...  33 us
  transfers between devices with their start and end apart: 9, of which 4 were waited for; matrix products, arithmetic and copies ran while one was open for 20% of the time, Pallas kernels for 32%

profile of v1, /device:TPU:0, one launch (start us, length us, event | category | flops | bytes accessed | tf_op | source)
XLA Modules:
  0.0 878.2 jit_solution(12404272955757641526)
XLA Ops:
  10.2 4.9 fusion.1
  20.8 4.9 copy.238
  25.7 8.1 select_convert_fusion.1
  36.2 36.2 %shard_map.356 = (bf16[1,8,64,1024]{3,2,1,0:T(8,128)(2,1)}, bf16[1,8,128,1024]{3,2,1,0:T(8,128)(2,1)}, bf16[1,8,128,512]{3,2,1,0:T(8,128)(2,1)}) custom-call(bf16[1,64,1024]{2,1,0:T(8,128)(2,1)} %bitcast.310, bf16[1,128,1024]{2,1,0:T(8,128)(2,1)} %bitcast.309, bf16[1,128,512]{2,1,0:T(8,128)(2,1)} %pad_bitcast_fusion.refs_2_), custom_call_target="tpu_custom_call" | custom-call | tf_op jit(solution)/shard_map/pallas_call | solution.py:265
  86.3 15.0 %pad_maximum_fusion = bf16[4,6272,256]{2,1,0:T(8,128)(2,1)} fusion(bf16[4,6272,4]{2,1,0:T(8,128)(2,1)} %copy.238, bf16[4,6272,252]{2,1,0:T(8,128)(2,1)} %select_convert_fusion.1), kind=kLoop, calls=%fused_computation.4 | loop fusion | flops 25690112 | bytes 25690112 | tf_op jit(solution)/shard_map/concatenate | solution.py:622
  101.2 6.5 select_convert_fusion
  107.8 10.8 %maximum_maximum_fusion.xt_ref = bf16[4,272,6272]{2,1,0:T(8,128)(2,1)} fusion(bf16[4,1,6272]{2,1,0:T(2,128)(2,1)S(1)} %copy-done.61, bf16[4,4,6272]{2,1,0:T(4,128)(2,1)S(1)} %copy-done.54, bf16[4,252,6272]{2,1,0:T(8,128)(2,1)} %select_convert_fusion, bf16[272]{0:T(512)(128)(2,1)S(1)} %pad.39.clone), kind=kLoop, calls=%fused_computation.3 | loop fusion | flops 54591488 | bytes 26543648 | tf_op jit(solution)/shard_map/concatenate | solution.py:613
  118.6 33.4 %shard_map.357 = (f32[4,272,512]{2,1,0:T(8,128)S(1)}, f32[4,8,512]{2,1,0:T(8,128)S(1)}) custom-call(bf16[25088,256]{1,0:T(8,128)(2,1)} %bitcast.266, bf16[4,272,6272]{2,1,0:T(8,128)(2,1)} %maximum_maximum_fusion.xt_ref, bf16[256,512]{1,0:T(8,128)(2,1)S(1)} %fusion.55.at_ref), custom_call_target="tpu_custom_call" | custom-call | flops 13153337344 | bytes 25690112 | tf_op jit(solution)/shard_map/pallas_call | solution.py:83
  152.7 4.6 all-to-all-start.1
  167.3 6.0 all-to-all-start
  179.2 98.0 %shard_map.358 = bf16[8,8,128,1024]{3,2,1,0:T(8,128)(2,1)} custom-call(bf16[8,128,1024]{2,1,0:T(8,128)(2,1)} %bitcast_dynamic-update-slice_fusion.9.refs_0_), custom_call_target="tpu_custom_call" | custom-call | tf_op jit(solution)/shard_map/pallas_call | solution.py:265
  278.4 12.0 %fusion.106 = (bf16[1,8,128,1024]{3,2,1,0:T(8,128)(2,1)}, bf16[1,8,128,1024]{3,2,1,0:T(8,128)(2,1)}, bf16[1,8,128,1024]{3,2,1,0:T(8,128)(2,1)}, bf16[1,8,128,102...) fusion(bf16[8,8,128,1024]{3,2,1,0:T(8,128)(2,1)} %shard_map.358), kind=kLoop, calls=%fused_computation.290 | loop fusion | bytes 33554432 | tf_op jit(solution)/shard_map/slice | solution.py:568
  290.6 9.4 %all-to-all-start.3 = ((bf16[8,64,1024]{2,1,0:T(8,128)(2,1)}), bf16[8,64,1024]{2,1,0:T(8,128)(2,1)}, u32[]{:S(2)}, u32[]{:S(2)}) async-start(bf16[8,64,1024]{2,1,0:T(8,128)(2,1)} %bitcast_select_fusion), calls=%async_computation.3 | async-start | bytes 2097152 | tf_op jit(solution)/shard_map/all_to_all | solution.py:704
  299.9 12.0 %all-gather.6.cloned.1.call-start = ((), (), s32[]{:S(2)}) async-start(), calls=%async_computation.6 | async-start | bytes 3145728 | tf_op jit(solution)/shard_map/all_gather | solution.py:676
  321.5 4.8 all-to-all-done.3
  327.4 3.5 fusion.115
  338.3 17.7 %all-gather.6.cloned.1.call-done = bf16[2,512,1024]{2,1,0:T(8,128)(2,1)} async-done(((bf16[2,256,1024]{2,1,0:T(8,128)(2,1)}), bf16[2,512,1024]{2,1,0:T(8,128)(2,1)}) %all-gather.6.cloned.1.call-update) | async-done | bytes 2097168 | tf_op jit(solution)/shard_map/all_gather | solution.py:676
  362.3 4.8 fusion.112
  367.1 4.4 bitcast_dynamic-update-slice_fusion
  385.8 5.9 multiply_reduce_fusion
  395.4 3.9 multiply_convert_fusion
  411.4 4.8 all-to-all-start.2
  428.4 3.5 fusion.16
  439.9 3.5 fusion.116
  445.3 5.3 reduce-scatter.2.cloned.1.call-done
  468.5 26.2 %all-gather.2 = f32[8,2,256]{2,1,0:T(2,128)S(1)} all-gather(f32[1,2,256]{2,1,0:T(2,128)S(1)} %maximum_bitcast_fusion.1), channel_id=2, replica_groups=mesh['img'=4,'pix'=8] {'pix'}, dimensions={0}, use_global_device_ids=true | all-gather | bytes 18432 | tf_op jit(solution)/shard_map/all_gather | solution.py:747
  504.6 114.6 %shard_map.360 = f32[9,128,1024]{2,1,0:T(8,128)} custom-call(bf16[7,8,256,128]{3,2,1,0:T(8,128)(2,1)S(1)} %bitcast.258, bf16[9,256,1024]{2,1,0:T(8,128)(2,1)} %get-tuple-element.176.gs_ref), custom_call_target="tpu_custom_call" | custom-call | tf_op jit(solution)/shard_map/pallas_call | solution.py:459
  620.3 33.0 %all-gather.1 = bf16[1,264,1024]{2,0,1:T(2,128)(2,1)S(1)} all-gather(bf16[1,33,1024]{2,0,1:T(2,128)(2,1)S(1)} %copy.270), channel_id=3, replica_groups=mesh['img'=4,'pix'=8] {'pix'}, dimensions={1}, use_global_device_ids=true | all-gather | bytes 608256 | tf_op jit(solution)/shard_map/all_gather | solution.py:804
  655.9 3.9 slice_bitcast_fusion.5
  667.8 66.5 %shard_map.359 = (f32[272,512]{1,0:T(8,128)S(1)}, f32[4,8,6272]{2,1,0:T(8,128)S(1)}) custom-call(bf16[25088,256]{1,0:T(8,128)(2,1)} %bitcast.267, bf16[4,272,6272]{2,1,0:T(8,128)(2,1)} %maximum_maximum_fusion.xt_ref, bf16[256,512]{1,0:T(8,128)(2,1)S(1)} %copy-done.3, bf16[4,256,512]{2,1,0:T(8,128)(2,1)S(1)} %copy.257.bt_ref, ...), custom_call_target="tpu_custom_call" | custom-call | flops 32883343360 | bytes 25690112 | tf_op jit(solution)/shard_map/pallas_call | solution.py:136
  739.6 37.5 %all-reduce.3 = (f32[261]{0:T(512)}, f32[1024]{0:T(1024)}, f32[1024]{0:T(1024)}, f32[1024]{0:T(1024)}) all-reduce(f32[261]{0:T(512)S(1)} %add.495, f32[1024]{0:T(1024)S(1)} %get-tuple-element.160, f32[1024]{0:T(1024)S(1)} %get-tuple-element.158, f32[1024]{0:T(1024)S(1)} %get-tuple-element.156), channel_id=1, replica_groups=mesh['img'=4,'pix'=8] {'img','pix'}, use_global_device_ids=true, to_apply=%region_34.35 | all-reduce | flops 3333 | bytes 26664 | tf_op jit(solution)/shard_map/psum | solution.py:759
  777.1 84.4 %all-reduce.9.cloned.1.call-done = f32[512,261]{0,1:T(8,128)} async-done(((f32[512,261]{0,1:T(8,128)}), f32[512,261]{0,1:T(8,128)}) %all-reduce.9.cloned.1.call-update) | async-done | bytes 534544 | tf_op jit(solution)/shard_map/psum | solution.py:759
  (371 shorter events, 173.0 us)
Async XLA Ops:
  7.2 305.0 %all-reduce.7.cloned.1.call-start = ((), (), s32[]{:S(2)}) async-start(), calls=%async_computation.5 | async-start | bytes 1081344 | tf_op jit(solution)/shard_map/psum | solution.py:553
  10.1 7.2 copy-start.49
  10.2 9.2 %copy-start.60 = (s32[4,6272]{1,0:T(4,128)S(1)}, s32[4,6272]{1,0:T(4,128)}, u32[]{:S(2)}) copy-start(s32[4,6272]{1,0:T(4,128)} %param.22) | copy-start | bytes 301060
  20.2 81.0 %copy-start.53 = (f32[4,6272]{1,0:T(4,128)}, f32[4,6272]{1,0:T(4,128)S(1)}, u32[]{:S(2)}) copy-start(f32[4,6272]{1,0:T(4,128)S(1)} %get-tuple-element.184) | copy-start | bytes 301060
  25.7 9.7 %copy-start.67 = (bf16[261,128]{1,0:T(8,128)(2,1)S(1)}, bf16[261,128]{1,0:T(8,128)(2,1)}, u32[]{:S(2)}) copy-start(bf16[261,128]{1,0:T(8,128)(2,1)} %param.27) | copy-start | bytes 200452
  33.8 42.6 %copy-start.73 = (f32[1024]{0:T(1024)S(1)}, f32[1024]{0:T(1024)}, u32[]{:S(2)}) copy-start(f32[1024]{0:T(1024)} %param.25) | copy-start | bytes 12292
  79.0 6.1 copy-start.23
  80.8 582.0 %copy-start.21 = (f32[256,261]{0,1:T(8,128)}, f32[256,261]{0,1:T(8,128)S(1)}, u32[]{:S(2)}) copy-start(f32[256,261]{0,1:T(8,128)S(1)} %maximum_maximum_fusion.1) | copy-start | bytes 801796
  86.3 32.4 %copy-start.2 = (bf16[256,512]{1,0:T(8,128)(2,1)}, bf16[256,512]{1,0:T(8,128)(2,1)S(1)}, u32[]{:S(2)}) copy-start(bf16[256,512]{1,0:T(8,128)(2,1)S(1)} %fusion.55.at_ref) | copy-start | bytes 786436
  101.2 6.6 copy-start.54
  101.2 6.6 copy-start.61
  152.7 14.6 %all-to-all-start.1 = ((f32[8,2,256]{2,1,0:T(2,128)}), f32[8,2,256]{2,1,0:T(2,128)S(1)}, u32[]{:S(2)}, u32[]{:S(2)}) async-start(f32[8,2,256]{2,1,0:T(2,128)} %reshape.687), calls=%async_computation.1 | async-start | bytes 32768 | tf_op jit(solution)/shard_map/all_to_all | solution.py:658
  166.2 7.1 copy-start.64
  166.2 7.8 copy-start.5
  167.3 123.2 %all-to-all-start = ((bf16[8,261,256]{2,1,0:T(8,128)(2,1)}), bf16[8,261,256]{2,1,0:T(8,128)(2,1)S(1)}, u32[]{:S(2)}, u32[]{:S(2)}) async-start(bf16[8,261,256]{2,1,0:T(8,128)(2,1)} %convert_element_type.266), calls=%async_computation | async-start | bytes 2162688 | tf_op jit(solution)/shard_map/all_to_all | solution.py:655
  179.2 98.1 %copy-start.55 = (bf16[4,64,1024]{2,1,0:T(8,128)(2,1)S(1)}, bf16[4,64,1024]{2,1,0:T(8,128)(2,1)}, u32[]{:S(2)}) copy-start(bf16[4,64,1024]{2,1,0:T(8,128)(2,1)} %param.41) | copy-start | bytes 1572868
  290.5 21.8 %copy-start.69 = (f32[261]{0:T(512)S(1)}, f32[261]{0:T(512)}, u32[]{:S(2)}) copy-start(f32[261]{0:T(512)} %param.24) | copy-start | bytes 3136
  290.6 35.8 %all-to-all-start.3 = ((bf16[8,64,1024]{2,1,0:T(8,128)(2,1)}), bf16[8,64,1024]{2,1,0:T(8,128)(2,1)}, u32[]{:S(2)}, u32[]{:S(2)}) async-start(bf16[8,64,1024]{2,1,0:T(8,128)(2,1)} %bitcast_select_fusion), calls=%async_computation.3 | async-start | bytes 2097152 | tf_op jit(solution)/shard_map/all_to_all | solution.py:704
  299.9 56.0 %all-gather.6.cloned.1.call-start = ((), (), s32[]{:S(2)}) async-start(), calls=%async_computation.6 | async-start | bytes 3145728 | tf_op jit(solution)/shard_map/all_gather | solution.py:676
  321.4 129.3 %reduce-scatter.2.cloned.1.call-start = ((), (), s32[]{:S(2)}) async-start(), calls=%async_computation.7 | async-start | bytes 3145728 | tf_op jit(solution)/shard_map/reduce_scatter | solution.py:725
  385.8 5.9 copy-start.59
  410.2 6.5 copy-start.75
  411.4 8.8 copy-start.74
  411.4 32.1 %all-to-all-start.2 = ((bf16[8,64,1024]{2,1,0:T(8,128)(2,1)}), bf16[8,64,1024]{2,1,0:T(8,128)(2,1)}, u32[]{:S(2)}, u32[]{:S(2)}) async-start(bf16[8,64,1024]{2,1,0:T(8,128)(2,1)} %bitcast_select_fusion.1), calls=%async_computation.2 | async-start | bytes 2097152 | tf_op jit(solution)/shard_map/all_to_all | solution.py:695
  416.1 246.7 %all-gather.8.cloned.1.call-start = ((), (), s32[]{:S(2)}) async-start(), calls=%async_computation.8 | async-start | bytes 1216512 | tf_op jit(solution)/shard_map/all_gather | solution.py:746
  468.2 393.3 %all-reduce.9.cloned.1.call-start = ((), (), s32[]{:S(2)}) async-start(), calls=%async_computation.9 | async-start | bytes 1081344 | tf_op jit(solution)/shard_map/psum | solution.py:759
  468.3 30.6 %copy-start.42 = (bf16[1,256,8,128]{3,1,2,0:T(8,128)(2,1)S(1)}, bf16[1,256,8,128]{3,1,2,0:T(8,128)(2,1)}, u32[]{:S(2)}) copy-start(bf16[1,256,8,128]{3,1,2,0:T(8,128)(2,1)} %copy.266) | copy-start | bytes 1572868
  619.2 35.2 %copy-start.62 = (bf16[261,128]{1,0:T(8,128)(2,1)S(1)}, bf16[261,128]{1,0:T(8,128)(2,1)}, u32[]{:S(2)}) copy-start(bf16[261,128]{1,0:T(8,128)(2,1)} %param.28) | copy-start | bytes 200452
  667.8 68.1 %copy-start.22 = (f32[256,261]{0,1:T(8,128)S(1)}, f32[256,261]{0,1:T(8,128)}, u32[]{:S(2)}) copy-start(f32[256,261]{0,1:T(8,128)} %copy-done.21) | copy-start | bytes 801796
  667.8 68.1 %copy-start.24 = (f32[512,261]{0,1:T(8,128)S(1)}, f32[512,261]{0,1:T(8,128)}, u32[]{:S(2)}) copy-start(f32[512,261]{0,1:T(8,128)} %copy-done.23) | copy-start | bytes 1603588
  735.9 125.6 %copy-start.32 = (bf16[1,8,128,512]{3,2,1,0:T(8,128)(2,1)S(1)}, bf16[1,8,128,512]{3,2,1,0:T(8,128)(2,1)}, u32[]{:S(2)}) copy-start(bf16[1,8,128,512]{3,2,1,0:T(8,128)(2,1)} %get-tuple-element.29) | copy-start | bytes 3145732
  737.4 126.1 %copy-start.6 = (bf16[1,8,64,1024]{3,2,1,0:T(8,128)(2,1)S(1)}, bf16[1,8,64,1024]{3,2,1,0:T(8,128)(2,1)}, u32[]{:S(2)}) copy-start(bf16[1,8,64,1024]{3,2,1,0:T(8,128)(2,1)} %get-tuple-element.27) | copy-start | bytes 3145732
  (58 other events, 156.5 us)
Sparse Core Ops, SparseCore 0:
  11.4 75.8 all-reduce.6
  321.5 34.3 all-gather.5
  407.6 43.0 reduce-scatter.1
  468.3 39.9 all-gather.7
  737.5 123.9 all-reduce.8

commit v2 on v1

--- a/solution.py
+++ b/solution.py
@@ -450,10 +450,8 @@
 def ring_reduce(xs, gs, collective_id):
     count = lax.axis_size("pix")
     teams = lax.axis_size("img") // 2
-    kinds, rows, columns = xs.shape
+    kinds, _, rows, depth = xs.shape
     number, _, width = gs.shape
-    depth = columns // count
-    xs = jnp.swapaxes(xs.reshape(kinds, rows, count, depth), 1, 2)
     anywhere = pl.BlockSpec(memory_space=pl.ANY)
     chunk = (depth, width // 4)
     return pl.pallas_call(
@@ -485,25 +483,695 @@
     )(xs, gs)
 
 
+def peers(count):
+    group, me = lax.axis_index("img"), lax.axis_index("pix")
+    return [(group, lax.rem(me + d, count)) for d in range(1, count)]
+
+
+def exchange_kernel(count, number, spread, *refs):
+    sources, targets = refs[:number], refs[number : 2 * number]
+    own_sem, send_sem, recv_sem = refs[2 * number :]
+    me = lax.axis_index("pix")
+    others = peers(count)
+    greet(others)
+
+    def piece(a, to):
+        return sources[a] if spread[a] else sources[a].at[to]
+
+    def push(a, d):
+        return pltpu.make_async_remote_copy(
+            piece(a, others[d][1]),
+            targets[a].at[me],
+            send_sem.at[a, d],
+            recv_sem.at[a, d],
+            device_id=others[d],
+            device_id_type=MESH,
+        )
+
+    def keep(a):
+        return pltpu.make_async_copy(piece(a, me), targets[a].at[me], own_sem.at[a])
+
+    for d in range(count - 1):
+        for a in range(number):
+            push(a, d).start()
+    for a in range(number):
+        keep(a).start()
+    for a in range(number):
+        keep(a).wait()
+        for d in range(count - 1):
+            push(a, d).wait()
+
+
+def exchange(arrays, spread, collective_id):
+    count = lax.axis_size("pix")
+    number = len(arrays)
+    anywhere = pl.BlockSpec(memory_space=pl.ANY)
+    shapes = [((count,) if flag else ()) + a.shape for a, flag in zip(arrays, spread)]
+    return pl.pallas_call(
+        functools.partial(exchange_kernel, count, number, spread),
+        out_shape=[jax.ShapeDtypeStruct(s, a.dtype) for s, a in zip(shapes, arrays)],
+        in_specs=[anywhere] * number,
+        out_specs=[anywhere] * number,
+        scratch_shapes=[DMA((number,)), DMA((number, count - 1)), DMA((number, count - 1))],
+        compiler_params=pltpu.CompilerParams(collective_id=collective_id, has_side_effects=True),
+    )(*arrays)
+
+
+def sum_kernel(
+    count,
+    crowd,
+    t_ref,
+    g_ref,
+    z_ref,
+    t_out,
+    g_out,
+    z_out,
+    t_in,
+    g_in,
+    t_img,
+    g_img,
+    own_sem,
+    send_sem,
+    recv_sem,
+    img_send,
+    img_recv,
+    last_send,
+    last_recv,
+):
+    group, me = lax.axis_index("img"), lax.axis_index("pix")
+    others = peers(count)
+    across = [(lax.rem(group + d, crowd), me) for d in range(1, crowd)]
+    greet(others + across)
+
+    def copy(source, target, sems, index, device):
+        return pltpu.make_async_remote_copy(
+            source,
+            target,
+            sems[0].at[index],
+            sems[1].at[index],
+            device_id=device,
+            device_id_type=MESH,
+        )
+
+    def scatter(d):
+        to = others[d][1]
+        sems = (send_sem, recv_sem)
+        return (
+            copy(t_ref.at[to], t_in.at[d], sems, (0, d), others[d]),
+            copy(g_ref.at[to], g_in.at[d], sems, (1, d), others[d]),
+        )
+
+    def spread(d):
+        return copy(z_ref, z_out.at[me], (send_sem, recv_sem), (2, d), others[d])
+
+    def over(d):
+        sems = (img_send, img_recv)
+        return (
+            copy(t_img.at[group], t_img.at[group], sems, (0, d), across[d]),
+            copy(g_img.at[group], g_img.at[group], sems, (1, d), across[d]),
+        )
+
+    def gather(d):
+        sems = (last_send, last_recv)
+        return (
+            copy(t_out.at[me], t_out.at[me], sems, (0, d), others[d]),
+            copy(g_out.at[me], g_out.at[me], sems, (1, d), others[d]),
+        )
+
+    for d in range(count - 1):
+        for part in scatter(d):
+            part.start()
+    for d in range(count - 1):
+        spread(d).start()
+    keep = pltpu.make_async_copy(z_ref, z_out.at[me], own_sem)
+    keep.start()
+    t_sum = t_ref[me].astype(f32)
+    g_sum = g_ref[me]
+    for d in range(count - 1):
+        for part in scatter(d):
+            part.wait_recv()
+        t_sum = t_sum + t_in[d].astype(f32)
+        g_sum = g_sum + g_in[d]
+    t_img[group] = t_sum.astype(bf16)
+    g_img[group] = g_sum
+    for d in range(crowd - 1):
+        for part in over(d):
+            part.start()
+    for d in range(crowd - 1):
+        for part in over(d):
+            part.wait_recv()
+    t_sum = t_img[0].astype(f32)
+    g_sum = g_img[0]
+    for i in range(1, crowd):
+        t_sum = t_sum + t_img[i].astype(f32)
+        g_sum = g_sum + g_img[i]
+    t_out[me] = t_sum.astype(bf16)
+    g_out[me] = g_sum
+    for d in range(count - 1):
+        for part in gather(d):
+            part.start()
+    keep.wait()
+    for d in range(count - 1):
+        for part in gather(d):
+            part.wait()
+        for part in scatter(d):
+            part.wait_send()
+        spread(d).wait()
+    for d in range(crowd - 1):
+        for part in over(d):
+            part.wait_send()
+
+
+def small_sums(t, g, z, collective_id):
+    count, crowd = lax.axis_size("pix"), lax.axis_size("img")
+    inside = pl.BlockSpec(memory_space=pltpu.VMEM)
+    return pl.pallas_call(
+        functools.partial(sum_kernel, count, crowd),
+        out_shape=[
+            jax.ShapeDtypeStruct(t.shape, bf16),
+            jax.ShapeDtypeStruct(g.shape, f32),
+            jax.ShapeDtypeStruct((count,) + z.shape, bf16),
+        ],
+        in_specs=[inside] * 3,
+        out_specs=[inside] * 3,
+        scratch_shapes=[
+            pltpu.VMEM((count - 1,) + t.shape[1:], bf16),
+            pltpu.VMEM((count - 1,) + g.shape[1:], f32),
+            pltpu.VMEM((crowd,) + t.shape[1:], bf16),
+            pltpu.VMEM((crowd,) + g.shape[1:], f32),
+            DMA,
+            DMA((3, count - 1)),
+            DMA((3, count - 1)),
+            DMA((2, crowd - 1)),
+            DMA((2, crowd - 1)),
+            DMA((2, count - 1)),
+            DMA((2, count - 1)),
+        ],
+        compiler_params=pltpu.CompilerParams(
+            collective_id=collective_id, has_side_effects=True, vmem_limit_bytes=24 * 2**20
+        ),
+    )(t, g, z)
+
+
+def gelu_parts(z):
+    slope = (2.0 / jnp.pi) ** 0.5
+    square = z * z
+    bend = jnp.tanh(slope * z * (1.0 + 0.044715 * square))
+    half = 0.5 * (1.0 + bend)
+    return z * half, half + 0.5 * z * (1.0 - bend * bend) * slope * (1.0 + 0.134145 * square)
+
+
+def latent_kernel(
+    count,
+    images,
+    part_ref,
+    stat_ref,
+    own_ref,
+    cot_ref,
+    mix_ref,
+    gain_ref,
+    in_gain_ref,
+    w_ref,
+    out_ref,
+    xs_ref,
+    gs_ref,
+    back_ref,
+    row_ref,
+    gain_out,
+    in_gain_out,
+    wv,
+    one,
+    two,
+    three,
+    pre,
+    grad,
+    flow,
+    low,
+    heads_q,
+    kv,
+    probs,
+    kv_out,
+    kv_in,
+    cot,
+    final,
+    mean,
+    w_sem,
+    kv_send,
+    kv_recv,
+    gkv_send,
+    gkv_recv,
+    cot_own,
+    cot_send,
+    cot_recv,
+    out_own,
+    out_send,
+    out_recv,
+):
+    rows, width = own_ref.shape
+    depth = xs_ref.shape[3]
+    sharers = count // images
+    latents = rows * sharers
+    per = count // sharers
+    rows_here = latents // count
+    spare = xs_ref.shape[3] - rows_here
+    group, me = lax.axis_index("img"), lax.axis_index("pix")
+    slot, image = lax.rem(me, sharers), me // sharers
+    block = 256
+    blocks = width // block
+    row_block = min(rows, 64)
+    up_one, down_one, m_query, m_key, m_value, m_out, up_two, down_two = range(8)
+    scale = HEAD_DIM ** (-0.5)
+
+    def load(k):
+        return pltpu.make_async_copy(w_ref.at[k], wv.at[k], w_sem.at[k])
+
+    for k in range(8):
+        load(k).start()
+    greet(peers(count))
+
+    def cot_push(i):
+        to = i * sharers + me // per
+        return to, pltpu.make_async_remote_copy(
+            cot_ref.at[i],
+            cot.at[lax.rem(me, per)],
+            cot_send.at[i],
+            cot_recv.at[lax.rem(me, per)],
+            device_id=(group, to),
+            device_id_type=MESH,
+        )
+
+    def cot_keep():
+        return pltpu.make_async_copy(cot_ref.at[image], cot.at[lax.rem(me, per)], cot_own)
+
+    for i in range(images):
+        to, copy = cot_push(i)
+
+        @pl.when(to != me)
+        def _():
+            copy.start()
+
+        @pl.when(to == me)
+        def _():
+            cot_keep().start()
+
+    def columns(j, wide=block):
+        return pl.ds(pl.multiple_of(j * wide, wide), wide)
+
+    def over_columns(body):
+        pl.loop(0, blocks)(body)
+
+    def over_rows(body):
+        @pl.loop(0, rows // row_block)
+        def _(r):
+            body(pl.ds(pl.multiple_of(r * row_block, 16), row_block))
+
+    def put_x(j, c, value):
+        for b in range(block // depth):
+            xs_ref[j, c * (block // depth) + b] = value[:, b * depth : (b + 1) * depth]
+
+    def centre(rows_f32):
+        average = jnp.mean(rows_f32, axis=1, keepdims=True)
+        centred = rows_f32 - average
+        spread = jnp.mean(centred * centred, axis=1, keepdims=True)
+        scale_rows = lax.rsqrt(spread + eps)
+        return centred * scale_rows, scale_rows
+
+    def norm(source, k, target):
+        def body(r):
+            target[r] = (centre(source[r])[0] * gain_ref[k : k + 1, :]).astype(bf16)
+
+        over_rows(body)
+
+    def norm_grad(source, k):
+        def body(r):
+            hat, scale_rows = centre(source[r])
+            given = flow[r]
+            gain_out[k : k + 1, :] += jnp.sum(given * hat, axis=0, keepdims=True)
+            given = given * gain_ref[k : k + 1, :]
+            along = jnp.mean(given * hat, axis=1, keepdims=True)
+            grad[r] += scale_rows * (given - jnp.mean(given, axis=1, keepdims=True) - hat * along)
+
+        over_rows(body)
+
+    gain_out[...] = jnp.zeros_like(gain_out)
+
+    top = jnp.max(stat_ref[:, 0:1, :], axis=0)
+    total = jnp.zeros_like(top)
+    for d in range(count):
+        total = total + jnp.exp2(stat_ref[d, 0:1, :] - top) * stat_ref[d, 1:2, :]
+    raw = jnp.zeros(part_ref.shape[1:], f32)
+    for d in range(count):
+        raw = raw + part_ref[d].astype(f32) * (jnp.exp2(stat_ref[d, 0:1, :] - top) / total)
+    mean[0] = raw
+    mean[1] = raw * in_gain_ref[...]
+    row_ref[...] = jnp.zeros_like(row_ref)
+    row_ref[0:1, :] = top + jnp.log(total) * LOG2E
+
+    tall = count * spare
+    mean_tall = mean[1]
+    if tall > mean_tall.shape[0]:
+        mean_tall = jnp.concatenate(
+            [mean_tall, jnp.zeros((tall - mean_tall.shape[0], rows), f32)], axis=0
+        )
+    share_rows = -(-mean.shape[1] // count)
+    share_rows = -(-share_rows // 8) * 8
+    place = lax.broadcasted_iota(jnp.int32, (rows_here, rows), 0)
+    source_row = lax.broadcasted_iota(jnp.int32, (rows_here, rows), 1) + slot * rows
+    for o in range(count):
+        picks = jnp.where(place + o * rows_here == source_row, 1.0, 0.0)
+        piece = [picks, mean_tall[o * share_rows : (o + 1) * share_rows]]
+        if spare > share_rows:
+            piece.append(jnp.zeros((spare - share_rows, rows), f32))
+        xs_ref[6, o] = jnp.concatenate(piece, axis=0).T.astype(bf16)
+
+    mean_low = mean[1].astype(bf16)
+
+    @over_columns
+    def _(j):
+        one[:, columns(j)] = own_ref[:, columns(j)] + mm_tn(mean_low, mix_ref[:, columns(j)])
+
+    def feed(source, target, k, up, down, normed, x_hidden, keep):
+        norm(source, k, normed)
+        load(up).wait()
+
+        @over_columns
+        def _(j):
+            value = mm_nt(normed[...], wv[up, columns(j), :])
+            pre[keep, :, columns(j)] = value
+            hidden = gelu_parts(value)[0].astype(bf16)
+            low[:, columns(j)] = hidden
+            put_x(x_hidden, j, hidden)
+
+        load(down).wait()
+
+        @over_columns
+        def _(j):
+            value = source[:, columns(j)] + mm(low[...], wv[down, :, columns(j)])
+            target[:, columns(j)] = value.astype(target.dtype)
+
+    def feed_back(source, k, up, down, branch, x_pre, keep):
+        @over_columns
+        def _(j):
+            value = mm_nt(branch[...], wv[down, columns(j), :])
+            value = (value * gelu_parts(pre[keep, :, columns(j)])[1]).astype(bf16)
+            low[:, columns(j)] = value
+            put_x(x_pre, j, value)
+
+        @over_columns
+        def _(j):
+            flow[:, columns(j)] = mm(low[...], wv[up, :, columns(j)])
+
+        norm_grad(source, k)
+
+    feed(one, two, 0, up_one, down_one, gs_ref.at[4], 3, 0)
+
+    norm(two, 1, low)
+
+    def write_blocks(j, value):
+        put_x(0, j, value)
+
+    @over_columns
+    def _(j):
+        write_blocks(j, low[:, columns(j)])
+
+    load(m_key).wait()
+    load(m_value).wait()
+
+    @over_columns
+    def _(j):
+        kv[0, slot, :, columns(j)] = mm(low[...], wv[m_key, :, columns(j)]).astype(bf16)
+        kv[1, slot, :, columns(j)] = mm(low[...], wv[m_value, :, columns(j)]).astype(bf16)
+
+    def sharer(d):
+        return (group, image * sharers + lax.rem(slot + d, sharers))
+
+    def kv_push(d):
+        return pltpu.make_async_remote_copy(
+            kv.at[:, slot],
+            kv.at[:, slot],
+            kv_send.at[d - 1],
+            kv_recv.at[d - 1],
+            device_id=sharer(d),
+            device_id_type=MESH,
+        )
+
+    for d in range(1, sharers):
+        kv_push(d).start()
+    load(m_query).wait()
+
+    @over_columns
+    def _(j):
+        heads_q[:, columns(j)] = mm(low[...], wv[m_query, :, columns(j)]).astype(bf16)
+
+    for d in range(1, sharers):
+        kv_push(d).wait_recv()
+
+    @pl.loop(0, HEADS)
+    def _(h):
+        c = columns(h, HEAD_DIM)
+        k_all = kv[0, :, :, c].reshape(latents, HEAD_DIM)
+        v_all = kv[1, :, :, c].reshape(latents, HEAD_DIM)
+        scores = mm_nt(heads_q[:, c], k_all) * scale
+        shifted = jnp.exp(scores - jnp.max(scores, axis=1, keepdims=True))
+        p = shifted / jnp.sum(shifted, axis=1, keepdims=True)
+        probs[h] = p
+        low[:, c] = mm(p.astype(bf16), v_all).astype(bf16)
+
+    @over_columns
+    def _(j):
+        put_x(1, j, low[:, columns(j)])
+
+    load(m_out).wait()
+
+    @over_columns
+    def _(j):
+        three[:, columns(j)] = two[:, columns(j)] + mm(low[...], wv[m_out, :, columns(j)])
+
+    feed(three, final, 2, up_two, down_two, gs_ref.at[6], 5, 1)
+
+    def out_push(b):
+        to = slot * per + b
+        return to, pltpu.make_async_remote_copy(
+            final.at[pl.ds(b * rows_here, rows_here)],
+            out_ref.at[image],
+            out_send.at[b],
+            out_recv.at[image],
+            device_id=(group, to),
+            device_id_type=MESH,
+        )
+
+    def out_keep():
+        mine = pl.ds(pl.multiple_of(lax.rem(me, per) * rows_here, 16), rows_here)
+        return pltpu.make_async_copy(final.at[mine], out_ref.at[image], out_own)
+
+    for b in range(per):
+        to, copy = out_push(b)
+
+        @pl.when(to != me)
+        def _():
+            copy.start()
+
+        @pl.when(to == me)
+        def _():
+            out_keep().start()
+
+    def cot_from(b):
+        return pltpu.make_async_remote_copy(
+            cot_ref.at[0],
+            cot.at[b],
+            cot_send.at[0],
+            cot_recv.at[b],
+            device_id=(group, me),
+            device_id_type=MESH,
+        )
+
+    for b in range(per):
+
+        @pl.when(slot * per + b != me)
+        def _():
+            cot_from(b).wait_recv()
+
+        @pl.when(slot * per + b == me)
+        def _():
+            cot_keep().wait()
+
+    given = cot[...].reshape(rows, width)
+    gs_ref[7] = given
+    grad[...] = given.astype(f32)
+    feed_back(three, 2, up_two, down_two, gs_ref.at[7], 4, 1)
+
+    gs_ref[3] = grad[...].astype(bf16)
+
+    @over_columns
+    def _(j):
+        low[:, columns(j)] = mm_nt(gs_ref[3], wv[m_out, columns(j), :]).astype(bf16)
+
+    @pl.loop(0, HEADS)
+    def _(h):
+        c = columns(h, HEAD_DIM)
+        k_all = kv[0, :, :, c].reshape(latents, HEAD_DIM)
+        v_all = kv[1, :, :, c].reshape(latents, HEAD_DIM)
+        p = probs[h]
+        g_mixed = low[:, c]
+        g_p = mm_nt(g_mixed, v_all)
+        g_v = mm_tn(p.astype(bf16), g_mixed)
+        delta = jnp.sum(p * g_p, axis=1, keepdims=True)
+        g_s = (p * (g_p - delta)).astype(bf16)
+        gs_ref[0, :, c] = (mm(g_s, k_all) * scale).astype(bf16)
+        g_k = mm_tn(g_s, heads_q[:, c]) * scale
+        kv_out[:, 0, :, c] = g_k.reshape(sharers, rows, HEAD_DIM).astype(bf16)
+        kv_out[:, 1, :, c] = g_v.reshape(sharers, rows, HEAD_DIM).astype(bf16)
+
+    def gkv_push(d):
+        to = lax.rem(slot + d, sharers)
+        return pltpu.make_async_remote_copy(
+            kv_out.at[to],
+            kv_in.at[d - 1],
+            gkv_send.at[d - 1],
+            gkv_recv.at[d - 1],
+            device_id=sharer(d),
+            device_id_type=MESH,
+        )
+
+    for d in range(1, sharers):
+        gkv_push(d).start()
+
+    @over_columns
+    def _(j):
+        flow[:, columns(j)] = mm_nt(gs_ref[0], wv[m_query, columns(j), :])
+
+    for d in range(1, sharers):
+        gkv_push(d).wait_recv()
+    for which in range(2):
+
+        @over_columns
+        def _(j):
+            value = kv_out[slot, which, :, columns(j)].astype(f32)
+            for d in range(1, sharers):
+                value = value + kv_in[d - 1, which, :, columns(j)].astype(f32)
+            gs_ref[1 + which, :, columns(j)] = value.astype(bf16)
+
+    @over_columns
+    def _(j):
+        flow[:, columns(j)] += mm_nt(gs_ref[1], wv[m_key, columns(j), :]) + mm_nt(
+            gs_ref[2], wv[m_value, columns(j), :]
+        )
+
+    norm_grad(two, 1)
+    gs_ref[5] = grad[...].astype(bf16)
+    feed_back(one, 0, up_one, down_one, gs_ref.at[5], 2, 0)
+    gs_ref[8] = grad[...].astype(bf16)
+    back = mm_nt(mix_ref[...], gs_ref[8])
+    back_ref[...] = back.astype(bf16)
+    row_ref[1:2, :] = jnp.sum(back * mean[1], axis=0, keepdims=True)
+    in_gain_out[...] = jnp.broadcast_to(
+        jnp.sum(back * mean[0], axis=1, keepdims=True), in_gain_out.shape
+    )
+
+    for i in range(images):
+        to, copy = cot_push(i)
+
+        @pl.when(to != me)
+        def _():
+            copy.wait_send()
+
+    for d in range(1, sharers):
+        kv_push(d).wait_send()
+        gkv_push(d).wait_send()
+
+    def out_from(i):
+        return pltpu.make_async_remote_copy(
+            final.at[pl.ds(0, rows_here)],
+            out_ref.at[i],
+            out_send.at[0],
+            out_recv.at[i],
+            device_id=(group, me),
+            device_id_type=MESH,
+        )
+
+    for b in range(per):
+        to, copy = out_push(b)
+
+        @pl.when(to != me)
+        def _():
+            copy.wait_send()
+
+    for i in range(images):
+        owner = i * sharers + me // per
+
+        @pl.when(owner != me)
+        def _():
+            out_from(i).wait_recv()
+
+        @pl.when(owner == me)
+        def _():
+            out_keep().wait()
+
+
+def latent_pass(parts, stats, own, cotangent, mix, gains, in_gain, whole, collective_id):
+    count = lax.axis_size("pix")
+    images, rows_here, width = cotangent.shape
+    rows = own.shape[0]
+    channels = mix.shape[0]
+    depth = width // count
+    sharers = count // images
+    per = count // sharers
+    inside = pl.BlockSpec(memory_space=pltpu.VMEM)
+    anywhere = pl.BlockSpec(memory_space=pl.ANY)
+    whole_f32 = pltpu.VMEM((rows, width), f32)
+    whole_low = pltpu.VMEM((rows, width), bf16)
+    shape = jax.ShapeDtypeStruct
+    return pl.pallas_call(
+        functools.partial(latent_kernel, count, images),
+        out_shape=[
+            shape((images, rows_here, width), bf16),
+            shape((7, count, rows, depth), bf16),
+            shape((9, rows, width), bf16),
+            shape((channels, rows), bf16),
+            shape((8, rows), f32),
+            shape((8, width), f32),
+            shape((channels, 128), f32),
+        ],
+        in_specs=[inside, inside, inside, anywhere, inside, inside, inside, anywhere],
+        out_specs=[anywhere] + [inside] * 6,
+        scratch_shapes=[
+            pltpu.VMEM((8, width, width), bf16),
+            whole_f32,
+            whole_f32,
+            whole_f32,
+            pltpu.VMEM((2, rows, width), f32),
+            whole_f32,
+            whole_f32,
+            whole_low,
+            whole_low,
+            pltpu.VMEM((2, sharers, rows, width), bf16),
+            pltpu.VMEM((HEADS, rows, rows * sharers), f32),
+            pltpu.VMEM((sharers, 2, rows, width), bf16),
+            pltpu.VMEM((max(sharers - 1, 1), 2, rows, width), bf16),
+            pltpu.VMEM((per, rows_here, width), bf16),
+            whole_low,
+            pltpu.VMEM((2, channels, rows), f32),
+            DMA((8,)),
+            DMA((sharers,)),
+            DMA((sharers,)),
+            DMA((sharers,)),
+            DMA((sharers,)),
+            DMA,
+            DMA((images,)),
+            DMA((per,)),
+            DMA,
+            DMA((per,)),
+            DMA((images,)),
+        ],
+        compiler_params=pltpu.CompilerParams(
+            collective_id=collective_id, has_side_effects=True, vmem_limit_bytes=60 * 2**20
+        ),
+    )(parts, stats, own, cotangent, mix, gains, in_gain, whole)
+
+
 def norm_back(resid, gain, grad):
     _, back = jax.vjp(layer_norm, resid, gain)
     return back(grad)
-
-
-def ffn(resid, gain, up_t, down):
-    normed = layer_norm(resid, gain).astype(bf16)
-    pre = mm_nt(normed, up_t)
-    hidden = jax.nn.gelu(pre).astype(bf16)
-    return resid + mm(hidden, down), (normed, pre, hidden)
-
-
-def ffn_back(resid, gain, up_t, down, saved, grad):
-    normed, pre, hidden = saved
-    branch = grad.astype(bf16)
-    _, gelu_back = jax.vjp(jax.nn.gelu, pre)
-    grad_pre = gelu_back(mm_nt(branch, down))[0].astype(bf16)
-    grad_input, grad_gain = norm_back(resid, gain, mm(grad_pre, up_t))
-    return grad + grad_input, grad_gain, grad_pre, branch
 
 
 def local(
@@ -540,8 +1208,7 @@
     depth = w_query.shape[0]
     channels = gain_input.shape[0]
     width_scale = width ** (-0.5)
-    head_scale = HEAD_DIM ** (-0.5)
-    groups = [[i * sharers + j for j in range(sharers)] for i in range(images)]
+    tall = -(-channels // 16) * 16
 
     side = -(-channels // 512) * 512
     key_t = jnp.pad(w_key.T, ((0, 0), (0, side - channels)))
@@ -564,9 +1231,7 @@
         ]
     )
     (whole,) = ring_gather([shards], 1)
-    up_one, down_one, self_query, self_key, self_value, self_out, up_two, down_two = [
-        whole[k].reshape(width, width) for k in range(8)
-    ]
+    whole = whole.reshape(8, width, width)
 
     lines = pixels // SIDE
     u, sin_u, cos_u = angles(me * lines + lax.iota(jnp.int32, lines))
@@ -652,113 +1317,74 @@
         split = value.reshape(images, lead, sharers, rows_own)
         return jnp.swapaxes(split, 1, 2).reshape(count, lead, rows_own)
 
-    raw_parts = lax.all_to_all(
-        by_owner(raw).astype(bf16), "pix", split_axis=0, concat_axis=0, tiled=True
+    raw = jnp.pad(raw, ((0, 0), (0, tall - channels), (0, 0)))
+    stat = jnp.pad(jnp.stack([tops, totals], axis=1), ((0, 0), (0, 6), (0, 0)))
+    raw_parts, stat_parts = exchange(
+        [by_owner(raw).astype(bf16), by_owner(stat)], (False, False), 3
     )
-    stat_parts = lax.all_to_all(
-        by_owner(jnp.stack([tops, totals], axis=1)), "pix", split_axis=0, concat_axis=0, tiled=True
+
+    own = lax.dynamic_slice_in_dim(latent_float, slot * rows_own, rows_own, 0)
+    latent_out, xs, gs, back_t, row_stats, gain_grads, in_gain = latent_pass(
+        raw_parts,
+        stat_parts,
+        own,
+        cotangent,
+        jnp.pad(value_out, ((0, tall - channels), (0, 0))),
+        jnp.stack([gain_mlp_one, gain_self, gain_mlp_two]),
+        jnp.pad(gain_input, (0, tall - channels))[:, None],
+        whole,
+        4,
     )
-    top = jnp.max(stat_parts[:, 0, :], axis=0)
-    share = jnp.exp2(stat_parts[:, 0, :] - top[None, :])
-    total = jnp.sum(share * stat_parts[:, 1, :], axis=0)
-    share = share / total[None, :]
-    raw_t = jnp.sum(raw_parts.astype(f32) * share[:, None, :], axis=0)
-    norm_log = top + jnp.log2(total)
-
-    mean_t = raw_t * gain_input[:, None]
-    mean_low = mean_t.astype(bf16)
-    own = lax.dynamic_slice_in_dim(latent_float, slot * rows_own, rows_own, 0)
-    resid_one = own + mm_tn(mean_low, value_out)
-    resid_two, saved_one = ffn(resid_one, gain_mlp_one, up_one, down_one)
-    normed_two = layer_norm(resid_two, gain_self).astype(bf16)
-    heads_q = mm(normed_two, self_query).astype(bf16).reshape(rows_own, HEADS, HEAD_DIM)
-    own_kv = jnp.stack([mm(normed_two, self_key), mm(normed_two, self_value)]).astype(bf16)
-    all_kv = lax.all_gather(own_kv, "pix", axis=1, tiled=True, axis_index_groups=groups)
-    heads_k, heads_v = [all_kv[k].reshape(latents, HEADS, HEAD_DIM) for k in range(2)]
-    scores = jnp.einsum("rhd,khd->hrk", heads_q, heads_k, preferred_element_type=f32) * head_scale
-    shifted = jnp.exp(scores - jnp.max(scores, axis=2, keepdims=True))
-    probs = shifted / jnp.sum(shifted, axis=2, keepdims=True)
-    probs_low = probs.astype(bf16)
-    mixed = (
-        jnp.einsum("hrk,khd->rhd", probs_low, heads_v, preferred_element_type=f32)
-        .reshape(rows_own, width)
-        .astype(bf16)
+    summed = ring_reduce(xs, gs, 2)
+
+    back_all, row_all = exchange([back_t, row_stats], (True, True), 5)
+
+    def by_image(value):
+        lead = value.shape[1]
+        split = value.reshape(images, sharers, lead, rows_own)
+        return jnp.swapaxes(split, 1, 2).reshape(images, lead, latents)
+
+    back_all = by_image(back_all)[:, :channels].astype(f32)
+    bt = jnp.einsum(
+        "kc,icq->ikq",
+        gained,
+        back_all,
+        precision=lax.Precision.HIGHEST,
+        preferred_element_type=f32,
+    ).astype(bf16)
+    grad_t, pixel_out = grad_pass(
+        x, xt, at, bt, a_low, jnp.swapaxes(bt, 1, 2), by_image(row_all)
     )
-    resid_three = resid_two + mm(mixed, self_out)
-    final, saved_two = ffn(resid_three, gain_mlp_two, up_two, down_two)
-
-    per = rows_own // rows_here
-    pieces = final.astype(bf16).reshape(per, rows_here, width)
-    target = lax.iota(jnp.int32, count)
-    mine = (target // per == slot)[:, None, None]
-    outgoing = jnp.where(mine, jnp.tile(pieces, (count // per, 1, 1)), jnp.zeros((), bf16))
-    incoming = lax.all_to_all(outgoing, "pix", split_axis=0, concat_axis=0, tiled=True)
-    incoming = incoming.reshape(images, sharers, rows_here, width)
-    latent_out = lax.dynamic_index_in_dim(incoming, me // per, axis=1, keepdims=False)
-
-    outgoing = jnp.where(
-        (lax.iota(jnp.int32, sharers) == me // per)[None, :, None, None],
-        cotangent[:, None],
-        jnp.zeros((), bf16),
-    ).reshape(count, rows_here, width)
-    incoming = lax.all_to_all(outgoing, "pix", split_axis=0, concat_axis=0, tiled=True)
-    grad_final = lax.dynamic_slice_in_dim(incoming, slot * per, per, 0).reshape(rows_own, width)
-    grad_final = grad_final.astype(f32)
-
-    grad_three, grad_gain_two, grad_pre_two, branch_two = ffn_back(
-        resid_three, gain_mlp_two, up_two, down_two, saved_two, grad_final
-    )
-    branch = grad_three.astype(bf16)
-    grad_mixed = mm_nt(branch, self_out).astype(bf16).reshape(rows_own, HEADS, HEAD_DIM)
-    grad_probs = jnp.einsum("rhd,khd->hrk", grad_mixed, heads_v, preferred_element_type=f32)
-    grad_v_all = jnp.einsum("hrk,rhd->khd", probs_low, grad_mixed, preferred_element_type=f32)
-    delta = jnp.sum(probs * grad_probs, axis=2, keepdims=True)
-    grad_scores = (probs * (grad_probs - delta)).astype(bf16)
-    grad_q = (
-        (jnp.einsum("hrk,khd->rhd", grad_scores, heads_k, preferred_element_type=f32) * head_scale)
-        .astype(bf16)
-        .reshape(rows_own, width)
-    )
-    grad_k_all = (
-        jnp.einsum("hrk,rhd->khd", grad_scores, heads_q, preferred_element_type=f32) * head_scale
-    )
-    grad_kv = lax.psum_scatter(
-        jnp.stack([grad_k_all, grad_v_all]).reshape(2, latents, width).astype(bf16),
-        "pix",
-        scatter_dimension=1,
-        tiled=True,
-        axis_index_groups=groups,
-    )
-    grad_k, grad_v = grad_kv[0], grad_kv[1]
-    grad_normed_two = (
-        mm_nt(grad_q, self_query) + mm_nt(grad_k, self_key) + mm_nt(grad_v, self_value)
-    )
-    grad_in_two, grad_gain_attn = norm_back(resid_two, gain_self, grad_normed_two)
-    grad_two = grad_three + grad_in_two
-    grad_one, grad_gain_one, grad_pre_one, branch_one = ffn_back(
-        resid_one, gain_mlp_one, up_one, down_one, saved_one, grad_two
-    )
-    grad_cross = grad_one.astype(bf16)
-    back_mat = mm_nt(grad_cross, value_out)
-    delta_one = jnp.sum(back_mat * mean_t.T, axis=1)
-    gain_part = jnp.sum(back_mat * raw_t.T, axis=0)
-
-    back_all = lax.all_gather(back_mat.astype(bf16), "pix", axis=0, tiled=True)
-    stats = lax.all_gather(jnp.stack([norm_log, delta_one]), "pix", axis=0)
-    stats = jnp.swapaxes(stats, 0, 1).reshape(2, images, latents)
-    stats = jnp.pad(jnp.swapaxes(stats, 0, 1), ((0, 0), (0, 6), (0, 0)))
-    back_x = exact(back_all.astype(f32), gained.T).astype(bf16).reshape(images, latents, CHANNELS)
-    grad_t, pixel_out = grad_pass(x, xt, at, jnp.swapaxes(back_x, 1, 2), a_low, back_x, stats)
     moved = (pixel_out[:, 4:7] - pixel_out[:, 7:8] / channels) - (
         (colours - average[:, None, :]) * scale[:, None, :]
     ) * (pixel_out[:, 0:1] / channels)
     grad_pixels = moved * (scale * keep)[:, None, :]
 
     grad_raw = exact(grad_t[:CHANNELS].T, table)
-    gain_part = gain_part + jnp.sum(score_mat * grad_raw, axis=0)
-    grad_raw, gain_in, gain_one, gain_attn, gain_two = lax.psum(
-        (grad_raw, gain_part, grad_gain_one, grad_gain_attn, grad_gain_two), ("img", "pix")
+    across = -(-channels // 128) * 128
+    cells = -(-(3 * width + channels) // (count * 1024)) * 1024
+    loose = jnp.concatenate([gain_grads[:3].reshape(-1), in_gain[:channels, 0]])
+    loose = jnp.pad(loose, (0, count * cells - loose.shape[0])).reshape(count, 8, cells // 8)
+    share_rows = -(-(-(-tall // count)) // 8) * 8
+    rest = summed[8]
+    spare = -(-share_rows // 16) * 16
+    cross_rows = jnp.pad(
+        rest[rows_here : rows_here + share_rows].astype(bf16), ((0, spare - share_rows), (0, 0))
     )
+    grad_raw, loose, cross_sum = small_sums(
+        jnp.pad(grad_raw, ((0, 0), (0, across - channels)))
+        .astype(bf16)
+        .reshape(count, rows_here, across),
+        loose,
+        cross_rows,
+        6,
+    )
+    grad_raw = grad_raw.reshape(latents, across)[:, :channels].astype(f32)
+    loose = loose.reshape(-1)
+    gain_one, gain_attn, gain_two = [loose[k * width : (k + 1) * width] for k in range(3)]
+    gain_in = loose[3 * width : 3 * width + channels] + jnp.sum(score_mat * grad_raw, axis=0)
+    cross_sum = cross_sum[:, :share_rows].reshape(-1, width)[:channels]
+
     grad_x = (grad_raw * (gain_input * width_scale)[None, :]).astype(bf16)
     query_grad = mm(grad_x, key_mat).astype(bf16)
     latent_cols = lax.dynamic_slice_in_dim(latent_normed, me * depth, depth, 1)
@@ -770,40 +1396,9 @@
     key_cols = w_key.shape[1]
     grad_w_key = mm_tn(grad_x, lax.dynamic_slice_in_dim(queries, me * key_cols, key_cols, 1))
 
-    share_rows = -(-channels // count)
-    picks = jnp.eye(rows_own, latents, dtype=bf16)
-    picks = jnp.roll(picks, slot * rows_own, axis=1).reshape(rows_own, count, rows_here)
-    mean_rows = jnp.pad(mean_low.T, ((0, 0), (0, share_rows * count - channels)))
-    mean_rows = mean_rows.reshape(rows_own, count, share_rows)
-    last = jnp.concatenate(
-        [picks, mean_rows, jnp.zeros((rows_own, count, depth - rows_here - share_rows), bf16)],
-        axis=2,
-    ).reshape(rows_own, width)
-    normed_one, _, hidden_one = saved_one
-    normed_last, _, hidden_last = saved_two
-    xs = jnp.stack(
-        [normed_two, mixed, grad_pre_one, hidden_one, grad_pre_two, hidden_last, last]
-    )
-    gs = jnp.stack(
-        [
-            grad_q,
-            grad_k,
-            grad_v,
-            branch,
-            normed_one,
-            branch_one,
-            normed_last,
-            branch_two,
-            grad_cross,
-        ]
-    )
-    summed = ring_reduce(xs, gs, 2)
     g_sq, g_sk, g_sv, g_so, g_up_one, g_down_one, g_up_two, g_down_two, rest = [
         summed[k] for k in range(9)
     ]
-    cross_sum = lax.all_gather(
-        rest[rows_here : rows_here + share_rows].astype(bf16), "pix", axis=0, tiled=True
-    )[:channels]
     grad_w_value = mm_nt(cross_sum, w_cross_out)
     grad_w_cross_out = mm_tn(w_value, cross_sum)
     grad_latent_array = rest[:rows_here] + grad_latent_own

time: 885 us -> 688 us (0.78)
  Pallas kernels: 349 us -> 533 us
  waiting for transfers between devices: 112 us -> 0.02 us
  blocking collectives: 96.7 us -> 0 us
  local copies, waits for them, and re-layouts: 111 us -> 46.2 us
  matrix products: 73.5 us -> 20.5 us
  starting transfers between devices: 37.3 us -> 0.04 us
  other arithmetic: 82.9 us -> 63.5 us
    pallas_call x0 -> x4, Pallas kernels: none -> 191 us  [the longest x1 101 us: latent_pass(): pl.pallas_call(functools.partial(latent_kernel, count, images), out_shape...]
    psum x1 -> x0, waiting for transfers between devices: 84.4 us -> none  [local(): lax.psum((grad_raw, gain_part, grad_gain_one, grad_gain_attn, grad_gain_t...]
    all_gather x2 -> x0, blocking collectives: 59.3 us -> none  [the longest x1 33 us: local(): lax.all_gather(rest[rows_here:rows_here + share_rows].astype(bf16), 'pix'...]
    psum x1 -> x0, blocking collectives: 37.5 us -> none  [local(): lax.psum((grad_raw, gain_part, grad_gain_one, grad_gain_attn, grad_gain_t...]
    all_to_all x4 -> x0, starting transfers between devices: 24.7 us -> none  [the longest x2 14.1 us: local(): lax.all_to_all(outgoing, 'pix', split_axis=0, concat_axis=0, tiled=True)]
    all_gather x2 -> x0, waiting for transfers between devices: 17.7 us -> none  [the longest x1 17.7 us: local(): lax.all_gather(own_kv, 'pix', axis=1, tiled=True, axis_index_groups=groups)]
    unnamed x189 -> x123, local copies, waits for them, and re-layouts: 40.4 us -> 23 us
    dot_general x12 -> x3, matrix products: 20.6 us -> 3.63 us  [mm_nt(): lax.dot_general(left, right, (((1,), (1,)), ((), ())), preferred_element_...]
  transfers between devices with their start and end apart: 9 -> 1, of which waited for: 4 -> 0; matrix products, arithmetic and copies ran while one was open for 20% -> 12% of each run, Pallas kernels for 32% -> 27%
where the time goes in v2:
time: 688 us; the launch traced here: 679 us
  Pallas kernels  533 us (77%)
  other arithmetic  63.5 us (9%)
  local copies, waits for them, and re-layouts  46.2 us (7%)
  matrix products  20.5 us (3%)
  between operations  15.6 us (2%)
    pallas_call x2, Pallas kernels, ring_gather(): pl.pallas_call(functools.partial(gather_kernel, count, shapes), out_shape...  124 us
    pallas_call x1, Pallas kernels, ring_reduce(): pl.pallas_call(functools.partial(reduce_kernel, count, teams), out_shape=...  118 us
    pallas_call x1, Pallas kernels, latent_pass(): pl.pallas_call(functools.partial(latent_kernel, count, images), out_shape...  101 us
    pallas_call x1, Pallas kernels, grad_pass(): pl.pallas_call(grad_kernel, grid=(images, steps), in_specs=[pl.BlockSpec(...  66.6 us
    pallas_call x1, Pallas kernels, small_sums(): pl.pallas_call(functools.partial(sum_kernel, count, crowd), out_shape=[ja...  45.3 us
    pallas_call x2, Pallas kernels, exchange(): pl.pallas_call(functools.partial(exchange_kernel, count, number, spread),...  45.1 us
    pallas_call x1, Pallas kernels, score_pass(): pl.pallas_call(score_kernel, grid=(images, steps), in_specs=[pl.BlockSpec...  33.4 us
    unnamed x123, local copies, waits for them, and re-layouts  23 us
  transfers between devices with their start and end apart: 1, of which 0 were waited for; matrix products, arithmetic and copies ran while one was open for 12% of the time, Pallas kernels for 27%

profile of v2, /device:TPU:0, one launch (start us, length us, event | category | flops | bytes accessed | tf_op | source)
XLA Modules:
  0.0 678.8 jit_solution(3105429194865773868)
XLA Ops:
  8.1 2.0 convolution_convert_fusion.3
  10.2 2.2 fusion.1
  12.4 3.6 fusion
  23.0 4.8 copy.114
  27.8 6.6 select_convert_fusion.1
  35.2 36.2 %shard_map.356 = (bf16[1,8,64,1024]{3,2,1,0:T(8,128)(2,1)}, bf16[1,8,128,1024]{3,2,1,0:T(8,128)(2,1)}, bf16[1,8,128,512]{3,2,1,0:T(8,128)(2,1)}) custom-call(bf16[1,64,1024]{2,1,0:T(8,128)(2,1)} %bitcast.150, bf16[1,128,1024]{2,1,0:T(8,128)(2,1)} %bitcast.149, bf16[1,128,512]{2,1,0:T(8,128)(2,1)} %pad_bitcast_fusion.refs_2_), custom_call_target="tpu_custom_call" | custom-call | tf_op jit(solution)/shard_map/pallas_call | solution.py:265
  81.6 8.1 %select_convert_fusion = bf16[4,252,6272]{2,1,0:T(8,128)(2,1)} fusion(f32[4,6272]{1,0:T(4,128)S(1)} %get-tuple-element.172, pred[252,6272]{1,0:T(8,128)(4,1)} %fusion.1), kind=kLoop, calls=%fused_computation | loop fusion | flops 6322176 | bytes 14325248 | tf_op jit(solution)/shard_map/convert_element_type | solution.py:1280
  89.8 16.1 %pad_maximum_fusion = bf16[4,6272,256]{2,1,0:T(8,128)(2,1)} fusion(bf16[4,6272,4]{2,1,0:T(8,128)(2,1)} %copy.114, bf16[4,6272,252]{2,1,0:T(8,128)(2,1)} %select_convert_fusion.1), kind=kLoop, calls=%fused_computation.3 | loop fusion | flops 25690112 | bytes 25690112 | tf_op jit(solution)/shard_map/concatenate | solution.py:1287
  105.9 5.9 maximum_maximum_fusion.xt_ref
  111.9 33.4 %shard_map.357 = (f32[4,272,512]{2,1,0:T(8,128)S(1)}, f32[4,8,512]{2,1,0:T(8,128)S(1)}) custom-call(bf16[25088,256]{1,0:T(8,128)(2,1)} %bitcast.135, bf16[4,272,6272]{2,1,0:T(8,128)(2,1)} %maximum_maximum_fusion.xt_ref, bf16[256,512]{1,0:T(8,128)(2,1)S(1)} %fusion.23.at_ref), custom_call_target="tpu_custom_call" | custom-call | flops 13153337344 | bytes 25690112 | tf_op jit(solution)/shard_map/pallas_call | solution.py:83
  145.3 2.1 fusion.4
  152.5 1.8 copy.119
  159.8 87.8 %shard_map.359 = bf16[8,8,128,1024]{3,2,1,0:T(8,128)(2,1)} custom-call(bf16[8,128,1024]{2,1,0:T(8,128)(2,1)} %copy-done.13), custom_call_target="tpu_custom_call" | custom-call | tf_op jit(solution)/shard_map/pallas_call | solution.py:265
  249.7 2.1 pad_maximum_fusion.1
  252.5 22.6 %shard_map.358 = (bf16[8,272,256]{2,1,0:T(8,128)(2,1)}, f32[8,8,256]{2,1,0:T(8,128)}) custom-call(bf16[8,272,256]{2,1,0:T(8,128)(2,1)} %bitcast.137, f32[8,8,256]{2,1,0:T(8,128)} %bitcast.148), custom_call_target="tpu_custom_call" | custom-call | tf_op jit(solution)/shard_map/pallas_call | solution.py:530
  276.8 1.9 pad.36.mix_ref
  278.7 100.9 %shard_map.360 = (bf16[4,64,1024]{2,1,0:T(8,128)(2,1)}, bf16[7,8,256,128]{3,2,1,0:T(8,128)(2,1)}, bf16[9,256,1024]{2,1,0:T(8,128)(2,1)}, bf16[272,256]{1,0:T(8,1...) custom-call(bf16[8,272,256]{2,1,0:T(8,128)(2,1)} %get-tuple-element.46.part_ref, ...), custom_call_target="tpu_custom_call" | custom-call | tf_op jit(solution)/shard_map/pallas_call | solution.py:1124
  379.6 2.0 copy-done.1
  381.7 117.6 %shard_map.363 = f32[9,128,1024]{2,1,0:T(8,128)} custom-call(bf16[7,8,256,128]{3,2,1,0:T(8,128)(2,1)S(1)} %copy-done.1, bf16[9,256,1024]{2,1,0:T(8,128)(2,1)} %get-tuple-element.55.gs_ref), custom_call_target="tpu_custom_call" | custom-call | tf_op jit(solution)/shard_map/pallas_call | solution.py:457
  500.4 22.5 %shard_map.361 = (bf16[8,272,256]{2,1,0:T(8,128)(2,1)}, f32[8,8,256]{2,1,0:T(8,128)}) custom-call(bf16[272,256]{1,0:T(8,128)(2,1)} %get-tuple-element.49.refs_0_, f32[8,256]{1,0:T(8,128)} %get-tuple-element.50.refs_1_), custom_call_target="tpu_custom_call" | custom-call | tf_op jit(solution)/shard_map/pallas_call | solution.py:530
  524.3 2.3 convolution_convert_fusion.1.b_ref
  528.9 66.6 %shard_map.362 = (f32[272,512]{1,0:T(8,128)S(1)}, f32[4,8,6272]{2,1,0:T(8,128)S(1)}) custom-call(bf16[25088,256]{1,0:T(8,128)(2,1)} %bitcast.136, bf16[4,272,6272]{2,1,0:T(8,128)(2,1)} %maximum_maximum_fusion.xt_ref, bf16[256,512]{1,0:T(8,128)(2,1)S(1)} %copy-done.3, bf16[4,256,512]{2,1,0:T(8,128)(2,1)S(1)} %copy.122.bt_ref, ...), custom_call_target="tpu_custom_call" | custom-call | flops 32883343360 | bytes 25690112 | tf_op jit(solution)/shard_map/pallas_call | solution.py:136
  596.5 45.3 %shard_map.364 = (bf16[8,64,384]{2,1,0:T(8,128)(2,1)S(1)}, f32[8,8,128]{2,1,0:T(8,128)S(1)}, bf16[8,48,1024]{2,1,0:T(8,128)(2,1)S(1)}) custom-call(bf16[8,64,384]{2,1,0:T(8,128)(2,1)S(1)} %bitcast.130, f32[8,8,128]{2,1,0:T(8,128)S(1)} %fusion.42.g_ref, bf16[48,1024]{1,0:T(8,128)(2,1)S(1)} %pad.40.z_ref), custom_call_target="tpu_custom_call" | custom-call | tf_op jit(solution)/shard_map/pallas_call | solution.py:648
  642.0 1.9 fusion.37
  643.8 2.0 convolution_convert_fusion
  646.0 4.4 slice_bitcast_fusion
  652.7 2.2 multiply_reduce_fusion
  654.9 2.1 fusion.55
  657.0 2.1 copy.127
  659.1 2.0 copy.128
  661.2 2.0 copy.126
  666.2 2.1 fusion.34
  (207 shorter events, 48.1 us)
Async XLA Ops:
  7.2 269.6 %all-reduce.10.cloned.1.call-start = ((), (), s32[]{:S(2)}) async-start(), calls=%async_computation | async-start | bytes 1081344 | tf_op jit(solution)/shard_map/psum | solution.py:1220
  10.2 9.2 %copy-start.16 = (bf16[4,3,6272]{2,0,1:T(4,128)(2,1)S(1)}, bf16[4,3,6272]{2,0,1:T(4,128)(2,1)}, u32[]{:S(2)}) copy-start(bf16[4,3,6272]{2,0,1:T(4,128)(2,1)} %param.21) | copy-start | bytes 451588
  10.2 9.7 %copy-start.28 = (s32[4,6272]{1,0:T(4,128)S(1)}, s32[4,6272]{1,0:T(4,128)}, u32[]{:S(2)}) copy-start(s32[4,6272]{1,0:T(4,128)} %param.22) | copy-start | bytes 301060
  20.8 7.0 %copy-start.14 = (f32[4,6272]{1,0:T(4,128)}, f32[4,6272]{1,0:T(4,128)S(1)}, u32[]{:S(2)}) copy-start(f32[4,6272]{1,0:T(4,128)S(1)} %get-tuple-element.173) | copy-start | bytes 301060
  20.8 60.8 %copy-start.21 = (f32[4,6272]{1,0:T(4,128)}, f32[4,6272]{1,0:T(4,128)S(1)}, u32[]{:S(2)}) copy-start(f32[4,6272]{1,0:T(4,128)S(1)} %get-tuple-element.172) | copy-start | bytes 301060
  27.8 6.6 copy-start.39
  34.4 40.3 %copy-start.41 = (f32[1024]{0:T(1024)S(1)}, f32[1024]{0:T(1024)}, u32[]{:S(2)}) copy-start(f32[1024]{0:T(1024)} %param.25) | copy-start | bytes 12292
  71.3 3.7 copy-start.50
  77.8 3.5 copy-start.10
  79.8 444.5 %copy-start.8 = (f32[256,261]{0,1:T(8,128)}, f32[256,261]{0,1:T(8,128)S(1)}, u32[]{:S(2)}) copy-start(f32[256,261]{0,1:T(8,128)S(1)} %maximum_maximum_fusion.1) | copy-start | bytes 801796
  81.6 30.3 %copy-start.2 = (bf16[256,512]{1,0:T(8,128)(2,1)}, bf16[256,512]{1,0:T(8,128)(2,1)S(1)}, u32[]{:S(2)}) copy-start(bf16[256,512]{1,0:T(8,128)(2,1)S(1)} %fusion.23.at_ref) | copy-start | bytes 786436
  89.8 16.1 %copy-start.5 = (bf16[4,252,6272]{2,1,0:T(8,128)(2,1)S(1)}, bf16[4,252,6272]{2,1,0:T(8,128)(2,1)}, u32[]{:S(2)}) copy-start(bf16[4,252,6272]{2,1,0:T(8,128)(2,1)} %select_convert_fusion) | copy-start | bytes 37933060
  89.8 16.1 %copy-start.23 = (bf16[4,4,6272]{2,1,0:T(4,128)(2,1)S(1)}, bf16[4,4,6272]{2,1,0:T(4,128)(2,1)}, u32[]{:S(2)}) copy-start(bf16[4,4,6272]{2,1,0:T(4,128)(2,1)} %multiply_convert_fusion.2) | copy-start | bytes 602116
  89.8 16.1 %copy-start.29 = (bf16[4,1,6272]{2,1,0:T(2,128)(2,1)S(1)}, bf16[4,1,6272]{2,1,0:T(2,128)(2,1)}, u32[]{:S(2)}) copy-start(bf16[4,1,6272]{2,1,0:T(2,128)(2,1)} %copy.115) | copy-start | bytes 150532
  154.3 4.0 copy-start.32
  154.3 4.0 copy-start.20
  154.3 4.0 copy-start.33
  247.6 27.5 %copy-start.45 = (f32[1024]{0:T(1024)S(1)}, f32[1024]{0:T(1024)}, u32[]{:S(2)}) copy-start(f32[1024]{0:T(1024)} %param.38) | copy-start | bytes 12292
  247.6 27.5 %copy-start.46 = (f32[1024]{0:T(1024)S(1)}, f32[1024]{0:T(1024)}, u32[]{:S(2)}) copy-start(f32[1024]{0:T(1024)} %param.33) | copy-start | bytes 12292
  247.6 27.5 %copy-start.47 = (f32[1024]{0:T(1024)S(1)}, f32[1024]{0:T(1024)}, u32[]{:S(2)}) copy-start(f32[1024]{0:T(1024)} %param.30) | copy-start | bytes 12292
  247.6 28.2 %copy-start.12 = (f32[512,1024]{1,0:T(8,128)S(1)}, f32[512,1024]{1,0:T(8,128)}, u32[]{:S(2)}) copy-start(f32[512,1024]{1,0:T(8,128)} %bitcast_convert_fusion) | copy-start | bytes 6291460
  381.7 118.6 %copy-start.42 = (f32[8,1024]{1,0:T(8,128)S(1)}, f32[8,1024]{1,0:T(8,128)}, u32[]{:S(2)}) copy-start(f32[8,1024]{1,0:T(8,128)} %get-tuple-element.57) | copy-start | bytes 98308
  381.7 118.6 %copy-start.36 = (f32[272,128]{1,0:T(8,128)S(1)}, f32[272,128]{1,0:T(8,128)}, u32[]{:S(2)}) copy-start(f32[272,128]{1,0:T(8,128)} %get-tuple-element.58) | copy-start | bytes 417796
  528.9 66.6 %copy-start.9 = (f32[256,261]{0,1:T(8,128)S(1)}, f32[256,261]{0,1:T(8,128)}, u32[]{:S(2)}) copy-start(f32[256,261]{0,1:T(8,128)} %copy-done.8) | copy-start | bytes 801796
  596.5 49.3 %copy-start.11 = (f32[512,261]{0,1:T(8,128)S(1)}, f32[512,261]{0,1:T(8,128)}, u32[]{:S(2)}) copy-start(f32[512,261]{0,1:T(8,128)} %copy-done.10) | copy-start | bytes 1603588
  645.8 6.9 %copy-start.18 = (bf16[512,1024]{1,0:T(8,128)(2,1)}, bf16[512,1024]{1,0:T(8,128)(2,1)S(1)}, u32[]{:S(2)}) copy-start(bf16[512,1024]{1,0:T(8,128)(2,1)S(1)} %convolution_convert_fusion) | copy-start | bytes 3145732
  646.0 4.5 copy-start.30
  657.0 7.0 %copy-start.15 = (f32[4,6272]{1,0:T(4,128)S(1)}, f32[4,6272]{1,0:T(4,128)}, u32[]{:S(2)}) copy-start(f32[4,6272]{1,0:T(4,128)} %copy-done.14) | copy-start | bytes 301060
  657.0 7.0 %copy-start.22 = (f32[4,6272]{1,0:T(4,128)S(1)}, f32[4,6272]{1,0:T(4,128)}, u32[]{:S(2)}) copy-start(f32[4,6272]{1,0:T(4,128)} %copy-done.21) | copy-start | bytes 301060
  657.0 7.1 %copy-start.27 = (f32[4,6272]{1,0:T(4,128)S(1)}, f32[4,6272]{1,0:T(4,128)}, u32[]{:S(2)}) copy-start(f32[4,6272]{1,0:T(4,128)} %get-tuple-element.174) | copy-start | bytes 301060
  661.2 5.0 copy-start.48
  664.1 6.6 copy-start.26
  (21 other events, 42.5 us)
Sparse Core Ops, SparseCore 0:
  11.4 75.7 all-reduce.9

commit v3 on v2

--- a/solution.py
+++ b/solution.py
@@ -54,114 +54,6 @@
     return 896 if pixels % 896 == 0 else pixels
 
 
-def score_kernel(x_ref, xt_ref, at_ref, u_ref, m_ref, acc, top):
-    step = pl.program_id(1)
-
-    @pl.when(step == 0)
-    def _():
-        acc[...] = jnp.zeros_like(acc)
-        top[...] = jnp.full_like(top, -jnp.inf)
-
-    scores = mm(x_ref[...], at_ref[...])
-    old = top[0:1, :]
-    new = jnp.maximum(old, jnp.max(scores, axis=0, keepdims=True))
-    weights = jnp.exp2(scores - new).astype(bf16)
-    acc[...] = acc[...] * jnp.exp2(old - new) + mm(xt_ref[0], weights)
-    top[...] = jnp.broadcast_to(new, top.shape)
-
-    @pl.when(step == pl.num_programs(1) - 1)
-    def _():
-        u_ref[0] = acc[...]
-        m_ref[0] = top[...]
-
-
-def score_pass(x, xt, at):
-    images, rows, pixels = xt.shape
-    tile = pixel_tile(pixels)
-    steps = pixels // tile
-    latents = at.shape[1]
-    return pl.pallas_call(
-        score_kernel,
-        grid=(images, steps),
-        in_specs=[
-            pl.BlockSpec((tile, CHANNELS), lambda i, t: (i * steps + t, 0)),
-            pl.BlockSpec((1, rows, tile), lambda i, t: (i, 0, t)),
-            pl.BlockSpec((CHANNELS, latents), lambda i, t: (0, 0)),
-        ],
-        out_specs=[
-            pl.BlockSpec((1, rows, latents), lambda i, t: (i, 0, 0)),
-            pl.BlockSpec((1, 8, latents), lambda i, t: (i, 0, 0)),
-        ],
-        out_shape=[
-            jax.ShapeDtypeStruct((images, rows, latents), f32),
-            jax.ShapeDtypeStruct((images, 8, latents), f32),
-        ],
-        scratch_shapes=[pltpu.VMEM((rows, latents), f32), pltpu.VMEM((8, latents), f32)],
-        compiler_params=pltpu.CompilerParams(vmem_limit_bytes=40 * 2**20),
-        cost_estimate=pl.CostEstimate(
-            flops=4 * images * pixels * CHANNELS * latents,
-            bytes_accessed=4 * images * pixels * CHANNELS,
-            transcendentals=images * pixels * latents,
-        ),
-    )(x, xt, at)
-
-
-def grad_kernel(x_ref, xt_ref, at_ref, bt_ref, a_ref, b_ref, stat_ref, t_ref, out_ref):
-    first = (pl.program_id(0) == 0) & (pl.program_id(1) == 0)
-
-    @pl.when(first)
-    def _():
-        t_ref[...] = jnp.zeros_like(t_ref)
-
-    x = x_ref[...]
-    scores = mm(x, at_ref[...])
-    grad_p = mm(x, bt_ref[0])
-    probs = jnp.exp2(scores - stat_ref[0, 0:1, :])
-    grad_s = (probs * (grad_p - stat_ref[0, 1:2, :])).astype(bf16)
-    probs = probs.astype(bf16)
-    t_ref[...] += mm(xt_ref[0], grad_s)
-    back = mm(grad_s, a_ref[...]) + mm(probs, b_ref[0])
-    along = jnp.sum(back * x.astype(f32), axis=1, keepdims=True)
-    half = back[:, CHANNELS - 128 :]
-    lane = lax.broadcasted_iota(jnp.int32, half.shape, 1)
-    half = jnp.where(lane == 120, along, half)
-    out_ref[0] = half.T[120:128, :]
-
-
-def grad_pass(x, xt, at, bt, a, b, stat):
-    images, rows, pixels = xt.shape
-    tile = pixel_tile(pixels)
-    steps = pixels // tile
-    latents = at.shape[1]
-    return pl.pallas_call(
-        grad_kernel,
-        grid=(images, steps),
-        in_specs=[
-            pl.BlockSpec((tile, CHANNELS), lambda i, t: (i * steps + t, 0)),
-            pl.BlockSpec((1, rows, tile), lambda i, t: (i, 0, t)),
-            pl.BlockSpec((CHANNELS, latents), lambda i, t: (0, 0)),
-            pl.BlockSpec((1, CHANNELS, latents), lambda i, t: (i, 0, 0)),
-            pl.BlockSpec((latents, CHANNELS), lambda i, t: (0, 0)),
-            pl.BlockSpec((1, latents, CHANNELS), lambda i, t: (i, 0, 0)),
-            pl.BlockSpec((1, 8, latents), lambda i, t: (i, 0, 0)),
-        ],
-        out_specs=[
-            pl.BlockSpec((rows, latents), lambda i, t: (0, 0)),
-            pl.BlockSpec((1, 8, tile), lambda i, t: (i, 0, t)),
-        ],
-        out_shape=[
-            jax.ShapeDtypeStruct((rows, latents), f32),
-            jax.ShapeDtypeStruct((images, 8, pixels), f32),
-        ],
-        compiler_params=pltpu.CompilerParams(vmem_limit_bytes=40 * 2**20),
-        cost_estimate=pl.CostEstimate(
-            flops=10 * images * pixels * CHANNELS * latents,
-            bytes_accessed=4 * images * pixels * CHANNELS,
-            transcendentals=images * pixels * latents,
-        ),
-    )(x, xt, at, bt, a, b, stat)
-
-
 MESH = pl.DeviceIdType.MESH
 DMA = pltpu.SemaphoreType.DMA
 
@@ -183,38 +75,119 @@
     pl.semaphore_wait(barrier, len(devices))
 
 
-def gather_kernel(count, shapes, *refs):
-    number = len(shapes)
-    sources, fulls = refs[:number], refs[number : 2 * number]
-    local_sem, send_sem, recv_sem, hand_send, hand_recv = refs[2 * number :]
+def hot_codes(tile):
+    pixel = lax.broadcasted_iota(jnp.int32, (tile, CHANNELS), 0)
+    channel = lax.broadcasted_iota(jnp.int32, (tile, CHANNELS), 1)
+    start = channel - SIDE - pixel // SIDE
+    code = jnp.where(start >= 0, start, -2)
+    code = jnp.where(channel < SIDE, jnp.where(channel == pixel % SIDE, -1, -2), code)
+    rows = jnp.where(channel >= CHANNELS - 4, -1, code)
+    return rows, jnp.where(channel >= CHANNELS - 4, -2, code).T
+
+
+def selector():
+    k = lax.broadcasted_iota(jnp.int32, (8, CHANNELS), 0)
+    channel = lax.broadcasted_iota(jnp.int32, (8, CHANNELS), 1)
+    own = channel - (CHANNELS - 8)
+    return jnp.where(jnp.where(own >= 4, own, 0) == k, 1.0, 0.0).astype(bf16)
+
+
+def build_x(values, base, code_ref, select_ref):
+    spread = mm_tn(values.astype(bf16), select_ref[...])
+    code = code_ref[...]
+    return jnp.where((code == -1) | (code == base), spread, 0.0).astype(bf16)
+
+
+def build_xt(values, base, code_ref):
+    code = code_ref[...]
+    hot = jnp.where((code == -1) | (code == base), values[0:1, :], 0.0)
+    last = hot[CHANNELS - 8 :, :]
+    k = lax.broadcasted_iota(jnp.int32, last.shape, 0)
+    last = jnp.where(k >= 4, values, last)
+    return jnp.concatenate([hot[: CHANNELS - 8, :], last], axis=0)
+
+
+def masked_xt(values, base, code_ref):
+    keep = values[1:2, :]
+    xt = (build_xt(values, base, code_ref) * keep).astype(bf16)
+    k = lax.broadcasted_iota(jnp.int32, (16, values.shape[1]), 0)
+    return jnp.concatenate([xt, jnp.where(k == 0, keep, 0.0).astype(bf16)], axis=0)
+
+
+def forward_kernel(
+    count,
+    images,
+    tile,
+    v_ref,
+    code_ref,
+    code_t_ref,
+    select_ref,
+    table_ref,
+    gained_ref,
+    gain_ref,
+    lat_ref,
+    wq_ref,
+    wk_ref,
+    w_ref,
+    lat_full,
+    wq_full,
+    wk_full,
+    w_full,
+    normed_ref,
+    query_ref,
+    a_ref,
+    at_ref,
+    alow_ref,
+    part_ref,
+    stat_ref,
+    lat_v,
+    wq_v,
+    wk_v,
+    acc,
+    top,
+    u_send,
+    s_send,
+    own_sem,
+    load_sem,
+    send_sem,
+    recv_sem,
+    hand_send,
+    hand_recv,
+    u_own,
+    u_out,
+    u_in,
+):
+    pixels = v_ref.shape[2]
+    steps = pixels // tile
+    lines = tile // SIDE
+    sharers = count // images
+    rows = part_ref.shape[2]
+    width = wq_ref.shape[2]
+    latents = normed_ref.shape[0]
     group, me = lax.axis_index("img"), lax.axis_index("pix")
     core = lax.rem(group, 2)
     place = ring_place(count)
     sides = ((group, ring_device(place + 1, count)), (group, ring_device(place - 1, count)))
     other = (group + 1 - 2 * core, me)
-    greet(sides + (other,))
-    own = [
-        pltpu.make_async_copy(sources[a], fulls[a].at[:, me], local_sem.at[a])
-        for a in range(number)
-    ]
-    for copy in own:
-        copy.start()
-    first = [sum(shape[0] for shape in shapes[:a]) for a in range(number)]
+    greet([other] + peers(count))
+    sources = (lat_ref, wq_ref, wk_ref, w_ref)
+    fulls = (lat_full, wq_full, wk_full, w_full)
+    mats = w_ref.shape[0]
 
     def spot(a, k, stage, way, source):
-        wide = shapes[a][2] // 4
+        wide = sources[a].shape[2] // 4
         columns = pl.ds(pl.multiple_of((core * 2 + way) * wide, 128), wide)
         if source:
             return sources[a].at[k, :, columns]
         origin = ring_device(place - stage if way == 0 else place + stage, count)
         return fulls[a].at[k, origin, :, columns]
 
-    def hop(a, k, stage, way):
+    def hop(a, k, stage, way, first=False):
         return pltpu.make_async_remote_copy(
-            spot(a, k, stage, way, stage == 0),
+            spot(a, k, stage, way, first),
             spot(a, k, stage, way, False),
-            send_sem.at[stage, way, first[a] + k],
-            recv_sem.at[stage, way, first[a] + k],
+            send_sem.at[stage, way, a + k],
+            recv_sem.at[stage, way, a + k],
             device_id=sides[way],
             device_id_type=MESH,
         )
@@ -224,63 +197,284 @@
         return pltpu.make_async_remote_copy(
             part,
             part,
-            hand_send.at[stage - 1, way, first[a] + k],
-            hand_recv.at[stage - 1, way, first[a] + k],
+            hand_send.at[stage - 1, way, a + k],
+            hand_recv.at[stage - 1, way, a + k],
             device_id=other,
             device_id_type=MESH,
         )
 
-    for stage in range(count):
-        for a in range(number):
-
-            @pl.loop(0, shapes[a][0])
-            def _(k):
-                for way in range(2):
-                    if stage > 0:
-                        hop(a, k, stage - 1, way).wait_recv()
-                    if stage < count - 1:
-                        hop(a, k, stage, way).start()
-                    if stage > 0:
-                        hand(a, k, stage, way).start()
-
+    def relay(a, k, stage, onward=True):
+        for way in range(2):
+            hop(a, k, stage - 1, way).wait_recv()
+            if onward:
+                hop(a, k, stage, way).start()
+            hand(a, k, stage, way).start()
+
+    own = [
+        pltpu.make_async_copy(sources[a], fulls[a].at[:, me], own_sem.at[a]) for a in range(4)
+    ]
+    for a in range(3):
+        for way in range(2):
+            hop(a, 0, 0, way, True).start()
     for copy in own:
+        copy.start()
+    for stage in range(1, count):
+        for a in range(3):
+            relay(a, 0, stage, stage < count - 1)
+        if stage <= mats:
+            for way in range(2):
+                hop(3, stage - 1, 0, way, True).start()
+    for k in range(count - 1, mats):
+        for way in range(2):
+            hop(3, k, 0, way, True).start()
+    for a in range(3):
+        own[a].wait()
+        for stage in range(1, count):
+            for way in range(2):
+                hand(a, 0, stage, way).wait_recv()
+
+    loads = [
+        pltpu.make_async_copy(full.at[0], held, load_sem.at[j])
+        for j, (full, held) in enumerate(((lat_full, lat_v), (wq_full, wq_v), (wk_full, wk_v)))
+    ]
+    for copy in loads:
+        copy.start()
+    loads[0].wait()
+    rows_here = lat_v.shape[1]
+
+    @pl.loop(0, count)
+    def _(o):
+        block = lat_v[o].astype(f32)
+        average = jnp.mean(block, axis=1, keepdims=True)
+        centred = block - average
+        spread = jnp.mean(centred * centred, axis=1, keepdims=True)
+        normed = (centred * lax.rsqrt(spread + eps) * gain_ref[...]).astype(bf16)
+        normed_ref[pl.ds(pl.multiple_of(o * rows_here, rows_here), rows_here), :] = normed
+
+    loads[1].wait()
+
+    @pl.loop(0, width // 256)
+    def _(j):
+        columns = pl.ds(pl.multiple_of(j * 256, 256), 256)
+        weight = wq_v[:, :, columns].reshape(width, 256)
+        query_ref[:, columns] = mm(normed_ref[...], weight).astype(bf16)
+
+    loads[2].wait()
+    a_ref[...] = mm(query_ref[...], wk_v[...].reshape(width, wk_v.shape[2])) * (width ** (-0.5))
+
+    def exact_nt(left, right):
+        return lax.dot_general(
+            left,
+            right,
+            (((1,), (1,)), ((), ())),
+            precision=lax.Precision.HIGHEST,
+            preferred_element_type=f32,
+        )
+
+    at_ref[...] = (exact_nt(gained_ref[...], a_ref[...]) * LOG2E).astype(bf16)
+    alow_ref[...] = exact_nt(a_ref[...], gained_ref[...]).astype(bf16)
+
+    relays = (count - 2) * mats
+
+    def relay_number(e):
+        relay(3, lax.rem(e, mats), 1 + e // mats)
+
+    def u_push(i, h):
+        to = i * sharers + h
+        sems = lambda which: dict(
+            send_sem=u_out.at[which, to],
+            recv_sem=u_in.at[which, me],
+            device_id=(group, to),
+            device_id_type=MESH,
+        )
+        return to, (
+            pltpu.make_async_remote_copy(u_send.at[i, h], part_ref.at[me], **sems(0)),
+            pltpu.make_async_remote_copy(s_send.at[i, h], stat_ref.at[me], **sems(1)),
+        )
+
+    def u_keep():
+        i, h = me // sharers, lax.rem(me, sharers)
+        return (
+            pltpu.make_async_copy(u_send.at[i, h], part_ref.at[me], u_own.at[0]),
+            pltpu.make_async_copy(s_send.at[i, h], stat_ref.at[me], u_own.at[1]),
+        )
+
+    @pl.loop(0, images * steps)
+    def _(t):
+        i, step = t // steps, lax.rem(t, steps)
+
+        @pl.when(t < relays)
+        def _():
+            relay_number(t)
+
+        @pl.when(step == 0)
+        def _():
+            acc[...] = jnp.zeros_like(acc)
+            top[...] = jnp.full_like(top, -jnp.inf)
+
+        values = v_ref[i, :, pl.ds(pl.multiple_of(step * tile, 128), tile)]
+        base = step * lines
+        x = build_x(values, base, code_ref, select_ref)
+        scores = mm(x, at_ref[...])
+        xt = masked_xt(values, base, code_t_ref)
+        old = top[0:1, :]
+        new = jnp.maximum(old, jnp.max(scores, axis=0, keepdims=True))
+        weights = jnp.exp2(scores - new).astype(bf16)
+        acc[...] = acc[...] * jnp.exp2(old - new) + mm(xt, weights)
+        top[...] = jnp.broadcast_to(new, top.shape)
+
+        @pl.when(step == steps - 1)
+        def _():
+            raw = jnp.dot(
+                table_ref[...],
+                acc[:CHANNELS, :],
+                precision=lax.Precision.HIGHEST,
+                preferred_element_type=f32,
+            ).astype(bf16)
+            stats = jnp.concatenate([top[0:1, :], acc[CHANNELS : CHANNELS + 1, :], top[0:6, :]], axis=0)
+            for h in range(sharers):
+                u_send[i, h] = raw[:, h * rows : (h + 1) * rows]
+                s_send[i, h] = stats[:, h * rows : (h + 1) * rows]
+            for h in range(sharers):
+                to, copies = u_push(i, h)
+
+                @pl.when(to != me)
+                def _():
+                    for copy in copies:
+                        copy.start()
+
+                @pl.when(to == me)
+                def _():
+                    for copy in u_keep():
+                        copy.start()
+
+    if images * steps < relays:
+
+        @pl.loop(images * steps, relays)
+        def _(e):
+            relay_number(e)
+
+    @pl.loop(0, mats)
+    def _(k):
+        relay(3, k, count - 1, False)
+
+    own[3].wait()
+    for a in range(3):
+        for way in range(2):
+            for stage in range(count - 1):
+                hop(a, 0, stage, way).wait_send()
+                hand(a, 0, stage + 1, way).wait_send()
+
+    @pl.loop(0, mats)
+    def _(k):
+        for way in range(2):
+            for stage in range(count - 1):
+                hop(3, k, stage, way).wait_send()
+                hand(3, k, stage + 1, way).wait()
+
+    def u_from(d):
+        source = lax.rem(me + d, count)
+        sems = lambda which: dict(
+            send_sem=u_out.at[which, source],
+            recv_sem=u_in.at[which, source],
+            device_id=(group, source),
+            device_id_type=MESH,
+        )
+        return (
+            pltpu.make_async_remote_copy(u_send.at[0, 0], part_ref.at[source], **sems(0)),
+            pltpu.make_async_remote_copy(s_send.at[0, 0], stat_ref.at[source], **sems(1)),
+        )
+
+    for copy in u_keep():
         copy.wait()
-    for stage in range(count):
-        for a in range(number):
-
-            @pl.loop(0, shapes[a][0])
-            def _(k):
-                for way in range(2):
-                    if stage < count - 1:
-                        hop(a, k, stage, way).wait_send()
-                    if stage > 0:
-                        hand(a, k, stage, way).wait()
-
-
-def ring_gather(arrays, collective_id):
+    for d in range(1, count):
+        for copy in u_from(d):
+            copy.wait()
+
+
+def forward_pass(values, table, gained, gain_latent, lat, wq, wk, shards, collective_id):
     count = lax.axis_size("pix")
-    shapes = [array.shape for array in arrays]
-    total = sum(shape[0] for shape in shapes)
+    images, _, pixels = values.shape
+    tile = pixel_tile(pixels)
+    rows_here, width = lat.shape[1:]
+    latents = rows_here * count
+    sharers = count // images
+    rows = latents // sharers
+    tall = table.shape[0]
+    mats = shards.shape[0]
+    inside = pl.BlockSpec(memory_space=pltpu.VMEM)
     anywhere = pl.BlockSpec(memory_space=pl.ANY)
+    shape = jax.ShapeDtypeStruct
+    codes, codes_t = hot_codes(tile)
+
+    def full(array):
+        return shape((array.shape[0], count) + array.shape[1:], array.dtype)
+
+    ring = DMA((count - 1, 2, 3 + mats))
     return pl.pallas_call(
-        functools.partial(gather_kernel, count, shapes),
-        out_shape=[
-            jax.ShapeDtypeStruct((shape[0], count) + shape[1:], array.dtype)
-            for shape, array in zip(shapes, arrays)
+        functools.partial(forward_kernel, count, images, tile),
+        out_shape=[full(lat), full(wq), full(wk), full(shards)]
+        + [
+            shape((latents, width), bf16),
+            shape((latents, width), bf16),
+            shape((latents, wk.shape[2]), f32),
+            shape((CHANNELS, latents), bf16),
+            shape((latents, CHANNELS), bf16),
+            shape((count, tall, rows), bf16),
+            shape((count, 8, rows), f32),
         ],
-        in_specs=[anywhere] * len(arrays),
-        out_specs=[anywhere] * len(arrays),
-        scratch_shapes=[DMA((len(arrays),))] + [DMA((count - 1, 2, total))] * 4,
-        compiler_params=pltpu.CompilerParams(collective_id=collective_id, has_side_effects=True),
-    )(*arrays)
-
-
-def reduce_kernel(
+        in_specs=[inside] * 7 + [anywhere] * 4,
+        out_specs=[anywhere] * 4 + [inside] * 5 + [anywhere] * 2,
+        scratch_shapes=[
+            pltpu.VMEM((count,) + lat.shape[1:], bf16),
+            pltpu.VMEM((count,) + wq.shape[1:], bf16),
+            pltpu.VMEM((count,) + wk.shape[1:], bf16),
+            pltpu.VMEM((CHANNELS + 16, latents), f32),
+            pltpu.VMEM((8, latents), f32),
+            pltpu.VMEM((images, sharers, tall, rows), bf16),
+            pltpu.VMEM((images, sharers, 8, rows), f32),
+            DMA((4,)),
+            DMA((3,)),
+            ring,
+            ring,
+            ring,
+            ring,
+            DMA((2,)),
+            DMA((2, count)),
+            DMA((2, count)),
+        ],
+        compiler_params=pltpu.CompilerParams(
+            collective_id=collective_id, has_side_effects=True, vmem_limit_bytes=48 * 2**20
+        ),
+    )(values, codes, codes_t, selector(), table, gained, gain_latent[None], lat, wq, wk, shards)
+
+
+def backward_kernel(
     count,
     teams,
+    images,
+    tile,
+    v_ref,
+    code_ref,
+    code_t_ref,
+    select_ref,
+    table_ref,
+    gained_ref,
+    at_ref,
+    a_ref,
+    back_ref,
+    row_ref,
     xs_ref,
     gs_ref,
+    t_ref,
+    pixel_ref,
     out_ref,
+    t_acc,
+    bt,
+    b_low,
+    stat,
+    back_all,
+    row_all,
     xv,
     gv,
     first,
@@ -297,9 +491,14 @@
     out_sem,
     hand_send,
     hand_recv,
+    back_send,
+    back_recv,
 ):
     number, rows, width = gs_ref.shape
     kinds = xs_ref.shape[0]
+    sharers = count // images
+    steps = v_ref.shape[2] // tile
+    lines = tile // SIDE
     depth = xs_ref.shape[3]
     half, wide = width // 2, width // 4
     group, me = lax.axis_index("img"), lax.axis_index("pix")
@@ -308,7 +507,38 @@
     sides = ((group, ring_device(place + 1, count)), (group, ring_device(place - 1, count)))
     other = (group + 1 - 2 * core, me)
     partners = [(lax.rem(team + d, teams) * 2 + core, me) for d in range(1, teams)]
-    greet(sides + (other,) + tuple(partners))
+    others = peers(count)
+    greet([other] + partners + others)
+
+    def back_push(d):
+        sems = lambda which: dict(
+            send_sem=back_send.at[which, d],
+            recv_sem=back_recv.at[which, me],
+            device_id=others[d],
+            device_id_type=MESH,
+        )
+        return (
+            pltpu.make_async_remote_copy(back_ref, back_all.at[me], **sems(0)),
+            pltpu.make_async_remote_copy(row_ref, row_all.at[me], **sems(1)),
+        )
+
+    def back_from(source):
+        sems = lambda which: dict(
+            send_sem=back_send.at[which, 0],
+            recv_sem=back_recv.at[which, source],
+            device_id=(group, source),
+            device_id_type=MESH,
+        )
+        return (
+            pltpu.make_async_remote_copy(back_ref, back_all.at[source], **sems(0)),
+            pltpu.make_async_remote_copy(row_ref, row_all.at[source], **sems(1)),
+        )
+
+    for d in range(count - 1):
+        for copy in back_push(d):
+            copy.start()
+    back_all[me] = back_ref[...]
+    row_all[me] = row_ref[...]
 
     mine = pl.ds(pl.multiple_of(core * rows, 16), rows)
 
@@ -351,8 +581,8 @@
         j = jnp.maximum(k - (number - kinds), 0)
         return mm_tn(xv[j, owner], gv[k, :, way * wide : (way + 1) * wide])
 
-    def hop(k, stage, way):
-        source = first.at[k, way] if stage == 0 else held.at[k, way, stage - 1]
+    def hop(k, stage, way, start=False):
+        source = first.at[k, way] if start else held.at[k, way, stage - 1]
         return pltpu.make_async_remote_copy(
             source,
             held.at[k, way, stage],
@@ -372,37 +602,106 @@
             device_id_type=MESH,
         )
 
-    for stage in range(count):
-
-        @pl.loop(0, number)
-        def _(k):
-            if stage == 0:
-                j = jnp.maximum(k - (number - kinds), 0)
-
-                @pl.when((k == 0) | (k > number - kinds))
+    def owner_at(stage, way):
+        return ring_device(place - stage - 1 if way == 0 else place + stage + 1, count)
+
+    @pl.loop(0, number)
+    def _(k):
+        j = jnp.maximum(k - (number - kinds), 0)
+
+        @pl.when((k == 0) | (k > number - kinds))
+        def _():
+            load_x(j).wait()
+            pair_x(j).wait_recv()
+
+        load_g(k).wait()
+        pair_g(k).wait_recv()
+        for way in range(2):
+            first[k, way] = part(k, owner_at(0, way), way).astype(bf16)
+            hop(k, 0, way, True).start()
+
+    def relay(k, stage):
+        for way in range(2):
+            own = part(k, owner_at(stage, way), way)
+            hop(k, stage - 1, way, True).wait_recv()
+            held[k, way, stage - 1] = (own + held[k, way, stage - 1].astype(f32)).astype(bf16)
+            hop(k, stage, way).start()
+
+    def relay_number(e):
+        relay(lax.rem(e, number), 1 + e // number)
+
+    relays = (count - 2) * number
+    tiles = images * steps
+    pace = min(2, relays // tiles)
+    t_acc[...] = jnp.zeros_like(t_acc)
+
+    @pl.loop(0, tiles)
+    def _(t):
+        image = lax.rem(t // steps + me // sharers, images)
+        step = lax.rem(t, steps)
+        for e in range(pace):
+            relay_number(t * pace + e)
+
+        @pl.when(step == 0)
+        def _():
+            for h in range(sharers):
+                source = image * sharers + h
+
+                @pl.when(source != me)
                 def _():
-                    load_x(j).wait()
-                    pair_x(j).wait_recv()
-
-                load_g(k).wait()
-                pair_g(k).wait_recv()
-            for way in range(2):
-                step = stage + 1
-                owner = ring_device(place - step if way == 0 else place + step, count)
-                total = part(k, owner, way)
-                if stage == 0:
-                    first[k, way] = total.astype(bf16)
-                    hop(k, 0, way).start()
-                else:
-                    hop(k, stage - 1, way).wait_recv()
-                    total = total + held[k, way, stage - 1].astype(f32)
-                    if stage < count - 1:
-                        held[k, way, stage - 1] = total.astype(bf16)
-                        hop(k, stage, way).start()
-                    else:
-                        across[team, k, way] = total.astype(bf16)
-                        for d in range(teams - 1):
-                            cross(k, way, d).start()
+                    for copy in back_from(source):
+                        copy.wait_recv()
+
+                here = slice(h * rows, (h + 1) * rows)
+                wide = jnp.dot(
+                    gained_ref[...],
+                    back_all[source].astype(f32),
+                    precision=lax.Precision.HIGHEST,
+                    preferred_element_type=f32,
+                )
+                bt[:, here] = wide.astype(bf16)
+                b_low[here, :] = wide.T.astype(bf16)
+                stat[:, here] = row_all[source]
+
+        span = pl.ds(pl.multiple_of(step * tile, 128), tile)
+        values = v_ref[image, :, span]
+        x = build_x(values, step * lines, code_ref, select_ref)
+        xt = masked_xt(values, step * lines, code_t_ref)
+        scores = mm(x, at_ref[...])
+        grad_p = mm(x, bt[...])
+        probs = jnp.exp2(scores - stat[0:1, :])
+        grad_s = (probs * (grad_p - stat[1:2, :])).astype(bf16)
+        probs = probs.astype(bf16)
+        t_acc[...] += mm(xt, grad_s)
+        back = mm(grad_s, a_ref[...]) + mm(probs, b_low[...])
+        along = jnp.sum(back * x.astype(f32), axis=1, keepdims=True)
+        half_back = back[:, CHANNELS - 128 :]
+        lane = lax.broadcasted_iota(jnp.int32, half_back.shape, 1)
+        half_back = jnp.where(lane == 120, along, half_back)
+        pixel_ref[image, :, span] = half_back.T[120:128, :]
+
+    t_ref[...] = lax.dot_general(
+        t_acc[:CHANNELS, :],
+        table_ref[...],
+        (((0,), (0,)), ((), ())),
+        precision=lax.Precision.HIGHEST,
+        preferred_element_type=f32,
+    ).astype(bf16)
+
+    if tiles * pace < relays:
+
+        @pl.loop(tiles * pace, relays)
+        def _(e):
+            relay_number(e)
+
+    @pl.loop(0, number)
+    def _(k):
+        for way in range(2):
+            own = part(k, me, way)
+            hop(k, count - 2, way, True).wait_recv()
+            across[team, k, way] = (own + held[k, way, count - 2].astype(f32)).astype(bf16)
+            for d in range(teams - 1):
+                cross(k, way, d).start()
 
     def finish(k):
         columns = pl.ds(pl.multiple_of(core * half, 128), half)
@@ -438,7 +737,7 @@
         pair_g(k).wait_send()
         for way in range(2):
             for stage in range(count - 1):
-                hop(k, stage, way).wait_send()
+                hop(k, stage, way, stage == 0).wait_send()
             for d in range(teams - 1):
                 cross(k, way, d).wait_send()
 
@@ -446,20 +745,41 @@
     def _(j):
         pair_x(j).wait_send()
 
-
-def ring_reduce(xs, gs, collective_id):
+    for d in range(count - 1):
+        for copy in back_push(d):
+            copy.wait_send()
+
+
+def backward_pass(values, table, gained, at, a, back, rows_in, xs, gs, collective_id):
     count = lax.axis_size("pix")
     teams = lax.axis_size("img") // 2
     kinds, _, rows, depth = xs.shape
     number, _, width = gs.shape
     anywhere = pl.BlockSpec(memory_space=pl.ANY)
+    inside = pl.BlockSpec(memory_space=pltpu.VMEM)
     chunk = (depth, width // 4)
+    images, _, pixels = values.shape
+    tile = pixel_tile(pixels)
+    latents = at.shape[1]
+    tall = back.shape[0]
+    codes, codes_t = hot_codes(tile)
+    shape = jax.ShapeDtypeStruct
     return pl.pallas_call(
-        functools.partial(reduce_kernel, count, teams),
-        out_shape=jax.ShapeDtypeStruct((number, depth, width), f32),
-        in_specs=[anywhere] * 2,
-        out_specs=anywhere,
+        functools.partial(backward_kernel, count, teams, images, tile),
+        out_shape=[
+            shape((latents, table.shape[1]), bf16),
+            shape((images, 8, pixels), f32),
+            shape((number, depth, width), f32),
+        ],
+        in_specs=[inside] * 10 + [anywhere] * 2,
+        out_specs=[inside] * 2 + [anywhere],
         scratch_shapes=[
+            pltpu.VMEM((CHANNELS + 16, latents), f32),
+            pltpu.VMEM((CHANNELS, latents), bf16),
+            pltpu.VMEM((latents, CHANNELS), bf16),
+            pltpu.VMEM((8, latents), f32),
+            pltpu.VMEM((count, tall, rows), bf16),
+            pltpu.VMEM((count, 8, rows), f32),
             pltpu.VMEM((kinds, count, 2 * rows, depth), bf16),
             pltpu.VMEM((number, 2 * rows, width // 2), bf16),
             pltpu.VMEM((number, 2) + chunk, bf16),
@@ -476,65 +796,18 @@
             DMA((number,)),
             DMA((number,)),
             DMA((number,)),
+            DMA((2, count)),
+            DMA((2, count)),
         ],
         compiler_params=pltpu.CompilerParams(
-            collective_id=collective_id, has_side_effects=True, vmem_limit_bytes=48 * 2**20
+            collective_id=collective_id, has_side_effects=True, vmem_limit_bytes=60 * 2**20
         ),
-    )(xs, gs)
+    )(values, codes, codes_t, selector(), table, gained, at, a, back, rows_in, xs, gs)
 
 
 def peers(count):
     group, me = lax.axis_index("img"), lax.axis_index("pix")
     return [(group, lax.rem(me + d, count)) for d in range(1, count)]
-
-
-def exchange_kernel(count, number, spread, *refs):
-    sources, targets = refs[:number], refs[number : 2 * number]
-    own_sem, send_sem, recv_sem = refs[2 * number :]
-    me = lax.axis_index("pix")
-    others = peers(count)
-    greet(others)
-
-    def piece(a, to):
-        return sources[a] if spread[a] else sources[a].at[to]
-
-    def push(a, d):
-        return pltpu.make_async_remote_copy(
-            piece(a, others[d][1]),
-            targets[a].at[me],
-            send_sem.at[a, d],
-            recv_sem.at[a, d],
-            device_id=others[d],
-            device_id_type=MESH,
-        )
-
-    def keep(a):
-        return pltpu.make_async_copy(piece(a, me), targets[a].at[me], own_sem.at[a])
-
-    for d in range(count - 1):
-        for a in range(number):
-            push(a, d).start()
-    for a in range(number):
-        keep(a).start()
-    for a in range(number):
-        keep(a).wait()
-        for d in range(count - 1):
-            push(a, d).wait()
-
-
-def exchange(arrays, spread, collective_id):
-    count = lax.axis_size("pix")
-    number = len(arrays)
-    anywhere = pl.BlockSpec(memory_space=pl.ANY)
-    shapes = [((count,) if flag else ()) + a.shape for a, flag in zip(arrays, spread)]
-    return pl.pallas_call(
-        functools.partial(exchange_kernel, count, number, spread),
-        out_shape=[jax.ShapeDtypeStruct(s, a.dtype) for s, a in zip(shapes, arrays)],
-        in_specs=[anywhere] * number,
-        out_specs=[anywhere] * number,
-        scratch_shapes=[DMA((number,)), DMA((number, count - 1)), DMA((number, count - 1))],
-        compiler_params=pltpu.CompilerParams(collective_id=collective_id, has_side_effects=True),
-    )(*arrays)
 
 
 def sum_kernel(
@@ -1212,11 +1485,6 @@
 
     side = -(-channels // 512) * 512
     key_t = jnp.pad(w_key.T, ((0, 0), (0, side - channels)))
-    latent_full, query_mat, key_full = ring_gather([latent_array[None], w_query[None], key_t[None]], 0)
-    latent_full = latent_full.reshape(latents, width)
-    query_mat = query_mat.reshape(width, width)
-    key_full = key_full.reshape(width, side)
-    key_mat = key_full[:, :channels].T
     value_out = lax.psum(mm(w_value, w_cross_out).astype(bf16), "pix")
     shards = jnp.stack(
         [
@@ -1230,8 +1498,6 @@
             w_down_two,
         ]
     )
-    (whole,) = ring_gather([shards], 1)
-    whole = whole.reshape(8, width, width)
 
     lines = pixels // SIDE
     u, sin_u, cos_u = angles(me * lines + lax.iota(jnp.int32, lines))
@@ -1268,60 +1534,39 @@
     scale = lax.rsqrt(spread + eps)
     keep = keep_mask.astype(f32)
 
-    position = lax.iota(jnp.int32, pixels)
-    column, line = position % SIDE, position // SIDE + SIDE
-    channel = lax.iota(jnp.int32, CHANNELS - 4)
-    hot = (channel[:, None] == column[None, :]) | (channel[:, None] == line[None, :])
-    small = jnp.concatenate(
-        [colours * scale[:, None, :], (-average * scale)[:, None, :]], axis=1
+    own_values = jnp.concatenate([colours, -average[:, None, :]], axis=1) * scale[:, None, :]
+    values = jnp.concatenate(
+        [scale[:, None], keep[:, None], jnp.zeros((images, 2, pixels), f32), own_values], axis=1
     )
-    xt = jnp.concatenate(
-        [
-            jnp.where(hot[None], (scale * keep)[:, None, :], 0.0).astype(bf16),
-            (small * keep[:, None, :]).astype(bf16),
-            keep[:, None, :].astype(bf16),
-            jnp.zeros((images, 15, pixels), bf16),
-        ],
-        axis=1,
+    gained = table * gain_input[None, :]
+    (
+        latent_full,
+        query_mat,
+        key_full,
+        whole,
+        latent_normed,
+        queries,
+        score_mat,
+        at,
+        a_low,
+        raw_parts,
+        stat_parts,
+    ) = forward_pass(
+        values,
+        jnp.pad(table.T, ((0, tall - channels), (0, 0))),
+        jnp.pad(gained, ((0, 0), (0, side - channels))),
+        gain_latent,
+        latent_array[None],
+        w_query[None],
+        key_t[None],
+        shards,
+        0,
     )
-    x = jnp.concatenate(
-        [
-            jnp.where(hot.T[None], scale[:, :, None], 0.0).astype(bf16),
-            jnp.swapaxes(small, 1, 2).astype(bf16),
-        ],
-        axis=2,
-    ).reshape(images * pixels, CHANNELS)
-
-    latent_float = latent_full.astype(f32)
-    latent_normed = layer_norm(latent_float, gain_latent).astype(bf16)
-    queries = mm(latent_normed, query_mat).astype(bf16)
-    gained = table * gain_input[None, :]
-    score_mat = mm_nt(queries, key_mat) * width_scale
-    score_x = exact(score_mat, gained.T)
-    at = (score_x.T * LOG2E).astype(bf16)
-    a_low = score_x.astype(bf16)
-
-    weighted, tops = score_pass(x, xt, at)
-    tops = tops[:, 0, :]
-    totals = weighted[:, CHANNELS, :]
-    raw = jnp.einsum(
-        "kc,ikq->icq",
-        table,
-        weighted[:, :CHANNELS, :],
-        precision=lax.Precision.HIGHEST,
-        preferred_element_type=f32,
-    )
-
-    def by_owner(value):
-        lead = value.shape[1]
-        split = value.reshape(images, lead, sharers, rows_own)
-        return jnp.swapaxes(split, 1, 2).reshape(count, lead, rows_own)
-
-    raw = jnp.pad(raw, ((0, 0), (0, tall - channels), (0, 0)))
-    stat = jnp.pad(jnp.stack([tops, totals], axis=1), ((0, 0), (0, 6), (0, 0)))
-    raw_parts, stat_parts = exchange(
-        [by_owner(raw).astype(bf16), by_owner(stat)], (False, False), 3
-    )
+    latent_float = latent_full.reshape(latents, width).astype(f32)
+    query_mat = query_mat.reshape(width, width)
+    key_mat = key_full.reshape(width, side)[:, :channels].T
+    score_mat = score_mat[:, :channels]
+    whole = whole.reshape(8, width, width)
 
     own = lax.dynamic_slice_in_dim(latent_float, slot * rows_own, rows_own, 0)
     latent_out, xs, gs, back_t, row_stats, gain_grads, in_gain = latent_pass(
@@ -1335,33 +1580,24 @@
         whole,
         4,
     )
-    summed = ring_reduce(xs, gs, 2)
-
-    back_all, row_all = exchange([back_t, row_stats], (True, True), 5)
-
-    def by_image(value):
-        lead = value.shape[1]
-        split = value.reshape(images, sharers, lead, rows_own)
-        return jnp.swapaxes(split, 1, 2).reshape(images, lead, latents)
-
-    back_all = by_image(back_all)[:, :channels].astype(f32)
-    bt = jnp.einsum(
-        "kc,icq->ikq",
-        gained,
-        back_all,
-        precision=lax.Precision.HIGHEST,
-        preferred_element_type=f32,
-    ).astype(bf16)
-    grad_t, pixel_out = grad_pass(
-        x, xt, at, bt, a_low, jnp.swapaxes(bt, 1, 2), by_image(row_all)
+    across = -(-channels // 128) * 128
+    grad_raw, pixel_out, summed = backward_pass(
+        values,
+        jnp.pad(table, ((0, 0), (0, across - channels))),
+        jnp.pad(gained, ((0, 0), (0, tall - channels))),
+        at,
+        a_low,
+        back_t,
+        row_stats,
+        xs,
+        gs,
+        2,
     )
     moved = (pixel_out[:, 4:7] - pixel_out[:, 7:8] / channels) - (
         (colours - average[:, None, :]) * scale[:, None, :]
     ) * (pixel_out[:, 0:1] / channels)
     grad_pixels = moved * (scale * keep)[:, None, :]
 
-    grad_raw = exact(grad_t[:CHANNELS].T, table)
-    across = -(-channels // 128) * 128
     cells = -(-(3 * width + channels) // (count * 1024)) * 1024
     loose = jnp.concatenate([gain_grads[:3].reshape(-1), in_gain[:channels, 0]])
     loose = jnp.pad(loose, (0, count * cells - loose.shape[0])).reshape(count, 8, cells // 8)
@@ -1372,9 +1608,7 @@
         rest[rows_here : rows_here + share_rows].astype(bf16), ((0, spare - share_rows), (0, 0))
     )
     grad_raw, loose, cross_sum = small_sums(
-        jnp.pad(grad_raw, ((0, 0), (0, across - channels)))
-        .astype(bf16)
-        .reshape(count, rows_here, across),
+        grad_raw.reshape(count, rows_here, across),
         loose,
         cross_rows,
         6,

time: 688 us -> 568 us (0.83); the launches traced: 679 us -> 567 us
  Pallas kernels: 533 us -> 484 us
  other arithmetic: 63.5 us -> 17 us
  matrix products: 20.5 us -> 10.9 us
    pallas_call x7 -> x2, Pallas kernels: 387 us -> 336 us  [the longest x1 188 us: backward_pass(): pl.pallas_call(functools.partial(backward_kernel, count, teams, images, t...]
    concatenate x3 -> x1, other arithmetic: 22.2 us -> 0.29 us  [local(): jnp.concatenate([scale[:, None], keep[:, None], jnp.zeros((images, 2, pix...]
    convert_element_type x9 -> x3, other arithmetic: 20 us -> 2.05 us  [the longest x1 1.74 us: local(): colours = rgb_pixels.astype(f32)]
    pallas_call x1, Pallas kernels: 101 us -> 110 us  [latent_pass(): pl.pallas_call(functools.partial(latent_kernel, count, images), out_shape...]
    pallas_call x1, Pallas kernels: 45.3 us -> 38 us  [small_sums(): pl.pallas_call(functools.partial(sum_kernel, count, crowd), out_shape=[ja...]
    unnamed x123 -> x98, local copies, waits for them, and re-layouts: 23 us -> 21.7 us
  transfers between devices with their start and end apart: 1 -> 1, of which waited for: 0 -> 0; matrix products, arithmetic and copies ran while one was open for 12% -> 6% of each run, Pallas kernels for 27% -> 26%
where the time goes in v3:
time: 568 us; the launch traced here: 567 us
  Pallas kernels  484 us (85%)
  local copies, waits for them, and re-layouts  40.3 us (7%)
  other arithmetic  17 us (3%)
  between operations  14.8 us (3%)
  matrix products  10.9 us (2%)
    pallas_call x1, Pallas kernels, backward_pass(): pl.pallas_call(functools.partial(backward_kernel, count, teams, images, t...  188 us
    pallas_call x1, Pallas kernels, forward_pass(): pl.pallas_call(functools.partial(forward_kernel, count, images, tile), ou...  147 us
    pallas_call x1, Pallas kernels, latent_pass(): pl.pallas_call(functools.partial(latent_kernel, count, images), out_shape...  110 us
    pallas_call x1, Pallas kernels, small_sums(): pl.pallas_call(functools.partial(sum_kernel, count, crowd), out_shape=[ja...  38 us
    unnamed x98, local copies, waits for them, and re-layouts  21.7 us
  transfers between devices with their start and end apart: 1, of which 0 were waited for; matrix products, arithmetic and copies ran while one was open for 6% of the time, Pallas kernels for 26%

profile of v3, /device:TPU:0, one launch (start us, length us, event | category | flops | bytes accessed | tf_op | source)
XLA Modules:
  0.0 567.3 jit_solution(5590948217665595839)
XLA Ops:
  8.1 2.0 convolution_convert_fusion.1
  10.2 1.5 multiply_reduce_fusion.3
  11.7 1.7 copy_convert_fusion
  17.3 1.0 add_rsqrt_fusion.1
  22.6 1.1 copy.73
  24.5 1.1 copy.74
  25.6 1.7 copy.72
  27.2 1.0 pad_bitcast_fusion.wk_ref
  28.3 1.7 bitcast_dynamic-update-slice_fusion.7
  30.0 1.7 bitcast_dynamic-update-slice_fusion.6
  31.7 1.7 bitcast_dynamic-update-slice_fusion.5
  33.3 1.7 bitcast_dynamic-update-slice_fusion.4
  37.8 147.1 %shard_map.356 = (bf16[1,8,64,1024]{3,2,1,0:T(8,128)(2,1)S(1)}, bf16[1,8,128,1024]{3,2,1,0:T(8,128)(2,1)}, bf16[1,8,128,512]{3,2,1,0:T(8,128)(2,1)}, bf16[8,8,12...) custom-call(f32[4,8,6272]{2,1,0:T(8,128)S(1)} %pad_maximum_fusion.v_, ...), custom_call_target="tpu_custom_call" | custom-call | tf_op jit(solution)/shard_map/pallas_call | solution.py:414
  186.2 1.8 pad.41.table_ref
  188.0 1.8 pad.42.gained_ref
  191.3 1.1 constant_dynamic-slice_fusion.own_ref
  192.4 1.9 pad.39.mix_ref
  194.3 110.5 %shard_map.357 = (bf16[4,64,1024]{2,1,0:T(8,128)(2,1)}, bf16[7,8,256,128]{3,2,1,0:T(8,128)(2,1)}, bf16[9,256,1024]{2,1,0:T(8,128)(2,1)}, bf16[272,256]{1,0:T(8,1...) custom-call(bf16[8,272,256]{2,1,0:T(8,128)(2,1)} %get-tuple-element.44.part_ref, ...), custom_call_target="tpu_custom_call" | custom-call | tf_op jit(solution)/shard_map/pallas_call | solution.py:1397
  304.8 188.5 %shard_map.358 = (bf16[512,384]{1,0:T(8,128)(2,1)}, f32[4,8,6272]{2,1,0:T(8,128)}, f32[9,128,1024]{2,1,0:T(8,128)}) custom-call(f32[4,8,6272]{2,1,0:T(8,128)} %copy-done.3, s32[896,256]{1,0:T(8,128)} %copy-done.1, s32[256,896]{1,0:T(8,128)} %copy-done.2, bf16[8,256]{1,0:T(8,128)(2,1)} %copy-done.11, f32[256,384]{1,0:T(8,128)} %pad.41.table_ref, ...), custom_call_target="tpu_custom_call" | custom-call | tf_op jit(solution)/shard_map/pallas_call | solution.py:767
  494.3 4.3 slice_bitcast_fusion
  498.8 38.0 %shard_map.359 = (bf16[8,64,384]{2,1,0:T(8,128)(2,1)S(1)}, f32[8,8,128]{2,1,0:T(8,128)S(1)}, bf16[8,48,1024]{2,1,0:T(8,128)(2,1)S(1)}) custom-call(bf16[8,64,384]{2,1,0:T(8,128)(2,1)S(1)} %bitcast.96, f32[8,8,128]{2,1,0:T(8,128)S(1)} %fusion.18.g_ref, bf16[48,1024]{1,0:T(8,128)(2,1)S(1)} %pad.44.z_ref), custom_call_target="tpu_custom_call" | custom-call | tf_op jit(solution)/shard_map/pallas_call | solution.py:921
  536.8 1.2 convolution_bitcast_fusion
  540.0 1.8 fusion.10
  541.8 2.0 fusion.15
  543.8 2.2 multiply_reduce_fusion
  546.0 1.5 fusion.32
  547.5 2.1 copy.79
  549.6 2.0 copy.80
  551.7 1.0 copy.78
  553.3 1.6 slice_multiply_fusion.1
  555.0 1.5 subtract_multiply_fusion
  557.9 1.7 fusion.13
  (163 shorter events, 21.1 us)
Async XLA Ops:
  7.2 185.2 %all-reduce.11.cloned.1.call-start = ((), (), s32[]{:S(2)}) async-start(), calls=%async_computation | async-start | bytes 1081344 | tf_op jit(solution)/shard_map/psum | solution.py:1488
  10.1 6.3 %copy-start.23 = (s32[4,6272]{1,0:T(4,128)S(1)}, s32[4,6272]{1,0:T(4,128)}, u32[]{:S(2)}) copy-start(s32[4,6272]{1,0:T(4,128)} %param.22) | copy-start | bytes 301060
  14.3 23.5 %copy-start.1 = (s32[896,256]{1,0:T(8,128)}, s32[896,256]{1,0:T(8,128)S(1)}, u32[]{:S(2)}) copy-start(s32[896,256]{1,0:T(8,128)S(1)} %fusion.1.code_ref) | copy-start | bytes 2752516
  14.6 23.1 %copy-start.2 = (s32[256,896]{1,0:T(8,128)}, s32[256,896]{1,0:T(8,128)S(1)}, u32[]{:S(2)}) copy-start(s32[256,896]{1,0:T(8,128)S(1)} %fusion.3.code_t_ref) | copy-start | bytes 2752516
  14.6 5.1 copy-start.31
  19.8 10.1 %copy-start.13 = (f32[256,261]{1,0:T(8,128)}, f32[256,261]{1,0:T(8,128)S(1)}, u32[]{:S(2)}) copy-start(f32[256,261]{1,0:T(8,128)S(1)} %get-tuple-element.141) | copy-start | bytes 801796
  19.9 10.1 %copy-start.14 = (f32[256,261]{1,0:T(8,128)}, f32[256,261]{1,0:T(8,128)S(1)}, u32[]{:S(2)}) copy-start(f32[256,261]{1,0:T(8,128)S(1)} %get-tuple-element.142) | copy-start | bytes 801796
  19.9 8.4 %copy-start.37 = (pred[256]{0:T(512)(128)(4,1)S(1)}, pred[256]{0:T(512)(128)(4,1)}, u32[]{:S(2)}) copy-start(pred[256]{0:T(512)(128)(4,1)} %broadcast_compare_fusion) | copy-start | bytes 772
  25.5 11.6 %copy-start.18 = (f32[4,6272]{1,0:T(4,128)S(1)}, f32[4,6272]{1,0:T(4,128)}, u32[]{:S(2)}) copy-start(f32[4,6272]{1,0:T(4,128)} %get-tuple-element.139) | copy-start | bytes 301060
  27.2 7.8 %copy-start.28 = (bf16[128,1024]{1,0:T(8,128)(2,1)S(1)}, bf16[128,1024]{1,0:T(8,128)(2,1)}, u32[]{:S(2)}) copy-start(bf16[128,1024]{1,0:T(8,128)(2,1)} %param.37) | copy-start | bytes 786436
  27.2 9.2 %copy-start.29 = (bf16[128,1024]{1,0:T(8,128)(2,1)S(1)}, bf16[128,1024]{1,0:T(8,128)(2,1)}, u32[]{:S(2)}) copy-start(bf16[128,1024]{1,0:T(8,128)(2,1)} %param.40) | copy-start | bytes 786436
  27.2 10.0 %copy-start.16 = (f32[4,3,6272]{2,1,0:T(4,128)S(1)}, f32[4,3,6272]{2,1,0:T(4,128)}, u32[]{:S(2)}) copy-start(f32[4,3,6272]{2,1,0:T(4,128)} %copy_convert_fusion) | copy-start | bytes 903172
  27.2 10.0 %copy-start.26 = (f32[4,1,6272]{2,1,0:T(1,128)S(1)}, f32[4,1,6272]{2,1,0:T(1,128)}, u32[]{:S(2)}) copy-start(f32[4,1,6272]{2,1,0:T(1,128)} %get-tuple-element.154) | copy-start | bytes 301060
  28.3 9.5 %copy-start.11 = (bf16[8,256]{1,0:T(8,128)(2,1)}, bf16[8,256]{1,0:T(8,128)(2,1)S(1)}, u32[]{:S(2)}) copy-start(bf16[8,256]{1,0:T(8,128)(2,1)S(1)} %select_convert_fusion.select_ref) | copy-start | bytes 12292
  29.9 7.5 %copy-start.24 = (f32[4,1,6272]{2,1,0:T(1,128)S(1)}, f32[4,1,6272]{2,1,0:T(1,128)}, u32[]{:S(2)}) copy-start(f32[4,1,6272]{2,1,0:T(1,128)} %copy.67) | copy-start | bytes 301060
  30.0 7.5 %copy-start.25 = (f32[4,1,6272]{2,1,0:T(1,128)S(1)}, f32[4,1,6272]{2,1,0:T(1,128)}, u32[]{:S(2)}) copy-start(f32[4,1,6272]{2,1,0:T(1,128)} %get-tuple-element.153) | copy-start | bytes 301060
  37.7 147.2 %copy-start.3 = (f32[4,8,6272]{2,1,0:T(8,128)}, f32[4,8,6272]{2,1,0:T(8,128)S(1)}, u32[]{:S(2)}) copy-start(f32[4,8,6272]{2,1,0:T(8,128)S(1)} %pad_maximum_fusion.v_ref) | copy-start | bytes 2408452
  185.3 5.4 copy-start.34
  185.3 5.4 copy-start.35
  185.3 5.3 copy-start.36
  190.7 353.2 %copy-start.32 = (f32[512]{0:T(512)}, f32[512]{0:T(512)S(1)}, u32[]{:S(2)}) copy-start(f32[512]{0:T(512)S(1)} %rsqrt.25) | copy-start | bytes 6148
  494.2 4.3 copy-start.33
  494.2 4.3 copy-start.30
  494.2 4.5 copy-start.5
  498.5 38.3 %copy-start.27 = (bf16[261,128]{1,0:T(8,128)(2,1)S(1)}, bf16[261,128]{1,0:T(8,128)(2,1)}, u32[]{:S(2)}) copy-start(bf16[261,128]{1,0:T(8,128)(2,1)} %param.28) | copy-start | bytes 200452
  498.7 40.3 %copy-start.19 = (f32[512,512]{1,0:T(8,128)S(1)}, f32[512,512]{1,0:T(8,128)}, u32[]{:S(2)}) copy-start(f32[512,512]{1,0:T(8,128)} %get-tuple-element.64) | copy-start | bytes 3145732
  539.2 4.6 copy-start.38
  547.5 4.2 copy-start.15
  547.5 7.5 %copy-start.17 = (bf16[4,3,6272]{2,0,1:T(4,128)(2,1)S(1)}, bf16[4,3,6272]{2,0,1:T(4,128)(2,1)}, u32[]{:S(2)}) copy-start(bf16[4,3,6272]{2,0,1:T(4,128)(2,1)} %param.21) | copy-start | bytes 451588
  547.5 7.5 %copy-start.21 = (f32[4,6272]{1,0:T(4,128)S(1)}, f32[4,6272]{1,0:T(4,128)}, u32[]{:S(2)}) copy-start(f32[4,6272]{1,0:T(4,128)} %get-tuple-element.138) | copy-start | bytes 301060
  547.5 7.5 %copy-start.22 = (f32[4,6272]{1,0:T(4,128)S(1)}, f32[4,6272]{1,0:T(4,128)}, u32[]{:S(2)}) copy-start(f32[4,6272]{1,0:T(4,128)} %get-tuple-element.140) | copy-start | bytes 301060
  552.7 7.0 %copy-start.20 = (bf16[4,64,1024]{2,1,0:T(8,128)(2,1)S(1)}, bf16[4,64,1024]{2,1,0:T(8,128)(2,1)}, u32[]{:S(2)}) copy-start(bf16[4,64,1024]{2,1,0:T(8,128)(2,1)} %get-tuple-element.195) | copy-start | bytes 1572868
  (9 other events, 16.8 us)
Sparse Core Ops, SparseCore 0:
  11.4 76.5 all-reduce.10

commit v4 on v3

--- a/solution.py
+++ b/solution.py
@@ -76,26 +76,11 @@
 
 
 def hot_codes(tile):
-    pixel = lax.broadcasted_iota(jnp.int32, (tile, CHANNELS), 0)
-    channel = lax.broadcasted_iota(jnp.int32, (tile, CHANNELS), 1)
+    pixel = lax.broadcasted_iota(jnp.int32, (CHANNELS, tile), 1)
+    channel = lax.broadcasted_iota(jnp.int32, (CHANNELS, tile), 0)
     start = channel - SIDE - pixel // SIDE
-    code = jnp.where(start >= 0, start, -2)
-    code = jnp.where(channel < SIDE, jnp.where(channel == pixel % SIDE, -1, -2), code)
-    rows = jnp.where(channel >= CHANNELS - 4, -1, code)
-    return rows, jnp.where(channel >= CHANNELS - 4, -2, code).T
-
-
-def selector():
-    k = lax.broadcasted_iota(jnp.int32, (8, CHANNELS), 0)
-    channel = lax.broadcasted_iota(jnp.int32, (8, CHANNELS), 1)
-    own = channel - (CHANNELS - 8)
-    return jnp.where(jnp.where(own >= 4, own, 0) == k, 1.0, 0.0).astype(bf16)
-
-
-def build_x(values, base, code_ref, select_ref):
-    spread = mm_tn(values.astype(bf16), select_ref[...])
-    code = code_ref[...]
-    return jnp.where((code == -1) | (code == base), spread, 0.0).astype(bf16)
+    code = jnp.where((start >= 0) & (channel < CHANNELS - 4), start, -2)
+    return jnp.where(channel < SIDE, jnp.where(channel == pixel % SIDE, -1, -2), code)
 
 
 def build_xt(values, base, code_ref):
@@ -107,11 +92,12 @@
     return jnp.concatenate([hot[: CHANNELS - 8, :], last], axis=0)
 
 
-def masked_xt(values, base, code_ref):
+def build_both(values, base, code_ref):
     keep = values[1:2, :]
-    xt = (build_xt(values, base, code_ref) * keep).astype(bf16)
+    xt = build_xt(values, base, code_ref).astype(bf16)
     k = lax.broadcasted_iota(jnp.int32, (16, values.shape[1]), 0)
-    return jnp.concatenate([xt, jnp.where(k == 0, keep, 0.0).astype(bf16)], axis=0)
+    ones = jnp.where(k == 0, keep, 0.0).astype(bf16)
+    return xt.T, jnp.concatenate([xt * keep.astype(bf16), ones], axis=0)
 
 
 def forward_kernel(
@@ -120,8 +106,6 @@
     tile,
     v_ref,
     code_ref,
-    code_t_ref,
-    select_ref,
     table_ref,
     gained_ref,
     gain_ref,
@@ -160,7 +144,8 @@
     pixels = v_ref.shape[2]
     steps = pixels // tile
     lines = tile // SIDE
-    sharers = count // images
+    owners = Owners(count, images)
+    sharers = owners.sharers
     rows = part_ref.shape[2]
     width = wq_ref.shape[2]
     latents = normed_ref.shape[0]
@@ -169,7 +154,7 @@
     place = ring_place(count)
     sides = ((group, ring_device(place + 1, count)), (group, ring_device(place - 1, count)))
     other = (group + 1 - 2 * core, me)
-    greet([other] + peers(count))
+    greet(plane(count))
     sources = (lat_ref, wq_ref, wk_ref, w_ref)
     fulls = (lat_full, wq_full, wk_full, w_full)
     mats = w_ref.shape[0]
@@ -280,11 +265,11 @@
         relay(3, lax.rem(e, mats), 1 + e // mats)
 
     def u_push(i, h):
-        to = i * sharers + h
+        to = owners.device(group, i, jnp.int32(h))
         sems = lambda which: dict(
-            send_sem=u_out.at[which, to],
+            send_sem=u_out.at[which, i * sharers + h],
             recv_sem=u_in.at[which, me],
-            device_id=(group, to),
+            device_id=to,
             device_id_type=MESH,
         )
         return to, (
@@ -293,7 +278,7 @@
         )
 
     def u_keep():
-        i, h = me // sharers, lax.rem(me, sharers)
+        i, h = owners.image, owners.slot
         return (
             pltpu.make_async_copy(u_send.at[i, h], part_ref.at[me], u_own.at[0]),
             pltpu.make_async_copy(s_send.at[i, h], stat_ref.at[me], u_own.at[1]),
@@ -314,14 +299,17 @@
 
         values = v_ref[i, :, pl.ds(pl.multiple_of(step * tile, 128), tile)]
         base = step * lines
-        x = build_x(values, base, code_ref, select_ref)
-        scores = mm(x, at_ref[...])
-        xt = masked_xt(values, base, code_t_ref)
-        old = top[0:1, :]
-        new = jnp.maximum(old, jnp.max(scores, axis=0, keepdims=True))
-        weights = jnp.exp2(scores - new).astype(bf16)
-        acc[...] = acc[...] * jnp.exp2(old - new) + mm(xt, weights)
-        top[...] = jnp.broadcast_to(new, top.shape)
+        x, xt = build_both(values, base, code_ref)
+        first, second = slice(0, tile // 2), slice(tile // 2, tile)
+        scores = [mm(x[half], at_ref[...]) for half in (first, second)]
+        old, total = top[0:1, :], acc[...]
+        for half, score in zip((first, second), scores):
+            new = jnp.maximum(old, jnp.max(score, axis=0, keepdims=True))
+            weights = jnp.exp2(score - new).astype(bf16)
+            total = total * jnp.exp2(old - new) + mm(xt[:, half], weights)
+            old = new
+        acc[...] = total
+        top[...] = jnp.broadcast_to(old, top.shape)
 
         @pl.when(step == steps - 1)
         def _():
@@ -338,12 +326,12 @@
             for h in range(sharers):
                 to, copies = u_push(i, h)
 
-                @pl.when(to != me)
+                @pl.when(jnp.logical_not(owners.is_me(to)))
                 def _():
                     for copy in copies:
                         copy.start()
 
-                @pl.when(to == me)
+                @pl.when(owners.is_me(to))
                 def _():
                     for copy in u_keep():
                         copy.start()
@@ -372,12 +360,11 @@
                 hop(3, k, stage, way).wait_send()
                 hand(3, k, stage + 1, way).wait()
 
-    def u_from(d):
-        source = lax.rem(me + d, count)
+    def u_from(source):
         sems = lambda which: dict(
-            send_sem=u_out.at[which, source],
+            send_sem=u_out.at[which, 0],
             recv_sem=u_in.at[which, source],
-            device_id=(group, source),
+            device_id=(owners.home, source),
             device_id_type=MESH,
         )
         return (
@@ -385,11 +372,27 @@
             pltpu.make_async_remote_copy(s_send.at[0, 0], stat_ref.at[source], **sems(1)),
         )
 
-    for copy in u_keep():
-        copy.wait()
-    for d in range(1, count):
-        for copy in u_from(d):
-            copy.wait()
+    for i in range(images):
+        for h in range(sharers):
+            to, copies = u_push(i, h)
+
+            @pl.when(jnp.logical_not(owners.is_me(to)))
+            def _():
+                for copy in copies:
+                    copy.wait_send()
+
+    for source in range(count):
+        local = owners.is_me((owners.home, source))
+
+        @pl.when(local)
+        def _():
+            for copy in u_keep():
+                copy.wait()
+
+        @pl.when(jnp.logical_not(local))
+        def _():
+            for copy in u_from(source):
+                copy.wait_recv()
 
 
 def forward_pass(values, table, gained, gain_latent, lat, wq, wk, shards, collective_id):
@@ -405,7 +408,6 @@
     inside = pl.BlockSpec(memory_space=pltpu.VMEM)
     anywhere = pl.BlockSpec(memory_space=pl.ANY)
     shape = jax.ShapeDtypeStruct
-    codes, codes_t = hot_codes(tile)
 
     def full(array):
         return shape((array.shape[0], count) + array.shape[1:], array.dtype)
@@ -423,7 +425,7 @@
             shape((count, tall, rows), bf16),
             shape((count, 8, rows), f32),
         ],
-        in_specs=[inside] * 7 + [anywhere] * 4,
+        in_specs=[inside] * 5 + [anywhere] * 4,
         out_specs=[anywhere] * 4 + [inside] * 5 + [anywhere] * 2,
         scratch_shapes=[
             pltpu.VMEM((count,) + lat.shape[1:], bf16),
@@ -446,7 +448,7 @@
         compiler_params=pltpu.CompilerParams(
             collective_id=collective_id, has_side_effects=True, vmem_limit_bytes=48 * 2**20
         ),
-    )(values, codes, codes_t, selector(), table, gained, gain_latent[None], lat, wq, wk, shards)
+    )(values, hot_codes(tile), table, gained, gain_latent[None], lat, wq, wk, shards)
 
 
 def backward_kernel(
@@ -456,8 +458,6 @@
     tile,
     v_ref,
     code_ref,
-    code_t_ref,
-    select_ref,
     table_ref,
     gained_ref,
     at_ref,
@@ -477,7 +477,7 @@
     row_all,
     xv,
     gv,
-    first,
+    terms,
     held,
     across,
     done,
@@ -496,10 +496,11 @@
 ):
     number, rows, width = gs_ref.shape
     kinds = xs_ref.shape[0]
-    sharers = count // images
+    owners = Owners(count, images)
+    sharers = owners.sharers
     steps = v_ref.shape[2] // tile
     lines = tile // SIDE
-    depth = xs_ref.shape[3]
+    depth = xs_ref.shape[1] // count
     half, wide = width // 2, width // 4
     group, me = lax.axis_index("img"), lax.axis_index("pix")
     core, team = lax.rem(group, 2), group // 2
@@ -507,26 +508,28 @@
     sides = ((group, ring_device(place + 1, count)), (group, ring_device(place - 1, count)))
     other = (group + 1 - 2 * core, me)
     partners = [(lax.rem(team + d, teams) * 2 + core, me) for d in range(1, teams)]
-    others = peers(count)
-    greet([other] + partners + others)
+    greet(plane(count) + partners)
+
+    own_index = owners.image * sharers + owners.slot
 
     def back_push(d):
+        to = (owners.home, lax.rem(me + d, count))
         sems = lambda which: dict(
             send_sem=back_send.at[which, d],
-            recv_sem=back_recv.at[which, me],
-            device_id=others[d],
+            recv_sem=back_recv.at[which, own_index],
+            device_id=to,
             device_id_type=MESH,
         )
-        return (
-            pltpu.make_async_remote_copy(back_ref, back_all.at[me], **sems(0)),
-            pltpu.make_async_remote_copy(row_ref, row_all.at[me], **sems(1)),
+        return to, (
+            pltpu.make_async_remote_copy(back_ref, back_all.at[own_index], **sems(0)),
+            pltpu.make_async_remote_copy(row_ref, row_all.at[own_index], **sems(1)),
         )
 
     def back_from(source):
         sems = lambda which: dict(
             send_sem=back_send.at[which, 0],
             recv_sem=back_recv.at[which, source],
-            device_id=(group, source),
+            device_id=(group, me),
             device_id_type=MESH,
         )
         return (
@@ -534,25 +537,30 @@
             pltpu.make_async_remote_copy(row_ref, row_all.at[source], **sems(1)),
         )
 
-    for d in range(count - 1):
-        for copy in back_push(d):
-            copy.start()
-    back_all[me] = back_ref[...]
-    row_all[me] = row_ref[...]
-
-    mine = pl.ds(pl.multiple_of(core * rows, 16), rows)
+    for d in range(count):
+        to, copies = back_push(d)
+
+        @pl.when(jnp.logical_not(owners.is_me(to)))
+        def _():
+            for copy in copies:
+                copy.start()
+
+        @pl.when(owners.is_me(to))
+        def _():
+            back_all[own_index] = back_ref[...]
+            row_all[own_index] = row_ref[...]
 
     def load_x(j):
-        return pltpu.make_async_copy(xs_ref.at[j], xv.at[j, :, mine], load_sem.at[0, j])
+        return pltpu.make_async_copy(xs_ref.at[j], xv.at[j, core], load_sem.at[0, j])
 
     def load_g(k):
         part = gs_ref.at[k, :, pl.ds(pl.multiple_of(core * half, 128), half)]
-        return pltpu.make_async_copy(part, gv.at[k, mine], load_sem.at[1, k])
+        return pltpu.make_async_copy(part, gv.at[k, core], load_sem.at[1, k])
 
     def pair_x(j):
         return pltpu.make_async_remote_copy(
             xs_ref.at[j],
-            xv.at[j, :, mine],
+            xv.at[j, core],
             pair_send.at[0, j],
             pair_recv.at[0, j],
             device_id=other,
@@ -563,7 +571,7 @@
         part = gs_ref.at[k, :, pl.ds(pl.multiple_of((1 - core) * half, 128), half)]
         return pltpu.make_async_remote_copy(
             part,
-            gv.at[k, mine],
+            gv.at[k, core],
             pair_send.at[1, k],
             pair_recv.at[1, k],
             device_id=other,
@@ -578,11 +586,11 @@
         pair_g(j).start()
 
     def part(k, owner, way):
-        j = jnp.maximum(k - (number - kinds), 0)
-        return mm_tn(xv[j, owner], gv[k, :, way * wide : (way + 1) * wide])
+        here = pl.ds(pl.multiple_of(owner * depth, depth), depth)
+        return terms.at[k, here, way * wide : (way + 1) * wide]
 
     def hop(k, stage, way, start=False):
-        source = first.at[k, way] if start else held.at[k, way, stage - 1]
+        source = part(k, owner_at(0, way), way) if start else held.at[k, way, stage - 1]
         return pltpu.make_async_remote_copy(
             source,
             held.at[k, way, stage],
@@ -616,13 +624,17 @@
 
         load_g(k).wait()
         pair_g(k).wait_recv()
+        for r in range(0, width, 256):
+            piece = slice(r, r + 256)
+            terms[k, piece, :] = (
+                mm(xv[j, 0, piece, :], gv[k, 0]) + mm(xv[j, 1, piece, :], gv[k, 1])
+            ).astype(bf16)
         for way in range(2):
-            first[k, way] = part(k, owner_at(0, way), way).astype(bf16)
             hop(k, 0, way, True).start()
 
     def relay(k, stage):
         for way in range(2):
-            own = part(k, owner_at(stage, way), way)
+            own = part(k, owner_at(stage, way), way)[...].astype(f32)
             hop(k, stage - 1, way, True).wait_recv()
             held[k, way, stage - 1] = (own + held[k, way, stage - 1].astype(f32)).astype(bf16)
             hop(k, stage, way).start()
@@ -637,7 +649,7 @@
 
     @pl.loop(0, tiles)
     def _(t):
-        image = lax.rem(t // steps + me // sharers, images)
+        image = lax.rem(t // steps + owners.image, images)
         step = lax.rem(t, steps)
         for e in range(pace):
             relay_number(t * pace + e)
@@ -647,7 +659,9 @@
             for h in range(sharers):
                 source = image * sharers + h
 
-                @pl.when(source != me)
+                sender = owners.device(group, image, jnp.int32(h))
+
+                @pl.when(jnp.logical_not(owners.is_me(sender)))
                 def _():
                     for copy in back_from(source):
                         copy.wait_recv()
@@ -665,20 +679,21 @@
 
         span = pl.ds(pl.multiple_of(step * tile, 128), tile)
         values = v_ref[image, :, span]
-        x = build_x(values, step * lines, code_ref, select_ref)
-        xt = masked_xt(values, step * lines, code_t_ref)
-        scores = mm(x, at_ref[...])
-        grad_p = mm(x, bt[...])
-        probs = jnp.exp2(scores - stat[0:1, :])
-        grad_s = (probs * (grad_p - stat[1:2, :])).astype(bf16)
-        probs = probs.astype(bf16)
-        t_acc[...] += mm(xt, grad_s)
-        back = mm(grad_s, a_ref[...]) + mm(probs, b_low[...])
-        along = jnp.sum(back * x.astype(f32), axis=1, keepdims=True)
-        half_back = back[:, CHANNELS - 128 :]
-        lane = lax.broadcasted_iota(jnp.int32, half_back.shape, 1)
-        half_back = jnp.where(lane == 120, along, half_back)
-        pixel_ref[image, :, span] = half_back.T[120:128, :]
+        x, xt = build_both(values, step * lines, code_ref)
+        halves = (slice(0, tile // 2), slice(tile // 2, tile))
+        products = [(mm(x[half], at_ref[...]), mm(x[half], bt[...])) for half in halves]
+        kept, ends = [], []
+        for half, (scores, grad_p) in zip(halves, products):
+            probs = jnp.exp2(scores - stat[0:1, :])
+            grad_s = (probs * (grad_p - stat[1:2, :])).astype(bf16)
+            kept.append(grad_s)
+            back = mm(grad_s, a_ref[...]) + mm(probs.astype(bf16), b_low[...])
+            along = jnp.sum(back * x[half].astype(f32), axis=1, keepdims=True)
+            end = back[:, CHANNELS - 128 :]
+            lane = lax.broadcasted_iota(jnp.int32, end.shape, 1)
+            ends.append(jnp.where(lane == 120, along, end))
+        t_acc[...] += mm(xt, jnp.concatenate(kept, axis=0))
+        pixel_ref[image, :, span] = jnp.concatenate(ends, axis=0).T[120:128, :]
 
     t_ref[...] = lax.dot_general(
         t_acc[:CHANNELS, :],
@@ -697,7 +712,7 @@
     @pl.loop(0, number)
     def _(k):
         for way in range(2):
-            own = part(k, me, way)
+            own = part(k, me, way)[...].astype(f32)
             hop(k, count - 2, way, True).wait_recv()
             across[team, k, way] = (own + held[k, way, count - 2].astype(f32)).astype(bf16)
             for d in range(teams - 1):
@@ -745,16 +760,21 @@
     def _(j):
         pair_x(j).wait_send()
 
-    for d in range(count - 1):
-        for copy in back_push(d):
-            copy.wait_send()
+    for d in range(count):
+        to, copies = back_push(d)
+
+        @pl.when(jnp.logical_not(owners.is_me(to)))
+        def _():
+            for copy in copies:
+                copy.wait_send()
 
 
 def backward_pass(values, table, gained, at, a, back, rows_in, xs, gs, collective_id):
     count = lax.axis_size("pix")
     teams = lax.axis_size("img") // 2
-    kinds, _, rows, depth = xs.shape
+    kinds, _, rows = xs.shape
     number, _, width = gs.shape
+    depth = xs.shape[1] // count
     anywhere = pl.BlockSpec(memory_space=pl.ANY)
     inside = pl.BlockSpec(memory_space=pltpu.VMEM)
     chunk = (depth, width // 4)
@@ -762,7 +782,6 @@
     tile = pixel_tile(pixels)
     latents = at.shape[1]
     tall = back.shape[0]
-    codes, codes_t = hot_codes(tile)
     shape = jax.ShapeDtypeStruct
     return pl.pallas_call(
         functools.partial(backward_kernel, count, teams, images, tile),
@@ -771,7 +790,7 @@
             shape((images, 8, pixels), f32),
             shape((number, depth, width), f32),
         ],
-        in_specs=[inside] * 10 + [anywhere] * 2,
+        in_specs=[inside] * 8 + [anywhere] * 2,
         out_specs=[inside] * 2 + [anywhere],
         scratch_shapes=[
             pltpu.VMEM((CHANNELS + 16, latents), f32),
@@ -780,9 +799,9 @@
             pltpu.VMEM((8, latents), f32),
             pltpu.VMEM((count, tall, rows), bf16),
             pltpu.VMEM((count, 8, rows), f32),
-            pltpu.VMEM((kinds, count, 2 * rows, depth), bf16),
-            pltpu.VMEM((number, 2 * rows, width // 2), bf16),
-            pltpu.VMEM((number, 2) + chunk, bf16),
+            pltpu.VMEM((kinds, 2, xs.shape[1], rows), bf16),
+            pltpu.VMEM((number, 2, rows, width // 2), bf16),
+            pltpu.VMEM((number, xs.shape[1], width // 2), bf16),
             pltpu.VMEM((number, 2, count - 1) + chunk, bf16),
             pltpu.VMEM((teams, number, 2) + chunk, bf16),
             pltpu.VMEM((number, depth, width // 2), f32),
@@ -802,12 +821,40 @@
         compiler_params=pltpu.CompilerParams(
             collective_id=collective_id, has_side_effects=True, vmem_limit_bytes=60 * 2**20
         ),
-    )(values, codes, codes_t, selector(), table, gained, at, a, back, rows_in, xs, gs)
+    )(values, hot_codes(tile), table, gained, at, a, back, rows_in, xs, gs)
 
 
 def peers(count):
     group, me = lax.axis_index("img"), lax.axis_index("pix")
     return [(group, lax.rem(me + d, count)) for d in range(1, count)]
+
+
+def plane(count):
+    group, me = lax.axis_index("img"), lax.axis_index("pix")
+    other = group + 1 - 2 * lax.rem(group, 2)
+    return peers(count) + [(other, lax.rem(me + d, count)) for d in range(count)]
+
+
+class Owners:
+    def __init__(self, count, images):
+        self.group, self.me = lax.axis_index("img"), lax.axis_index("pix")
+        self.core = lax.rem(self.group, 2)
+        self.base = self.group - self.core
+        self.images = images
+        self.chips = count // (2 * images)
+        self.sharers = 2 * self.chips
+        self.slot = lax.rem(self.me, self.chips) * 2 + self.core
+        image = self.me // self.chips
+        self.image = lax.rem(image, images)
+        self.home = self.base + image // images
+
+    def device(self, group, image, slot):
+        core = lax.rem(group, 2)
+        chip = (core * self.images + image) * self.chips + slot // 2
+        return self.base + lax.rem(slot, 2), chip
+
+    def is_me(self, device):
+        return (device[0] == self.group) & (device[1] == self.me)
 
 
 def sum_kernel(
@@ -1001,14 +1048,15 @@
     out_recv,
 ):
     rows, width = own_ref.shape
-    depth = xs_ref.shape[3]
-    sharers = count // images
+    depth = width // count
+    owners = Owners(count, images)
+    sharers = owners.sharers
     latents = rows * sharers
     per = count // sharers
     rows_here = latents // count
-    spare = xs_ref.shape[3] - rows_here
+    spare = depth - rows_here
     group, me = lax.axis_index("img"), lax.axis_index("pix")
-    slot, image = lax.rem(me, sharers), me // sharers
+    slot, image, home = owners.slot, owners.image, owners.home
     block = 256
     blocks = width // block
     row_block = min(rows, 64)
@@ -1020,16 +1068,16 @@
 
     for k in range(8):
         load(k).start()
-    greet(peers(count))
+    greet(plane(count))
 
     def cot_push(i):
-        to = i * sharers + me // per
+        to = owners.device(group, i, me // per)
         return to, pltpu.make_async_remote_copy(
             cot_ref.at[i],
             cot.at[lax.rem(me, per)],
             cot_send.at[i],
             cot_recv.at[lax.rem(me, per)],
-            device_id=(group, to),
+            device_id=to,
             device_id_type=MESH,
         )
 
@@ -1039,11 +1087,11 @@
     for i in range(images):
         to, copy = cot_push(i)
 
-        @pl.when(to != me)
+        @pl.when(jnp.logical_not(owners.is_me(to)))
         def _():
             copy.start()
 
-        @pl.when(to == me)
+        @pl.when(owners.is_me(to))
         def _():
             cot_keep().start()
 
@@ -1059,8 +1107,7 @@
             body(pl.ds(pl.multiple_of(r * row_block, 16), row_block))
 
     def put_x(j, c, value):
-        for b in range(block // depth):
-            xs_ref[j, c * (block // depth) + b] = value[:, b * depth : (b + 1) * depth]
+        xs_ref[j, columns(c), :] = value.T
 
     def centre(rows_f32):
         average = jnp.mean(rows_f32, axis=1, keepdims=True)
@@ -1115,7 +1162,7 @@
         piece = [picks, mean_tall[o * share_rows : (o + 1) * share_rows]]
         if spare > share_rows:
             piece.append(jnp.zeros((spare - share_rows, rows), f32))
-        xs_ref[6, o] = jnp.concatenate(piece, axis=0).T.astype(bf16)
+        xs_ref[6, o * depth : (o + 1) * depth, :] = jnp.concatenate(piece, axis=0).astype(bf16)
 
     mean_low = mean[1].astype(bf16)
 
@@ -1176,7 +1223,7 @@
         kv[1, slot, :, columns(j)] = mm(low[...], wv[m_value, :, columns(j)]).astype(bf16)
 
     def sharer(d):
-        return (group, image * sharers + lax.rem(slot + d, sharers))
+        return owners.device(home, image, lax.rem(slot + d, sharers))
 
     def kv_push(d):
         return pltpu.make_async_remote_copy(
@@ -1223,13 +1270,13 @@
     feed(three, final, 2, up_two, down_two, gs_ref.at[6], 5, 1)
 
     def out_push(b):
-        to = slot * per + b
+        to = (home, slot * per + b)
         return to, pltpu.make_async_remote_copy(
             final.at[pl.ds(b * rows_here, rows_here)],
             out_ref.at[image],
             out_send.at[b],
             out_recv.at[image],
-            device_id=(group, to),
+            device_id=to,
             device_id_type=MESH,
         )
 
@@ -1240,11 +1287,11 @@
     for b in range(per):
         to, copy = out_push(b)
 
-        @pl.when(to != me)
+        @pl.when(jnp.logical_not(owners.is_me(to)))
         def _():
             copy.start()
 
-        @pl.when(to == me)
+        @pl.when(owners.is_me(to))
         def _():
             out_keep().start()
 
@@ -1260,11 +1307,13 @@
 
     for b in range(per):
 
-        @pl.when(slot * per + b != me)
+        local = owners.is_me((home, slot * per + b))
+
+        @pl.when(jnp.logical_not(local))
         def _():
             cot_from(b).wait_recv()
 
-        @pl.when(slot * per + b == me)
+        @pl.when(local)
         def _():
             cot_keep().wait()
 
@@ -1344,7 +1393,7 @@
     for i in range(images):
         to, copy = cot_push(i)
 
-        @pl.when(to != me)
+        @pl.when(jnp.logical_not(owners.is_me(to)))
         def _():
             copy.wait_send()
 
@@ -1365,18 +1414,18 @@
     for b in range(per):
         to, copy = out_push(b)
 
-        @pl.when(to != me)
+        @pl.when(jnp.logical_not(owners.is_me(to)))
         def _():
             copy.wait_send()
 
     for i in range(images):
-        owner = i * sharers + me // per
-
-        @pl.when(owner != me)
+        local = owners.is_me(owners.device(group, i, me // per))
+
+        @pl.when(jnp.logical_not(local))
         def _():
             out_from(i).wait_recv()
 
-        @pl.when(owner == me)
+        @pl.when(local)
         def _():
             out_keep().wait()
 
@@ -1386,7 +1435,6 @@
     images, rows_here, width = cotangent.shape
     rows = own.shape[0]
     channels = mix.shape[0]
-    depth = width // count
     sharers = count // images
     per = count // sharers
     inside = pl.BlockSpec(memory_space=pltpu.VMEM)
@@ -1398,7 +1446,7 @@
         functools.partial(latent_kernel, count, images),
         out_shape=[
             shape((images, rows_here, width), bf16),
-            shape((7, count, rows, depth), bf16),
+            shape((7, width, rows), bf16),
             shape((9, rows, width), bf16),
             shape((channels, rows), bf16),
             shape((8, rows), f32),
@@ -1477,7 +1525,7 @@
     latents = rows_here * count
     sharers = count // images
     rows_own = latents // sharers
-    slot = me % sharers
+    slot = (me % (sharers // 2)) * 2 + lax.axis_index("img") % 2
     depth = w_query.shape[0]
     channels = gain_input.shape[0]
     width_scale = width ** (-0.5)

time: 568 us -> 462 us (0.81)
  Pallas kernels: 484 us -> 388 us
  local copies, waits for them, and re-layouts: 40.3 us -> 32.9 us
    pallas_call x1, Pallas kernels: 110 us -> 54.4 us  [latent_pass(): pl.pallas_call(functools.partial(latent_kernel, count, images), out_shape...]
    pallas_call x1, Pallas kernels: 188 us -> 144 us  [backward_pass(): pl.pallas_call(functools.partial(backward_kernel, count, teams, images, t...]
    unnamed x98 -> x92, local copies, waits for them, and re-layouts: 21.7 us -> 15.9 us
  transfers between devices with their start and end apart: 1 -> 1, of which waited for: 0 -> 0; matrix products, arithmetic and copies ran while one was open for 6% -> 5% of each run, Pallas kernels for 26% -> 33%
where the time goes in v4:
time: 462 us; the launch traced here: 461 us
  Pallas kernels  388 us (84%)
  local copies, waits for them, and re-layouts  32.9 us (7%)
  between operations  14.9 us (3%)
  other arithmetic  13.6 us (3%)
  matrix products  10.9 us (2%)
    pallas_call x1, Pallas kernels, forward_pass(): pl.pallas_call(functools.partial(forward_kernel, count, images, tile), ou...  152 us
    pallas_call x1, Pallas kernels, backward_pass(): pl.pallas_call(functools.partial(backward_kernel, count, teams, images, t...  144 us
    pallas_call x1, Pallas kernels, latent_pass(): pl.pallas_call(functools.partial(latent_kernel, count, images), out_shape...  54.4 us
    pallas_call x1, Pallas kernels, small_sums(): pl.pallas_call(functools.partial(sum_kernel, count, crowd), out_shape=[ja...  38 us
    unnamed x92, local copies, waits for them, and re-layouts  15.9 us
  transfers between devices with their start and end apart: 1, of which 0 were waited for; matrix products, arithmetic and copies ran while one was open for 5% of the time, Pallas kernels for 33%

profile of v4, /device:TPU:0, one launch (start us, length us, event | category | flops | bytes accessed | tf_op | source)
XLA Modules:
  0.0 460.7 jit_solution(10230008136019367605)
XLA Ops:
  7.3 0.9 copy-done
  8.1 2.0 convolution_convert_fusion.1
  10.2 1.5 multiply_reduce_fusion.3
  11.7 1.0 copy_convert_fusion
  14.1 0.8 convert_multiply_fusion.2
  19.1 1.7 bitcast_dynamic-update-slice_fusion.6
  20.8 1.7 bitcast_dynamic-update-slice_fusion.5
  24.6 1.7 bitcast_dynamic-update-slice_fusion.2.w_ref
  27.3 152.2 %shard_map.356 = (bf16[1,8,64,1024]{3,2,1,0:T(8,128)(2,1)S(1)}, bf16[1,8,128,1024]{3,2,1,0:T(8,128)(2,1)}, bf16[1,8,128,512]{3,2,1,0:T(8,128)(2,1)S(1)}, bf16[8,...) custom-call(f32[4,8,6272]{2,1,0:T(8,128)S(1)} %pad_maximum_fusion.v_, ...), custom_call_target="tpu_custom_call" | custom-call | tf_op jit(solution)/shard_map/pallas_call | solution.py:416
  181.2 1.8 pad.41.table_ref
  183.0 1.8 pad.42.gained_ref
  186.3 1.1 constant_dynamic-slice_fusion.own_ref
  187.4 1.9 pad.39.mix_ref
  189.3 54.4 %shard_map.357 = (bf16[4,64,1024]{2,1,0:T(8,128)(2,1)}, bf16[7,1024,256]{2,1,0:T(8,128)(2,1)}, bf16[9,256,1024]{2,1,0:T(8,128)(2,1)}, bf16[272,256]{1,0:T(8,128)...) custom-call(bf16[8,272,256]{2,1,0:T(8,128)(2,1)} %get-tuple-element.44.part_ref, ...), custom_call_target="tpu_custom_call" | custom-call | tf_op jit(solution)/shard_map/pallas_call | solution.py:1445
  243.7 143.8 %shard_map.358 = (bf16[512,384]{1,0:T(8,128)(2,1)}, f32[4,8,6272]{2,1,0:T(8,128)}, f32[9,128,1024]{2,1,0:T(8,128)}) custom-call(f32[4,8,6272]{2,1,0:T(8,128)} %copy-done.2, s32[256,896]{1,0:T(8,128)} %copy-done.1, f32[256,384]{1,0:T(8,128)} %pad.41.table_ref, f32[256,272]{1,0:T(8,128)} %pad.42.gained_ref, bf16[256,512]{1,0:T(8,128)(2,1)} %copy-done.6, ...), custom_call_target="tpu_custom_call" | custom-call | tf_op jit(solution)/shard_map/pallas_call | solution.py:786
  387.4 0.9 fusion.15
  388.4 4.3 slice_bitcast_fusion
  392.9 38.0 %shard_map.359 = (bf16[8,64,384]{2,1,0:T(8,128)(2,1)S(1)}, f32[8,8,128]{2,1,0:T(8,128)S(1)}, bf16[8,48,1024]{2,1,0:T(8,128)(2,1)S(1)}) custom-call(bf16[8,64,384]{2,1,0:T(8,128)(2,1)S(1)} %bitcast.96, f32[8,8,128]{2,1,0:T(8,128)S(1)} %fusion.16.g_ref, bf16[48,1024]{1,0:T(8,128)(2,1)S(1)} %pad.44.z_ref), custom_call_target="tpu_custom_call" | custom-call | tf_op jit(solution)/shard_map/pallas_call | solution.py:968
  431.0 1.2 convolution_bitcast_fusion
  432.2 1.0 fusion.6
  434.1 1.8 fusion.8
  436.0 2.0 fusion.13
  438.0 2.1 multiply_reduce_fusion
  440.2 0.8 fusion.30
  441.0 2.1 copy.79
  443.1 2.0 copy.80
  445.1 1.0 copy.78
  446.7 1.6 slice_multiply_fusion.1
  448.4 1.5 subtract_multiply_fusion
  449.9 0.8 copy.77
  451.3 1.7 fusion.11
  453.1 0.8 copy.106
  (153 shorter events, 14.1 us)
Async XLA Ops:
  7.2 6.8 %copy-start.22 = (s32[4,6272]{1,0:T(4,128)S(1)}, s32[4,6272]{1,0:T(4,128)}, u32[]{:S(2)}) copy-start(s32[4,6272]{1,0:T(4,128)} %param.22) | copy-start | bytes 301060
  7.2 180.1 %all-reduce.11.cloned.1.call-start = ((), (), s32[]{:S(2)}) async-start(), calls=%async_computation | async-start | bytes 1081344 | tf_op jit(solution)/shard_map/psum | solution.py:1536
  11.6 4.4 copy-start.31
  16.0 2.0 copy-start.25
  16.2 2.9 copy-start.14
  16.2 2.9 copy-start.15
  16.2 2.0 copy-start.30
  16.2 2.2 copy-start.26
  18.2 4.2 copy-start.27
  18.3 4.8 %copy-start.28 = (bf16[128,1024]{1,0:T(8,128)(2,1)S(1)}, bf16[128,1024]{1,0:T(8,128)(2,1)}, u32[]{:S(2)}) copy-start(bf16[128,1024]{1,0:T(8,128)(2,1)} %param.37) | copy-start | bytes 786436
  23.9 3.3 copy-start.3
  23.9 3.4 copy-start.5
  23.9 3.4 copy-start.8
  23.9 3.4 copy-start.10
  26.8 152.7 %copy-start.2 = (f32[4,8,6272]{2,1,0:T(8,128)}, f32[4,8,6272]{2,1,0:T(8,128)S(1)}, u32[]{:S(2)}) copy-start(f32[4,8,6272]{2,1,0:T(8,128)S(1)} %pad_maximum_fusion.v_ref) | copy-start | bytes 2408452
  27.2 152.3 %copy-start.1 = (s32[256,896]{1,0:T(8,128)}, s32[256,896]{1,0:T(8,128)S(1)}, u32[]{:S(2)}) copy-start(s32[256,896]{1,0:T(8,128)S(1)} %select_select_fusion.code_ref) | copy-start | bytes 2752516
  179.9 5.7 %copy-start.33 = (f32[1024]{0:T(1024)S(1)}, f32[1024]{0:T(1024)}, u32[]{:S(2)}) copy-start(f32[1024]{0:T(1024)} %param.38) | copy-start | bytes 12292
  179.9 5.7 %copy-start.34 = (f32[1024]{0:T(1024)S(1)}, f32[1024]{0:T(1024)}, u32[]{:S(2)}) copy-start(f32[1024]{0:T(1024)} %param.33) | copy-start | bytes 12292
  179.9 5.7 %copy-start.35 = (f32[1024]{0:T(1024)S(1)}, f32[1024]{0:T(1024)}, u32[]{:S(2)}) copy-start(f32[1024]{0:T(1024)} %param.30) | copy-start | bytes 12292
  388.4 4.3 copy-start.32
  388.4 4.3 copy-start.29
  388.4 4.5 copy-start.4
  392.7 38.3 %copy-start.23 = (bf16[261,128]{1,0:T(8,128)(2,1)S(1)}, bf16[261,128]{1,0:T(8,128)(2,1)}, u32[]{:S(2)}) copy-start(bf16[261,128]{1,0:T(8,128)(2,1)} %param.28) | copy-start | bytes 200452
  392.8 40.4 %copy-start.18 = (f32[512,512]{1,0:T(8,128)S(1)}, f32[512,512]{1,0:T(8,128)}, u32[]{:S(2)}) copy-start(f32[512,512]{1,0:T(8,128)} %get-tuple-element.64) | copy-start | bytes 3145732
  430.9 2.4 copy-start.13
  433.3 4.6 %copy-start.11 = (f32[1024]{0:T(1024)S(1)}, f32[1024]{0:T(1024)}, u32[]{:S(2)}) copy-start(f32[1024]{0:T(1024)} %param.25) | copy-start | bytes 12292
  433.4 4.6 %copy-start.36 = (bf16[1,8,128,1024]{3,2,1,0:T(8,128)(2,1)S(1)}, bf16[1,8,128,1024]{3,2,1,0:T(8,128)(2,1)}, u32[]{:S(2)}) copy-start(bf16[1,8,128,1024]{3,2,1,0:T(8,128)(2,1)} %get-tuple-element.62) | copy-start | bytes 6291460
  440.9 4.2 copy-start.16
  440.9 7.5 %copy-start.17 = (bf16[4,3,6272]{2,0,1:T(4,128)(2,1)S(1)}, bf16[4,3,6272]{2,0,1:T(4,128)(2,1)}, u32[]{:S(2)}) copy-start(bf16[4,3,6272]{2,0,1:T(4,128)(2,1)} %param.21) | copy-start | bytes 451588
  440.9 7.5 %copy-start.20 = (f32[4,6272]{1,0:T(4,128)S(1)}, f32[4,6272]{1,0:T(4,128)}, u32[]{:S(2)}) copy-start(f32[4,6272]{1,0:T(4,128)} %get-tuple-element.138) | copy-start | bytes 301060
  440.9 7.5 %copy-start.21 = (f32[4,6272]{1,0:T(4,128)S(1)}, f32[4,6272]{1,0:T(4,128)}, u32[]{:S(2)}) copy-start(f32[4,6272]{1,0:T(4,128)} %get-tuple-element.140) | copy-start | bytes 301060
  446.1 7.0 %copy-start.19 = (bf16[4,64,1024]{2,1,0:T(8,128)(2,1)S(1)}, bf16[4,64,1024]{2,1,0:T(8,128)(2,1)}, u32[]{:S(2)}) copy-start(bf16[4,64,1024]{2,1,0:T(8,128)(2,1)} %get-tuple-element.195) | copy-start | bytes 1572868
  (6 other events, 5.9 us)
Sparse Core Ops, SparseCore 0:
  11.4 78.3 all-reduce.10

commit v5 on v4

--- a/solution.py
+++ b/solution.py
@@ -33,13 +33,6 @@
 
 def mm_tn(left, right):
     return lax.dot_general(left, right, (((0,), (0,)), ((), ())), preferred_element_type=f32)
-
-
-def layer_norm(rows, gain):
-    average = jnp.mean(rows, axis=-1, keepdims=True)
-    centred = rows - average
-    spread = jnp.mean(centred * centred, axis=-1, keepdims=True)
-    return centred * lax.rsqrt(spread + eps) * gain
 
 
 def angles(index):
@@ -101,6 +94,39 @@
 
 
 def forward_kernel(
+    count,
+    images,
+    tile,
+    mats,
+    v_ref,
+    code_ref,
+    table_ref,
+    gained_ref,
+    gain_ref,
+    lat_ref,
+    wq_ref,
+    wk_ref,
+    *refs,
+):
+    shards = refs[:mats]
+    forward_body(
+        count,
+        images,
+        tile,
+        v_ref,
+        code_ref,
+        table_ref,
+        gained_ref,
+        gain_ref,
+        lat_ref,
+        wq_ref,
+        wk_ref,
+        shards,
+        *refs[mats:],
+    )
+
+
+def forward_body(
     count,
     images,
     tile,
@@ -112,7 +138,7 @@
     lat_ref,
     wq_ref,
     wk_ref,
-    w_ref,
+    shards,
     lat_full,
     wq_full,
     wk_full,
@@ -124,15 +150,11 @@
     alow_ref,
     part_ref,
     stat_ref,
-    lat_v,
-    wq_v,
-    wk_v,
     acc,
     top,
     u_send,
     s_send,
     own_sem,
-    load_sem,
     send_sem,
     recv_sem,
     hand_send,
@@ -147,7 +169,7 @@
     owners = Owners(count, images)
     sharers = owners.sharers
     rows = part_ref.shape[2]
-    width = wq_ref.shape[2]
+    width = wq_ref.shape[1]
     latents = normed_ref.shape[0]
     group, me = lax.axis_index("img"), lax.axis_index("pix")
     core = lax.rem(group, 2)
@@ -155,30 +177,33 @@
     sides = ((group, ring_device(place + 1, count)), (group, ring_device(place - 1, count)))
     other = (group + 1 - 2 * core, me)
     greet(plane(count))
-    sources = (lat_ref, wq_ref, wk_ref, w_ref)
+    sources = (lat_ref, wq_ref, wk_ref)
     fulls = (lat_full, wq_full, wk_full, w_full)
-    mats = w_ref.shape[0]
-
-    def spot(a, k, stage, way, source):
-        wide = sources[a].shape[2] // 4
-        columns = pl.ds(pl.multiple_of((core * 2 + way) * wide, 128), wide)
+    mats = len(shards)
+
+    reach = count // 2
+
+    def spot(a, k, stage, way, last, source=False):
+        wide = fulls[a].shape[3] // 4
+        begin = (core * 2 + way) * wide if last else core * 2 * wide
+        columns = pl.ds(pl.multiple_of(begin, 128), wide if last else 2 * wide)
         if source:
-            return sources[a].at[k, :, columns]
+            return (sources[a] if a < 3 else shards[k]).at[:, columns]
         origin = ring_device(place - stage if way == 0 else place + stage, count)
         return fulls[a].at[k, origin, :, columns]
 
-    def hop(a, k, stage, way, first=False):
+    def hop(a, k, stage, way, first=False, last=False):
         return pltpu.make_async_remote_copy(
-            spot(a, k, stage, way, first),
-            spot(a, k, stage, way, False),
+            spot(a, k, stage, way, last, first),
+            spot(a, k, stage, way, last),
             send_sem.at[stage, way, a + k],
             recv_sem.at[stage, way, a + k],
             device_id=sides[way],
             device_id_type=MESH,
         )
 
-    def hand(a, k, stage, way):
-        part = spot(a, k, stage, way, False)
+    def hand(a, k, stage, way, last=False):
+        part = spot(a, k, stage, way, last)
         return pltpu.make_async_remote_copy(
             part,
             part,
@@ -188,64 +213,80 @@
             device_id_type=MESH,
         )
 
-    def relay(a, k, stage, onward=True):
+    def relay(a, k, stage):
         for way in range(2):
             hop(a, k, stage - 1, way).wait_recv()
-            if onward:
+
+            @pl.when(stage == reach - 1)
+            def _():
+                hop(a, k, stage, way, last=True).start()
+
+            @pl.when(stage != reach - 1)
+            def _():
                 hop(a, k, stage, way).start()
+
             hand(a, k, stage, way).start()
 
+    def relay_end(a, k):
+        for way in range(2):
+            hop(a, k, reach - 1, way, last=True).wait_recv()
+            hand(a, k, reach, way, last=True).start()
+
+    def start_ring(a, k):
+        for way in range(2):
+            hop(a, k, 0, way, True, reach == 1).start()
+
+    def sent(a, k):
+        for way in range(2):
+            for stage in range(reach):
+                last = stage == reach - 1
+                hop(a, k, stage, way, stage == 0, last).wait_send()
+                hand(a, k, stage + 1, way, last).wait_send()
+
+    def handed(a, k):
+        for way in range(2):
+            for stage in range(1, reach + 1):
+                hand(a, k, stage, way, stage == reach).wait_recv()
+
     own = [
-        pltpu.make_async_copy(sources[a], fulls[a].at[:, me], own_sem.at[a]) for a in range(4)
+        pltpu.make_async_copy(shards[k], fulls[3].at[k, me], own_sem.at[k]) for k in range(mats)
     ]
     for a in range(3):
-        for way in range(2):
-            hop(a, 0, 0, way, True).start()
+        start_ring(a, 0)
+    for a in range(3):
+        fulls[a][0, me] = sources[a][...]
     for copy in own:
         copy.start()
-    for stage in range(1, count):
+    each = -(-mats // reach)
+    for stage in range(1, reach + 1):
         for a in range(3):
-            relay(a, 0, stage, stage < count - 1)
-        if stage <= mats:
-            for way in range(2):
-                hop(3, stage - 1, 0, way, True).start()
-    for k in range(count - 1, mats):
-        for way in range(2):
-            hop(3, k, 0, way, True).start()
+            if stage < reach:
+                relay(a, 0, jnp.int32(stage))
+            else:
+                relay_end(a, 0)
+        for k in range((stage - 1) * each, min(stage * each, mats)):
+            start_ring(3, k)
     for a in range(3):
-        own[a].wait()
-        for stage in range(1, count):
-            for way in range(2):
-                hand(a, 0, stage, way).wait_recv()
-
-    loads = [
-        pltpu.make_async_copy(full.at[0], held, load_sem.at[j])
-        for j, (full, held) in enumerate(((lat_full, lat_v), (wq_full, wq_v), (wk_full, wk_v)))
-    ]
-    for copy in loads:
-        copy.start()
-    loads[0].wait()
-    rows_here = lat_v.shape[1]
+        handed(a, 0)
+
+    rows_here = lat_ref.shape[0]
 
     @pl.loop(0, count)
     def _(o):
-        block = lat_v[o].astype(f32)
+        block = lat_full[0, o].astype(f32)
         average = jnp.mean(block, axis=1, keepdims=True)
         centred = block - average
         spread = jnp.mean(centred * centred, axis=1, keepdims=True)
         normed = (centred * lax.rsqrt(spread + eps) * gain_ref[...]).astype(bf16)
         normed_ref[pl.ds(pl.multiple_of(o * rows_here, rows_here), rows_here), :] = normed
 
-    loads[1].wait()
-
     @pl.loop(0, width // 256)
     def _(j):
         columns = pl.ds(pl.multiple_of(j * 256, 256), 256)
-        weight = wq_v[:, :, columns].reshape(width, 256)
+        weight = wq_full[0, :, :, columns].reshape(width, 256)
         query_ref[:, columns] = mm(normed_ref[...], weight).astype(bf16)
 
-    loads[2].wait()
-    a_ref[...] = mm(query_ref[...], wk_v[...].reshape(width, wk_v.shape[2])) * (width ** (-0.5))
+    a_ref[...] = mm(query_ref[...], wk_full[0].reshape(width, wk_ref.shape[1])) * (width ** (-0.5))
 
     def exact_nt(left, right):
         return lax.dot_general(
@@ -259,7 +300,9 @@
     at_ref[...] = (exact_nt(gained_ref[...], a_ref[...]) * LOG2E).astype(bf16)
     alow_ref[...] = exact_nt(a_ref[...], gained_ref[...]).astype(bf16)
 
-    relays = (count - 2) * mats
+    table_t = table_ref[...].T[: part_ref.shape[1], :]
+
+    relays = (reach - 1) * mats
 
     def relay_number(e):
         relay(3, lax.rem(e, mats), 1 + e // mats)
@@ -314,7 +357,7 @@
         @pl.when(step == steps - 1)
         def _():
             raw = jnp.dot(
-                table_ref[...],
+                table_t,
                 acc[:CHANNELS, :],
                 precision=lax.Precision.HIGHEST,
                 preferred_element_type=f32,
@@ -344,21 +387,16 @@
 
     @pl.loop(0, mats)
     def _(k):
-        relay(3, k, count - 1, False)
-
-    own[3].wait()
+        relay_end(3, k)
+
+    for copy in own:
+        copy.wait()
     for a in range(3):
-        for way in range(2):
-            for stage in range(count - 1):
-                hop(a, 0, stage, way).wait_send()
-                hand(a, 0, stage + 1, way).wait_send()
-
-    @pl.loop(0, mats)
-    def _(k):
-        for way in range(2):
-            for stage in range(count - 1):
-                hop(3, k, stage, way).wait_send()
-                hand(3, k, stage + 1, way).wait()
+        sent(a, 0)
+
+    for k in range(mats):
+        sent(3, k)
+        handed(3, k)
 
     def u_from(source):
         sems = lambda which: dict(
@@ -395,48 +433,43 @@
                 copy.wait_recv()
 
 
-def forward_pass(values, table, gained, gain_latent, lat, wq, wk, shards, collective_id):
+def forward_pass(values, table, gained, gain_latent, lat, wq, wk, shards, tall, collective_id):
     count = lax.axis_size("pix")
     images, _, pixels = values.shape
     tile = pixel_tile(pixels)
-    rows_here, width = lat.shape[1:]
+    rows_here, width = lat.shape
     latents = rows_here * count
     sharers = count // images
     rows = latents // sharers
-    tall = table.shape[0]
-    mats = shards.shape[0]
+    mats = len(shards)
     inside = pl.BlockSpec(memory_space=pltpu.VMEM)
     anywhere = pl.BlockSpec(memory_space=pl.ANY)
     shape = jax.ShapeDtypeStruct
 
-    def full(array):
-        return shape((array.shape[0], count) + array.shape[1:], array.dtype)
-
-    ring = DMA((count - 1, 2, 3 + mats))
+    def full(array, number=1):
+        return shape((number, count) + array.shape, array.dtype)
+
+    ring = DMA((count // 2, 2, 3 + mats))
     return pl.pallas_call(
-        functools.partial(forward_kernel, count, images, tile),
-        out_shape=[full(lat), full(wq), full(wk), full(shards)]
+        functools.partial(forward_kernel, count, images, tile, mats),
+        out_shape=[full(lat), full(wq), full(wk), full(shards[0], mats)]
         + [
             shape((latents, width), bf16),
             shape((latents, width), bf16),
-            shape((latents, wk.shape[2]), f32),
+            shape((latents, wk.shape[1]), f32),
             shape((CHANNELS, latents), bf16),
             shape((latents, CHANNELS), bf16),
             shape((count, tall, rows), bf16),
             shape((count, 8, rows), f32),
         ],
-        in_specs=[inside] * 5 + [anywhere] * 4,
-        out_specs=[anywhere] * 4 + [inside] * 5 + [anywhere] * 2,
+        in_specs=[inside] * (8 + mats),
+        out_specs=[inside] * 3 + [anywhere] + [inside] * 5 + [anywhere] * 2,
         scratch_shapes=[
-            pltpu.VMEM((count,) + lat.shape[1:], bf16),
-            pltpu.VMEM((count,) + wq.shape[1:], bf16),
-            pltpu.VMEM((count,) + wk.shape[1:], bf16),
             pltpu.VMEM((CHANNELS + 16, latents), f32),
             pltpu.VMEM((8, latents), f32),
             pltpu.VMEM((images, sharers, tall, rows), bf16),
             pltpu.VMEM((images, sharers, 8, rows), f32),
-            DMA((4,)),
-            DMA((3,)),
+            DMA((mats,)),
             ring,
             ring,
             ring,
@@ -448,7 +481,7 @@
         compiler_params=pltpu.CompilerParams(
             collective_id=collective_id, has_side_effects=True, vmem_limit_bytes=48 * 2**20
         ),
-    )(values, hot_codes(tile), table, gained, gain_latent[None], lat, wq, wk, shards)
+    )(values, hot_codes(tile), table, gained, gain_latent[None], lat, wq, wk, *shards)
 
 
 def backward_kernel(
@@ -456,6 +489,7 @@
     teams,
     images,
     tile,
+    channels,
     v_ref,
     code_ref,
     table_ref,
@@ -464,11 +498,21 @@
     a_ref,
     back_ref,
     row_ref,
+    gain_ref,
     xs_ref,
     gs_ref,
-    t_ref,
+    t_out,
+    g_out,
+    z_out,
     pixel_ref,
     out_ref,
+    t_raw,
+    t_in,
+    t_img,
+    g_raw,
+    g_in,
+    g_img,
+    z_own,
     t_acc,
     bt,
     b_low,
@@ -493,6 +537,16 @@
     hand_recv,
     back_send,
     back_recv,
+    sum_send,
+    sum_recv,
+    img_send,
+    img_recv,
+    last_send,
+    last_recv,
+    z_send,
+    z_recv,
+    z_hand_send,
+    z_hand_recv,
 ):
     number, rows, width = gs_ref.shape
     kinds = xs_ref.shape[0]
@@ -508,7 +562,60 @@
     sides = ((group, ring_device(place + 1, count)), (group, ring_device(place - 1, count)))
     other = (group + 1 - 2 * core, me)
     partners = [(lax.rem(team + d, teams) * 2 + core, me) for d in range(1, teams)]
-    greet(plane(count) + partners)
+    crowd = 2 * teams
+    others = peers(count)
+    same_place = [(lax.rem(group + d, crowd), me) for d in range(1, crowd)]
+    far = [
+        (lax.rem(team + d, teams) * 2 + c, me) for d in range(1, teams) for c in range(2)
+    ]
+    greet(plane(count) + far)
+
+    def send(source, target, sems, index, device):
+        return pltpu.make_async_remote_copy(
+            source,
+            target,
+            sems[0].at[index],
+            sems[1].at[index],
+            device_id=device,
+            device_id_type=MESH,
+        )
+
+    def scatter(d):
+        to, sems = others[d][1], (sum_send, sum_recv)
+        return (
+            send(t_raw.at[to], t_in.at[d], sems, (0, d), others[d]),
+            send(g_raw.at[to], g_in.at[d], sems, (1, d), others[d]),
+        )
+
+    def over(d):
+        sems = (img_send, img_recv)
+        return (
+            send(t_img.at[group], t_img.at[group], sems, (0, d), same_place[d]),
+            send(g_img.at[group], g_img.at[group], sems, (1, d), same_place[d]),
+        )
+
+    def gather(d):
+        sems = (last_send, last_recv)
+        return (
+            send(t_out.at[me], t_out.at[me], sems, (0, d), others[d]),
+            send(g_out.at[me], g_out.at[me], sems, (1, d), others[d]),
+        )
+
+    def z_push(d):
+        return send(z_own, z_out.at[core, me], (z_send, z_recv), d, others[d])
+
+    def z_hand():
+        return pltpu.make_async_remote_copy(
+            z_out.at[core],
+            z_out.at[core],
+            z_hand_send,
+            z_hand_recv,
+            device_id=other,
+            device_id_type=MESH,
+        )
+
+    for o in range(count):
+        g_raw[o] = gain_ref[:, o * depth : (o + 1) * depth]
 
     own_index = owners.image * sharers + owners.slot
 
@@ -578,43 +685,59 @@
             device_id_type=MESH,
         )
 
-    for j in range(number):
-        if j < kinds:
+    order = [number - 1] + list(range(number - 1))
+    for k in order:
+        j = max(k - (number - kinds), 0)
+        if k == 0 or k > number - kinds:
             load_x(j).start()
             pair_x(j).start()
-        load_g(j).start()
-        pair_g(j).start()
-
-    def part(k, owner, way):
-        here = pl.ds(pl.multiple_of(owner * depth, depth), depth)
-        return terms.at[k, here, way * wide : (way + 1) * wide]
+        load_g(k).start()
+        pair_g(k).start()
+
+    def turn(k):
+        return lax.rem(k + number - 1, number)
+
+    reach = count // 2
+
+    def owner_at(stage, way):
+        ahead = reach - stage
+        return ring_device(place + ahead if way == 0 else place - ahead, count)
+
+    def rows_of(owner):
+        return pl.ds(pl.multiple_of(owner * depth, depth), depth)
+
+    def quarter(q):
+        return slice(q * wide, (q + 1) * wide)
 
     def hop(k, stage, way, start=False):
-        source = part(k, owner_at(0, way), way) if start else held.at[k, way, stage - 1]
+        if start:
+            source = terms.at[k, rows_of(owner_at(0, way)), quarter(way)]
+            target = held.at[k, way, 0, :, quarter(way)]
+        else:
+            source = held.at[k, way, stage - 1]
+            target = held.at[k, way, stage]
         return pltpu.make_async_remote_copy(
             source,
-            held.at[k, way, stage],
+            target,
             send_sem.at[stage, way, k],
             recv_sem.at[stage, way, k],
             device_id=sides[way],
             device_id_type=MESH,
         )
 
-    def cross(k, way, d):
+    def cross(k, d):
         return pltpu.make_async_remote_copy(
-            across.at[team, k, way],
-            across.at[team, k, way],
-            cross_send.at[d, way, k],
-            cross_recv.at[d, way, k],
+            across.at[team, k],
+            across.at[team, k],
+            cross_send.at[d, k],
+            cross_recv.at[d, k],
             device_id=partners[d],
             device_id_type=MESH,
         )
 
-    def owner_at(stage, way):
-        return ring_device(place - stage - 1 if way == 0 else place + stage + 1, count)
-
     @pl.loop(0, number)
     def _(k):
+        k = turn(k)
         j = jnp.maximum(k - (number - kinds), 0)
 
         @pl.when((k == 0) | (k > number - kinds))
@@ -634,17 +757,30 @@
 
     def relay(k, stage):
         for way in range(2):
-            own = part(k, owner_at(stage, way), way)[...].astype(f32)
-            hop(k, stage - 1, way, True).wait_recv()
-            held[k, way, stage - 1] = (own + held[k, way, stage - 1].astype(f32)).astype(bf16)
+            here = rows_of(owner_at(stage, way))
+
+            @pl.when(stage == 1)
+            def _():
+                hop(k, 0, way, True).wait_recv()
+                both = terms[k, here, quarter(way)].astype(f32)
+                both = both + held[k, way, 0, :, quarter(way)].astype(f32)
+                held[k, way, 0, :, quarter(way)] = both.astype(bf16)
+                held[k, way, 0, :, quarter(1 - way)] = terms[k, here, quarter(1 - way)]
+
+            @pl.when(stage > 1)
+            def _():
+                hop(k, stage - 1, way).wait_recv()
+                both = terms[k, here, :].astype(f32) + held[k, way, stage - 1].astype(f32)
+                held[k, way, stage - 1] = both.astype(bf16)
+
             hop(k, stage, way).start()
 
     def relay_number(e):
-        relay(lax.rem(e, number), 1 + e // number)
-
-    relays = (count - 2) * number
+        relay(turn(lax.rem(e, number)), 1 + e // number)
+
+    relays = (reach - 1) * number
     tiles = images * steps
-    pace = min(2, relays // tiles)
+    pace = min(-(-relays // tiles), 2)
     t_acc[...] = jnp.zeros_like(t_acc)
 
     @pl.loop(0, tiles)
@@ -652,7 +788,10 @@
         image = lax.rem(t // steps + owners.image, images)
         step = lax.rem(t, steps)
         for e in range(pace):
-            relay_number(t * pace + e)
+
+            @pl.when(t * pace + e < relays)
+            def _():
+                relay_number(t * pace + e)
 
         @pl.when(step == 0)
         def _():
@@ -668,7 +807,7 @@
 
                 here = slice(h * rows, (h + 1) * rows)
                 wide = jnp.dot(
-                    gained_ref[...],
+                    gained_ref[:, : back_ref.shape[0]],
                     back_all[source].astype(f32),
                     precision=lax.Precision.HIGHEST,
                     preferred_element_type=f32,
@@ -693,15 +832,22 @@
             lane = lax.broadcasted_iota(jnp.int32, end.shape, 1)
             ends.append(jnp.where(lane == 120, along, end))
         t_acc[...] += mm(xt, jnp.concatenate(kept, axis=0))
-        pixel_ref[image, :, span] = jnp.concatenate(ends, axis=0).T[120:128, :]
-
-    t_ref[...] = lax.dot_general(
+        ends = jnp.concatenate(ends, axis=0).T[120:128, :] * (values[0:1, :] * values[1:2, :])
+        hat = values[4:7, :] + values[7:8, :]
+        mean_part = ends[7:8, :] + hat * ends[0:1, :]
+        pixel_ref[image, :, span] = ends[4:7, :] - mean_part * (1.0 / channels)
+
+    t_sum = lax.dot_general(
         t_acc[:CHANNELS, :],
-        table_ref[...],
+        table_ref[:, : t_raw.shape[2]],
         (((0,), (0,)), ((), ())),
         precision=lax.Precision.HIGHEST,
         preferred_element_type=f32,
-    ).astype(bf16)
+    )
+    t_raw[...] = t_sum.astype(bf16).reshape(t_raw.shape)
+    for d in range(count - 1):
+        for copy in scatter(d):
+            copy.start()
 
     if tiles * pace < relays:
 
@@ -711,12 +857,27 @@
 
     @pl.loop(0, number)
     def _(k):
+        k = turn(k)
         for way in range(2):
-            own = part(k, me, way)[...].astype(f32)
-            hop(k, count - 2, way, True).wait_recv()
-            across[team, k, way] = (own + held[k, way, count - 2].astype(f32)).astype(bf16)
-            for d in range(teams - 1):
-                cross(k, way, d).start()
+            hop(k, reach - 1, way, reach == 1).wait_recv()
+        total = terms[k, rows_of(me), :].astype(f32)
+        for way in range(2):
+            total = total + held[k, way, reach - 1].astype(f32)
+        across[team, k] = total.astype(bf16)
+        for d in range(teams - 1):
+            cross(k, d).start()
+
+    t_sum, g_sum = t_raw[me].astype(f32), g_raw[me]
+    for d in range(count - 1):
+        for copy in scatter(d):
+            copy.wait_recv()
+        t_sum = t_sum + t_in[d].astype(f32)
+        g_sum = g_sum + g_in[d]
+    t_img[group] = t_sum.astype(bf16)
+    g_img[group] = g_sum
+    for d in range(crowd - 1):
+        for copy in over(d):
+            copy.start()
 
     def finish(k):
         columns = pl.ds(pl.multiple_of(core * half, 128), half)
@@ -735,15 +896,49 @@
 
     @pl.loop(0, number)
     def _(k):
-        for way in range(2):
-            for d in range(teams - 1):
-                cross(k, way, d).wait_recv()
-            total = across[0, k, way].astype(f32)
-            for t in range(1, teams):
-                total = total + across[t, k, way].astype(f32)
-            done[k, :, way * wide : (way + 1) * wide] = total
+        k = turn(k)
+        for d in range(teams - 1):
+            cross(k, d).wait_recv()
+        total = across[0, k].astype(f32)
+        for t in range(1, teams):
+            total = total + across[t, k].astype(f32)
+        done[k] = total
         finish(k).start()
         hand(k).start()
+
+        @pl.when(k == number - 1)
+        def _():
+            rows_here = t_raw.shape[1]
+            mine = done[number - 1, rows_here : rows_here + z_own.shape[0], :].astype(bf16)
+            z_own[...] = mine
+            z_out[core, me] = mine
+            for d in range(count - 1):
+                z_push(d).start()
+
+    for d in range(crowd - 1):
+        for copy in over(d):
+            copy.wait_recv()
+    t_sum, g_sum = t_img[0].astype(f32), g_img[0]
+    for i in range(1, crowd):
+        t_sum = t_sum + t_img[i].astype(f32)
+        g_sum = g_sum + g_img[i]
+    t_out[me] = t_sum.astype(bf16)
+    g_out[me] = g_sum
+    for d in range(count - 1):
+        for copy in gather(d):
+            copy.start()
+    for d in range(count - 1):
+        z_push(d).wait()
+    z_hand().start()
+    for d in range(count - 1):
+        for copy in gather(d):
+            copy.wait()
+        for copy in scatter(d):
+            copy.wait_send()
+    for d in range(crowd - 1):
+        for copy in over(d):
+            copy.wait_send()
+    z_hand().wait()
 
     @pl.loop(0, number)
     def _(k):
@@ -751,10 +946,10 @@
         hand(k).wait()
         pair_g(k).wait_send()
         for way in range(2):
-            for stage in range(count - 1):
+            for stage in range(reach):
                 hop(k, stage, way, stage == 0).wait_send()
-            for d in range(teams - 1):
-                cross(k, way, d).wait_send()
+        for d in range(teams - 1):
+            cross(k, d).wait_send()
 
     @pl.loop(0, kinds)
     def _(j):
@@ -769,7 +964,9 @@
                 copy.wait_send()
 
 
-def backward_pass(values, table, gained, at, a, back, rows_in, xs, gs, collective_id):
+def backward_pass(
+    values, table, gained, at, a, back, rows_in, gains, xs, gs, channels, collective_id
+):
     count = lax.axis_size("pix")
     teams = lax.axis_size("img") // 2
     kinds, _, rows = xs.shape
@@ -777,22 +974,35 @@
     depth = xs.shape[1] // count
     anywhere = pl.BlockSpec(memory_space=pl.ANY)
     inside = pl.BlockSpec(memory_space=pltpu.VMEM)
-    chunk = (depth, width // 4)
+    chunk = (depth, width // 2)
     images, _, pixels = values.shape
     tile = pixel_tile(pixels)
     latents = at.shape[1]
     tall = back.shape[0]
     shape = jax.ShapeDtypeStruct
+    rows_here = latents // count
+    t_shape = shape((count, rows_here, -(-channels // 128) * 128), bf16)
+    g_shape = shape((count, 8, depth), f32)
+    spare = min(-(-share_rows(channels, count) // 16) * 16, depth - rows_here)
     return pl.pallas_call(
-        functools.partial(backward_kernel, count, teams, images, tile),
+        functools.partial(backward_kernel, count, teams, images, tile, channels),
         out_shape=[
-            shape((latents, table.shape[1]), bf16),
-            shape((images, 8, pixels), f32),
+            t_shape,
+            g_shape,
+            shape((2, count, spare, width // 2), bf16),
+            shape((images, 3, pixels), f32),
             shape((number, depth, width), f32),
         ],
-        in_specs=[inside] * 8 + [anywhere] * 2,
-        out_specs=[inside] * 2 + [anywhere],
+        in_specs=[inside] * 9 + [anywhere] * 2,
+        out_specs=[inside] * 4 + [anywhere],
         scratch_shapes=[
+            pltpu.VMEM(t_shape.shape, bf16),
+            pltpu.VMEM((count - 1,) + t_shape.shape[1:], bf16),
+            pltpu.VMEM((2 * teams,) + t_shape.shape[1:], bf16),
+            pltpu.VMEM(g_shape.shape, f32),
+            pltpu.VMEM((count - 1,) + g_shape.shape[1:], f32),
+            pltpu.VMEM((2 * teams,) + g_shape.shape[1:], f32),
+            pltpu.VMEM((spare, width // 2), bf16),
             pltpu.VMEM((CHANNELS + 16, latents), f32),
             pltpu.VMEM((CHANNELS, latents), bf16),
             pltpu.VMEM((latents, CHANNELS), bf16),
@@ -802,26 +1012,36 @@
             pltpu.VMEM((kinds, 2, xs.shape[1], rows), bf16),
             pltpu.VMEM((number, 2, rows, width // 2), bf16),
             pltpu.VMEM((number, xs.shape[1], width // 2), bf16),
-            pltpu.VMEM((number, 2, count - 1) + chunk, bf16),
-            pltpu.VMEM((teams, number, 2) + chunk, bf16),
+            pltpu.VMEM((number, 2, count // 2) + chunk, bf16),
+            pltpu.VMEM((teams, number) + chunk, bf16),
             pltpu.VMEM((number, depth, width // 2), f32),
             DMA((2, number)),
             DMA((2, number)),
             DMA((2, number)),
-            DMA((count - 1, 2, number)),
-            DMA((count - 1, 2, number)),
-            DMA((teams - 1, 2, number)),
-            DMA((teams - 1, 2, number)),
+            DMA((count // 2, 2, number)),
+            DMA((count // 2, 2, number)),
+            DMA((teams - 1, number)),
+            DMA((teams - 1, number)),
             DMA((number,)),
             DMA((number,)),
             DMA((number,)),
             DMA((2, count)),
             DMA((2, count)),
+            DMA((2, count - 1)),
+            DMA((2, count - 1)),
+            DMA((2, 2 * teams - 1)),
+            DMA((2, 2 * teams - 1)),
+            DMA((2, count - 1)),
+            DMA((2, count - 1)),
+            DMA((count - 1,)),
+            DMA((count - 1,)),
+            DMA,
+            DMA,
         ],
         compiler_params=pltpu.CompilerParams(
             collective_id=collective_id, has_side_effects=True, vmem_limit_bytes=60 * 2**20
         ),
-    )(values, hot_codes(tile), table, gained, at, a, back, rows_in, xs, gs)
+    )(values, hot_codes(tile), table, gained, at, a, back, rows_in, gains, xs, gs)
 
 
 def peers(count):
@@ -857,140 +1077,9 @@
         return (device[0] == self.group) & (device[1] == self.me)
 
 
-def sum_kernel(
-    count,
-    crowd,
-    t_ref,
-    g_ref,
-    z_ref,
-    t_out,
-    g_out,
-    z_out,
-    t_in,
-    g_in,
-    t_img,
-    g_img,
-    own_sem,
-    send_sem,
-    recv_sem,
-    img_send,
-    img_recv,
-    last_send,
-    last_recv,
-):
-    group, me = lax.axis_index("img"), lax.axis_index("pix")
-    others = peers(count)
-    across = [(lax.rem(group + d, crowd), me) for d in range(1, crowd)]
-    greet(others + across)
-
-    def copy(source, target, sems, index, device):
-        return pltpu.make_async_remote_copy(
-            source,
-            target,
-            sems[0].at[index],
-            sems[1].at[index],
-            device_id=device,
-            device_id_type=MESH,
-        )
-
-    def scatter(d):
-        to = others[d][1]
-        sems = (send_sem, recv_sem)
-        return (
-            copy(t_ref.at[to], t_in.at[d], sems, (0, d), others[d]),
-            copy(g_ref.at[to], g_in.at[d], sems, (1, d), others[d]),
-        )
-
-    def spread(d):
-        return copy(z_ref, z_out.at[me], (send_sem, recv_sem), (2, d), others[d])
-
-    def over(d):
-        sems = (img_send, img_recv)
-        return (
-            copy(t_img.at[group], t_img.at[group], sems, (0, d), across[d]),
-            copy(g_img.at[group], g_img.at[group], sems, (1, d), across[d]),
-        )
-
-    def gather(d):
-        sems = (last_send, last_recv)
-        return (
-            copy(t_out.at[me], t_out.at[me], sems, (0, d), others[d]),
-            copy(g_out.at[me], g_out.at[me], sems, (1, d), others[d]),
-        )
-
-    for d in range(count - 1):
-        for part in scatter(d):
-            part.start()
-    for d in range(count - 1):
-        spread(d).start()
-    keep = pltpu.make_async_copy(z_ref, z_out.at[me], own_sem)
-    keep.start()
-    t_sum = t_ref[me].astype(f32)
-    g_sum = g_ref[me]
-    for d in range(count - 1):
-        for part in scatter(d):
-            part.wait_recv()
-        t_sum = t_sum + t_in[d].astype(f32)
-        g_sum = g_sum + g_in[d]
-    t_img[group] = t_sum.astype(bf16)
-    g_img[group] = g_sum
-    for d in range(crowd - 1):
-        for part in over(d):
-            part.start()
-    for d in range(crowd - 1):
-        for part in over(d):
-            part.wait_recv()
-    t_sum = t_img[0].astype(f32)
-    g_sum = g_img[0]
-    for i in range(1, crowd):
-        t_sum = t_sum + t_img[i].astype(f32)
-        g_sum = g_sum + g_img[i]
-    t_out[me] = t_sum.astype(bf16)
-    g_out[me] = g_sum
-    for d in range(count - 1):
-        for part in gather(d):
-            part.start()
-    keep.wait()
-    for d in range(count - 1):
-        for part in gather(d):
-            part.wait()
-        for part in scatter(d):
-            part.wait_send()
-        spread(d).wait()
-    for d in range(crowd - 1):
-        for part in over(d):
-            part.wait_send()
-
-
-def small_sums(t, g, z, collective_id):
-    count, crowd = lax.axis_size("pix"), lax.axis_size("img")
-    inside = pl.BlockSpec(memory_space=pltpu.VMEM)
-    return pl.pallas_call(
-        functools.partial(sum_kernel, count, crowd),
-        out_shape=[
-            jax.ShapeDtypeStruct(t.shape, bf16),
-            jax.ShapeDtypeStruct(g.shape, f32),
-            jax.ShapeDtypeStruct((count,) + z.shape, bf16),
-        ],
-        in_specs=[inside] * 3,
-        out_specs=[inside] * 3,
-        scratch_shapes=[
-            pltpu.VMEM((count - 1,) + t.shape[1:], bf16),
-            pltpu.VMEM((count - 1,) + g.shape[1:], f32),
-            pltpu.VMEM((crowd,) + t.shape[1:], bf16),
-            pltpu.VMEM((crowd,) + g.shape[1:], f32),
-            DMA,
-            DMA((3, count - 1)),
-            DMA((3, count - 1)),
-            DMA((2, crowd - 1)),
-            DMA((2, crowd - 1)),
-            DMA((2, count - 1)),
-            DMA((2, count - 1)),
-        ],
-        compiler_params=pltpu.CompilerParams(
-            collective_id=collective_id, has_side_effects=True, vmem_limit_bytes=24 * 2**20
-        ),
-    )(t, g, z)
+def share_rows(channels, count):
+    channels = -(-channels // 16) * 16
+    return -(-(-(-channels // count)) // 8) * 8
 
 
 def gelu_parts(z):
@@ -1012,13 +1101,14 @@
     gain_ref,
     in_gain_ref,
     w_ref,
+    late_up,
+    late_down,
     out_ref,
     xs_ref,
     gs_ref,
     back_ref,
     row_ref,
     gain_out,
-    in_gain_out,
     wv,
     one,
     two,
@@ -1035,7 +1125,14 @@
     cot,
     final,
     mean,
+    own_v,
+    own_sem,
     w_sem,
+    ring_own,
+    ring_send,
+    ring_recv,
+    hand_send,
+    hand_recv,
     kv_send,
     kv_recv,
     gkv_send,
@@ -1047,7 +1144,7 @@
     out_send,
     out_recv,
 ):
-    rows, width = own_ref.shape
+    rows, width = one.shape
     depth = width // count
     owners = Owners(count, images)
     sharers = owners.sharers
@@ -1066,9 +1163,76 @@
     def load(k):
         return pltpu.make_async_copy(w_ref.at[k], wv.at[k], w_sem.at[k])
 
-    for k in range(8):
+    early, late_refs = w_ref.shape[0], (late_up, late_down)
+    late = len(late_refs)
+    own_copy = pltpu.make_async_copy(
+        own_ref.at[pl.ds(pl.multiple_of(slot * rows, 16), rows)], own_v, own_sem
+    )
+    own_copy.start()
+    for k in range(early):
         load(k).start()
     greet(plane(count))
+
+    core = lax.rem(group, 2)
+    ring = ring_place(count)
+    sides = ((group, ring_device(ring + 1, count)), (group, ring_device(ring - 1, count)))
+    other = (group + 1 - 2 * core, me)
+
+    reach = count // 2
+
+    def spot(k, stage, way, last, source=False):
+        begin = (core * 2 + way) * (width // 4) if last else core * (width // 2)
+        some = pl.ds(pl.multiple_of(begin, 128), width // 4 if last else width // 2)
+        if source:
+            return late_refs[k].at[:, some]
+        origin = ring_device(ring - stage if way == 0 else ring + stage, count)
+        here = pl.ds(pl.multiple_of(origin * depth, depth), depth)
+        return wv.at[early + k, here, some]
+
+    def hop(k, stage, way, start=False, last=False):
+        return pltpu.make_async_remote_copy(
+            spot(k, stage, way, last, start),
+            spot(k, stage, way, last),
+            ring_send.at[stage, way, k],
+            ring_recv.at[stage, way, k],
+            device_id=sides[way],
+            device_id_type=MESH,
+        )
+
+    def hand(k, stage, way, last=False):
+        return pltpu.make_async_remote_copy(
+            spot(k, stage, way, last),
+            spot(k, stage, way, last),
+            hand_send.at[stage - 1, way, k],
+            hand_recv.at[stage - 1, way, k],
+            device_id=other,
+            device_id_type=MESH,
+        )
+
+    def ring_keep(k):
+        here = pl.ds(pl.multiple_of(me * depth, depth), depth)
+        return pltpu.make_async_copy(late_refs[k], wv.at[early + k, here], ring_own.at[k])
+
+    for k in range(late):
+        for way in range(2):
+            hop(k, 0, way, True, reach == 1).start()
+        ring_keep(k).start()
+
+    def relays(first, end):
+        for stage in range(first, min(end, reach + 1)):
+            for k in range(late):
+                for way in range(2):
+                    last = stage == reach
+                    hop(k, stage - 1, way, last=last).wait_recv()
+                    if stage < reach:
+                        hop(k, stage, way, last=stage == reach - 1).start()
+                    hand(k, stage, way, last).start()
+
+    def arrived(k):
+        ring_keep(k).wait()
+        for stage in range(1, reach + 1):
+            for way in range(2):
+                hand(k, stage, way, stage == reach).wait_recv()
 
     def cot_push(i):
         to = owners.device(group, i, me // per)
@@ -1098,8 +1262,8 @@
     def columns(j, wide=block):
         return pl.ds(pl.multiple_of(j * wide, wide), wide)
 
-    def over_columns(body):
-        pl.loop(0, blocks)(body)
+    def over_columns(body, times=blocks):
+        pl.loop(0, times)(body)
 
     def over_rows(body):
         @pl.loop(0, rows // row_block)
@@ -1153,41 +1317,49 @@
         mean_tall = jnp.concatenate(
             [mean_tall, jnp.zeros((tall - mean_tall.shape[0], rows), f32)], axis=0
         )
-    share_rows = -(-mean.shape[1] // count)
-    share_rows = -(-share_rows // 8) * 8
+    share = share_rows(mean.shape[1], count)
     place = lax.broadcasted_iota(jnp.int32, (rows_here, rows), 0)
     source_row = lax.broadcasted_iota(jnp.int32, (rows_here, rows), 1) + slot * rows
     for o in range(count):
         picks = jnp.where(place + o * rows_here == source_row, 1.0, 0.0)
-        piece = [picks, mean_tall[o * share_rows : (o + 1) * share_rows]]
-        if spare > share_rows:
-            piece.append(jnp.zeros((spare - share_rows, rows), f32))
+        piece = [picks, mean_tall[o * share : (o + 1) * share]]
+        if spare > share:
+            piece.append(jnp.zeros((spare - share, rows), f32))
         xs_ref[6, o * depth : (o + 1) * depth, :] = jnp.concatenate(piece, axis=0).astype(bf16)
 
     mean_low = mean[1].astype(bf16)
 
-    @over_columns
-    def _(j):
-        one[:, columns(j)] = own_ref[:, columns(j)] + mm_tn(mean_low, mix_ref[:, columns(j)])
+    def make_one(j):
+        one[:, columns(j)] = own_v[:, columns(j)].astype(f32) + mm_tn(mean_low, mix_ref[:, columns(j)])
+
+    own_copy.wait()
+    over_columns(make_one)
+
+    def ready(k):
+        if k < early:
+            load(k).wait()
+        else:
+            arrived(k - early)
 
     def feed(source, target, k, up, down, normed, x_hidden, keep):
         norm(source, k, normed)
-        load(up).wait()
-
-        @over_columns
-        def _(j):
+        ready(up)
+
+        def make_hidden(j):
             value = mm_nt(normed[...], wv[up, columns(j), :])
             pre[keep, :, columns(j)] = value
             hidden = gelu_parts(value)[0].astype(bf16)
             low[:, columns(j)] = hidden
             put_x(x_hidden, j, hidden)
 
-        load(down).wait()
-
-        @over_columns
-        def _(j):
+        over_columns(make_hidden)
+        ready(down)
+
+        def make_branch(j):
             value = source[:, columns(j)] + mm(low[...], wv[down, :, columns(j)])
             target[:, columns(j)] = value.astype(target.dtype)
+
+        over_columns(make_branch)
 
     def feed_back(source, k, up, down, branch, x_pre, keep):
         @over_columns
@@ -1204,23 +1376,19 @@
         norm_grad(source, k)
 
     feed(one, two, 0, up_one, down_one, gs_ref.at[4], 3, 0)
+    relays(1, 2)
 
     norm(two, 1, low)
-
-    def write_blocks(j, value):
-        put_x(0, j, value)
-
-    @over_columns
-    def _(j):
-        write_blocks(j, low[:, columns(j)])
 
     load(m_key).wait()
     load(m_value).wait()
 
-    @over_columns
-    def _(j):
+    def make_kv(j):
+        put_x(0, j, low[:, columns(j)])
         kv[0, slot, :, columns(j)] = mm(low[...], wv[m_key, :, columns(j)]).astype(bf16)
         kv[1, slot, :, columns(j)] = mm(low[...], wv[m_value, :, columns(j)]).astype(bf16)
+
+    over_columns(make_kv)
 
     def sharer(d):
         return owners.device(home, image, lax.rem(slot + d, sharers))
@@ -1246,8 +1414,7 @@
     for d in range(1, sharers):
         kv_push(d).wait_recv()
 
-    @pl.loop(0, HEADS)
-    def _(h):
+    def attend(h):
         c = columns(h, HEAD_DIM)
         k_all = kv[0, :, :, c].reshape(latents, HEAD_DIM)
         v_all = kv[1, :, :, c].reshape(latents, HEAD_DIM)
@@ -1257,16 +1424,22 @@
         probs[h] = p
         low[:, c] = mm(p.astype(bf16), v_all).astype(bf16)
 
+    relays(2, 3)
+    pl.loop(0, HEADS // 2)(attend)
+    relays(3, 4)
+    pl.loop(HEADS // 2, HEADS)(attend)
+
     @over_columns
     def _(j):
         put_x(1, j, low[:, columns(j)])
 
-    load(m_out).wait()
+    ready(m_out)
 
     @over_columns
     def _(j):
         three[:, columns(j)] = two[:, columns(j)] + mm(low[...], wv[m_out, :, columns(j)])
 
+    relays(4, reach + 1)
     feed(three, final, 2, up_two, down_two, gs_ref.at[6], 5, 1)
 
     def out_push(b):
@@ -1386,9 +1559,10 @@
     back = mm_nt(mix_ref[...], gs_ref[8])
     back_ref[...] = back.astype(bf16)
     row_ref[1:2, :] = jnp.sum(back * mean[1], axis=0, keepdims=True)
-    in_gain_out[...] = jnp.broadcast_to(
-        jnp.sum(back * mean[0], axis=1, keepdims=True), in_gain_out.shape
+    in_gain = jnp.broadcast_to(
+        jnp.sum(back * mean[0], axis=1, keepdims=True), (back.shape[0], 128)
     )
+    gain_out[3:4, : back.shape[0]] = in_gain.T[0:1, :]
 
     for i in range(images):
         to, copy = cot_push(i)
@@ -1400,6 +1574,12 @@
     for d in range(1, sharers):
         kv_push(d).wait_send()
         gkv_push(d).wait_send()
+    for k in range(late):
+        for stage in range(reach):
+            for way in range(2):
+                last = stage == reach - 1
+                hop(k, stage, way, stage == 0, last).wait_send()
+                hand(k, stage + 1, way, last).wait_send()
 
     def out_from(i):
         return pltpu.make_async_remote_copy(
@@ -1430,10 +1610,9 @@
             out_keep().wait()
 
 
-def latent_pass(parts, stats, own, cotangent, mix, gains, in_gain, whole, collective_id):
+def latent_pass(parts, stats, own, cotangent, mix, gains, in_gain, whole, late, rows, collective_id):
     count = lax.axis_size("pix")
     images, rows_here, width = cotangent.shape
-    rows = own.shape[0]
     channels = mix.shape[0]
     sharers = count // images
     per = count // sharers
@@ -1441,6 +1620,7 @@
     anywhere = pl.BlockSpec(memory_space=pl.ANY)
     whole_f32 = pltpu.VMEM((rows, width), f32)
     whole_low = pltpu.VMEM((rows, width), bf16)
+    ring = DMA((count // 2, 2, len(late)))
     shape = jax.ShapeDtypeStruct
     return pl.pallas_call(
         functools.partial(latent_kernel, count, images),
@@ -1451,10 +1631,9 @@
             shape((channels, rows), bf16),
             shape((8, rows), f32),
             shape((8, width), f32),
-            shape((channels, 128), f32),
         ],
-        in_specs=[inside, inside, inside, anywhere, inside, inside, inside, anywhere],
-        out_specs=[anywhere] + [inside] * 6,
+        in_specs=[inside] * 2 + [anywhere] * 2 + [inside] * 3 + [anywhere] * 3,
+        out_specs=[anywhere] + [inside] * 5,
         scratch_shapes=[
             pltpu.VMEM((8, width, width), bf16),
             whole_f32,
@@ -1472,7 +1651,14 @@
             pltpu.VMEM((per, rows_here, width), bf16),
             whole_low,
             pltpu.VMEM((2, channels, rows), f32),
-            DMA((8,)),
+            whole_low,
+            DMA,
+            DMA((whole.shape[0],)),
+            DMA((len(late),)),
+            ring,
+            ring,
+            ring,
+            ring,
             DMA((sharers,)),
             DMA((sharers,)),
             DMA((sharers,)),
@@ -1487,12 +1673,143 @@
         compiler_params=pltpu.CompilerParams(
             collective_id=collective_id, has_side_effects=True, vmem_limit_bytes=60 * 2**20
         ),
-    )(parts, stats, own, cotangent, mix, gains, in_gain, whole)
-
-
-def norm_back(resid, gain, grad):
-    _, back = jax.vjp(layer_norm, resid, gain)
-    return back(grad)
+    )(parts, stats, own, cotangent, mix, gains, in_gain, whole, *late)
+
+
+def tail_kernel(
+    count,
+    channels,
+    t_ref,
+    g_ref,
+    z_ref,
+    a_ref,
+    lat_ref,
+    qcols_ref,
+    ncols_ref,
+    wq_ref,
+    wk_ref,
+    wv_ref,
+    wco_ref,
+    gain_ref,
+    lat_gain_ref,
+    sum_ref,
+    lat_out,
+    lat_gain_out,
+    gains_out,
+    wq_out,
+    wk_out,
+    wv_out,
+    wco_out,
+    up_one_out,
+    up_two_out,
+    down_one_out,
+    down_two_out,
+    sq_out,
+    sk_out,
+    sv_out,
+    so_out,
+    z_v,
+    query_grad,
+    flow,
+):
+    me = lax.axis_index("pix")
+    width = wq_ref.shape[0]
+    depth = wco_ref.shape[0]
+    rows_here = lat_out.shape[0]
+    latents = lat_ref.shape[0]
+    across = t_ref.shape[1]
+    for k, to in (
+        (0, sq_out),
+        (1, sk_out),
+        (2, sv_out),
+        (3, so_out),
+        (5, down_one_out),
+        (7, down_two_out),
+    ):
+        to[...] = sum_ref[k]
+    t = t_ref[...].astype(f32)
+    tx = (t * (gain_ref[...] * width ** (-0.5))).astype(bf16)
+    for o in range(count):
+        gains_out[:, o * depth : (o + 1) * depth] = g_ref[o]
+    row = jnp.sum(a_ref[:, :across] * t, axis=0, keepdims=True)
+    gains_out[3:4, :across] += row
+    wk_out[...] = mm_tn(tx, qcols_ref[...])[:channels]
+
+    @pl.loop(0, width // 256)
+    def _(j):
+        columns = pl.ds(pl.multiple_of(j * 256, 256), 256)
+        query_grad[:, columns] = mm_nt(tx, wk_ref[columns, :across]).astype(bf16)
+
+    @pl.loop(0, width // 256)
+    def _(j):
+        columns = pl.ds(pl.multiple_of(j * 256, 256), 256)
+        wq_out[:, columns] = mm_tn(ncols_ref[...], query_grad[:, columns])
+        flow[:, columns] = mm_nt(query_grad[...], wq_ref[columns, :])
+
+    share = share_rows(channels, count)
+    half = width // 2
+    for o in range(count):
+        for h in range(2):
+            z_v[o * share : (o + 1) * share, h * half : (h + 1) * half] = z_ref[h, o, :share].astype(f32)
+    cross = z_v[...].astype(bf16)
+    wv_out[...] = mm_nt(cross, wco_ref[...])[:channels]
+    wco_out[...] = mm_tn(wv_ref[...], cross)
+
+    up_one_out[...] = sum_ref[4].T
+    up_two_out[...] = sum_ref[6].T
+    lat_gain_out[...] = jnp.zeros_like(lat_gain_out)
+
+    @pl.loop(0, count)
+    def _(o):
+        here = pl.ds(pl.multiple_of(o * rows_here, rows_here), rows_here)
+        rows = lat_ref[here, :].astype(f32)
+        average = jnp.mean(rows, axis=1, keepdims=True)
+        centred = rows - average
+        scale = lax.rsqrt(jnp.mean(centred * centred, axis=1, keepdims=True) + eps)
+        hat = centred * scale
+        given = flow[here, :]
+        lat_gain_out[...] += jnp.sum(given * hat, axis=0, keepdims=True)
+
+        @pl.when(o == me)
+        def _():
+            gained = given * lat_gain_ref[...]
+            along = jnp.mean(gained * hat, axis=1, keepdims=True)
+            moved = scale * (gained - jnp.mean(gained, axis=1, keepdims=True) - hat * along)
+            lat_out[...] = moved + sum_ref[8, :rows_here, :]
+
+
+def tail_pass(t, g, z, a, lat, qcols, ncols, wq, wk, wv, wco, gain, lat_gain, summed, channels):
+    count = z.shape[1]
+    _, depth, width = summed.shape
+    latents = lat.shape[0]
+    share = share_rows(channels, count)
+    inside = pl.BlockSpec(memory_space=pltpu.VMEM)
+    anywhere = pl.BlockSpec(memory_space=pl.ANY)
+    shape = lambda *dims: jax.ShapeDtypeStruct(dims, f32)
+    plain = shape(depth, width)
+    return pl.pallas_call(
+        functools.partial(tail_kernel, count, channels),
+        out_shape=[
+            shape(latents // count, width),
+            shape(1, width),
+            shape(8, width),
+            plain,
+            shape(channels, depth),
+            shape(channels, depth),
+            plain,
+            shape(width, depth),
+            shape(width, depth),
+        ]
+        + [plain] * 6,
+        in_specs=[inside] * 14,
+        out_specs=[inside] * 15,
+        scratch_shapes=[
+            pltpu.VMEM((count * share, width), f32),
+            pltpu.VMEM((latents, width), bf16),
+            pltpu.VMEM((latents, width), f32),
+        ],
+        compiler_params=pltpu.CompilerParams(vmem_limit_bytes=48 * 2**20),
+    )(t, g, z, a, lat, qcols, ncols, wq, wk, wv, wco, gain, lat_gain, summed)
 
 
 def local(
@@ -1525,27 +1842,16 @@
     latents = rows_here * count
     sharers = count // images
     rows_own = latents // sharers
-    slot = (me % (sharers // 2)) * 2 + lax.axis_index("img") % 2
     depth = w_query.shape[0]
     channels = gain_input.shape[0]
-    width_scale = width ** (-0.5)
     tall = -(-channels // 16) * 16
 
     side = -(-channels // 512) * 512
     key_t = jnp.pad(w_key.T, ((0, 0), (0, side - channels)))
-    value_out = lax.psum(mm(w_value, w_cross_out).astype(bf16), "pix")
-    shards = jnp.stack(
-        [
-            w_up_one.T,
-            w_down_one,
-            w_self_query,
-            w_self_key,
-            w_self_value,
-            w_self_out,
-            w_up_two.T,
-            w_down_two,
-        ]
-    )
+    value_pad = jnp.pad(w_value, ((0, tall - channels), (0, 0)))
+    value_out = lax.psum(mm(value_pad, w_cross_out).astype(bf16), "pix")
+    shards = [w_up_one.T, w_down_one, w_self_query, w_self_key, w_self_value, w_self_out]
+    late = [w_up_two.T, w_down_two]
 
     lines = pixels // SIDE
     u, sin_u, cos_u = angles(me * lines + lax.iota(jnp.int32, lines))
@@ -1586,7 +1892,8 @@
     values = jnp.concatenate(
         [scale[:, None], keep[:, None], jnp.zeros((images, 2, pixels), f32), own_values], axis=1
     )
-    gained = table * gain_input[None, :]
+    table = jnp.pad(table, ((0, 0), (0, side - channels)))
+    gained = table * jnp.pad(gain_input, (0, side - channels))[None, :]
     (
         latent_full,
         query_mat,
@@ -1601,89 +1908,85 @@
         stat_parts,
     ) = forward_pass(
         values,
-        jnp.pad(table.T, ((0, tall - channels), (0, 0))),
-        jnp.pad(gained, ((0, 0), (0, side - channels))),
+        table,
+        gained,
         gain_latent,
-        latent_array[None],
-        w_query[None],
-        key_t[None],
+        latent_array,
+        w_query,
+        key_t,
         shards,
+        tall,
         0,
     )
-    latent_float = latent_full.reshape(latents, width).astype(f32)
-    query_mat = query_mat.reshape(width, width)
-    key_mat = key_full.reshape(width, side)[:, :channels].T
-    score_mat = score_mat[:, :channels]
-    whole = whole.reshape(8, width, width)
-
-    own = lax.dynamic_slice_in_dim(latent_float, slot * rows_own, rows_own, 0)
-    latent_out, xs, gs, back_t, row_stats, gain_grads, in_gain = latent_pass(
+    latent_full = latent_full.reshape(latents, width)
+    whole = whole.reshape(-1, width, width)
+
+    latent_out, xs, gs, back_t, row_stats, gain_grads = latent_pass(
         raw_parts,
         stat_parts,
-        own,
+        latent_full,
         cotangent,
-        jnp.pad(value_out, ((0, tall - channels), (0, 0))),
+        value_out,
         jnp.stack([gain_mlp_one, gain_self, gain_mlp_two]),
         jnp.pad(gain_input, (0, tall - channels))[:, None],
         whole,
+        late,
+        rows_own,
         4,
     )
     across = -(-channels // 128) * 128
-    grad_raw, pixel_out, summed = backward_pass(
+    grad_raw, gain_sums, cross_sum, grad_pixels, summed = backward_pass(
         values,
-        jnp.pad(table, ((0, 0), (0, across - channels))),
-        jnp.pad(gained, ((0, 0), (0, tall - channels))),
+        table,
+        gained,
         at,
         a_low,
         back_t,
         row_stats,
+        gain_grads,
         xs,
         gs,
+        channels,
         2,
     )
-    moved = (pixel_out[:, 4:7] - pixel_out[:, 7:8] / channels) - (
-        (colours - average[:, None, :]) * scale[:, None, :]
-    ) * (pixel_out[:, 0:1] / channels)
-    grad_pixels = moved * (scale * keep)[:, None, :]
-
-    cells = -(-(3 * width + channels) // (count * 1024)) * 1024
-    loose = jnp.concatenate([gain_grads[:3].reshape(-1), in_gain[:channels, 0]])
-    loose = jnp.pad(loose, (0, count * cells - loose.shape[0])).reshape(count, 8, cells // 8)
-    share_rows = -(-(-(-tall // count)) // 8) * 8
-    rest = summed[8]
-    spare = -(-share_rows // 16) * 16
-    cross_rows = jnp.pad(
-        rest[rows_here : rows_here + share_rows].astype(bf16), ((0, spare - share_rows), (0, 0))
+
+    share = share_rows(channels, count)
+    (
+        grad_latent_array,
+        gain_latent_sum,
+        gain_sums,
+        grad_w_query,
+        grad_w_key,
+        grad_w_value,
+        grad_w_cross_out,
+        g_up_one,
+        g_up_two,
+        g_down_one,
+        g_down_two,
+        g_sq,
+        g_sk,
+        g_sv,
+        g_so,
+    ) = tail_pass(
+        grad_raw.reshape(latents, across),
+        gain_sums,
+        cross_sum,
+        score_mat,
+        latent_full,
+        lax.dynamic_slice_in_dim(queries, me * depth, depth, 1),
+        lax.dynamic_slice_in_dim(latent_normed, me * depth, depth, 1),
+        query_mat.reshape(width, width),
+        key_full.reshape(width, side),
+        jnp.pad(w_value, ((0, share * count - channels), (0, 0))),
+        w_cross_out,
+        jnp.pad(gain_input, (0, across - channels))[None],
+        gain_latent[None],
+        summed,
+        channels,
     )
-    grad_raw, loose, cross_sum = small_sums(
-        grad_raw.reshape(count, rows_here, across),
-        loose,
-        cross_rows,
-        6,
-    )
-    grad_raw = grad_raw.reshape(latents, across)[:, :channels].astype(f32)
-    loose = loose.reshape(-1)
-    gain_one, gain_attn, gain_two = [loose[k * width : (k + 1) * width] for k in range(3)]
-    gain_in = loose[3 * width : 3 * width + channels] + jnp.sum(score_mat * grad_raw, axis=0)
-    cross_sum = cross_sum[:, :share_rows].reshape(-1, width)[:channels]
-
-    grad_x = (grad_raw * (gain_input * width_scale)[None, :]).astype(bf16)
-    query_grad = mm(grad_x, key_mat).astype(bf16)
-    latent_cols = lax.dynamic_slice_in_dim(latent_normed, me * depth, depth, 1)
-    grad_w_query = mm_tn(latent_cols, query_grad)
-    grad_latent_full, grad_gain_latent = norm_back(
-        latent_float, gain_latent, mm_nt(query_grad, query_mat)
-    )
-    grad_latent_own = lax.dynamic_slice_in_dim(grad_latent_full, me * rows_here, rows_here, 0)
-    key_cols = w_key.shape[1]
-    grad_w_key = mm_tn(grad_x, lax.dynamic_slice_in_dim(queries, me * key_cols, key_cols, 1))
-
-    g_sq, g_sk, g_sv, g_so, g_up_one, g_down_one, g_up_two, g_down_two, rest = [
-        summed[k] for k in range(9)
-    ]
-    grad_w_value = mm_nt(cross_sum, w_cross_out)
-    grad_w_cross_out = mm_tn(w_value, cross_sum)
-    grad_latent_array = rest[:rows_here] + grad_latent_own
+    gain_one, gain_attn, gain_two = gain_sums[0], gain_sums[1], gain_sums[2]
+    gain_in = gain_sums[3, :channels]
+    grad_gain_latent = gain_latent_sum[0]
     return (
         latent_out,
         grad_pixels,
@@ -1695,7 +1998,7 @@
         grad_w_value,
         grad_w_cross_out,
         gain_one,
-        g_up_one.T,
+        g_up_one,
         g_down_one,
         gain_attn,
         g_sq,
@@ -1703,7 +2006,7 @@
         g_sv,
         g_so,
         gain_two,
-        g_up_two.T,
+        g_up_two,
         g_down_two,
     )
 

time: 462 us -> 410 us (0.89)
  Pallas kernels: 388 us -> 364 us
  local copies, waits for them, and re-layouts: 32.9 us -> 20.8 us
  matrix products: 10.9 us -> 2.19 us
  other arithmetic: 13.6 us -> 7.56 us
    pallas_call x2, Pallas kernels: 190 us -> 144 us  [the longest x1 132 us: forward_pass(): pl.pallas_call(functools.partial(forward_kernel, count, images, tile, mat...]
    pallas_call x1, Pallas kernels: 54.4 us -> 69.1 us  [latent_pass(): pl.pallas_call(functools.partial(latent_kernel, count, images), out_shape...]
    dot_general x5 -> x0, matrix products: 8.22 us -> none  [the longest x3 5.09 us: mm_tn(): lax.dot_general(left, right, (((0,), (0,)), ((), ())), preferred_element_...]
    pallas_call x1, Pallas kernels: 144 us -> 151 us  [backward_pass(): pl.pallas_call(functools.partial(backward_kernel, count, teams, images, t...]
    pad x6 -> x4, local copies, waits for them, and re-layouts: 6.24 us -> 1.4 us  [the longest x1 0.69 us: local(): gained = table * jnp.pad(gain_input, (0, side - channels))[None, :]]
    unnamed x92 -> x69, local copies, waits for them, and re-layouts: 15.9 us -> 12.9 us
  transfers between devices with their start and end apart: 1 -> 1, of which waited for: 0 -> 0; matrix products, arithmetic and copies ran while one was open for 5% -> 4% of each run, Pallas kernels for 33% -> 32%
where the time goes in v5:
time: 410 us
  Pallas kernels  364 us (89%)
  local copies, waits for them, and re-layouts  20.8 us (5%)
  between operations  14.6 us (4%)
  other arithmetic  7.56 us (2%)
    pallas_call x1, Pallas kernels, backward_pass(): pl.pallas_call(functools.partial(backward_kernel, count, teams, images, t...  151 us
    pallas_call x1, Pallas kernels, forward_pass(): pl.pallas_call(functools.partial(forward_kernel, count, images, tile, mat...  132 us
    pallas_call x1, Pallas kernels, latent_pass(): pl.pallas_call(functools.partial(latent_kernel, count, images), out_shape...  69.1 us
    unnamed x69, local copies, waits for them, and re-layouts  12.9 us
    pallas_call x1, Pallas kernels, tail_pass(): pl.pallas_call(functools.partial(tail_kernel, count, channels), out_shape...  12.1 us
  transfers between devices with their start and end apart: 1, of which 0 were waited for; matrix products, arithmetic and copies ran while one was open for 4% of the time, Pallas kernels for 32%

profile of v5, /device:TPU:0, one launch (start us, length us, event | category | flops | bytes accessed | tf_op | source)
XLA Modules:
  0.0 409.5 jit_solution(4805377771022578260)
XLA Ops:
  7.3 2.2 convolution_convert_fusion
  9.5 1.5 multiply_reduce_fusion
  11.0 1.0 copy_convert_fusion
  12.1 0.7 pad.29
  12.8 0.7 pad.32
  13.5 0.7 pad.34
  14.4 0.6 add_reduce_fusion.1
  15.5 1.0 add_rsqrt_fusion.1
  16.5 0.7 broadcast_in_dim.52
  18.4 0.8 copy.63
  19.3 0.8 broadcast_in_dim.62.in_gain_ref
  21.0 1.4 pad_maximum_fusion.v_ref
  22.8 1.1 copy-done.11
  23.9 0.9 copy-done.12
  24.8 0.9 copy-done.13
  25.8 0.9 copy-done.14
  26.8 0.9 copy-done.15
  27.7 0.9 copy-done.18
  28.6 131.8 %shard_map.356 = (bf16[1,8,64,1024]{3,2,1,0:T(8,128)(2,1)}, bf16[1,8,128,1024]{3,2,1,0:T(8,128)(2,1)}, bf16[1,8,128,512]{3,2,1,0:T(8,128)(2,1)}, bf16[6,8,128,10...) custom-call(f32[4,8,6272]{2,1,0:T(8,128)S(1)} %pad_maximum_fusion.v_, ...), custom_call_target="tpu_custom_call" | custom-call | tf_op jit(solution)/shard_map/pallas_call | solution.py:453
  160.5 0.7 copy-done.17
  161.2 0.6 copy-done.19
  161.8 0.7 pad_maximum_fusion.1.gain_ref
  162.5 0.9 constant_dynamic-slice_fusion.ncols_ref
  163.4 0.9 constant_dynamic-slice_fusion.1.qcols_ref
  164.4 69.1 %shard_map.357 = (bf16[4,64,1024]{2,1,0:T(8,128)(2,1)}, bf16[7,1024,256]{2,1,0:T(8,128)(2,1)}, bf16[9,256,1024]{2,1,0:T(8,128)(2,1)}, bf16[272,256]{1,0:T(8,128)...) custom-call(bf16[8,272,256]{2,1,0:T(8,128)(2,1)} %get-tuple-element.57.part_ref, f32[8,8,256]{2,1,0:T(8,128)} %copy-done.19, ...), custom_call_target="tpu_custom_call" | custom-call | tf_op jit(solution)/shard_map/pallas_call | solution.py:1625
  233.5 151.3 %shard_map.358 = (bf16[8,64,384]{2,1,0:T(8,128)(2,1)}, f32[8,8,128]{2,1,0:T(8,128)}, bf16[2,8,48,512]{3,2,1,0:T(8,128)(2,1)}, f32[4,3,6272]{2,1,0:T(4,128)}, f32[9,128,1024]{2,1,0:T(8,128)}) custom-call(f32[4,8,6272]{2,1,0:T(8,128)} %copy-done.1, s32[256,896]{1,0:T(8,128)} %copy-done, f32[256,512]{1,0:T(8,128)} %copy-done.3, f32[256,512]{1,0:T(8,128)} %copy-done.2, ...), custom_call_target="tpu_custom_call" | custom-call | tf_op jit(solution)/shard_map/pallas_call | solution.py:987
  384.9 1.1 copy-done.8
  386.0 1.0 copy-done.9
  387.0 0.8 copy-done.20
  387.8 12.1 %shard_map.359 = (f32[64,1024]{1,0:T(8,128)}, f32[1,1024]{1,0:T(1,128)}, f32[8,1024]{1,0:T(8,128)S(1)}, f32[128,1024]{1,0:T(8,128)}, f32[261,128]{1,0:T(8,128)},...) custom-call(bf16[512,384]{1,0:T(8,128)(2,1)S(1)} %bitcast.24, ...), custom_call_target="tpu_custom_call" | custom-call | tf_op jit(solution)/shard_map/pallas_call | solution.py:1790
  401.1 0.8 copy.65
  401.9 0.8 copy.78
  (99 shorter events, 4.5 us)
Async XLA Ops:
  7.2 11.1 %copy-start.24 = (bf16[261,128]{1,0:T(8,128)(2,1)S(1)}, bf16[261,128]{1,0:T(8,128)(2,1)}, u32[]{:S(2)}) copy-start(bf16[261,128]{1,0:T(8,128)(2,1)} %param.28) | copy-start | bytes 200452
  7.2 9.3 %copy-start.27 = (s32[4,6272]{1,0:T(4,128)S(1)}, s32[4,6272]{1,0:T(4,128)}, u32[]{:S(2)}) copy-start(s32[4,6272]{1,0:T(4,128)} %param.22) | copy-start | bytes 301060
  7.2 10.8 %copy-start.25 = (bf16[1024,128]{1,0:T(8,128)(2,1)S(1)}, bf16[1024,128]{1,0:T(8,128)(2,1)}, u32[]{:S(2)}) copy-start(bf16[1024,128]{1,0:T(8,128)(2,1)} %param.31) | copy-start | bytes 786436
  7.2 11.0 %copy-start.28 = (bf16[261,128]{1,0:T(8,128)(2,1)S(1)}, bf16[261,128]{1,0:T(8,128)(2,1)}, u32[]{:S(2)}) copy-start(bf16[261,128]{1,0:T(8,128)(2,1)} %param.27) | copy-start | bytes 200452
  7.2 11.2 %copy-start.26 = (bf16[1024,128]{1,0:T(8,128)(2,1)S(1)}, bf16[1024,128]{1,0:T(8,128)(2,1)}, u32[]{:S(2)}) copy-start(bf16[1024,128]{1,0:T(8,128)(2,1)} %param.39) | copy-start | bytes 786436
  7.2 157.1 %all-reduce.9.cloned.1.call-start = ((), (), s32[]{:S(2)}) async-start(), calls=%async_computation | async-start | bytes 1114112 | tf_op jit(solution)/shard_map/psum | solution.py:1852
  19.2 3.5 copy-start.10
  19.2 3.5 copy-start.21
  20.7 139.8 %copy-start.2 = (f32[256,512]{1,0:T(8,128)}, f32[256,512]{1,0:T(8,128)S(1)}, u32[]{:S(2)}) copy-start(f32[256,512]{1,0:T(8,128)S(1)} %get-tuple-element.160.gained_ref) | copy-start | bytes 1572868
  20.7 139.8 %copy-start.3 = (f32[256,512]{1,0:T(8,128)}, f32[256,512]{1,0:T(8,128)S(1)}, u32[]{:S(2)}) copy-start(f32[256,512]{1,0:T(8,128)S(1)} %get-tuple-element.161.table_ref) | copy-start | bytes 1572868
  20.9 140.9 %copy-start.29 = (f32[1024]{0:T(1024)S(1)}, f32[1024]{0:T(1024)}, u32[]{:S(2)}) copy-start(f32[1024]{0:T(1024)} %param.38) | copy-start | bytes 12292
  20.9 140.9 %copy-start.30 = (f32[1024]{0:T(1024)S(1)}, f32[1024]{0:T(1024)}, u32[]{:S(2)}) copy-start(f32[1024]{0:T(1024)} %param.33) | copy-start | bytes 12292
  20.9 140.8 %copy-start.31 = (f32[1024]{0:T(1024)S(1)}, f32[1024]{0:T(1024)}, u32[]{:S(2)}) copy-start(f32[1024]{0:T(1024)} %param.30) | copy-start | bytes 12292
  22.3 211.1 %copy-start.1 = (f32[4,8,6272]{2,1,0:T(8,128)}, f32[4,8,6272]{2,1,0:T(8,128)S(1)}, u32[]{:S(2)}) copy-start(f32[4,8,6272]{2,1,0:T(8,128)S(1)} %pad_maximum_fusion.v_ref) | copy-start | bytes 2408452
  22.7 210.8 %copy-start = (s32[256,896]{1,0:T(8,128)}, s32[256,896]{1,0:T(8,128)S(1)}, u32[]{:S(2)}) copy-start(s32[256,896]{1,0:T(8,128)S(1)} %select_select_fusion.code_ref) | copy-start | bytes 2752516
  22.7 1.2 copy-start.11
  23.9 1.0 copy-start.12
  24.8 1.0 copy-start.13
  25.8 1.0 copy-start.14
  26.7 0.9 copy-start.15
  27.7 0.9 copy-start.18
  160.4 0.7 copy-start.17
  161.8 1.6 copy-start.16
  233.5 151.4 %copy-start.4 = (bf16[1,8,64,1024]{3,2,1,0:T(8,128)(2,1)S(1)}, bf16[1,8,64,1024]{3,2,1,0:T(8,128)(2,1)}, u32[]{:S(2)}) copy-start(bf16[1,8,64,1024]{3,2,1,0:T(8,128)(2,1)} %get-tuple-element.59) | copy-start | bytes 3145732
  233.5 151.4 %copy-start.5 = (bf16[1,8,128,512]{3,2,1,0:T(8,128)(2,1)S(1)}, bf16[1,8,128,512]{3,2,1,0:T(8,128)(2,1)}, u32[]{:S(2)}) copy-start(bf16[1,8,128,512]{3,2,1,0:T(8,128)(2,1)} %get-tuple-element.77) | copy-start | bytes 3145732
  233.5 151.4 %copy-start.6 = (f32[512,512]{1,0:T(8,128)S(1)}, f32[512,512]{1,0:T(8,128)}, u32[]{:S(2)}) copy-start(f32[512,512]{1,0:T(8,128)} %get-tuple-element.73.a_ref) | copy-start | bytes 3145732
  233.5 151.4 %copy-start.7 = (bf16[128,1024]{1,0:T(8,128)(2,1)S(1)}, bf16[128,1024]{1,0:T(8,128)(2,1)}, u32[]{:S(2)}) copy-start(bf16[128,1024]{1,0:T(8,128)(2,1)} %wco_ref.1) | copy-start | bytes 786436
  384.9 1.1 copy-start.8
  386.0 1.0 copy-start.9
  387.0 0.8 copy-start.20
  387.8 13.3 %copy-start.23 = (f32[4,3,6272]{2,1,0:T(4,128)S(1)}, f32[4,3,6272]{2,1,0:T(4,128)}, u32[]{:S(2)}) copy-start(f32[4,3,6272]{2,1,0:T(4,128)} %get-tuple-element.135) | copy-start | bytes 903172
  387.8 14.1 %copy-start.22 = (bf16[4,64,1024]{2,1,0:T(8,128)(2,1)S(1)}, bf16[4,64,1024]{2,1,0:T(8,128)(2,1)}, u32[]{:S(2)}) copy-start(bf16[4,64,1024]{2,1,0:T(8,128)(2,1)} %get-tuple-element.203) | copy-start | bytes 1572868
  (1 other events, 0.6 us)
Sparse Core Ops, SparseCore 0:
  11.5 78.6 all-reduce.8

commit v6 on v5

--- a/solution.py
+++ b/solution.py
@@ -95,6 +95,7 @@
 
 def forward_kernel(
     count,
+    teams,
     images,
     tile,
     mats,
@@ -106,11 +107,14 @@
     lat_ref,
     wq_ref,
     wk_ref,
+    wv_ref,
+    wco_ref,
     *refs,
 ):
     shards = refs[:mats]
     forward_body(
         count,
+        teams,
         images,
         tile,
         v_ref,
@@ -121,6 +125,8 @@
         lat_ref,
         wq_ref,
         wk_ref,
+        wv_ref,
+        wco_ref,
         shards,
         *refs[mats:],
     )
@@ -128,6 +134,7 @@
 
 def forward_body(
     count,
+    teams,
     images,
     tile,
     v_ref,
@@ -138,6 +145,8 @@
     lat_ref,
     wq_ref,
     wk_ref,
+    wv_ref,
+    wco_ref,
     shards,
     lat_full,
     wq_full,
@@ -148,8 +157,11 @@
     a_ref,
     at_ref,
     alow_ref,
+    mix_ref,
     part_ref,
     stat_ref,
+    mix_raw,
+    mix_in,
     acc,
     top,
     u_send,
@@ -159,6 +171,11 @@
     recv_sem,
     hand_send,
     hand_recv,
+    mix_send,
+    mix_recv,
+    mix_hand,
+    x_send,
+    x_recv,
     u_own,
     u_out,
     u_in,
@@ -176,7 +193,9 @@
     place = ring_place(count)
     sides = ((group, ring_device(place + 1, count)), (group, ring_device(place - 1, count)))
     other = (group + 1 - 2 * core, me)
-    greet(plane(count))
+    team = group // 2
+    partners = [(lax.rem(team + d, teams) * 2 + core, me) for d in range(1, teams)]
+    greet(plane(count) + partners)
     sources = (lat_ref, wq_ref, wk_ref)
     fulls = (lat_full, wq_full, wk_full, w_full)
     mats = len(shards)
@@ -236,6 +255,58 @@
         for way in range(2):
             hop(a, k, 0, way, True, reach == 1).start()
 
+    alone = 2
+
+    def at_home(k):
+        return (k < alone) | (lax.rem(jnp.int32(k), teams) == team)
+
+    def over_x(k, stage, way, d, last=False):
+        part = spot(3, k, stage, way, last)
+        return pltpu.make_async_remote_copy(
+            part,
+            part,
+            x_send.at[d, stage - 1, way, k],
+            x_recv.at[stage - 1, way, k],
+            device_id=partners[d],
+            device_id_type=MESH,
+        )
+
+    def pass_x(k, stage, last=False):
+        @pl.when(k >= alone)
+        def _():
+            for way in range(2):
+                for d in range(teams - 1):
+                    over_x(k, stage, way, d, last).start()
+
+    def take_x(k, stage, last=False):
+        for way in range(2):
+            over_x(k, stage, way, 0, last).wait_recv()
+            hand(3, k, stage, way, last).start()
+
+    def relay_weight(k, stage):
+        home = at_home(k)
+
+        @pl.when(home)
+        def _():
+            relay(3, k, stage)
+            pass_x(k, stage)
+
+        @pl.when(jnp.logical_not(home) & (stage > 1))
+        def _():
+            take_x(k, stage - 1)
+
+    def relay_weight_end(k):
+        home = at_home(k)
+
+        @pl.when(home)
+        def _():
+            relay_end(3, k)
+            pass_x(k, reach, True)
+
+        @pl.when(jnp.logical_not(home))
+        def _():
+            take_x(k, reach - 1)
+
     def sent(a, k):
         for way in range(2):
             for stage in range(reach):
@@ -253,6 +324,48 @@
     ]
     for a in range(3):
         start_ring(a, 0)
+    others = peers(count)
+    used = -(-part_ref.shape[1] // mix_raw.shape[1])
+
+    def mix_copy(source, target, stage, index, device):
+        return pltpu.make_async_remote_copy(
+            source,
+            target,
+            mix_send.at[stage, index],
+            mix_recv.at[stage, index],
+            device_id=device,
+            device_id_type=MESH,
+        )
+
+    def mix_scatter(d):
+        return mix_copy(mix_raw.at[others[d][1]], mix_in.at[d], 0, d, others[d])
+
+    def mix_gather(d):
+        return mix_copy(mix_ref.at[core, me], mix_ref.at[core, me], 1, d, others[d])
+
+    def mix_from(d):
+        source = lax.rem(me + count - 1 - d, count)
+        return source, mix_copy(mix_ref.at[core, source], mix_ref.at[core, source], 1, d, others[d])
+
+    def mix_pass():
+        return pltpu.make_async_remote_copy(
+            mix_ref.at[core],
+            mix_ref.at[core],
+            mix_hand.at[0],
+            mix_hand.at[1],
+            device_id=other,
+            device_id_type=MESH,
+        )
+
+    half = width // 2
+    columns = pl.ds(pl.multiple_of(core * half, 128), half)
+    mix_raw[...] = mm(wv_ref[...], wco_ref[:, columns]).astype(bf16).reshape(mix_raw.shape)
+    for d in range(count - 1):
+
+        @pl.when(others[d][1] < used)
+        def _():
+            mix_scatter(d).start()
+
     for a in range(3):
         fulls[a][0, me] = sources[a][...]
     for copy in own:
@@ -265,11 +378,31 @@
             else:
                 relay_end(a, 0)
         for k in range((stage - 1) * each, min(stage * each, mats)):
-            start_ring(3, k)
+
+            @pl.when(at_home(k))
+            def _():
+                start_ring(3, k)
+
+
+    @pl.when(me < used)
+    def _():
+        total = mix_raw[me].astype(f32)
+        for d in range(count - 1):
+            mix_scatter(d).wait_recv()
+            total = total + mix_in[d].astype(f32)
+        mix_ref[core, me] = total.astype(bf16)
+        for d in range(count - 1):
+            mix_gather(d).start()
+
     for a in range(3):
         handed(a, 0)
 
     rows_here = lat_ref.shape[0]
+    relays = (reach - 1) * mats
+    early = min(relays, width // 256)
+
+    def relay_number(e):
+        relay_weight(lax.rem(e, mats), 1 + e // mats)
 
     @pl.loop(0, count)
     def _(o):
@@ -282,6 +415,10 @@
 
     @pl.loop(0, width // 256)
     def _(j):
+        @pl.when(j < early)
+        def _():
+            relay_number(j)
+
         columns = pl.ds(pl.multiple_of(j * 256, 256), 256)
         weight = wq_full[0, :, :, columns].reshape(width, 256)
         query_ref[:, columns] = mm(normed_ref[...], weight).astype(bf16)
@@ -302,11 +439,6 @@
 
     table_t = table_ref[...].T[: part_ref.shape[1], :]
 
-    relays = (reach - 1) * mats
-
-    def relay_number(e):
-        relay(3, lax.rem(e, mats), 1 + e // mats)
-
     def u_push(i, h):
         to = owners.device(group, i, jnp.int32(h))
         sems = lambda which: dict(
@@ -331,9 +463,9 @@
     def _(t):
         i, step = t // steps, lax.rem(t, steps)
 
-        @pl.when(t < relays)
-        def _():
-            relay_number(t)
+        @pl.when(t + early < relays)
+        def _():
+            relay_number(t + early)
 
         @pl.when(step == 0)
         def _():
@@ -379,23 +511,65 @@
                     for copy in u_keep():
                         copy.start()
 
-    if images * steps < relays:
-
-        @pl.loop(images * steps, relays)
+    if images * steps + early < relays:
+
+        @pl.loop(images * steps + early, relays)
         def _(e):
             relay_number(e)
 
-    @pl.loop(0, mats)
+    for d in range(count - 1):
+        source, copy = mix_from(d)
+
+        @pl.when(source < used)
+        def _():
+            copy.wait_recv()
+
+    for o in range(used, count):
+        mix_ref[core, o] = jnp.zeros_like(mix_raw[0])
+    mix_pass().start()
+
+    pl.loop(0, mats)(relay_weight_end)
+
+    @pl.loop(alone, mats)
     def _(k):
-        relay_end(3, k)
+        @pl.when(jnp.logical_not(at_home(k)))
+        def _():
+            take_x(k, reach, True)
 
     for copy in own:
         copy.wait()
+    mix_pass().wait()
+    for d in range(count - 1):
+
+        @pl.when(others[d][1] < used)
+        def _():
+            mix_scatter(d).wait_send()
+
+        @pl.when(me < used)
+        def _():
+            mix_gather(d).wait_send()
+
     for a in range(3):
         sent(a, 0)
 
     for k in range(mats):
-        sent(3, k)
+        home = at_home(k)
+
+        @pl.when(home)
+        def _():
+            sent(3, k)
+            if k >= alone:
+                for stage in range(1, reach + 1):
+                    for way in range(2):
+                        for d in range(teams - 1):
+                            over_x(k, stage, way, d, stage == reach).wait_send()
+
+        @pl.when(jnp.logical_not(home))
+        def _():
+            for way in range(2):
+                for stage in range(1, reach + 1):
+                    hand(3, k, stage, way, stage == reach).wait_send()
+
         handed(3, k)
 
     def u_from(source):
@@ -433,7 +607,9 @@
                 copy.wait_recv()
 
 
-def forward_pass(values, table, gained, gain_latent, lat, wq, wk, shards, tall, collective_id):
+def forward_pass(
+    values, table, gained, gain_latent, lat, wq, wk, wv, wco, shards, tall, collective_id
+):
     count = lax.axis_size("pix")
     images, _, pixels = values.shape
     tile = pixel_tile(pixels)
@@ -451,7 +627,7 @@
 
     ring = DMA((count // 2, 2, 3 + mats))
     return pl.pallas_call(
-        functools.partial(forward_kernel, count, images, tile, mats),
+        functools.partial(forward_kernel, count, lax.axis_size("img") // 2, images, tile, mats),
         out_shape=[full(lat), full(wq), full(wk), full(shards[0], mats)]
         + [
             shape((latents, width), bf16),
@@ -459,12 +635,15 @@
             shape((latents, wk.shape[1]), f32),
             shape((CHANNELS, latents), bf16),
             shape((latents, CHANNELS), bf16),
+            shape((2, count, wv.shape[0] // count, width // 2), bf16),
             shape((count, tall, rows), bf16),
             shape((count, 8, rows), f32),
         ],
-        in_specs=[inside] * (8 + mats),
-        out_specs=[inside] * 3 + [anywhere] + [inside] * 5 + [anywhere] * 2,
+        in_specs=[inside] * (10 + mats),
+        out_specs=[inside] * 3 + [anywhere] + [inside] * 6 + [anywhere] * 2,
         scratch_shapes=[
+            pltpu.VMEM((count, wv.shape[0] // count, width // 2), bf16),
+            pltpu.VMEM((count - 1, wv.shape[0] // count, width // 2), bf16),
             pltpu.VMEM((CHANNELS + 16, latents), f32),
             pltpu.VMEM((8, latents), f32),
             pltpu.VMEM((images, sharers, tall, rows), bf16),
@@ -474,6 +653,11 @@
             ring,
             ring,
             ring,
+            DMA((2, count - 1)),
+            DMA((2, count - 1)),
+            DMA((2,)),
+            DMA((max(lax.axis_size("img") // 2 - 1, 1), count // 2, 2, mats)),
+            DMA((count // 2, 2, mats)),
             DMA((2,)),
             DMA((2, count)),
             DMA((2, count)),
@@ -481,7 +665,7 @@
         compiler_params=pltpu.CompilerParams(
             collective_id=collective_id, has_side_effects=True, vmem_limit_bytes=48 * 2**20
         ),
-    )(values, hot_codes(tile), table, gained, gain_latent[None], lat, wq, wk, *shards)
+    )(values, hot_codes(tile), table, gained, gain_latent[None], lat, wq, wk, wv, wco, *shards)
 
 
 def backward_kernel(
@@ -537,6 +721,7 @@
     hand_recv,
     back_send,
     back_recv,
+    pass_send,
     sum_send,
     sum_recv,
     img_send,
@@ -620,7 +805,7 @@
     own_index = owners.image * sharers + owners.slot
 
     def back_push(d):
-        to = (owners.home, lax.rem(me + d, count))
+        to = (owners.home, lax.rem(me + 2 * d, count))
         sems = lambda which: dict(
             send_sem=back_send.at[which, d],
             recv_sem=back_recv.at[which, own_index],
@@ -644,7 +829,24 @@
             pltpu.make_async_remote_copy(row_ref, row_all.at[source], **sems(1)),
         )
 
-    for d in range(count):
+    def back_hand(block):
+        to = (group, me + 1 - 2 * lax.rem(me, 2))
+        sems = lambda which: dict(
+            send_sem=pass_send.at[which, block],
+            recv_sem=back_recv.at[which, block],
+            device_id=to,
+            device_id_type=MESH,
+        )
+        return (
+            pltpu.make_async_remote_copy(back_all.at[block], back_all.at[block], **sems(0)),
+            pltpu.make_async_remote_copy(row_all.at[block], row_all.at[block], **sems(1)),
+        )
+
+    def back_owner(image, slot):
+        sender = owners.device(group, image, slot)
+        return sender, lax.rem(sender[1], 2) == lax.rem(me, 2)
+
+    for d in range(count // 2):
         to, copies = back_push(d)
 
         @pl.when(jnp.logical_not(owners.is_me(to)))
@@ -755,6 +957,19 @@
         for way in range(2):
             hop(k, 0, way, True).start()
 
+    for block in range(count):
+        sender, direct = back_owner(block // sharers, jnp.int32(block % sharers))
+
+        @pl.when(direct)
+        def _():
+            @pl.when(jnp.logical_not(owners.is_me(sender)))
+            def _():
+                for copy in back_from(block):
+                    copy.wait_recv()
+
+            for copy in back_hand(block):
+                copy.start()
+
     def relay(k, stage):
         for way in range(2):
             here = rows_of(owner_at(stage, way))
@@ -775,32 +990,95 @@
 
             hop(k, stage, way).start()
 
-    def relay_number(e):
-        relay(turn(lax.rem(e, number)), 1 + e // number)
-
-    relays = (reach - 1) * number
+    def finish(k):
+        columns = pl.ds(pl.multiple_of(core * half, 128), half)
+        return pltpu.make_async_copy(done.at[k], out_ref.at[k, :, columns], out_sem.at[k])
+
+    def hand(k):
+        columns = pl.ds(pl.multiple_of(core * half, 128), half)
+        return pltpu.make_async_remote_copy(
+            done.at[k],
+            out_ref.at[k, :, columns],
+            hand_send.at[k],
+            hand_recv.at[k],
+            device_id=other,
+            device_id_type=MESH,
+        )
+
+    def settle(k):
+        for way in range(2):
+            hop(k, reach - 1, way, reach == 1).wait_recv()
+        total = terms[k, rows_of(me), :].astype(f32)
+        for way in range(2):
+            total = total + held[k, way, reach - 1].astype(f32)
+        across[team, k] = total.astype(bf16)
+        for d in range(teams - 1):
+            cross(k, d).start()
+
+    span_k = 3 if number % 3 == 0 else number
+    groups = number // span_k
+    events = reach * number
+
+    def complete(k):
+        for d in range(teams - 1):
+            cross(k, d).wait_recv()
+        total = across[0, k].astype(f32)
+        for t in range(1, teams):
+            total = total + across[t, k].astype(f32)
+        done[k] = total
+        finish(k).start()
+        hand(k).start()
+
+        @pl.when(k == number - 1)
+        def _():
+            rows_here = t_raw.shape[1]
+            mine = done[number - 1, rows_here : rows_here + z_own.shape[0], :].astype(bf16)
+            z_own[...] = mine
+            z_out[core, me] = mine
+            for d in range(count - 1):
+                z_push(d).start()
+
+    def event(e):
+        block, k = e // span_k, lax.rem(e, span_k)
+        block = jnp.where(block == 0, 0, block + 1)
+        g, slot = block // reach, lax.rem(block, reach)
+        settles = (slot == 1) | (g == groups)
+
+        @pl.when(settles)
+        def _():
+            settle(turn((g - 1) * span_k + k))
+
+            @pl.when(g > 1)
+            def _():
+                complete(turn((g - 2) * span_k + k))
+
+        @pl.when(jnp.logical_not(settles))
+        def _():
+            relay(turn(g * span_k + k), jnp.maximum(slot, 1))
+
     tiles = images * steps
-    pace = min(-(-relays // tiles), 2)
+    paced = tiles * 5 // 8
+    middle = (paced + events) // 2
     t_acc[...] = jnp.zeros_like(t_acc)
 
     @pl.loop(0, tiles)
     def _(t):
         image = lax.rem(t // steps + owners.image, images)
         step = lax.rem(t, steps)
-        for e in range(pace):
-
-            @pl.when(t * pace + e < relays)
-            def _():
-                relay_number(t * pace + e)
+        e = t * 5 // 8
+
+        @pl.when((t + 1) * 5 // 8 > e)
+        def _():
+            event(e)
 
         @pl.when(step == 0)
         def _():
             for h in range(sharers):
                 source = image * sharers + h
 
-                sender = owners.device(group, image, jnp.int32(h))
-
-                @pl.when(jnp.logical_not(owners.is_me(sender)))
+                _, direct = back_owner(image, jnp.int32(h))
+
+                @pl.when(jnp.logical_not(direct))
                 def _():
                     for copy in back_from(source):
                         copy.wait_recv()
@@ -849,24 +1127,7 @@
         for copy in scatter(d):
             copy.start()
 
-    if tiles * pace < relays:
-
-        @pl.loop(tiles * pace, relays)
-        def _(e):
-            relay_number(e)
-
-    @pl.loop(0, number)
-    def _(k):
-        k = turn(k)
-        for way in range(2):
-            hop(k, reach - 1, way, reach == 1).wait_recv()
-        total = terms[k, rows_of(me), :].astype(f32)
-        for way in range(2):
-            total = total + held[k, way, reach - 1].astype(f32)
-        across[team, k] = total.astype(bf16)
-        for d in range(teams - 1):
-            cross(k, d).start()
-
+    pl.loop(paced, middle)(event)
     t_sum, g_sum = t_raw[me].astype(f32), g_raw[me]
     for d in range(count - 1):
         for copy in scatter(d):
@@ -879,41 +1140,11 @@
         for copy in over(d):
             copy.start()
 
-    def finish(k):
-        columns = pl.ds(pl.multiple_of(core * half, 128), half)
-        return pltpu.make_async_copy(done.at[k], out_ref.at[k, :, columns], out_sem.at[k])
-
-    def hand(k):
-        columns = pl.ds(pl.multiple_of(core * half, 128), half)
-        return pltpu.make_async_remote_copy(
-            done.at[k],
-            out_ref.at[k, :, columns],
-            hand_send.at[k],
-            hand_recv.at[k],
-            device_id=other,
-            device_id_type=MESH,
-        )
-
-    @pl.loop(0, number)
+    pl.loop(middle, events)(event)
+
+    @pl.loop((groups - 1) * span_k, number)
     def _(k):
-        k = turn(k)
-        for d in range(teams - 1):
-            cross(k, d).wait_recv()
-        total = across[0, k].astype(f32)
-        for t in range(1, teams):
-            total = total + across[t, k].astype(f32)
-        done[k] = total
-        finish(k).start()
-        hand(k).start()
-
-        @pl.when(k == number - 1)
-        def _():
-            rows_here = t_raw.shape[1]
-            mine = done[number - 1, rows_here : rows_here + z_own.shape[0], :].astype(bf16)
-            z_own[...] = mine
-            z_out[core, me] = mine
-            for d in range(count - 1):
-                z_push(d).start()
+        complete(turn(k))
 
     for d in range(crowd - 1):
         for copy in over(d):
@@ -955,12 +1186,20 @@
     def _(j):
         pair_x(j).wait_send()
 
-    for d in range(count):
+    for d in range(count // 2):
         to, copies = back_push(d)
 
         @pl.when(jnp.logical_not(owners.is_me(to)))
         def _():
             for copy in copies:
+                copy.wait_send()
+
+    for block in range(count):
+        _, direct = back_owner(block // sharers, jnp.int32(block % sharers))
+
+        @pl.when(direct)
+        def _():
+            for copy in back_hand(block):
                 copy.wait_send()
 
 
@@ -1025,6 +1264,7 @@
             DMA((number,)),
             DMA((number,)),
             DMA((number,)),
+            DMA((2, count)),
             DMA((2, count)),
             DMA((2, count)),
             DMA((2, count - 1)),
@@ -1330,7 +1570,10 @@
     mean_low = mean[1].astype(bf16)
 
     def make_one(j):
-        one[:, columns(j)] = own_v[:, columns(j)].astype(f32) + mm_tn(mean_low, mix_ref[:, columns(j)])
+        one[:, columns(j)] = own_v[:, columns(j)].astype(f32) + mm_tn(
+            mean_low,
+            mix_ref[j // (blocks // 2), : mean.shape[1], columns(lax.rem(j, blocks // 2))],
+        )
 
     own_copy.wait()
     over_columns(make_one)
@@ -1424,10 +1667,10 @@
         probs[h] = p
         low[:, c] = mm(p.astype(bf16), v_all).astype(bf16)
 
+    pl.loop(0, HEADS // 2)(attend)
     relays(2, 3)
-    pl.loop(0, HEADS // 2)(attend)
+    pl.loop(HEADS // 2, HEADS)(attend)
     relays(3, 4)
-    pl.loop(HEADS // 2, HEADS)(attend)
 
     @over_columns
     def _(j):
@@ -1556,7 +1799,9 @@
     gs_ref[5] = grad[...].astype(bf16)
     feed_back(one, 0, up_one, down_one, gs_ref.at[5], 2, 0)
     gs_ref[8] = grad[...].astype(bf16)
-    back = mm_nt(mix_ref[...], gs_ref[8])
+    half = width // 2
+    back = mm_nt(mix_ref[0, : mean.shape[1], :], gs_ref[8, :, :half])
+    back = back + mm_nt(mix_ref[1, : mean.shape[1], :], gs_ref[8, :, half:])
     back_ref[...] = back.astype(bf16)
     row_ref[1:2, :] = jnp.sum(back * mean[1], axis=0, keepdims=True)
     in_gain = jnp.broadcast_to(
@@ -1613,7 +1858,7 @@
 def latent_pass(parts, stats, own, cotangent, mix, gains, in_gain, whole, late, rows, collective_id):
     count = lax.axis_size("pix")
     images, rows_here, width = cotangent.shape
-    channels = mix.shape[0]
+    channels = parts.shape[1]
     sharers = count // images
     per = count // sharers
     inside = pl.BlockSpec(memory_space=pltpu.VMEM)
@@ -1848,8 +2093,8 @@
 
     side = -(-channels // 512) * 512
     key_t = jnp.pad(w_key.T, ((0, 0), (0, side - channels)))
-    value_pad = jnp.pad(w_value, ((0, tall - channels), (0, 0)))
-    value_out = lax.psum(mm(value_pad, w_cross_out).astype(bf16), "pix")
+    blocks = -(-tall // (16 * count)) * 16 * count
+    value_pad = jnp.pad(w_value, ((0, blocks - channels), (0, 0)))
     shards = [w_up_one.T, w_down_one, w_self_query, w_self_key, w_self_value, w_self_out]
     late = [w_up_two.T, w_down_two]
 
@@ -1904,6 +2149,7 @@
         score_mat,
         at,
         a_low,
+        value_out,
         raw_parts,
         stat_parts,
     ) = forward_pass(
@@ -1914,6 +2160,8 @@
         latent_array,
         w_query,
         key_t,
+        value_pad,
+        w_cross_out,
         shards,
         tall,
         0,
@@ -1926,7 +2174,7 @@
         stat_parts,
         latent_full,
         cotangent,
-        value_out,
+        value_out.reshape(2, blocks, width // 2),
         jnp.stack([gain_mlp_one, gain_self, gain_mlp_two]),
         jnp.pad(gain_input, (0, tall - channels))[:, None],
         whole,

time: 410 us -> 379 us (0.924)
  between operations: 14.6 us -> 1.24 us
  Pallas kernels: 364 us -> 351 us
    pallas_call x1, Pallas kernels: 132 us -> 121 us  [forward_pass(): pl.pallas_call(functools.partial(forward_kernel, count, lax.axis_size('im...]
    unnamed x69 -> x63, local copies, waits for them, and re-layouts: 12.9 us -> 13.6 us
  transfers between devices with their start and end apart: 1 -> 0, of which waited for: 0 -> 0; matrix products, arithmetic and copies ran while one was open for 4% -> 0% of each run, Pallas kernels for 32% -> 0%
where the time goes in v6:
time: 379 us; the launch traced here: 378 us
  Pallas kernels  351 us (93%)
  local copies, waits for them, and re-layouts  18.3 us (5%)
  other arithmetic  7.71 us (2%)
    pallas_call x1, Pallas kernels, backward_pass(): pl.pallas_call(functools.partial(backward_kernel, count, teams, images, t...  149 us
    pallas_call x1, Pallas kernels, forward_pass(): pl.pallas_call(functools.partial(forward_kernel, count, lax.axis_size('im...  121 us
    pallas_call x1, Pallas kernels, latent_pass(): pl.pallas_call(functools.partial(latent_kernel, count, images), out_shape...  68.6 us
    unnamed x63, local copies, waits for them, and re-layouts  13.6 us
    pallas_call x1, Pallas kernels, tail_pass(): pl.pallas_call(functools.partial(tail_kernel, count, channels), out_shape...  12.1 us

profile of v6, /device:TPU:0, one launch (start us, length us, event | category | flops | bytes accessed | tf_op | source)
XLA Modules:
  0.0 378.0 jit_solution(4414020633798202862)
XLA Ops:
  0.7 0.3 add_reduce_fusion.3
  1.0 0.6 add_reduce_fusion.1
  1.8 1.5 multiply_reduce_fusion
  3.5 0.3 add_rsqrt_fusion.1
  4.0 1.1 copy_convert_fusion
  5.3 0.9 convert_element_type.96
  6.4 0.3 pad_maximum_fusion.v_ref
  7.7 1.3 select_select_fusion.code_ref
  9.0 1.1 copy.62
  10.1 1.0 copy.61
  11.3 0.9 copy-done.13
  12.2 0.9 copy-done.14
  13.1 0.9 copy-done.15
  14.1 121.4 %shard_map.356 = (bf16[1,8,64,1024]{3,2,1,0:T(8,128)(2,1)}, bf16[1,8,128,1024]{3,2,1,0:T(8,128)(2,1)}, bf16[1,8,128,512]{3,2,1,0:T(8,128)(2,1)}, bf16[6,8,128,10...) custom-call(f32[4,8,6272]{2,1,0:T(8,128)S(1)} %pad_maximum_fusion.v_, ...), custom_call_target="tpu_custom_call" | custom-call | tf_op jit(solution)/shard_map/pallas_call | solution.py:629
  135.5 0.9 copy-done.7
  136.4 0.7 copy-done.16
  137.1 0.7 copy-done.17
  137.8 1.8 copy.63
  139.6 0.8 broadcast_in_dim.62.in_gain_ref
  140.4 0.6 pad_maximum_fusion.1.gain_ref
  141.0 68.6 %shard_map.357 = (bf16[4,64,1024]{2,1,0:T(8,128)(2,1)}, bf16[7,1024,256]{2,1,0:T(8,128)(2,1)}, bf16[9,256,1024]{2,1,0:T(8,128)(2,1)}, bf16[272,256]{1,0:T(8,128)...) custom-call(bf16[8,272,256]{2,1,0:T(8,128)(2,1)} %get-tuple-element.58.part_ref, f32[8,8,256]{2,1,0:T(8,128)} %copy-done.19, ...), custom_call_target="tpu_custom_call" | custom-call | tf_op jit(solution)/shard_map/pallas_call | solution.py:1870
  209.6 148.6 %shard_map.358 = (bf16[8,64,384]{2,1,0:T(8,128)(2,1)}, f32[8,8,128]{2,1,0:T(8,128)}, bf16[2,8,48,512]{3,2,1,0:T(8,128)(2,1)}, f32[4,3,6272]{2,1,0:T(4,128)}, f32[9,128,1024]{2,1,0:T(8,128)}) custom-call(f32[4,8,6272]{2,1,0:T(8,128)} %copy-done, s32[256,896]{1,0:T(8,128)} %select_select_fusion.code_ref, f32[256,512]{1,0:T(8,128)} %copy-done.2, ...), custom_call_target="tpu_custom_call" | custom-call | tf_op jit(solution)/shard_map/pallas_call | solution.py:1226
  358.3 0.9 constant_dynamic-slice_fusion.ncols_ref
  359.2 0.9 constant_dynamic-slice_fusion.1.qcols_ref
  360.2 1.1 copy-done.8
  361.3 1.0 copy-done.9
  362.3 0.8 copy-done.20
  363.1 12.1 %shard_map.359 = (f32[64,1024]{1,0:T(8,128)}, f32[1,1024]{1,0:T(1,128)}, f32[8,1024]{1,0:T(8,128)S(1)}, f32[128,1024]{1,0:T(8,128)}, f32[261,128]{1,0:T(8,128)},...) custom-call(bf16[512,384]{1,0:T(8,128)(2,1)S(1)} %bitcast.25, ...), custom_call_target="tpu_custom_call" | custom-call | tf_op jit(solution)/shard_map/pallas_call | solution.py:2035
  375.2 0.6 fusion.14
  375.8 0.6 slice_reduce_fusion
  376.4 0.8 copy.65
  377.2 0.8 copy.77
  (90 shorter events, 1.9 us)
Async XLA Ops:
  0.7 6.8 %copy-start.25 = (f32[261]{0:T(512)S(1)}, f32[261]{0:T(512)}, u32[]{:S(2)}) copy-start(f32[261]{0:T(512)} %param.24) | copy-start | bytes 3136
  3.8 7.4 %copy-start.24 = (bf16[261,128]{1,0:T(8,128)(2,1)S(1)}, bf16[261,128]{1,0:T(8,128)(2,1)}, u32[]{:S(2)}) copy-start(bf16[261,128]{1,0:T(8,128)(2,1)} %param.28) | copy-start | bytes 200452
  3.9 7.3 %copy-start.6 = (bf16[128,1024]{1,0:T(8,128)(2,1)S(1)}, bf16[128,1024]{1,0:T(8,128)(2,1)}, u32[]{:S(2)}) copy-start(bf16[128,1024]{1,0:T(8,128)(2,1)} %wco_ref.3) | copy-start | bytes 786436
  3.9 7.3 %copy-start.10 = (bf16[128,1024]{1,0:T(8,128)(2,1)S(1)}, bf16[128,1024]{1,0:T(8,128)(2,1)}, u32[]{:S(2)}) copy-start(bf16[128,1024]{1,0:T(8,128)(2,1)} %wq_ref.1) | copy-start | bytes 786436
  3.9 7.3 %copy-start.11 = (bf16[128,1024]{1,0:T(8,128)(2,1)S(1)}, bf16[128,1024]{1,0:T(8,128)(2,1)}, u32[]{:S(2)}) copy-start(bf16[128,1024]{1,0:T(8,128)(2,1)} %refs_1_.1) | copy-start | bytes 786436
  3.9 7.3 %copy-start.12 = (bf16[128,1024]{1,0:T(8,128)(2,1)S(1)}, bf16[128,1024]{1,0:T(8,128)(2,1)}, u32[]{:S(2)}) copy-start(bf16[128,1024]{1,0:T(8,128)(2,1)} %refs_2_.1) | copy-start | bytes 786436
  3.9 7.3 %copy-start.18 = (bf16[64,1024]{1,0:T(8,128)(2,1)S(1)}, bf16[64,1024]{1,0:T(8,128)(2,1)}, u32[]{:S(2)}) copy-start(bf16[64,1024]{1,0:T(8,128)(2,1)} %lat_ref.1) | copy-start | bytes 393220
  3.9 7.3 %copy-start.21 = (f32[1024]{0:T(1024)S(1)}, f32[1024]{0:T(1024)}, u32[]{:S(2)}) copy-start(f32[1024]{0:T(1024)} %param.25) | copy-start | bytes 12292
  6.6 128.8 %copy-start = (f32[4,8,6272]{2,1,0:T(8,128)}, f32[4,8,6272]{2,1,0:T(8,128)S(1)}, u32[]{:S(2)}) copy-start(f32[4,8,6272]{2,1,0:T(8,128)S(1)} %pad_maximum_fusion.v_ref) | copy-start | bytes 2408452
  7.5 132.9 %copy-start.26 = (f32[1024]{0:T(1024)S(1)}, f32[1024]{0:T(1024)}, u32[]{:S(2)}) copy-start(f32[1024]{0:T(1024)} %param.38) | copy-start | bytes 12292
  7.5 132.9 %copy-start.27 = (f32[1024]{0:T(1024)S(1)}, f32[1024]{0:T(1024)}, u32[]{:S(2)}) copy-start(f32[1024]{0:T(1024)} %param.33) | copy-start | bytes 12292
  7.5 132.9 %copy-start.28 = (f32[1024]{0:T(1024)S(1)}, f32[1024]{0:T(1024)}, u32[]{:S(2)}) copy-start(f32[1024]{0:T(1024)} %param.30) | copy-start | bytes 12292
  7.6 202.0 %copy-start.1 = (f32[256,512]{1,0:T(8,128)}, f32[256,512]{1,0:T(8,128)S(1)}, u32[]{:S(2)}) copy-start(f32[256,512]{1,0:T(8,128)S(1)} %get-tuple-element.162.gained_ref) | copy-start | bytes 1572868
  7.6 202.0 %copy-start.2 = (f32[256,512]{1,0:T(8,128)}, f32[256,512]{1,0:T(8,128)S(1)}, u32[]{:S(2)}) copy-start(f32[256,512]{1,0:T(8,128)S(1)} %get-tuple-element.163.table_ref) | copy-start | bytes 1572868
  11.2 1.0 copy-start.13
  12.2 0.9 copy-start.14
  13.1 0.9 copy-start.15
  135.5 0.9 copy-start.7
  136.4 0.7 copy-start.16
  137.1 0.7 copy-start.17
  137.8 3.2 copy-start.19
  209.6 150.5 %copy-start.3 = (bf16[1,8,64,1024]{3,2,1,0:T(8,128)(2,1)S(1)}, bf16[1,8,64,1024]{3,2,1,0:T(8,128)(2,1)}, u32[]{:S(2)}) copy-start(bf16[1,8,64,1024]{3,2,1,0:T(8,128)(2,1)} %get-tuple-element.60) | copy-start | bytes 3145732
  209.6 150.5 %copy-start.4 = (bf16[1,8,128,512]{3,2,1,0:T(8,128)(2,1)S(1)}, bf16[1,8,128,512]{3,2,1,0:T(8,128)(2,1)}, u32[]{:S(2)}) copy-start(bf16[1,8,128,512]{3,2,1,0:T(8,128)(2,1)} %get-tuple-element.79) | copy-start | bytes 3145732
  209.6 150.5 %copy-start.5 = (f32[512,512]{1,0:T(8,128)S(1)}, f32[512,512]{1,0:T(8,128)}, u32[]{:S(2)}) copy-start(f32[512,512]{1,0:T(8,128)} %get-tuple-element.75.a_ref) | copy-start | bytes 3145732
  360.2 1.1 copy-start.8
  361.3 1.0 copy-start.9
  362.3 0.8 copy-start.20
  363.1 13.3 %copy-start.23 = (f32[4,3,6272]{2,1,0:T(4,128)S(1)}, f32[4,3,6272]{2,1,0:T(4,128)}, u32[]{:S(2)}) copy-start(f32[4,3,6272]{2,1,0:T(4,128)} %get-tuple-element.137) | copy-start | bytes 903172
  363.1 14.1 %copy-start.22 = (bf16[4,64,1024]{2,1,0:T(8,128)(2,1)S(1)}, bf16[4,64,1024]{2,1,0:T(8,128)(2,1)}, u32[]{:S(2)}) copy-start(bf16[4,64,1024]{2,1,0:T(8,128)(2,1)} %get-tuple-element.205) | copy-start | bytes 1572868

commit v7 on v6

--- a/solution.py
+++ b/solution.py
@@ -255,7 +255,7 @@
         for way in range(2):
             hop(a, k, 0, way, True, reach == 1).start()
 
-    alone = 2
+    alone = 0
 
     def at_home(k):
         return (k < alone) | (lax.rem(jnp.int32(k), teams) == team)
@@ -360,12 +360,6 @@
     half = width // 2
     columns = pl.ds(pl.multiple_of(core * half, 128), half)
     mix_raw[...] = mm(wv_ref[...], wco_ref[:, columns]).astype(bf16).reshape(mix_raw.shape)
-    for d in range(count - 1):
-
-        @pl.when(others[d][1] < used)
-        def _():
-            mix_scatter(d).start()
-
     for a in range(3):
         fulls[a][0, me] = sources[a][...]
     for copy in own:
@@ -384,6 +378,57 @@
                 start_ring(3, k)
 
 
+    for d in range(count - 1):
+
+        @pl.when(others[d][1] < used)
+        def _():
+            mix_scatter(d).start()
+
+    for a in range(3):
+        handed(a, 0)
+
+    rows_here = lat_ref.shape[0]
+    relays = (reach - 1) * mats
+    early = min(relays, width // 256)
+
+    def relay_number(e):
+        relay_weight(lax.rem(e, mats), 1 + e // mats)
+
+    @pl.loop(0, count)
+    def _(o):
+        block = lat_full[0, o].astype(f32)
+        average = jnp.mean(block, axis=1, keepdims=True)
+        centred = block - average
+        spread = jnp.mean(centred * centred, axis=1, keepdims=True)
+        normed = (centred * lax.rsqrt(spread + eps) * gain_ref[...]).astype(bf16)
+        normed_ref[pl.ds(pl.multiple_of(o * rows_here, rows_here), rows_here), :] = normed
+
+    @pl.loop(0, width // 256)
+    def _(j):
+        @pl.when(j < early)
+        def _():
+            relay_number(j)
+
+        columns = pl.ds(pl.multiple_of(j * 256, 256), 256)
+        weight = wq_full[0, :, :, columns].reshape(width, 256)
+        query_ref[:, columns] = mm(normed_ref[...], weight).astype(bf16)
+
+    a_ref[...] = mm(query_ref[...], wk_full[0].reshape(width, wk_ref.shape[1])) * (width ** (-0.5))
+
+    def exact_nt(left, right):
+        return lax.dot_general(
+            left,
+            right,
+            (((1,), (1,)), ((), ())),
+            precision=lax.Precision.HIGHEST,
+            preferred_element_type=f32,
+        )
+
+    at_ref[...] = (exact_nt(gained_ref[...], a_ref[...]) * LOG2E).astype(bf16)
+    alow_ref[...] = exact_nt(a_ref[...], gained_ref[...]).astype(bf16)
+
+    table_t = table_ref[...].T[: part_ref.shape[1], :]
+
     @pl.when(me < used)
     def _():
         total = mix_raw[me].astype(f32)
@@ -393,51 +438,6 @@
         mix_ref[core, me] = total.astype(bf16)
         for d in range(count - 1):
             mix_gather(d).start()
-
-    for a in range(3):
-        handed(a, 0)
-
-    rows_here = lat_ref.shape[0]
-    relays = (reach - 1) * mats
-    early = min(relays, width // 256)
-
-    def relay_number(e):
-        relay_weight(lax.rem(e, mats), 1 + e // mats)
-
-    @pl.loop(0, count)
-    def _(o):
-        block = lat_full[0, o].astype(f32)
-        average = jnp.mean(block, axis=1, keepdims=True)
-        centred = block - average
-        spread = jnp.mean(centred * centred, axis=1, keepdims=True)
-        normed = (centred * lax.rsqrt(spread + eps) * gain_ref[...]).astype(bf16)
-        normed_ref[pl.ds(pl.multiple_of(o * rows_here, rows_here), rows_here), :] = normed
-
-    @pl.loop(0, width // 256)
-    def _(j):
-        @pl.when(j < early)
-        def _():
-            relay_number(j)
-
-        columns = pl.ds(pl.multiple_of(j * 256, 256), 256)
-        weight = wq_full[0, :, :, columns].reshape(width, 256)
-        query_ref[:, columns] = mm(normed_ref[...], weight).astype(bf16)
-
-    a_ref[...] = mm(query_ref[...], wk_full[0].reshape(width, wk_ref.shape[1])) * (width ** (-0.5))
-
-    def exact_nt(left, right):
-        return lax.dot_general(
-            left,
-            right,
-            (((1,), (1,)), ((), ())),
-            precision=lax.Precision.HIGHEST,
-            preferred_element_type=f32,
-        )
-
-    at_ref[...] = (exact_nt(gained_ref[...], a_ref[...]) * LOG2E).astype(bf16)
-    alow_ref[...] = exact_nt(a_ref[...], gained_ref[...]).astype(bf16)
-
-    table_t = table_ref[...].T[: part_ref.shape[1], :]
 
     def u_push(i, h):
         to = owners.device(group, i, jnp.int32(h))
@@ -722,6 +722,8 @@
     back_send,
     back_recv,
     pass_send,
+    foreign_send,
+    foreign_recv,
     sum_send,
     sum_recv,
     img_send,
@@ -887,7 +889,31 @@
             device_id_type=MESH,
         )
 
-    order = [number - 1] + list(range(number - 1))
+    low, high = (4, 8) if number == 9 and count > 4 and 4 % teams == 0 else (0, 0)
+    if teams == 1:
+        low, high = 0, 0
+    reach = count // 2
+
+    def alone(k):
+        return (k >= low) & (k < high)
+
+    def at_home(k):
+        return jnp.logical_not(alone(k)) | (lax.rem(k, teams) == team)
+
+    def foreign(k, sender, way, stage):
+        slot = (k // teams) * teams + sender
+        rows_in = pl.ds((way * reach + stage) * depth, depth)
+        return pltpu.make_async_remote_copy(
+            terms.at[k, rows_in],
+            held.at[slot, way, stage],
+            foreign_send.at[way, stage, k],
+            foreign_recv.at[sender, way, stage, k],
+            device_id=(lax.rem(k, teams) * 2 + core, me),
+            device_id_type=MESH,
+        )
+
+    pieces = [(way, stage) for way in range(2) for stage in range(reach)]
+    order = [(i + low) % number for i in range(number)] if high else list(range(number))
     for k in order:
         j = max(k - (number - kinds), 0)
         if k == 0 or k > number - kinds:
@@ -898,8 +924,6 @@
 
     def turn(k):
         return lax.rem(k + number - 1, number)
-
-    reach = count // 2
 
     def owner_at(stage, way):
         ahead = reach - stage
@@ -938,8 +962,8 @@
         )
 
     @pl.loop(0, number)
-    def _(k):
-        k = turn(k)
+    def _(i):
+        k = lax.rem(i + low, number)
         j = jnp.maximum(k - (number - kinds), 0)
 
         @pl.when((k == 0) | (k > number - kinds))
@@ -954,8 +978,31 @@
             terms[k, piece, :] = (
                 mm(xv[j, 0, piece, :], gv[k, 0]) + mm(xv[j, 1, piece, :], gv[k, 1])
             ).astype(bf16)
-        for way in range(2):
-            hop(k, 0, way, True).start()
+
+        @pl.when(jnp.logical_not(alone(k)))
+        def _():
+            for way in range(2):
+                hop(k, 0, way, True).start()
+
+        @pl.when(jnp.logical_not(at_home(k)))
+        def _():
+            for way, stage in pieces:
+                foreign(k, team, way, stage).start()
+
+    def launch(k):
+        @pl.when(at_home(k))
+        def _():
+            for way, stage in pieces:
+                here = pl.ds((way * reach + stage) * depth, depth)
+                total = terms[k, here, :].astype(f32)
+                for d in range(1, teams):
+                    sender = lax.rem(team + d, teams)
+                    foreign(k, sender, way, stage).wait_recv()
+                    slot = (k // teams) * teams + sender
+                    total = total + held[slot, way, stage].astype(f32)
+                terms[k, here, :] = total.astype(bf16)
+            for way in range(2):
+                hop(k, 0, way, True).start()
 
     for block in range(count):
         sender, direct = back_owner(block // sharers, jnp.int32(block % sharers))
@@ -1019,13 +1066,36 @@
     groups = number // span_k
     events = reach * number
 
+    def cross_from(k, d):
+        return pltpu.make_async_remote_copy(
+            across.at[team, k],
+            across.at[team, k],
+            cross_send.at[0, k],
+            cross_recv.at[d, k],
+            device_id=partners[0] if teams > 1 else other,
+            device_id_type=MESH,
+        )
+
     def complete(k):
-        for d in range(teams - 1):
-            cross(k, d).wait_recv()
-        total = across[0, k].astype(f32)
-        for t in range(1, teams):
-            total = total + across[t, k].astype(f32)
-        done[k] = total
+        @pl.when(jnp.logical_not(alone(k)))
+        def _():
+            for d in range(teams - 1):
+                cross(k, d).wait_recv()
+            total = across[0, k].astype(f32)
+            for t in range(1, teams):
+                total = total + across[t, k].astype(f32)
+            done[k] = total
+
+        @pl.when(alone(k))
+        def _():
+            home = lax.rem(k, teams)
+
+            @pl.when(home != team)
+            def _():
+                cross_from(k, lax.rem(team + 2 * teams - home - 1, teams)).wait_recv()
+
+            done[k] = across[home, k].astype(f32)
+
         finish(k).start()
         hand(k).start()
 
@@ -1046,7 +1116,11 @@
 
         @pl.when(settles)
         def _():
-            settle(turn((g - 1) * span_k + k))
+            one = turn((g - 1) * span_k + k)
+
+            @pl.when(at_home(one))
+            def _():
+                settle(one)
 
             @pl.when(g > 1)
             def _():
@@ -1054,10 +1128,24 @@
 
         @pl.when(jnp.logical_not(settles))
         def _():
-            relay(turn(g * span_k + k), jnp.maximum(slot, 1))
+            one = turn(g * span_k + k)
+
+            @pl.when(at_home(one))
+            def _():
+                relay(one, jnp.maximum(slot, 1))
+
+            if high:
+
+                @pl.when((g == 0) & (slot == reach - 1) & (k == span_k - 1))
+                def _():
+                    launch(jnp.int32(low))
+
+                @pl.when((g == 1) & (slot == 2))
+                def _():
+                    launch(low + 1 + k)
 
     tiles = images * steps
-    paced = tiles * 5 // 8
+    paced = tiles
     middle = (paced + events) // 2
     t_acc[...] = jnp.zeros_like(t_acc)
 
@@ -1065,9 +1153,9 @@
     def _(t):
         image = lax.rem(t // steps + owners.image, images)
         step = lax.rem(t, steps)
-        e = t * 5 // 8
-
-        @pl.when((t + 1) * 5 // 8 > e)
+        e = t
+
+        @pl.when(t + 1 > e)
         def _():
             event(e)
 
@@ -1176,11 +1264,19 @@
         finish(k).wait()
         hand(k).wait()
         pair_g(k).wait_send()
-        for way in range(2):
-            for stage in range(reach):
-                hop(k, stage, way, stage == 0).wait_send()
-        for d in range(teams - 1):
-            cross(k, d).wait_send()
+
+        @pl.when(at_home(k))
+        def _():
+            for way in range(2):
+                for stage in range(reach):
+                    hop(k, stage, way, stage == 0).wait_send()
+            for d in range(teams - 1):
+                cross(k, d).wait_send()
+
+        @pl.when(jnp.logical_not(at_home(k)))
+        def _():
+            for way, stage in pieces:
+                foreign(k, team, way, stage).wait_send()
 
     @pl.loop(0, kinds)
     def _(j):
@@ -1267,6 +1363,8 @@
             DMA((2, count)),
             DMA((2, count)),
             DMA((2, count)),
+            DMA((2, count // 2, number)),
+            DMA((teams, 2, count // 2, number)),
             DMA((2, count - 1)),
             DMA((2, count - 1)),
             DMA((2, 2 * teams - 1)),

time: 379 us -> 355 us (0.937)
  Pallas kernels: 351 us -> 327 us
    pallas_call x1, Pallas kernels: 149 us -> 134 us  [backward_pass(): pl.pallas_call(functools.partial(backward_kernel, count, teams, images, t...]
    pallas_call x1, Pallas kernels: 121 us -> 112 us  [forward_pass(): pl.pallas_call(functools.partial(forward_kernel, count, lax.axis_size('im...]
where the time goes in v7:
time: 355 us; the launch traced here: 354 us
  Pallas kernels  327 us (92%)
  local copies, waits for them, and re-layouts  18.3 us (5%)
  other arithmetic  7.71 us (2%)
    pallas_call x1, Pallas kernels, backward_pass(): pl.pallas_call(functools.partial(backward_kernel, count, teams, images, t...  134 us
    pallas_call x1, Pallas kernels, forward_pass(): pl.pallas_call(functools.partial(forward_kernel, count, lax.axis_size('im...  112 us
    pallas_call x1, Pallas kernels, latent_pass(): pl.pallas_call(functools.partial(latent_kernel, count, images), out_shape...  68.9 us
    unnamed x63, local copies, waits for them, and re-layouts  13.6 us
    pallas_call x1, Pallas kernels, tail_pass(): pl.pallas_call(functools.partial(tail_kernel, count, channels), out_shape...  12.1 us

profile of v7, /device:TPU:0, one launch (start us, length us, event | category | flops | bytes accessed | tf_op | source)
XLA Modules:
  0.0 354.2 jit_solution(1285381938488272772)
XLA Ops:
  0.7 0.3 add_reduce_fusion.3
  1.0 0.6 add_reduce_fusion.1
  1.8 1.5 multiply_reduce_fusion
  3.5 0.3 add_rsqrt_fusion.1
  4.0 1.1 copy_convert_fusion
  5.3 0.9 convert_element_type.96
  6.4 0.3 pad_maximum_fusion.v_ref
  7.7 1.3 select_select_fusion.code_ref
  9.0 1.1 copy.62
  10.1 1.0 copy.61
  11.3 0.9 copy-done.13
  12.2 0.9 copy-done.14
  13.1 0.9 copy-done.15
  14.1 111.6 %shard_map.356 = (bf16[1,8,64,1024]{3,2,1,0:T(8,128)(2,1)}, bf16[1,8,128,1024]{3,2,1,0:T(8,128)(2,1)}, bf16[1,8,128,512]{3,2,1,0:T(8,128)(2,1)}, bf16[6,8,128,10...) custom-call(f32[4,8,6272]{2,1,0:T(8,128)S(1)} %pad_maximum_fusion.v_, ...), custom_call_target="tpu_custom_call" | custom-call | tf_op jit(solution)/shard_map/pallas_call | solution.py:629
  125.7 0.9 copy-done.7
  126.6 0.7 copy-done.16
  127.3 0.7 copy-done.17
  128.0 1.8 copy.63
  129.8 0.8 broadcast_in_dim.62.in_gain_ref
  130.6 0.6 pad_maximum_fusion.1.gain_ref
  131.2 68.9 %shard_map.357 = (bf16[4,64,1024]{2,1,0:T(8,128)(2,1)}, bf16[7,1024,256]{2,1,0:T(8,128)(2,1)}, bf16[9,256,1024]{2,1,0:T(8,128)(2,1)}, bf16[272,256]{1,0:T(8,128)...) custom-call(bf16[8,272,256]{2,1,0:T(8,128)(2,1)} %get-tuple-element.58.part_ref, f32[8,8,256]{2,1,0:T(8,128)} %copy-done.19, ...), custom_call_target="tpu_custom_call" | custom-call | tf_op jit(solution)/shard_map/pallas_call | solution.py:1968
  200.1 134.3 %shard_map.358 = (bf16[8,64,384]{2,1,0:T(8,128)(2,1)}, f32[8,8,128]{2,1,0:T(8,128)}, bf16[2,8,48,512]{3,2,1,0:T(8,128)(2,1)}, f32[4,3,6272]{2,1,0:T(4,128)}, f32[9,128,1024]{2,1,0:T(8,128)}) custom-call(f32[4,8,6272]{2,1,0:T(8,128)} %copy-done, s32[256,896]{1,0:T(8,128)} %select_select_fusion.code_ref, f32[256,512]{1,0:T(8,128)} %copy-done.2, ...), custom_call_target="tpu_custom_call" | custom-call | tf_op jit(solution)/shard_map/pallas_call | solution.py:1322
  334.4 0.9 constant_dynamic-slice_fusion.ncols_ref
  335.3 0.9 constant_dynamic-slice_fusion.1.qcols_ref
  336.3 1.1 copy-done.8
  337.5 1.0 copy-done.9
  338.5 0.8 copy-done.20
  339.2 12.1 %shard_map.359 = (f32[64,1024]{1,0:T(8,128)}, f32[1,1024]{1,0:T(1,128)}, f32[8,1024]{1,0:T(8,128)S(1)}, f32[128,1024]{1,0:T(8,128)}, f32[261,128]{1,0:T(8,128)},...) custom-call(bf16[512,384]{1,0:T(8,128)(2,1)S(1)} %bitcast.25, ...), custom_call_target="tpu_custom_call" | custom-call | tf_op jit(solution)/shard_map/pallas_call | solution.py:2133
  351.4 0.6 fusion.14
  352.0 0.6 slice_reduce_fusion
  352.6 0.8 copy.65
  353.4 0.8 copy.77
  (90 shorter events, 1.9 us)
Async XLA Ops:
  0.7 6.8 %copy-start.25 = (f32[261]{0:T(512)S(1)}, f32[261]{0:T(512)}, u32[]{:S(2)}) copy-start(f32[261]{0:T(512)} %param.24) | copy-start | bytes 3136
  3.8 7.4 %copy-start.24 = (bf16[261,128]{1,0:T(8,128)(2,1)S(1)}, bf16[261,128]{1,0:T(8,128)(2,1)}, u32[]{:S(2)}) copy-start(bf16[261,128]{1,0:T(8,128)(2,1)} %param.28) | copy-start | bytes 200452
  3.9 7.3 %copy-start.6 = (bf16[128,1024]{1,0:T(8,128)(2,1)S(1)}, bf16[128,1024]{1,0:T(8,128)(2,1)}, u32[]{:S(2)}) copy-start(bf16[128,1024]{1,0:T(8,128)(2,1)} %wco_ref.3) | copy-start | bytes 786436
  3.9 7.3 %copy-start.10 = (bf16[128,1024]{1,0:T(8,128)(2,1)S(1)}, bf16[128,1024]{1,0:T(8,128)(2,1)}, u32[]{:S(2)}) copy-start(bf16[128,1024]{1,0:T(8,128)(2,1)} %wq_ref.1) | copy-start | bytes 786436
  3.9 7.3 %copy-start.11 = (bf16[128,1024]{1,0:T(8,128)(2,1)S(1)}, bf16[128,1024]{1,0:T(8,128)(2,1)}, u32[]{:S(2)}) copy-start(bf16[128,1024]{1,0:T(8,128)(2,1)} %refs_1_.1) | copy-start | bytes 786436
  3.9 7.3 %copy-start.12 = (bf16[128,1024]{1,0:T(8,128)(2,1)S(1)}, bf16[128,1024]{1,0:T(8,128)(2,1)}, u32[]{:S(2)}) copy-start(bf16[128,1024]{1,0:T(8,128)(2,1)} %refs_2_.1) | copy-start | bytes 786436
  3.9 7.3 %copy-start.18 = (bf16[64,1024]{1,0:T(8,128)(2,1)S(1)}, bf16[64,1024]{1,0:T(8,128)(2,1)}, u32[]{:S(2)}) copy-start(bf16[64,1024]{1,0:T(8,128)(2,1)} %lat_ref.1) | copy-start | bytes 393220
  3.9 7.3 %copy-start.21 = (f32[1024]{0:T(1024)S(1)}, f32[1024]{0:T(1024)}, u32[]{:S(2)}) copy-start(f32[1024]{0:T(1024)} %param.25) | copy-start | bytes 12292
  6.6 119.1 %copy-start = (f32[4,8,6272]{2,1,0:T(8,128)}, f32[4,8,6272]{2,1,0:T(8,128)S(1)}, u32[]{:S(2)}) copy-start(f32[4,8,6272]{2,1,0:T(8,128)S(1)} %pad_maximum_fusion.v_ref) | copy-start | bytes 2408452
  7.5 123.2 %copy-start.26 = (f32[1024]{0:T(1024)S(1)}, f32[1024]{0:T(1024)}, u32[]{:S(2)}) copy-start(f32[1024]{0:T(1024)} %param.38) | copy-start | bytes 12292
  7.5 123.1 %copy-start.27 = (f32[1024]{0:T(1024)S(1)}, f32[1024]{0:T(1024)}, u32[]{:S(2)}) copy-start(f32[1024]{0:T(1024)} %param.33) | copy-start | bytes 12292
  7.5 123.1 %copy-start.28 = (f32[1024]{0:T(1024)S(1)}, f32[1024]{0:T(1024)}, u32[]{:S(2)}) copy-start(f32[1024]{0:T(1024)} %param.30) | copy-start | bytes 12292
  7.6 192.5 %copy-start.1 = (f32[256,512]{1,0:T(8,128)}, f32[256,512]{1,0:T(8,128)S(1)}, u32[]{:S(2)}) copy-start(f32[256,512]{1,0:T(8,128)S(1)} %get-tuple-element.162.gained_ref) | copy-start | bytes 1572868
  7.6 192.5 %copy-start.2 = (f32[256,512]{1,0:T(8,128)}, f32[256,512]{1,0:T(8,128)S(1)}, u32[]{:S(2)}) copy-start(f32[256,512]{1,0:T(8,128)S(1)} %get-tuple-element.163.table_ref) | copy-start | bytes 1572868
  11.2 1.0 copy-start.13
  12.2 0.9 copy-start.14
  13.1 0.9 copy-start.15
  125.7 0.9 copy-start.7
  126.6 0.7 copy-start.16
  127.3 0.7 copy-start.17
  128.0 3.2 copy-start.19
  200.1 136.2 %copy-start.3 = (bf16[1,8,64,1024]{3,2,1,0:T(8,128)(2,1)S(1)}, bf16[1,8,64,1024]{3,2,1,0:T(8,128)(2,1)}, u32[]{:S(2)}) copy-start(bf16[1,8,64,1024]{3,2,1,0:T(8,128)(2,1)} %get-tuple-element.60) | copy-start | bytes 3145732
  200.1 136.2 %copy-start.4 = (bf16[1,8,128,512]{3,2,1,0:T(8,128)(2,1)S(1)}, bf16[1,8,128,512]{3,2,1,0:T(8,128)(2,1)}, u32[]{:S(2)}) copy-start(bf16[1,8,128,512]{3,2,1,0:T(8,128)(2,1)} %get-tuple-element.79) | copy-start | bytes 3145732
  200.1 136.2 %copy-start.5 = (f32[512,512]{1,0:T(8,128)S(1)}, f32[512,512]{1,0:T(8,128)}, u32[]{:S(2)}) copy-start(f32[512,512]{1,0:T(8,128)} %get-tuple-element.75.a_ref) | copy-start | bytes 3145732
  336.3 1.1 copy-start.8
  337.5 1.0 copy-start.9
  338.5 0.8 copy-start.20
  339.2 13.3 %copy-start.23 = (f32[4,3,6272]{2,1,0:T(4,128)S(1)}, f32[4,3,6272]{2,1,0:T(4,128)}, u32[]{:S(2)}) copy-start(f32[4,3,6272]{2,1,0:T(4,128)} %get-tuple-element.137) | copy-start | bytes 903172
  339.2 14.1 %copy-start.22 = (bf16[4,64,1024]{2,1,0:T(8,128)(2,1)S(1)}, bf16[4,64,1024]{2,1,0:T(8,128)(2,1)}, u32[]{:S(2)}) copy-start(bf16[4,64,1024]{2,1,0:T(8,128)(2,1)} %get-tuple-element.205) | copy-start | bytes 1572868

commit v8 on v7

--- a/solution.py
+++ b/solution.py
@@ -255,7 +255,7 @@
         for way in range(2):
             hop(a, k, 0, way, True, reach == 1).start()
 
-    alone = 0
+    alone = 1
 
     def at_home(k):
         return (k < alone) | (lax.rem(jnp.int32(k), teams) == team)
@@ -1439,7 +1439,6 @@
     gain_ref,
     in_gain_ref,
     w_ref,
-    late_up,
     late_down,
     out_ref,
     xs_ref,
@@ -1501,7 +1500,7 @@
     def load(k):
         return pltpu.make_async_copy(w_ref.at[k], wv.at[k], w_sem.at[k])
 
-    early, late_refs = w_ref.shape[0], (late_up, late_down)
+    early, late_refs = w_ref.shape[0], (late_down,)
     late = len(late_refs)
     own_copy = pltpu.make_async_copy(
         own_ref.at[pl.ds(pl.multiple_of(slot * rows, 16), rows)], own_v, own_sem
@@ -1694,6 +1693,8 @@
             put_x(x_hidden, j, hidden)
 
         over_columns(make_hidden)
+        if down >= early:
+            relays(4, reach + 1)
         ready(down)
 
         def make_branch(j):
@@ -1780,7 +1781,6 @@
     def _(j):
         three[:, columns(j)] = two[:, columns(j)] + mm(low[...], wv[m_out, :, columns(j)])
 
-    relays(4, reach + 1)
     feed(three, final, 2, up_two, down_two, gs_ref.at[6], 5, 1)
 
     def out_push(b):
@@ -1975,7 +1975,7 @@
             shape((8, rows), f32),
             shape((8, width), f32),
         ],
-        in_specs=[inside] * 2 + [anywhere] * 2 + [inside] * 3 + [anywhere] * 3,
+        in_specs=[inside] * 2 + [anywhere] * 2 + [inside] * 3 + [anywhere] * 2,
         out_specs=[anywhere] + [inside] * 5,
         scratch_shapes=[
             pltpu.VMEM((8, width, width), bf16),
@@ -2193,8 +2193,16 @@
     key_t = jnp.pad(w_key.T, ((0, 0), (0, side - channels)))
     blocks = -(-tall // (16 * count)) * 16 * count
     value_pad = jnp.pad(w_value, ((0, blocks - channels), (0, 0)))
-    shards = [w_up_one.T, w_down_one, w_self_query, w_self_key, w_self_value, w_self_out]
-    late = [w_up_two.T, w_down_two]
+    shards = [
+        w_up_one.T,
+        w_down_one,
+        w_self_query,
+        w_self_key,
+        w_self_value,
+        w_self_out,
+        w_up_two.T,
+    ]
+    late = [w_down_two]
 
     lines = pixels // SIDE
     u, sin_u, cos_u = angles(me * lines + lax.iota(jnp.int32, lines))

time: 355 us -> 352 us (level)
    pallas_call x1, Pallas kernels: 68.9 us -> 60.2 us  [latent_pass(): pl.pallas_call(functools.partial(latent_kernel, count, images), out_shape...]
    pallas_call x1, Pallas kernels: 112 us -> 120 us  [forward_pass(): pl.pallas_call(functools.partial(forward_kernel, count, lax.axis_size('im...]
    unnamed x63 -> x67, local copies, waits for them, and re-layouts: 13.6 us -> 12 us
where the time goes in v8:
time: 352 us; the launch traced here: 351 us
  Pallas kernels  325 us (92%)
  local copies, waits for them, and re-layouts  16.7 us (5%)
  other arithmetic  7.63 us (2%)
    pallas_call x1, Pallas kernels, backward_pass(): pl.pallas_call(functools.partial(backward_kernel, count, teams, images, t...  133 us
    pallas_call x1, Pallas kernels, forward_pass(): pl.pallas_call(functools.partial(forward_kernel, count, lax.axis_size('im...  120 us
    pallas_call x1, Pallas kernels, latent_pass(): pl.pallas_call(functools.partial(latent_kernel, count, images), out_shape...  60.2 us
    pallas_call x1, Pallas kernels, tail_pass(): pl.pallas_call(functools.partial(tail_kernel, count, channels), out_shape...  12.1 us
    unnamed x67, local copies, waits for them, and re-layouts  12 us

profile of v8, /device:TPU:0, one launch (start us, length us, event | category | flops | bytes accessed | tf_op | source)
XLA Modules:
  0.0 350.9 jit_solution(6608653813234592056)
XLA Ops:
  0.7 0.3 add_reduce_fusion.3
  1.0 0.6 add_reduce_fusion.1
  1.8 1.5 multiply_reduce_fusion
  3.5 0.3 add_rsqrt_fusion.1
  3.9 1.0 copy_convert_fusion
  5.2 0.9 convert_element_type.96
  6.3 0.3 pad_maximum_fusion.v_ref
  6.9 0.2 concatenate.17
  7.7 1.3 select_select_fusion.code_ref
  9.1 1.1 copy.63
  10.5 0.9 copy-done.12
  11.4 0.9 copy-done.13
  12.4 0.9 copy-done.14
  13.3 0.9 copy-done.15
  14.3 119.7 %shard_map.356 = (bf16[1,8,64,1024]{3,2,1,0:T(8,128)(2,1)}, bf16[1,8,128,1024]{3,2,1,0:T(8,128)(2,1)}, bf16[1,8,128,512]{3,2,1,0:T(8,128)(2,1)}, bf16[7,8,128,10...) custom-call(f32[4,8,6272]{2,1,0:T(8,128)S(1)} %pad_maximum_fusion.v_, ...), custom_call_target="tpu_custom_call" | custom-call | tf_op jit(solution)/shard_map/pallas_call | solution.py:629
  134.0 0.9 copy-done.7
  134.8 0.7 copy-done.16
  135.5 0.7 copy-done.17
  136.2 0.8 broadcast_in_dim.62.in_gain_ref
  137.0 0.6 pad_maximum_fusion.1.gain_ref
  137.6 60.2 %shard_map.357 = (bf16[4,64,1024]{2,1,0:T(8,128)(2,1)}, bf16[7,1024,256]{2,1,0:T(8,128)(2,1)}, bf16[9,256,1024]{2,1,0:T(8,128)(2,1)}, bf16[272,256]{1,0:T(8,128)...) custom-call(bf16[8,272,256]{2,1,0:T(8,128)(2,1)} %get-tuple-element.58.part_ref, f32[8,8,256]{2,1,0:T(8,128)} %copy-done.19, ...), custom_call_target="tpu_custom_call" | custom-call | tf_op jit(solution)/shard_map/pallas_call | solution.py:1968
  197.9 133.2 %shard_map.358 = (bf16[8,64,384]{2,1,0:T(8,128)(2,1)}, f32[8,8,128]{2,1,0:T(8,128)}, bf16[2,8,48,512]{3,2,1,0:T(8,128)(2,1)}, f32[4,3,6272]{2,1,0:T(4,128)}, f32[9,128,1024]{2,1,0:T(8,128)}) custom-call(f32[4,8,6272]{2,1,0:T(8,128)} %copy-done, s32[256,896]{1,0:T(8,128)} %select_select_fusion.code_ref, f32[256,512]{1,0:T(8,128)} %copy-done.2, ...), custom_call_target="tpu_custom_call" | custom-call | tf_op jit(solution)/shard_map/pallas_call | solution.py:1322
  331.1 0.9 constant_dynamic-slice_fusion.ncols_ref
  332.0 0.9 constant_dynamic-slice_fusion.1.qcols_ref
  333.1 1.1 copy-done.8
  334.2 1.0 copy-done.9
  335.2 0.8 copy-done.20
  335.9 12.1 %shard_map.359 = (f32[64,1024]{1,0:T(8,128)}, f32[1,1024]{1,0:T(1,128)}, f32[8,1024]{1,0:T(8,128)S(1)}, f32[128,1024]{1,0:T(8,128)}, f32[261,128]{1,0:T(8,128)},...) custom-call(bf16[512,384]{1,0:T(8,128)(2,1)S(1)} %bitcast.26, ...), custom_call_target="tpu_custom_call" | custom-call | tf_op jit(solution)/shard_map/pallas_call | solution.py:2133
  348.1 0.6 fusion.14
  348.7 0.6 slice_reduce_fusion
  349.3 0.8 copy.65
  350.1 0.8 copy.77
  (94 shorter events, 1.9 us)
Async XLA Ops:
  0.7 6.7 %copy-start.27 = (f32[261]{0:T(512)S(1)}, f32[261]{0:T(512)}, u32[]{:S(2)}) copy-start(f32[261]{0:T(512)} %param.24) | copy-start | bytes 3136
  3.3 5.7 %copy-start.25 = (bf16[1024,128]{1,0:T(8,128)(2,1)S(1)}, bf16[1024,128]{1,0:T(8,128)(2,1)}, u32[]{:S(2)}) copy-start(bf16[1024,128]{1,0:T(8,128)(2,1)} %param.31) | copy-start | bytes 786436
  3.9 6.3 %copy-start.26 = (bf16[261,128]{1,0:T(8,128)(2,1)S(1)}, bf16[261,128]{1,0:T(8,128)(2,1)}, u32[]{:S(2)}) copy-start(bf16[261,128]{1,0:T(8,128)(2,1)} %param.27) | copy-start | bytes 200452
  3.9 6.5 %copy-start.24 = (bf16[261,128]{1,0:T(8,128)(2,1)S(1)}, bf16[261,128]{1,0:T(8,128)(2,1)}, u32[]{:S(2)}) copy-start(bf16[261,128]{1,0:T(8,128)(2,1)} %param.28) | copy-start | bytes 200452
  4.9 5.5 %copy-start.6 = (bf16[128,1024]{1,0:T(8,128)(2,1)S(1)}, bf16[128,1024]{1,0:T(8,128)(2,1)}, u32[]{:S(2)}) copy-start(bf16[128,1024]{1,0:T(8,128)(2,1)} %wco_ref.3) | copy-start | bytes 786436
  5.0 5.5 %copy-start.10 = (bf16[128,1024]{1,0:T(8,128)(2,1)S(1)}, bf16[128,1024]{1,0:T(8,128)(2,1)}, u32[]{:S(2)}) copy-start(bf16[128,1024]{1,0:T(8,128)(2,1)} %wq_ref.1) | copy-start | bytes 786436
  5.0 5.5 %copy-start.11 = (bf16[128,1024]{1,0:T(8,128)(2,1)S(1)}, bf16[128,1024]{1,0:T(8,128)(2,1)}, u32[]{:S(2)}) copy-start(bf16[128,1024]{1,0:T(8,128)(2,1)} %refs_1_.1) | copy-start | bytes 786436
  5.0 5.5 %copy-start.18 = (bf16[64,1024]{1,0:T(8,128)(2,1)S(1)}, bf16[64,1024]{1,0:T(8,128)(2,1)}, u32[]{:S(2)}) copy-start(bf16[64,1024]{1,0:T(8,128)(2,1)} %lat_ref.1) | copy-start | bytes 393220
  5.0 5.5 %copy-start.21 = (f32[1024]{0:T(1024)S(1)}, f32[1024]{0:T(1024)}, u32[]{:S(2)}) copy-start(f32[1024]{0:T(1024)} %param.25) | copy-start | bytes 12292
  6.6 127.3 %copy-start = (f32[4,8,6272]{2,1,0:T(8,128)}, f32[4,8,6272]{2,1,0:T(8,128)S(1)}, u32[]{:S(2)}) copy-start(f32[4,8,6272]{2,1,0:T(8,128)S(1)} %pad_maximum_fusion.v_ref) | copy-start | bytes 2408452
  7.4 129.6 %copy-start.28 = (f32[1024]{0:T(1024)S(1)}, f32[1024]{0:T(1024)}, u32[]{:S(2)}) copy-start(f32[1024]{0:T(1024)} %param.38) | copy-start | bytes 12292
  7.4 129.6 %copy-start.29 = (f32[1024]{0:T(1024)S(1)}, f32[1024]{0:T(1024)}, u32[]{:S(2)}) copy-start(f32[1024]{0:T(1024)} %param.33) | copy-start | bytes 12292
  7.4 129.6 %copy-start.30 = (f32[1024]{0:T(1024)S(1)}, f32[1024]{0:T(1024)}, u32[]{:S(2)}) copy-start(f32[1024]{0:T(1024)} %param.30) | copy-start | bytes 12292
  7.6 190.3 %copy-start.1 = (f32[256,512]{1,0:T(8,128)}, f32[256,512]{1,0:T(8,128)S(1)}, u32[]{:S(2)}) copy-start(f32[256,512]{1,0:T(8,128)S(1)} %get-tuple-element.162.gained_ref) | copy-start | bytes 1572868
  7.6 190.3 %copy-start.2 = (f32[256,512]{1,0:T(8,128)}, f32[256,512]{1,0:T(8,128)S(1)}, u32[]{:S(2)}) copy-start(f32[256,512]{1,0:T(8,128)S(1)} %get-tuple-element.163.table_ref) | copy-start | bytes 1572868
  10.5 1.0 copy-start.12
  11.4 0.9 copy-start.13
  12.4 0.9 copy-start.14
  13.3 0.9 copy-start.15
  134.0 0.9 copy-start.7
  134.8 0.7 copy-start.16
  135.5 0.7 copy-start.17
  136.2 1.4 copy-start.19
  197.9 135.1 %copy-start.3 = (bf16[1,8,64,1024]{3,2,1,0:T(8,128)(2,1)S(1)}, bf16[1,8,64,1024]{3,2,1,0:T(8,128)(2,1)}, u32[]{:S(2)}) copy-start(bf16[1,8,64,1024]{3,2,1,0:T(8,128)(2,1)} %get-tuple-element.60) | copy-start | bytes 3145732
  197.9 135.1 %copy-start.4 = (bf16[1,8,128,512]{3,2,1,0:T(8,128)(2,1)S(1)}, bf16[1,8,128,512]{3,2,1,0:T(8,128)(2,1)}, u32[]{:S(2)}) copy-start(bf16[1,8,128,512]{3,2,1,0:T(8,128)(2,1)} %get-tuple-element.79) | copy-start | bytes 3145732
  197.9 135.1 %copy-start.5 = (f32[512,512]{1,0:T(8,128)S(1)}, f32[512,512]{1,0:T(8,128)}, u32[]{:S(2)}) copy-start(f32[512,512]{1,0:T(8,128)} %get-tuple-element.75.a_ref) | copy-start | bytes 3145732
  333.0 1.1 copy-start.8
  334.2 1.0 copy-start.9
  335.2 0.8 copy-start.20
  335.9 13.3 %copy-start.23 = (f32[4,3,6272]{2,1,0:T(4,128)S(1)}, f32[4,3,6272]{2,1,0:T(4,128)}, u32[]{:S(2)}) copy-start(f32[4,3,6272]{2,1,0:T(4,128)} %get-tuple-element.137) | copy-start | bytes 903172
  335.9 14.1 %copy-start.22 = (bf16[4,64,1024]{2,1,0:T(8,128)(2,1)S(1)}, bf16[4,64,1024]{2,1,0:T(8,128)(2,1)}, u32[]{:S(2)}) copy-start(bf16[4,64,1024]{2,1,0:T(8,128)(2,1)} %get-tuple-element.205) | copy-start | bytes 1572868

commit v9 on v8

--- a/solution.py
+++ b/solution.py
@@ -389,7 +389,7 @@
 
     rows_here = lat_ref.shape[0]
     relays = (reach - 1) * mats
-    early = min(relays, width // 256)
+    early = min(relays, width // 256 + 3)
 
     def relay_number(e):
         relay_weight(lax.rem(e, mats), 1 + e // mats)
@@ -403,11 +403,13 @@
         normed = (centred * lax.rsqrt(spread + eps) * gain_ref[...]).astype(bf16)
         normed_ref[pl.ds(pl.multiple_of(o * rows_here, rows_here), rows_here), :] = normed
 
+    pl.loop(0, min(early, 3))(relay_number)
+
     @pl.loop(0, width // 256)
     def _(j):
-        @pl.when(j < early)
-        def _():
-            relay_number(j)
+        @pl.when(j + 3 < early)
+        def _():
+            relay_number(j + 3)
 
         columns = pl.ds(pl.multiple_of(j * 256, 256), 256)
         weight = wq_full[0, :, :, columns].reshape(width, 256)

time: 352 us -> 349 us (level)
    pallas_call x1, Pallas kernels: 120 us -> 113 us  [forward_pass(): pl.pallas_call(functools.partial(forward_kernel, count, lax.axis_size('im...]
where the time goes in v9:
time: 349 us; the launch traced here: 348 us
  Pallas kernels  322 us (92%)
  local copies, waits for them, and re-layouts  16.7 us (5%)
  other arithmetic  7.63 us (2%)
    pallas_call x1, Pallas kernels, backward_pass(): pl.pallas_call(functools.partial(backward_kernel, count, teams, images, t...  134 us
    pallas_call x1, Pallas kernels, forward_pass(): pl.pallas_call(functools.partial(forward_kernel, count, lax.axis_size('im...  113 us
    pallas_call x1, Pallas kernels, latent_pass(): pl.pallas_call(functools.partial(latent_kernel, count, images), out_shape...  63 us
    pallas_call x1, Pallas kernels, tail_pass(): pl.pallas_call(functools.partial(tail_kernel, count, channels), out_shape...  12.1 us
    unnamed x67, local copies, waits for them, and re-layouts  12 us

profile of v9, /device:TPU:0, one launch (start us, length us, event | category | flops | bytes accessed | tf_op | source)
XLA Modules:
  0.0 347.7 jit_solution(11588744322133944511)
XLA Ops:
  0.7 0.3 add_reduce_fusion.3
  1.0 0.6 add_reduce_fusion.1
  1.8 1.5 multiply_reduce_fusion
  3.5 0.3 add_rsqrt_fusion.1
  3.9 1.0 copy_convert_fusion
  5.2 0.9 convert_element_type.96
  6.3 0.3 pad_maximum_fusion.v_ref
  6.9 0.2 concatenate.17
  7.7 1.3 select_select_fusion.code_ref
  9.1 1.1 copy.63
  10.5 0.9 copy-done.12
  11.4 0.9 copy-done.13
  12.4 0.9 copy-done.14
  13.3 0.9 copy-done.15
  14.3 113.4 %shard_map.356 = (bf16[1,8,64,1024]{3,2,1,0:T(8,128)(2,1)}, bf16[1,8,128,1024]{3,2,1,0:T(8,128)(2,1)}, bf16[1,8,128,512]{3,2,1,0:T(8,128)(2,1)}, bf16[7,8,128,10...) custom-call(f32[4,8,6272]{2,1,0:T(8,128)S(1)} %pad_maximum_fusion.v_, ...), custom_call_target="tpu_custom_call" | custom-call | tf_op jit(solution)/shard_map/pallas_call | solution.py:631
  127.7 0.9 copy-done.7
  128.6 0.7 copy-done.16
  129.3 0.7 copy-done.17
  130.0 0.8 broadcast_in_dim.62.in_gain_ref
  130.8 0.6 pad_maximum_fusion.1.gain_ref
  131.4 63.0 %shard_map.357 = (bf16[4,64,1024]{2,1,0:T(8,128)(2,1)}, bf16[7,1024,256]{2,1,0:T(8,128)(2,1)}, bf16[9,256,1024]{2,1,0:T(8,128)(2,1)}, bf16[272,256]{1,0:T(8,128)...) custom-call(bf16[8,272,256]{2,1,0:T(8,128)(2,1)} %get-tuple-element.58.part_ref, f32[8,8,256]{2,1,0:T(8,128)} %copy-done.19, ...), custom_call_target="tpu_custom_call" | custom-call | tf_op jit(solution)/shard_map/pallas_call | solution.py:1970
  194.4 133.5 %shard_map.358 = (bf16[8,64,384]{2,1,0:T(8,128)(2,1)}, f32[8,8,128]{2,1,0:T(8,128)}, bf16[2,8,48,512]{3,2,1,0:T(8,128)(2,1)}, f32[4,3,6272]{2,1,0:T(4,128)}, f32[9,128,1024]{2,1,0:T(8,128)}) custom-call(f32[4,8,6272]{2,1,0:T(8,128)} %copy-done, s32[256,896]{1,0:T(8,128)} %select_select_fusion.code_ref, f32[256,512]{1,0:T(8,128)} %copy-done.2, ...), custom_call_target="tpu_custom_call" | custom-call | tf_op jit(solution)/shard_map/pallas_call | solution.py:1324
  328.0 0.9 constant_dynamic-slice_fusion.ncols_ref
  328.9 0.9 constant_dynamic-slice_fusion.1.qcols_ref
  329.9 1.1 copy-done.8
  331.0 1.0 copy-done.9
  332.0 0.8 copy-done.20
  332.8 12.1 %shard_map.359 = (f32[64,1024]{1,0:T(8,128)}, f32[1,1024]{1,0:T(1,128)}, f32[8,1024]{1,0:T(8,128)S(1)}, f32[128,1024]{1,0:T(8,128)}, f32[261,128]{1,0:T(8,128)},...) custom-call(bf16[512,384]{1,0:T(8,128)(2,1)S(1)} %bitcast.26, ...), custom_call_target="tpu_custom_call" | custom-call | tf_op jit(solution)/shard_map/pallas_call | solution.py:2135
  344.9 0.6 fusion.14
  345.5 0.6 slice_reduce_fusion
  346.1 0.8 copy.65
  346.9 0.8 copy.77
  (94 shorter events, 1.9 us)
Async XLA Ops:
  0.7 6.7 %copy-start.27 = (f32[261]{0:T(512)S(1)}, f32[261]{0:T(512)}, u32[]{:S(2)}) copy-start(f32[261]{0:T(512)} %param.24) | copy-start | bytes 3136
  3.3 5.7 %copy-start.25 = (bf16[1024,128]{1,0:T(8,128)(2,1)S(1)}, bf16[1024,128]{1,0:T(8,128)(2,1)}, u32[]{:S(2)}) copy-start(bf16[1024,128]{1,0:T(8,128)(2,1)} %param.31) | copy-start | bytes 786436
  3.9 6.3 %copy-start.26 = (bf16[261,128]{1,0:T(8,128)(2,1)S(1)}, bf16[261,128]{1,0:T(8,128)(2,1)}, u32[]{:S(2)}) copy-start(bf16[261,128]{1,0:T(8,128)(2,1)} %param.27) | copy-start | bytes 200452
  3.9 6.5 %copy-start.24 = (bf16[261,128]{1,0:T(8,128)(2,1)S(1)}, bf16[261,128]{1,0:T(8,128)(2,1)}, u32[]{:S(2)}) copy-start(bf16[261,128]{1,0:T(8,128)(2,1)} %param.28) | copy-start | bytes 200452
  4.9 5.5 %copy-start.6 = (bf16[128,1024]{1,0:T(8,128)(2,1)S(1)}, bf16[128,1024]{1,0:T(8,128)(2,1)}, u32[]{:S(2)}) copy-start(bf16[128,1024]{1,0:T(8,128)(2,1)} %wco_ref.3) | copy-start | bytes 786436
  5.0 5.5 %copy-start.10 = (bf16[128,1024]{1,0:T(8,128)(2,1)S(1)}, bf16[128,1024]{1,0:T(8,128)(2,1)}, u32[]{:S(2)}) copy-start(bf16[128,1024]{1,0:T(8,128)(2,1)} %wq_ref.1) | copy-start | bytes 786436
  5.0 5.5 %copy-start.11 = (bf16[128,1024]{1,0:T(8,128)(2,1)S(1)}, bf16[128,1024]{1,0:T(8,128)(2,1)}, u32[]{:S(2)}) copy-start(bf16[128,1024]{1,0:T(8,128)(2,1)} %refs_1_.1) | copy-start | bytes 786436
  5.0 5.5 %copy-start.18 = (bf16[64,1024]{1,0:T(8,128)(2,1)S(1)}, bf16[64,1024]{1,0:T(8,128)(2,1)}, u32[]{:S(2)}) copy-start(bf16[64,1024]{1,0:T(8,128)(2,1)} %lat_ref.1) | copy-start | bytes 393220
  5.0 5.5 %copy-start.21 = (f32[1024]{0:T(1024)S(1)}, f32[1024]{0:T(1024)}, u32[]{:S(2)}) copy-start(f32[1024]{0:T(1024)} %param.25) | copy-start | bytes 12292
  6.6 121.1 %copy-start = (f32[4,8,6272]{2,1,0:T(8,128)}, f32[4,8,6272]{2,1,0:T(8,128)S(1)}, u32[]{:S(2)}) copy-start(f32[4,8,6272]{2,1,0:T(8,128)S(1)} %pad_maximum_fusion.v_ref) | copy-start | bytes 2408452
  7.4 123.3 %copy-start.28 = (f32[1024]{0:T(1024)S(1)}, f32[1024]{0:T(1024)}, u32[]{:S(2)}) copy-start(f32[1024]{0:T(1024)} %param.38) | copy-start | bytes 12292
  7.4 123.3 %copy-start.29 = (f32[1024]{0:T(1024)S(1)}, f32[1024]{0:T(1024)}, u32[]{:S(2)}) copy-start(f32[1024]{0:T(1024)} %param.33) | copy-start | bytes 12292
  7.4 123.3 %copy-start.30 = (f32[1024]{0:T(1024)S(1)}, f32[1024]{0:T(1024)}, u32[]{:S(2)}) copy-start(f32[1024]{0:T(1024)} %param.30) | copy-start | bytes 12292
  7.6 186.8 %copy-start.1 = (f32[256,512]{1,0:T(8,128)}, f32[256,512]{1,0:T(8,128)S(1)}, u32[]{:S(2)}) copy-start(f32[256,512]{1,0:T(8,128)S(1)} %get-tuple-element.162.gained_ref) | copy-start | bytes 1572868
  7.6 186.8 %copy-start.2 = (f32[256,512]{1,0:T(8,128)}, f32[256,512]{1,0:T(8,128)S(1)}, u32[]{:S(2)}) copy-start(f32[256,512]{1,0:T(8,128)S(1)} %get-tuple-element.163.table_ref) | copy-start | bytes 1572868
  10.5 1.0 copy-start.12
  11.4 0.9 copy-start.13
  12.4 0.9 copy-start.14
  13.3 0.9 copy-start.15
  127.7 0.9 copy-start.7
  128.6 0.7 copy-start.16
  129.3 0.7 copy-start.17
  130.0 1.4 copy-start.19
  194.4 135.5 %copy-start.3 = (bf16[1,8,64,1024]{3,2,1,0:T(8,128)(2,1)S(1)}, bf16[1,8,64,1024]{3,2,1,0:T(8,128)(2,1)}, u32[]{:S(2)}) copy-start(bf16[1,8,64,1024]{3,2,1,0:T(8,128)(2,1)} %get-tuple-element.60) | copy-start | bytes 3145732
  194.4 135.5 %copy-start.4 = (bf16[1,8,128,512]{3,2,1,0:T(8,128)(2,1)S(1)}, bf16[1,8,128,512]{3,2,1,0:T(8,128)(2,1)}, u32[]{:S(2)}) copy-start(bf16[1,8,128,512]{3,2,1,0:T(8,128)(2,1)} %get-tuple-element.79) | copy-start | bytes 3145732
  194.4 135.5 %copy-start.5 = (f32[512,512]{1,0:T(8,128)S(1)}, f32[512,512]{1,0:T(8,128)}, u32[]{:S(2)}) copy-start(f32[512,512]{1,0:T(8,128)} %get-tuple-element.75.a_ref) | copy-start | bytes 3145732
  329.9 1.1 copy-start.8
  331.0 1.0 copy-start.9
  332.0 0.8 copy-start.20
  332.8 13.3 %copy-start.23 = (f32[4,3,6272]{2,1,0:T(4,128)S(1)}, f32[4,3,6272]{2,1,0:T(4,128)}, u32[]{:S(2)}) copy-start(f32[4,3,6272]{2,1,0:T(4,128)} %get-tuple-element.137) | copy-start | bytes 903172
  332.8 14.1 %copy-start.22 = (bf16[4,64,1024]{2,1,0:T(8,128)(2,1)S(1)}, bf16[4,64,1024]{2,1,0:T(8,128)(2,1)}, u32[]{:S(2)}) copy-start(bf16[4,64,1024]{2,1,0:T(8,128)(2,1)} %get-tuple-element.205) | copy-start | bytes 1572868
